TPU v7x, 32 devices: a whole 2x2x4 slice. The times are simulated.
32 devices in a mesh: row: 8 (over z, y), col: 4 (over x, core).
Axes of the slice: x: 2, y: 2, z: 4, core: 2. Of those that a mesh axis runs over, the one named last changes fastest.
Arguments:
- features: float32 [8192, 128], P(('col', 'row')), may hold values from -6 to 6
- weight: float32 [128, 128], replicated, may hold values from -4 to 4
- bias_vector: float32 [128], replicated, may hold values from -4 to 4
- out_grad: float32 [8192, 128], P(('row', 'col')), may hold values from -6 to 6
- adj_tiles: int32 [8, 4, 128, 128, 128], P('row', 'col'), may hold values 0 or 1
- tile_slots: int32 [8, 4, 128], P('row', 'col'), may hold values from 0 to 127, as said below
- tile_counts: int32 [8, 4], P('row', 'col'), may hold values from 17 to 128, as said below
Outputs:
- activated: float32 [8192, 128], P(('row', 'col'))
- feature_grad: float32 [8192, 128], P(('col', 'row'))
- weight_grad: float32 [128, 128], replicated
- bias_grad: float32 [128], replicated
Inputs may be any that keep to these rules, and one draw needn't show every extreme that they name: `tile_slots`: each block's slots name distinct positions r * 16 + c of its 8 x 16 tiles. Some block is full in every draw; slots from tile_counts on are ignored.
All inputs are finite; a program needn't handle non-finite values. No bound on the sum of `adj_tiles` on one device may be relied on, other than what follows from the above.
Results may differ from a plain program's by a relative error of at most 0.0003.
Values sent between devices are 32-bit elements; how exact they have to be, the bound alone decides.
No kernel may reach another device: no remote copies, remote signals or barrier semaphores. Data moves between devices by JAX's collectives and lax.ppermute only.
A program may use at most 128 MiB of HBM per device.

v0:
```python
import jax
import jax.numpy as jnp
from jax import lax
from jax.sharding import PartitionSpec as P

TILE = 128


def dense_step(aggregated, weight, bias_vector, cotangent):
    preact = jnp.dot(aggregated, weight, precision=lax.Precision.HIGHEST) + bias_vector
    logistic = jax.nn.sigmoid(preact)
    activated = preact * logistic
    pre_grad = cotangent * logistic * (1.0 + preact * (1.0 - logistic))
    weight_part = jnp.dot(aggregated.T, pre_grad, precision=lax.Precision.HIGHEST)
    bias_part = jnp.sum(pre_grad, axis=0)
    back_rows = jnp.dot(pre_grad, weight.T, precision=lax.Precision.HIGHEST)
    return (activated, weight_part, bias_part, back_rows)


def local(features, weight, bias_vector, out_grad, adj_tiles, tile_slots, tile_counts):
    row_count = lax.axis_size("row")
    col_count = lax.axis_size("col")
    node_rows = features.shape[0]
    width = features.shape[1]
    tile_rows = node_rows * col_count // TILE
    tile_cols = node_rows * row_count // TILE
    adjacency = adj_tiles[0, 0].astype(jnp.float32)
    slots = tile_slots[0, 0]
    slot_total = slots.shape[0]
    live_mask = (jnp.arange(slot_total) < tile_counts[0, 0]).astype(jnp.float32)
    tile_row = slots // tile_cols
    tile_col = slots % tile_cols
    row_select = (tile_row[:, None] == jnp.arange(tile_rows)[None, :]).astype(
        jnp.float32
    ) * live_mask[:, None]
    col_select = (tile_col[:, None] == jnp.arange(tile_cols)[None, :]).astype(
        jnp.float32
    ) * live_mask[:, None]
    dst_partial = jnp.dot(
        row_select.T, jnp.sum(adjacency, axis=2), precision=lax.Precision.HIGHEST
    ).reshape(-1)
    src_partial = jnp.dot(
        col_select.T, jnp.sum(adjacency, axis=1), precision=lax.Precision.HIGHEST
    ).reshape(-1)
    src_scale = lax.rsqrt(
        1.0 + lax.psum_scatter(src_partial, "row", scatter_dimension=0, tiled=True)
    )
    scaled = features * src_scale[:, None]
    gathered = lax.all_gather(scaled, "row", axis=0, tiled=True)
    taken = jnp.take(gathered.reshape(tile_cols, TILE, width), tile_col, axis=0)
    product = jnp.einsum(
        "kab,kbh->kah",
        adjacency,
        taken,
        precision=lax.Precision.HIGHEST,
        preferred_element_type=jnp.float32,
    )
    partial_value = jnp.einsum(
        "kr,kah->rah",
        row_select,
        product,
        precision=lax.Precision.HIGHEST,
        preferred_element_type=jnp.float32,
    ).reshape(tile_rows * TILE, width)
    cotangent = lax.all_gather(out_grad, "col", axis=0, tiled=True)
    dst_scale = lax.rsqrt(1.0 + lax.psum(dst_partial, "col"))
    aggregated = lax.psum(partial_value, "col") * dst_scale[:, None]
    activated_block, weight_part, bias_part, back_rows = dense_step(
        aggregated, weight, bias_vector, cotangent
    )
    weight_grad, bias_grad = lax.psum((weight_part, bias_part), "row")
    row_grads = back_rows * dst_scale[:, None]
    activated = lax.dynamic_slice_in_dim(
        activated_block, lax.axis_index("col") * node_rows, node_rows, 0
    )
    taken_back = jnp.take(row_grads.reshape(tile_rows, TILE, width), tile_row, axis=0)
    product_back = jnp.einsum(
        "kab,kah->kbh",
        adjacency,
        taken_back,
        precision=lax.Precision.HIGHEST,
        preferred_element_type=jnp.float32,
    )
    partial_back = jnp.einsum(
        "kc,kbh->cbh",
        col_select,
        product_back,
        precision=lax.Precision.HIGHEST,
        preferred_element_type=jnp.float32,
    ).reshape(tile_cols * TILE, width)
    feature_grad = (
        lax.psum_scatter(partial_back, "row", scatter_dimension=0, tiled=True) * src_scale[:, None]
    )
    return (activated, feature_grad, weight_grad, bias_grad)


def solution(mesh):
    return jax.shard_map(
        local,
        mesh=mesh,
        in_specs=(
            P(("col", "row"), None),
            P(),
            P(),
            P(("row", "col"), None),
            P("row", "col", None, None, None),
            P("row", "col", None),
            P("row", "col"),
        ),
        out_specs=(P(("row", "col"), None), P(("col", "row"), None), P(), P()),
        check_vma=False,
    )
```

profile of v0, /device:TPU:0, one launch (start us, length us, event | category | flops | bytes accessed | tf_op | source)
XLA Modules:
  0.0 339.9 jit_solution(7302882445227194683)
XLA Ops:
  8.0 5.7 %convert_reduce_fusion = (f32[128,128]{1,0:T(8,128)S(1)}, f32[128,128]{1,0:T(8,128)S(1)}) fusion(s32[1,1,128,128,128]{4,3,2,1,0:T(8,128)} %param.11), kind=kLoop, calls=%fused_computation.9 | loop fusion | flops 6258688 | bytes 8519680 | tf_op jit(solution)/shard_map/reduce_sum | solution.py:40
  13.9 23.4 %all-reduce = f32[2048]{0:T(1024)S(1)} all-reduce(f32[2048]{0:T(1024)S(1)} %convolution_bitcast_fusion), channel_id=2, replica_groups=mesh['row'=8,'col'=4] {'row'}, use_global_device_ids=true, to_apply=%region_1.2.clone | all-reduce | flops 2048 | bytes 16384
  38.7 0.8 broadcast_multiply_fusion.1
  39.7 7.4 %all_gather.7 = f32[1024,128]{1,0:T(8,128)S(1)} all-gather(f32[256,128]{1,0:T(8,128)S(1)} %copy-done.2), channel_id=1, replica_groups=mesh['row'=8,'col'=4] {'col'}, dimensions={0}, use_global_device_ids=true | all-gather | bytes 655360 | tf_op jit(solution)/shard_map/all_gather | solution.py:65
  47.1 30.0 %all-gather.2.cloned.1.call-done = f32[2048,128]{1,0:T(8,128)} async-done(((f32[256,128]{1,0:T(8,128)}), f32[2048,128]{1,0:T(8,128)}) %all-gather.2.cloned.1.call-update) | async-done | bytes 1048592 | tf_op jit(solution)/shard_map/all_gather | solution.py:49
  77.0 5.5 %gather_fusion = f32[128,128,128]{2,1,0:T(8,128)} fusion(f32[16,128,128]{2,1,0:T(8,128)} %bitcast.77, s32[1024]{0:T(1024)S(1)} %pad_clamp_fusion.1), kind=kCustom, calls=%fused_computation | custom fusion | bytes 16777728 | tf_op jit(solution)/shard_map/jit(_take)/gather | solution.py:50
  82.6 21.5 %fusion.12 = f32[128,128,128]{1,2,0:T(8,128)} fusion(s32[1,1,128,128,128]{4,3,2,1,0:T(8,128)} %param.11, f32[128,128,128]{2,1,0:T(8,128)} %gather_fusion, pred[128]{0:T(512)(128)(4,1)S(1)} %get-tuple-element.15), kind=kOutput, calls=%fused_computation.16 | convolution fusion | flops 3225419776 | bytes 25165952 | tf_op jit(solution)/shard_map/kab,kbh->kah/dot_general | solution.py:51
  104.1 9.3 %copy.18 = f32[128,128,128]{2,0,1:T(8,128)} copy(f32[128,128,128]{1,2,0:T(8,128)} %fusion.12) | data formatting | bytes 16777216 | tf_op jit(solution)/shard_map/kab,kbh->kah/dot_general | solution.py:51
  113.4 6.3 %fusion.30 = f32[8,128,128]{2,0,1:T(8,128)S(1)} fusion(f32[128,128,128]{2,0,1:T(8,128)} %copy.18, f32[128]{0:T(128)S(1)} %get-tuple-element.18, s32[128]{0:T(128)S(1)} %get-tuple-element.9), kind=kOutput, calls=%fused_computation.38 | convolution fusion | flops 201328640 | bytes 8913920 | tf_op jit(solution)/shard_map/kr,kah->rah/dot_general | solution.py:58
  119.7 0.9 copy.19
  120.7 5.7 %psum.29 = f32[1024]{0:T(1024)S(1)} all-reduce(f32[1024]{0:T(1024)S(1)} %convolution_bitcast_fusion.1), channel_id=1, replica_groups=mesh['row'=8,'col'=4] {'col'}, use_global_device_ids=true, to_apply=%region_4.5 | all-reduce | flops 1024 | bytes 8192 | tf_op jit(solution)/shard_map/psum | solution.py:66
  126.4 26.3 %all-reduce.4.cloned.1.call-done = f32[1024,128]{1,0:T(8,128)} async-done(((f32[1024,128]{1,0:T(8,128)}), f32[1024,128]{1,0:T(8,128)}) %all-reduce.4.cloned.1.call-update) | async-done | bytes 524304 | tf_op jit(solution)/shard_map/psum | solution.py:67
  152.7 1.8 fusion.52
  155.1 4.3 %gather_fusion.1 = f32[128,128,128]{2,1,0:T(8,128)} fusion(f32[8,128,128]{2,1,0:T(8,128)S(1)} %bitcast.76, s32[1024]{0:T(1024)S(1)} %pad_clamp_fusion), kind=kCustom, calls=%fused_computation.1 | custom fusion | bytes 16777728 | tf_op jit(solution)/shard_map/jit(_take)/gather | solution.py:76
  159.4 19.7 %fusion.17 = f32[128,128,128]{1,2,0:T(8,128)} fusion(s32[1,1,128,128,128]{4,3,2,1,0:T(8,128)} %param.11, f32[128,128,128]{2,1,0:T(8,128)} %gather_fusion.1, pred[128]{0:T(512)(128)(4,1)S(1)} %get-tuple-element.8), kind=kOutput, calls=%fused_computation.17 | convolution fusion | flops 3225419776 | bytes 25165952 | tf_op jit(solution)/shard_map/kab,kah->kbh/dot_general | solution.py:77
  179.1 9.3 %copy.21 = f32[128,128,128]{2,0,1:T(8,128)} copy(f32[128,128,128]{1,2,0:T(8,128)} %fusion.17) | data formatting | bytes 16777216 | tf_op jit(solution)/shard_map/kab,kah->kbh/dot_general | solution.py:77
  188.4 6.4 %fusion.28 = f32[16,128,128]{2,0,1:T(8,128)S(1)} fusion(f32[128,128,128]{2,0,1:T(8,128)} %copy.21, f32[128]{0:T(128)S(1)} %get-tuple-element.18, s32[128]{0:T(128)S(1)} %get-tuple-element.16), kind=kOutput, calls=%fused_computation.34 | convolution fusion | flops 402657280 | bytes 9438208 | tf_op jit(solution)/shard_map/kc,kbh->cbh/dot_general | solution.py:84
  194.8 1.3 copy.22
  196.2 21.9 %psum.31 = f32[128]{0:T(128)} all-reduce(f32[128]{0:T(128)S(1)} %get-tuple-element.6), channel_id=1, replica_groups=mesh['row'=8,'col'=4] {'row'}, use_global_device_ids=true, to_apply=%region_8.9 | all-reduce | flops 128 | bytes 1024 | tf_op jit(solution)/shard_map/psum | solution.py:71
  218.1 1.8 fusion.22
  220.6 39.5 %reduce-scatter.2.cloned.1.call-done = f32[256,128]{1,0:T(8,128)} async-done(((f32[2048,128]{1,0:T(8,128)}), f32[256,128]{1,0:T(8,128)}) %reduce-scatter.2.cloned.1.call-update) | async-done | bytes 131088 | tf_op jit(solution)/shard_map/reduce_scatter | solution.py:92
  260.1 1.7 broadcast_multiply_fusion
  261.8 70.1 %all-reduce.6.cloned.1.call-done = f32[128,128]{1,0:T(8,128)} async-done(((f32[128,128]{1,0:T(8,128)}), f32[128,128]{1,0:T(8,128)}) %all-reduce.6.cloned.1.call-update) | async-done | bytes 65552 | tf_op jit(solution)/shard_map/psum | solution.py:71
  331.9 1.5 copy.28
  (33 shorter events, 2.5 us)
Async XLA Ops:
  7.2 145.5 %copy-start = (f32[128,128]{1,0:T(8,128)S(1)}, f32[128,128]{1,0:T(8,128)}, u32[]{:S(2)}) copy-start(f32[128,128]{1,0:T(8,128)} %param.8) | copy-start | bytes 196612
  7.2 30.2 %copy-start.6 = (u32[32]{0:T(128)S(1)}, u32[32]{0:T(128)}, u32[]{:S(2)}) copy-start(u32[32]{0:T(128)} %constant.79) | copy-start | bytes 388
  7.2 6.6 %copy-start.4 = (s32[1,1,128]{2,1,0:T(1,128)S(1)}, s32[1,1,128]{2,1,0:T(1,128)}, u32[]{:S(2)}) copy-start(s32[1,1,128]{2,1,0:T(1,128)} %param.12) | copy-start | bytes 1540
  7.2 31.5 %copy-start.3 = (f32[256,128]{1,0:T(8,128)S(1)}, f32[256,128]{1,0:T(8,128)}, u32[]{:S(2)}) copy-start(f32[256,128]{1,0:T(8,128)} %param.7) | copy-start | bytes 393220
  7.2 32.5 %copy-start.2 = (f32[256,128]{1,0:T(8,128)S(1)}, f32[256,128]{1,0:T(8,128)}, u32[]{:S(2)}) copy-start(f32[256,128]{1,0:T(8,128)} %param.10) | copy-start | bytes 393220
  7.2 69.8 %all-gather.2.cloned.1.call-start = ((), (), s32[]{:S(2)}) async-start(), calls=%async_computation.1 | async-start | bytes 1179648 | tf_op jit(solution)/shard_map/all_gather | solution.py:49
  39.5 113.2 %all-reduce.4.cloned.1.call-start = ((), (), s32[]{:S(2)}) async-start(), calls=%async_computation.2 | async-start | bytes 1048576 | tf_op jit(solution)/shard_map/psum | solution.py:67
  113.4 39.3 %copy-start.5 = (f32[128]{0:T(128)S(1)}, f32[128]{0:T(128)}, u32[]{:S(2)}) copy-start(f32[128]{0:T(128)} %param.9) | copy-start | bytes 1540
  120.6 139.5 %reduce-scatter.2.cloned.1.call-start = ((), (), s32[]{:S(2)}) async-start(), calls=%async_computation.3 | async-start | bytes 1179648 | tf_op jit(solution)/shard_map/reduce_scatter | solution.py:92
  188.4 29.7 %copy-start.1 = (f32[1024,128]{1,0:T(8,128)S(1)}, f32[1024,128]{1,0:T(8,128)}, u32[]{:S(2)}) copy-start(f32[1024,128]{1,0:T(8,128)} %all-reduce.4.cloned.1.call-done) | copy-start | bytes 1572868
  196.2 135.7 %all-reduce.6.cloned.1.call-start = ((), (), s32[]{:S(2)}) async-start(), calls=%async_computation.4 | async-start | bytes 131072 | tf_op jit(solution)/shard_map/psum | solution.py:71
Sparse Core Ops, SparseCore 0:
  39.6 37.3 all-gather.1
  120.8 31.8 all-reduce.3
  196.3 63.7 reduce-scatter.1
  264.4 67.4 all-reduce.5
where the time goes:
time: 340 us
  waiting for transfers between devices  166 us (49%)
  matrix products  58.5 us (17%)
  blocking collectives  58.3 us (17%)
  local copies, waits for them, and re-layouts  32.7 us (10%)
  between operations  15.3 us (4%)
  other arithmetic  8.96 us (3%)
    psum x1, waiting for transfers between devices, local(): weight_grad, bias_grad = lax.psum((weight_part, bias_part), 'row')  70.1 us
    reduce_scatter x1, waiting for transfers between devices, local(): lax.psum_scatter(partial_back, 'row', scatter_dimension=0, tiled=True)  39.5 us
    all_gather x1, waiting for transfers between devices, local(): gathered = lax.all_gather(scaled, 'row', axis=0, tiled=True)  30 us
    psum x1, waiting for transfers between devices, local(): aggregated = lax.psum(partial_value, 'col') * dst_scale[:, None]  26.3 us
    unnamed x1, blocking collectives  23.4 us
    psum x1, blocking collectives, local(): weight_grad, bias_grad = lax.psum((weight_part, bias_part), 'row')  21.9 us
    dot_general x1, matrix products, local(): jnp.einsum('kab,kbh->kah', adjacency, taken, precision=lax.Precision.HIGH...  21.5 us
    dot_general x1, matrix products, local(): jnp.einsum('kab,kah->kbh', adjacency, taken_back, precision=lax.Precision...  19.7 us
  transfers between devices with their start and end apart: 4, of which 4 were waited for; matrix products, arithmetic and copies ran while one was open for 1% of the time, Pallas kernels for 0%

commit v1 on v0

v1 whole, which is shorter than its diff:
```python
import functools

import jax
import jax.numpy as jnp
from jax import lax
from jax.experimental import pallas as pl
from jax.experimental.pallas import tpu as pltpu
from jax.sharding import PartitionSpec as P

TILE = 128
PAD = 8
F32 = jnp.float32
BF16 = jnp.bfloat16
HIGHEST = lax.Precision.HIGHEST
VMEM_LIMIT = 56 * 1024 * 1024


def nt_dot(lhs, rhs, **kw):
    return lax.dot_general(lhs, rhs, (((1,), (1,)), ((), ())), preferred_element_type=F32, **kw)


def tn_dot(lhs, rhs, **kw):
    return lax.dot_general(lhs, rhs, (((0,), (0,)), ((), ())), preferred_element_type=F32, **kw)


def split(value):
    high = value.astype(BF16)
    low = (value - high.astype(F32)).astype(BF16)
    return high, low


def vmem_specs(count):
    return [pl.BlockSpec(memory_space=pltpu.VMEM)] * count


def params():
    return pltpu.CompilerParams(vmem_limit_bytes=VMEM_LIMIT)


def cost(flops, moved):
    return pl.CostEstimate(flops=int(flops), bytes_accessed=int(moved), transcendentals=0)


def densify_kernel(
    tile_rows, tile_cols, pieces, slots_ref, counts_ref, tiles_hbm,
    dense_ref, col_ref, row_ref, tiles, col_acc, row_acc, sems,
):
    slot_total = tiles.shape[0]
    piece = slot_total // pieces
    copies = [
        pltpu.make_async_copy(
            tiles_hbm.at[pl.ds(p * piece, piece)], tiles.at[pl.ds(p * piece, piece)], sems.at[p]
        )
        for p in range(pieces)
    ]
    for copy in copies:
        copy.start()
    if slot_total < tile_rows * tile_cols:
        dense_ref[...] = jnp.zeros_like(dense_ref)
    col_acc[...] = jnp.zeros_like(col_acc)
    row_acc[...] = jnp.zeros_like(row_acc)
    live = counts_ref[0]

    def place(k, carry):
        slot = slots_ref[k]
        r = slot // tile_cols
        c = slot % tile_cols
        keep = jnp.where(k < live, 1, 0)
        tile = tiles[k] * keep
        dense_ref[
            pl.ds(pl.multiple_of(r * TILE, TILE), TILE), pl.ds(pl.multiple_of(c * TILE, TILE), TILE)
        ] = tile.astype(F32).astype(BF16)
        col_acc[c] += jnp.sum(tile.reshape(TILE // 8, 8, TILE), axis=0)
        row_acc[r] += tile
        return carry

    for p in range(pieces):
        copies[p].wait()
        lax.fori_loop(p * piece, (p + 1) * piece, place, 0, unroll=4)
    col_ref[...] = jnp.sum(col_acc[...], axis=1).astype(F32)
    ones = jnp.ones((8, TILE), BF16)
    for r in range(tile_rows):
        sums = nt_dot(ones, row_acc[r].astype(F32).astype(BF16))
        row_ref[pl.ds(r, 1), :] = sums[0:1, :]


def densify(slots, counts, tiles, tile_rows, tile_cols):
    slot_total = tiles.shape[0]
    pieces = 8
    rows, cols = tile_rows * TILE, tile_cols * TILE
    return pl.pallas_call(
        functools.partial(densify_kernel, tile_rows, tile_cols, pieces),
        out_shape=(
            jax.ShapeDtypeStruct((rows, cols), BF16),
            jax.ShapeDtypeStruct((tile_cols, TILE), F32),
            jax.ShapeDtypeStruct((tile_rows, TILE), F32),
        ),
        in_specs=[
            pl.BlockSpec(memory_space=pltpu.SMEM),
            pl.BlockSpec(memory_space=pltpu.SMEM),
            pl.BlockSpec(memory_space=pl.ANY),
        ],
        out_specs=tuple(vmem_specs(3)),
        scratch_shapes=[
            pltpu.VMEM(tiles.shape, jnp.int32),
            pltpu.VMEM((tile_cols, 8, TILE), jnp.int32),
            pltpu.VMEM((tile_rows, TILE, TILE), jnp.int32),
            pltpu.SemaphoreType.DMA((pieces,)),
        ],
        compiler_params=params(),
        cost_estimate=cost(0, slot_total * TILE * TILE * 4 + rows * cols * 2),
        name="densify",
    )(slots, counts, tiles)


def scales_kernel(parts, own_tiles, *refs):
    sums, (wide_ref, own_ref) = refs[:parts], refs[parts:]
    total = sums[0][...]
    for ref in sums[1:]:
        total = total + ref[...]
    scale = lax.rsqrt(1.0 + total)
    tile_cols = scale.shape[0]
    for c in range(tile_cols):
        wide_ref[pl.ds(c * TILE, TILE), :] = jnp.broadcast_to(scale[c : c + 1, :], (TILE, TILE)).T
    own_ref[...] = scale


def source_scales(sums, own_tiles):
    tile_cols = sums[0].shape[0]
    return pl.pallas_call(
        functools.partial(scales_kernel, len(sums), own_tiles),
        out_shape=(
            jax.ShapeDtypeStruct((tile_cols * TILE, TILE), F32),
            jax.ShapeDtypeStruct((tile_cols, TILE), F32),
        ),
        in_specs=vmem_specs(len(sums)),
        out_specs=tuple(vmem_specs(2)),
        compiler_params=params(),
        cost_estimate=cost(0, tile_cols * TILE * TILE * 8),
        name="source_scales",
    )(*sums)


def forward_kernel(row_count, col_count, *refs):
    dense_ref, wide_ref, row_ref = refs[:3]
    blocks = refs[3 : 3 + row_count]
    outs = refs[3 + row_count : 3 + row_count + col_count]
    rhs = refs[-1]
    row = lax.axis_index("row")
    col = lax.axis_index("col")
    node_rows, width = blocks[0].shape
    for m in range(row_count):
        start = pl.multiple_of((row ^ m) * node_rows, node_rows)
        high, low = split(blocks[m][...] * wide_ref[pl.ds(start, node_rows), :])
        rhs[pl.ds(start, node_rows), :width] = high
        rhs[pl.ds(start, node_rows), width:] = low
    own_tiles = node_rows // TILE
    for m in list(range(1, col_count)) + [0]:
        peer = col ^ m
        start = pl.multiple_of(peer * node_rows, node_rows)
        both = jnp.dot(dense_ref[pl.ds(start, node_rows), :], rhs[...], preferred_element_type=F32)
        outs[m][pl.ds(0, node_rows), :] = both[:, :width] + both[:, width:]
        outs[m][pl.ds(node_rows, PAD), :] = jnp.zeros((PAD, width), F32)
        for t in range(own_tiles):
            outs[m][pl.ds(node_rows + t, 1), :] = row_ref[pl.ds(peer * own_tiles + t, 1), :]


def forward(dense, wide, row_sums, blocks, row_count, col_count):
    node_rows, width = blocks[0].shape
    rows, cols = dense.shape
    return pl.pallas_call(
        functools.partial(forward_kernel, row_count, col_count),
        out_shape=tuple(
            jax.ShapeDtypeStruct((node_rows + PAD, width), F32) for _ in range(col_count)
        ),
        in_specs=vmem_specs(3 + row_count),
        out_specs=tuple(vmem_specs(col_count)),
        scratch_shapes=[pltpu.VMEM((cols, 2 * width), BF16)],
        compiler_params=params(),
        cost_estimate=cost(4 * rows * cols * width, rows * cols * 2),
        name="forward",
    )(dense, wide, row_sums, *blocks)


def node_kernel(parts, *refs):
    pieces = refs[:parts]
    cot_ref, weight_ref, bias_ref, act_ref, back_ref, grad_ref = refs[parts:]
    node_rows, width = cot_ref.shape
    total = pieces[0][...]
    for ref in pieces[1:]:
        total = total + ref[...]
    own_tiles = node_rows // TILE
    scale = lax.rsqrt(1.0 + total[node_rows:, :])
    wide = jnp.concatenate(
        [jnp.broadcast_to(scale[t : t + 1, :], (TILE, TILE)).T for t in range(own_tiles)], axis=0
    )
    flat = jnp.concatenate([scale[t : t + 1, :] for t in range(own_tiles)], axis=1)
    weight = weight_ref[...]
    aggregated = total[:node_rows, :] * wide
    preact = (
        jnp.dot(aggregated, weight, precision=HIGHEST, preferred_element_type=F32) + bias_ref[...]
    )
    logistic = jax.nn.sigmoid(preact)
    act_ref[...] = preact * logistic
    pre_grad = cot_ref[...] * logistic * (1.0 + preact * (1.0 - logistic))
    back_ref[...] = nt_dot(weight, pre_grad, precision=HIGHEST) * flat
    grad_ref[pl.ds(0, width), :] = tn_dot(aggregated, pre_grad, precision=HIGHEST)
    grad_ref[pl.ds(width, PAD), :] = jnp.broadcast_to(
        jnp.sum(pre_grad, axis=0, keepdims=True), (PAD, width)
    )


def node_step(pieces, cotangent, weight, bias):
    node_rows, width = cotangent.shape
    return pl.pallas_call(
        functools.partial(node_kernel, len(pieces)),
        out_shape=(
            jax.ShapeDtypeStruct((node_rows, width), F32),
            jax.ShapeDtypeStruct((width, node_rows), F32),
            jax.ShapeDtypeStruct((width + PAD, width), F32),
        ),
        in_specs=vmem_specs(len(pieces) + 3),
        out_specs=tuple(vmem_specs(3)),
        compiler_params=params(),
        cost_estimate=cost(6 * 6 * node_rows * width * width, 4 * 8 * node_rows * width),
        name="node_step",
    )(*pieces, cotangent, weight, bias)


def backward_kernel(row_count, col_count, grad_parts, *refs):
    dense_ref = refs[0]
    blocks = refs[1 : 1 + col_count]
    grads = refs[1 + col_count : 1 + col_count + grad_parts]
    rest = refs[1 + col_count + grad_parts :]
    outs, sum_ref, lhs = rest[:row_count], rest[row_count], rest[row_count + 1]
    row = lax.axis_index("row")
    col = lax.axis_index("col")
    width, node_rows = blocks[0].shape
    for m in range(col_count):
        start = pl.multiple_of((col ^ m) * node_rows, node_rows)
        high, low = split(blocks[m][...])
        lhs[:width, pl.ds(start, node_rows)] = high
        lhs[width:, pl.ds(start, node_rows)] = low
    for m in list(range(1, row_count)) + [0]:
        start = pl.multiple_of((row ^ m) * node_rows, node_rows)
        both = jnp.dot(lhs[...], dense_ref[:, pl.ds(start, node_rows)], preferred_element_type=F32)
        outs[m][...] = both[:width, :] + both[width:, :]
    total = grads[0][...]
    for ref in grads[1:]:
        total = total + ref[...]
    sum_ref[...] = total


def backward(dense, blocks, grads, row_count):
    width, node_rows = blocks[0].shape
    rows, cols = dense.shape
    return pl.pallas_call(
        functools.partial(backward_kernel, row_count, len(blocks), len(grads)),
        out_shape=tuple(jax.ShapeDtypeStruct((width, node_rows), F32) for _ in range(row_count))
        + (jax.ShapeDtypeStruct(grads[0].shape, F32),),
        in_specs=vmem_specs(1 + len(blocks) + len(grads)),
        out_specs=tuple(vmem_specs(row_count + 1)),
        scratch_shapes=[pltpu.VMEM((2 * width, rows), BF16)],
        compiler_params=params(),
        cost_estimate=cost(4 * rows * cols * width, rows * cols * 2),
        name="backward",
    )(dense, *blocks, *grads)


def sums_kernel(counts, *refs):
    outs = refs[sum(counts) :]
    at = 0
    for out_ref, count in zip(outs, counts):
        total = refs[at][...]
        for ref in refs[at + 1 : at + count]:
            total = total + ref[...]
        out_ref[...] = total
        at += count


def sums(*groups):
    flat = [array for group in groups for array in group]
    return pl.pallas_call(
        functools.partial(sums_kernel, tuple(len(group) for group in groups)),
        out_shape=tuple(jax.ShapeDtypeStruct(group[0].shape, F32) for group in groups),
        in_specs=vmem_specs(len(flat)),
        out_specs=tuple(vmem_specs(len(groups))),
        compiler_params=params(),
        cost_estimate=cost(0, sum(4 * array.size for array in flat)),
        name="sums",
    )(*flat)


def finish_kernel(parts, grad_parts, *refs):
    pieces = refs[:parts]
    grads = refs[parts : parts + grad_parts]
    scale_ref, out_ref, weight_ref, bias_ref = refs[parts + grad_parts :]
    row = lax.axis_index("row")
    total = pieces[0][...]
    for ref in pieces[1:]:
        total = total + ref[...]
    width, node_rows = total.shape
    own_tiles = node_rows // TILE
    for t in range(own_tiles):
        part = total[:, t * TILE : (t + 1) * TILE] * scale_ref[pl.ds(row * own_tiles + t, 1), :]
        out_ref[pl.ds(t * TILE, TILE), :] = part.T
    total = grads[0][...]
    for ref in grads[1:]:
        total = total + ref[...]
    weight_ref[...] = total[:width, :]
    bias_ref[...] = total[width : width + 1, :]


def finish(pieces, grads, scale):
    width, node_rows = pieces[0].shape
    return pl.pallas_call(
        functools.partial(finish_kernel, len(pieces), len(grads)),
        out_shape=(
            jax.ShapeDtypeStruct((node_rows, width), F32),
            jax.ShapeDtypeStruct((width, width), F32),
            jax.ShapeDtypeStruct((1, width), F32),
        ),
        in_specs=vmem_specs(len(pieces) + len(grads) + 1),
        out_specs=tuple(vmem_specs(3)),
        compiler_params=params(),
        cost_estimate=cost(0, 4 * 6 * node_rows * width),
        name="finish",
    )(*pieces, *grads, scale)


def swap(value, axis, mask):
    count = lax.axis_size(axis)
    return lax.ppermute(value, axis, [(i, i ^ mask) for i in range(count)])


def local(features, weight, bias_vector, out_grad, adj_tiles, tile_slots, tile_counts):
    row_count = lax.axis_size("row")
    col_count = lax.axis_size("col")
    node_rows, width = features.shape
    tile_rows = node_rows * col_count // TILE
    tile_cols = node_rows * row_count // TILE
    top = row_count // 2

    blocks = [None] * row_count
    blocks[0] = features
    blocks[top] = swap(features, "row", top)
    for m in range(1, top):
        blocks[m] = swap(features, "row", m)
    for m in range(1, top):
        blocks[top | m] = swap(blocks[top], "row", m)

    dense, col_sums, row_sums = densify(
        tile_slots[0, 0], tile_counts[0], adj_tiles[0, 0], tile_rows, tile_cols
    )
    col_parts = [col_sums] + [swap(col_sums, "row", m) for m in range(1, row_count)]
    wide, scale = source_scales(col_parts, node_rows // TILE)
    partial = forward(dense, wide, row_sums, blocks, row_count, col_count)
    pieces = [partial[0]] + [swap(partial[m], "col", m) for m in range(1, col_count)]
    activated, back, grads = node_step(pieces, out_grad, weight, bias_vector[None, :])

    backs = [back] + [swap(back, "col", m) for m in range(1, col_count)]
    late = 2
    early = [m for m in range(1, row_count) if not m & late]
    grad_parts = [grads] + [swap(grads, "row", m) for m in early]
    out = backward(dense, backs, grad_parts, row_count)
    chunks, grads = out[:row_count], out[row_count]

    ahead = [chunks[top]] + [swap(chunks[top | m], "row", m) for m in range(1, top)]
    mine = [chunks[0]] + [swap(chunks[m], "row", m) for m in range(1, top)]
    grad_parts = [grads] + [swap(grads, "col", m) for m in range(1, col_count)]
    passed, grads = sums(ahead, grad_parts)
    mine.append(swap(passed, "row", top))
    grad_parts = [grads, swap(grads, "row", late)]
    feature_grad, weight_grad, bias_grad = finish(mine, grad_parts, scale)
    return activated, feature_grad, weight_grad, bias_grad[0]


def solution(mesh):
    return jax.shard_map(
        local,
        mesh=mesh,
        in_specs=(
            P(("col", "row"), None),
            P(),
            P(),
            P(("row", "col"), None),
            P("row", "col", None, None, None),
            P("row", "col", None),
            P("row", "col"),
        ),
        out_specs=(P(("row", "col"), None), P(("col", "row"), None), P(), P()),
        check_vma=False,
    )
```

time: 340 us -> 98.4 us (0.29)
  waiting for transfers between devices: 166 us -> 30.6 us
  matrix products: 58.5 us -> 0 us
  blocking collectives: 58.3 us -> 0 us
  starting transfers between devices: 0.16 us -> 37.3 us
  local copies, waits for them, and re-layouts: 32.7 us -> 3.96 us
  Pallas kernels: 0 us -> 24.8 us
  between operations: 15.3 us -> 1.56 us
  other arithmetic: 8.96 us -> 0 us
    psum x2 -> x0, waiting for transfers between devices: 96.4 us -> none  [the longest x1 70.1 us: local(): weight_grad, bias_grad = lax.psum((weight_part, bias_part), 'row')]
    dot_general x9 -> x0, matrix products: 58.5 us -> none  [the longest x1 21.5 us: local(): jnp.einsum('kab,kbh->kah', adjacency, taken, precision=lax.Precision.HIGH...]
    reduce_scatter x1 -> x0, waiting for transfers between devices: 39.5 us -> none  [local(): lax.psum_scatter(partial_back, 'row', scatter_dimension=0, tiled=True)]
    ppermute x0 -> x34, starting transfers between devices: none -> 37.3 us  [swap(): return lax.ppermute(value, axis, [(i, i ^ mask) for i in range(count)])]
    ppermute x0 -> x34, waiting for transfers between devices: none -> 30.6 us  [swap(): return lax.ppermute(value, axis, [(i, i ^ mask) for i in range(count)])]
    all_gather x1 -> x0, waiting for transfers between devices: 30 us -> none  [local(): gathered = lax.all_gather(scaled, 'row', axis=0, tiled=True)]
    psum x2 -> x0, blocking collectives: 27.5 us -> none  [the longest x1 21.9 us: local(): weight_grad, bias_grad = lax.psum((weight_part, bias_part), 'row')]
    pallas_call x0 -> x7, Pallas kernels: none -> 24.8 us  [the longest x1 6.39 us: densify(): pl.pallas_call(functools.partial(densify_kernel, tile_rows, tile_cols, pi...]
  transfers between devices with their start and end apart: 4 -> 34, of which waited for: 4 -> 18; matrix products, arithmetic and copies ran while one was open for 1% -> 0% of each run, Pallas kernels for 0% -> 11%
where the time goes in v1:
time: 98.4 us; the launch traced here: 98.1 us
  starting transfers between devices  37.3 us (38%)
  waiting for transfers between devices  30.6 us (31%)
  Pallas kernels  24.8 us (25%)
  local copies, waits for them, and re-layouts  3.96 us (4%)
  between operations  1.56 us (2%)
    ppermute x34, starting transfers between devices, swap(): return lax.ppermute(value, axis, [(i, i ^ mask) for i in range(count)])  37.3 us
    ppermute x34, waiting for transfers between devices, swap(): return lax.ppermute(value, axis, [(i, i ^ mask) for i in range(count)])  30.6 us
    pallas_call x1, Pallas kernels, densify(): pl.pallas_call(functools.partial(densify_kernel, tile_rows, tile_cols, pi...  6.39 us
    pallas_call x1, Pallas kernels, forward(): pl.pallas_call(functools.partial(forward_kernel, row_count, col_count), o...  4.95 us
    pallas_call x1, Pallas kernels, backward(): pl.pallas_call(functools.partial(backward_kernel, row_count, len(blocks),...  4.63 us
    unnamed x70, local copies, waits for them, and re-layouts  3.96 us
    pallas_call x1, Pallas kernels, node_step(): pl.pallas_call(functools.partial(node_kernel, len(pieces)), out_shape=(ja...  2.72 us
    pallas_call x1, Pallas kernels, source_scales(): pl.pallas_call(functools.partial(scales_kernel, len(sums), own_tiles), ou...  2.17 us
  transfers between devices with their start and end apart: 34, of which 18 were waited for; matrix products, arithmetic and copies ran while one was open for 0% of the time, Pallas kernels for 11%

profile of v1, /device:TPU:0, one launch (start us, length us, event | category | flops | bytes accessed | tf_op | source)
XLA Modules:
  0.0 98.1 jit_solution(13363355066934543248)
XLA Ops:
  0.6 4.1 %collective-permute-start.10 = (f32[256,128]{1,0:T(8,128)}, f32[256,128]{1,0:T(8,128)S(1)}, u32[]{:S(2)}, u32[]{:S(2)}) collective-permute-start(f32[256,128]{1,0:T(8,128)} %refs_3_.1), channel_id=1, source_target_pairs={{0,16},{4,20},{8,24},{12,28},{16,0},{20,4},{24,8},{28,12},{1,17},{... | collective-permute-start | bytes 393224 | tf_op jit(solution)/shard_map/ppermute | solution.py:333
  4.7 2.5 %collective-permute-start.9 = (f32[256,128]{1,0:T(8,128)}, f32[256,128]{1,0:T(8,128)S(1)}, u32[]{:S(2)}, u32[]{:S(2)}) collective-permute-start(f32[256,128]{1,0:T(8,128)} %refs_3_.1), channel_id=1, source_target_pairs={{0,12},{4,8},{8,4},{12,0},{16,28},{20,24},{24,20},{28,16},{1,13},{... | collective-permute-start | bytes 393224 | tf_op jit(solution)/shard_map/ppermute | solution.py:333
  7.9 6.4 %densify.1 = (bf16[1024,2048]{1,0:T(8,128)(2,1)}, f32[16,128]{1,0:T(8,128)}, f32[8,128]{1,0:T(8,128)}) custom-call(s32[128]{0:T(128)} %bitcast.7, s32[1]{0:T(128)} %bitcast.5.counts_ref, s32[128,128,128]{2,1,0:T(8,128)} %bitcast.6), custom_call_target="tpu_custom_call" | custom-call | bytes 12582912 | tf_op jit(solution)/shard_map/densify/pallas_call | solution.py:91
  14.4 3.8 %collective-permute-start.5 = (f32[16,128]{1,0:T(8,128)}, f32[16,128]{1,0:T(8,128)S(1)}, u32[]{:S(2)}, u32[]{:S(2)}) collective-permute-start(f32[16,128]{1,0:T(8,128)} %get-tuple-element.31.refs_0_), channel_id=1, source_target_pairs={{0,24},{4,28},{8,16},{12,20},{16,8},{20,12},{24,0},{28,4},{1,25},{... | collective-permute-start | bytes 24584 | tf_op jit(solution)/shard_map/ppermute | solution.py:333
  18.2 2.8 %collective-permute-done.6.refs_7_ = f32[16,128]{1,0:T(8,128)S(1)} collective-permute-done((f32[16,128]{1,0:T(8,128)}, f32[16,128]{1,0:T(8,128)S(1)}, u32[]{:S(2)}, u32[]{:S(2)}) %collective-permute-start.6) | collective-permute-done | bytes 8224 | tf_op jit(solution)/shard_map/ppermute | solution.py:333
  22.1 1.8 %collective-permute-done.4.refs_5_ = f32[16,128]{1,0:T(8,128)S(1)} collective-permute-done((f32[16,128]{1,0:T(8,128)}, f32[16,128]{1,0:T(8,128)S(1)}, u32[]{:S(2)}, u32[]{:S(2)}) %collective-permute-start.4) | collective-permute-done | bytes 8224 | tf_op jit(solution)/shard_map/ppermute | solution.py:333
  24.0 1.7 %collective-permute-done.3.refs_4_ = f32[16,128]{1,0:T(8,128)S(1)} collective-permute-done((f32[16,128]{1,0:T(8,128)}, f32[16,128]{1,0:T(8,128)S(1)}, u32[]{:S(2)}, u32[]{:S(2)}) %collective-permute-start.3) | collective-permute-done | bytes 8224 | tf_op jit(solution)/shard_map/ppermute | solution.py:333
  32.8 2.2 %source_scales.1 = (f32[2048,128]{1,0:T(8,128)}, f32[16,128]{1,0:T(8,128)}) custom-call(f32[16,128]{1,0:T(8,128)} %get-tuple-element.31.refs_0_, f32[16,128]{1,0:T(8,128)} %copy-done.34, f32[16,128]{1,0:T(8,128)} %copy-done.33, f32[16,128]{1,0:T(8,128)} %copy-done.32, f32[16,128]{1,0:T(8,128)} %copy-done.31, f32[16,128]{1,0:T(8,128)} %copy-done.30, ...), custom_call_target="tpu_custom_call" | custom-call | bytes 2097152 | tf_op jit(solution)/shard_map/source_scales/pallas_call | solution.py:130
  37.1 4.9 %forward.1 = (f32[264,128]{1,0:T(8,128)}, f32[264,128]{1,0:T(8,128)}, f32[264,128]{1,0:T(8,128)}, f32[264,128]{1,0:T(8,128)}) custom-call(bf16[1024,2048]{1,0:T(8,128)(2,1)} %get-tuple-element.30.refs_0_, f32[2048,128]{1,0:T(8,128)} %get-tuple-element.32.refs_1_, f32[8,128]{1,0:T(8,128)} %get-tuple-element.33.refs_2_, f32[256,128]{1,0:T(8,128)} %refs_3_.1, ...), custom_call_target="tpu_custom_call" | custom-call | flops 1073741824 | bytes 4194304 | tf_op jit(solution)/shard_map/forward/pallas_call | solution.py:171
  43.9 4.8 %collective-permute-done.15.refs_2_ = f32[264,128]{1,0:T(8,128)S(1)} collective-permute-done((f32[264,128]{1,0:T(8,128)}, f32[264,128]{1,0:T(8,128)S(1)}, u32[]{:S(2)}, u32[]{:S(2)}) %collective-permute-start.15) | collective-permute-done | bytes 135200 | tf_op jit(solution)/shard_map/ppermute | solution.py:333
  48.7 2.0 %collective-permute-done.16.refs_3_ = f32[264,128]{1,0:T(8,128)S(1)} collective-permute-done((f32[264,128]{1,0:T(8,128)}, f32[264,128]{1,0:T(8,128)S(1)}, u32[]{:S(2)}, u32[]{:S(2)}) %collective-permute-start.16) | collective-permute-done | bytes 135200 | tf_op jit(solution)/shard_map/ppermute | solution.py:333
  51.4 2.7 %node_step.1 = (f32[256,128]{1,0:T(8,128)}, f32[128,256]{1,0:T(8,128)}, f32[136,128]{1,0:T(8,128)}) custom-call(f32[264,128]{1,0:T(8,128)} %get-tuple-element.34.refs_0_, f32[264,128]{1,0:T(8,128)} %copy-done, f32[264,128]{1,0:T(8,128)} %copy-done.1, f32[264,128]{1,0:T(8,128)} %copy-done.2, f32[256,128]{1,0:T(8,128)} %refs_4_.1, f32[128,128]{1,0:T(8,128)} %refs_5_.1, ...), custom_call_target="tpu_custom_call" | custom-call | flops 150994944 | bytes 1048576 | tf_op jit(solution)/shard_map/node_step/pallas_call | solution.py:215
  54.1 2.2 %collective-permute-start.22 = (f32[136,128]{1,0:T(8,128)}, f32[136,128]{1,0:T(8,128)S(1)}, u32[]{:S(2)}, u32[]{:S(2)}) collective-permute-start(f32[136,128]{1,0:T(8,128)} %get-tuple-element.40.refs_5_), channel_id=1, source_target_pairs={{0,20},{4,16},{8,28},{12,24},{16,4},{20,0},{24,12},{28,8},{1,21},{... | collective-permute-start | bytes 208904 | tf_op jit(solution)/shard_map/ppermute | solution.py:333
  59.6 2.4 %collective-permute-done.22.refs_8_ = f32[136,128]{1,0:T(8,128)S(1)} collective-permute-done((f32[136,128]{1,0:T(8,128)}, f32[136,128]{1,0:T(8,128)S(1)}, u32[]{:S(2)}, u32[]{:S(2)}) %collective-permute-start.22) | collective-permute-done | bytes 69664 | tf_op jit(solution)/shard_map/ppermute | solution.py:333
  63.2 2.0 %collective-permute-done.21.refs_7_ = f32[136,128]{1,0:T(8,128)S(1)} collective-permute-done((f32[136,128]{1,0:T(8,128)}, f32[136,128]{1,0:T(8,128)S(1)}, u32[]{:S(2)}, u32[]{:S(2)}) %collective-permute-start.21) | collective-permute-done | bytes 69664 | tf_op jit(solution)/shard_map/ppermute | solution.py:333
  67.9 4.6 %backward.1 = (f32[128,256]{1,0:T(8,128)}, f32[128,256]{1,0:T(8,128)}, f32[128,256]{1,0:T(8,128)}, f32[128,256]{1,0:T(8,128)}, f32[128,256]{1,0:T(8,128)}, /*ind...) custom-call(bf16[1024,2048]{1,0:T(8,128)(2,1)} %get-tuple-element.30.refs_0_, ...), custom_call_target="tpu_custom_call" | custom-call | flops 1073741824 | bytes 4194304 | tf_op jit(solution)/shard_map/backward/pallas_call | solution.py:257
  74.2 1.9 %collective-permute-start.28 = (f32[128,256]{1,0:T(8,128)}, f32[128,256]{1,0:T(8,128)S(1)}, u32[]{:S(2)}, u32[]{:S(2)}) collective-permute-start(f32[128,256]{1,0:T(8,128)} %get-tuple-element.48), channel_id=1, source_target_pairs={{0,12},{4,8},{8,4},{12,0},{16,28},{20,24},{24,20},{28,16},{1,13},{... | collective-permute-start | bytes 393224 | tf_op jit(solution)/shard_map/ppermute | solution.py:333
  77.6 3.5 %collective-permute-done.30.refs_6_ = f32[136,128]{1,0:T(8,128)S(1)} collective-permute-done((f32[136,128]{1,0:T(8,128)}, f32[136,128]{1,0:T(8,128)S(1)}, u32[]{:S(2)}, u32[]{:S(2)}) %collective-permute-start.30) | collective-permute-done | bytes 69664 | tf_op jit(solution)/shard_map/ppermute | solution.py:333
  82.6 2.0 %collective-permute-start.25 = (f32[128,256]{1,0:T(8,128)}, f32[128,256]{1,0:T(8,128)S(1)}, u32[]{:S(2)}, u32[]{:S(2)}) collective-permute-start(f32[128,256]{1,0:T(8,128)} %get-tuple-element.44), channel_id=1, source_target_pairs={{0,12},{4,8},{8,4},{12,0},{16,28},{20,24},{24,20},{28,16},{1,13},{... | collective-permute-start | bytes 393224 | tf_op jit(solution)/shard_map/ppermute | solution.py:333
  85.3 1.9 %sums.1 = (f32[128,256]{1,0:T(8,128)}, f32[136,128]{1,0:T(8,128)}) custom-call(f32[128,256]{1,0:T(8,128)} %get-tuple-element.45.refs_0_, f32[128,256]{1,0:T(8,128)} %copy-done.11, f32[128,256]{1,0:T(8,128)} %copy-done.12, f32[128,256]{1,0:T(8,128)} %copy-done.14, f32[136,128]{1,0:T(8,128)} %get-tuple-element.49.refs_4_, f32[136,128]{1,0:T(8,128)} %copy-done.26, ...), custom_call_target="tpu_custom_call" | custom-call | bytes 802816 | tf_op jit(solution)/shard_map/sums/pallas_call | solution.py:283
  88.3 1.7 %collective-permute-start.33 = (f32[136,128]{1,0:T(8,128)}, f32[136,128]{1,0:T(8,128)S(1)}, u32[]{:S(2)}, u32[]{:S(2)}) collective-permute-start(f32[136,128]{1,0:T(8,128)} %get-tuple-element.51.refs_5_), channel_id=1, source_target_pairs={{0,8},{4,12},{8,0},{12,4},{16,24},{20,28},{24,16},{28,20},{1,9},{5... | collective-permute-start | bytes 208904 | tf_op jit(solution)/shard_map/ppermute | solution.py:333
  91.1 2.2 %collective-permute-done.33.refs_6_ = f32[136,128]{1,0:T(8,128)S(1)} collective-permute-done((f32[136,128]{1,0:T(8,128)}, f32[136,128]{1,0:T(8,128)S(1)}, u32[]{:S(2)}, u32[]{:S(2)}) %collective-permute-start.33) | collective-permute-done | bytes 69664 | tf_op jit(solution)/shard_map/ppermute | solution.py:333
  93.3 2.2 %collective-permute-done.32.refs_4_ = f32[128,256]{1,0:T(8,128)S(1)} collective-permute-done((f32[128,256]{1,0:T(8,128)}, f32[128,256]{1,0:T(8,128)S(1)}, u32[]{:S(2)}, u32[]{:S(2)}) %collective-permute-start.32) | collective-permute-done | bytes 131104 | tf_op jit(solution)/shard_map/ppermute | solution.py:333
  96.2 2.0 %finish.1 = (f32[256,128]{1,0:T(8,128)}, f32[128,128]{1,0:T(8,128)}, f32[1,128]{1,0:T(1,128)}) custom-call(f32[128,256]{1,0:T(8,128)} %get-tuple-element.41.refs_0_, f32[128,256]{1,0:T(8,128)} %copy-done.6, f32[128,256]{1,0:T(8,128)} %copy-done.7, f32[128,256]{1,0:T(8,128)} %copy-done.10, f32[128,256]{1,0:T(8,128)} %copy-done.20, ...), custom_call_target="tpu_custom_call" | custom-call | bytes 786432 | tf_op jit(solution)/shard_map/finish/pallas_call | solution.py:316
  (121 shorter events, 28.2 us)
Async XLA Ops:
  0.6 28.6 %collective-permute-start.10 = (f32[256,128]{1,0:T(8,128)}, f32[256,128]{1,0:T(8,128)S(1)}, u32[]{:S(2)}, u32[]{:S(2)}) collective-permute-start(f32[256,128]{1,0:T(8,128)} %refs_3_.1), channel_id=1, source_target_pairs={{0,16},{4,20},{8,24},{12,28},{16,0},{20,4},{24,8},{28,12},{1,17},{... | collective-permute-start | bytes 393224 | tf_op jit(solution)/shard_map/ppermute | solution.py:333
  4.7 26.5 %collective-permute-start.9 = (f32[256,128]{1,0:T(8,128)}, f32[256,128]{1,0:T(8,128)S(1)}, u32[]{:S(2)}, u32[]{:S(2)}) collective-permute-start(f32[256,128]{1,0:T(8,128)} %refs_3_.1), channel_id=1, source_target_pairs={{0,12},{4,8},{8,4},{12,0},{16,28},{20,24},{24,20},{28,16},{1,13},{... | collective-permute-start | bytes 393224 | tf_op jit(solution)/shard_map/ppermute | solution.py:333
  14.3 6.6 %collective-permute-start.6 = (f32[16,128]{1,0:T(8,128)}, f32[16,128]{1,0:T(8,128)S(1)}, u32[]{:S(2)}, u32[]{:S(2)}) collective-permute-start(f32[16,128]{1,0:T(8,128)} %get-tuple-element.31.refs_0_), channel_id=1, source_target_pairs={{0,28},{4,24},{8,20},{12,16},{16,12},{20,8},{24,4},{28,0},{1,29},{... | collective-permute-start | bytes 24584 | tf_op jit(solution)/shard_map/ppermute | solution.py:333
  14.4 7.6 %collective-permute-start.5 = (f32[16,128]{1,0:T(8,128)}, f32[16,128]{1,0:T(8,128)S(1)}, u32[]{:S(2)}, u32[]{:S(2)}) collective-permute-start(f32[16,128]{1,0:T(8,128)} %get-tuple-element.31.refs_0_), channel_id=1, source_target_pairs={{0,24},{4,28},{8,16},{12,20},{16,8},{20,12},{24,0},{28,4},{1,25},{... | collective-permute-start | bytes 24584 | tf_op jit(solution)/shard_map/ppermute | solution.py:333
  18.2 5.7 %collective-permute-start.4 = (f32[16,128]{1,0:T(8,128)}, f32[16,128]{1,0:T(8,128)S(1)}, u32[]{:S(2)}, u32[]{:S(2)}) collective-permute-start(f32[16,128]{1,0:T(8,128)} %get-tuple-element.31.refs_0_), channel_id=1, source_target_pairs={{0,20},{4,16},{8,28},{12,24},{16,4},{20,0},{24,12},{28,8},{1,21},{... | collective-permute-start | bytes 24584 | tf_op jit(solution)/shard_map/ppermute | solution.py:333
  26.9 8.0 %collective-permute-start.8 = (f32[256,128]{1,0:T(8,128)S(1)}, f32[256,128]{1,0:T(8,128)S(1)}, u32[]{:S(2)}, u32[]{:S(2)}) collective-permute-start(f32[256,128]{1,0:T(8,128)S(1)} %copy-done.3), channel_id=1, source_target_pairs={{0,8},{4,12},{8,0},{12,4},{16,24},{20,28},{24,16},{28,20},{1,9},{5... | collective-permute-start | bytes 393224 | tf_op jit(solution)/shard_map/ppermute | solution.py:333
  27.8 7.2 %collective-permute-start.7 = (f32[256,128]{1,0:T(8,128)S(1)}, f32[256,128]{1,0:T(8,128)S(1)}, u32[]{:S(2)}, u32[]{:S(2)}) collective-permute-start(f32[256,128]{1,0:T(8,128)S(1)} %copy-done.3), channel_id=1, source_target_pairs={{0,4},{4,0},{8,12},{12,8},{16,20},{20,16},{24,28},{28,24},{1,5},{5... | collective-permute-start | bytes 393224 | tf_op jit(solution)/shard_map/ppermute | solution.py:333
  29.2 5.9 %collective-permute-start.13 = (f32[256,128]{1,0:T(8,128)S(1)}, f32[256,128]{1,0:T(8,128)S(1)}, u32[]{:S(2)}, u32[]{:S(2)}) collective-permute-start(f32[256,128]{1,0:T(8,128)S(1)} %collective-permute-done.10.refs_7_), channel_id=1, source_target_pairs={{0,12},{4,8},{8,4},{12,0},{16,28},{20,24},{24,20},{28,16},{1,13},{... | collective-permute-start | bytes 393224 | tf_op jit(solution)/shard_map/ppermute | solution.py:333
  31.3 5.2 %collective-permute-start.11 = (f32[256,128]{1,0:T(8,128)S(1)}, f32[256,128]{1,0:T(8,128)S(1)}, u32[]{:S(2)}, u32[]{:S(2)}) collective-permute-start(f32[256,128]{1,0:T(8,128)S(1)} %collective-permute-done.10.refs_7_), channel_id=1, source_target_pairs={{0,4},{4,0},{8,12},{12,8},{16,20},{20,16},{24,28},{28,24},{1,5},{5... | collective-permute-start | bytes 393224 | tf_op jit(solution)/shard_map/ppermute | solution.py:333
  42.1 6.6 %collective-permute-start.15 = (f32[264,128]{1,0:T(8,128)}, f32[264,128]{1,0:T(8,128)S(1)}, u32[]{:S(2)}, u32[]{:S(2)}) collective-permute-start(f32[264,128]{1,0:T(8,128)} %get-tuple-element.36), channel_id=1, source_target_pairs={{0,2},{1,3},{2,0},{3,1},{4,6},{5,7},{6,4},{7,5},{8,10},{9,11},{10,... | collective-permute-start | bytes 405512 | tf_op jit(solution)/shard_map/ppermute | solution.py:333
  43.6 7.1 %collective-permute-start.16 = (f32[264,128]{1,0:T(8,128)}, f32[264,128]{1,0:T(8,128)S(1)}, u32[]{:S(2)}, u32[]{:S(2)}) collective-permute-start(f32[264,128]{1,0:T(8,128)} %get-tuple-element.37), channel_id=1, source_target_pairs={{0,3},{1,2},{2,1},{3,0},{4,7},{5,6},{6,5},{7,4},{8,11},{9,10},{10,... | collective-permute-start | bytes 405512 | tf_op jit(solution)/shard_map/ppermute | solution.py:333
  54.1 7.8 %collective-permute-start.22 = (f32[136,128]{1,0:T(8,128)}, f32[136,128]{1,0:T(8,128)S(1)}, u32[]{:S(2)}, u32[]{:S(2)}) collective-permute-start(f32[136,128]{1,0:T(8,128)} %get-tuple-element.40.refs_5_), channel_id=1, source_target_pairs={{0,20},{4,16},{8,28},{12,24},{16,4},{20,0},{24,12},{28,8},{1,21},{... | collective-permute-start | bytes 208904 | tf_op jit(solution)/shard_map/ppermute | solution.py:333
  56.3 10.2 %collective-permute-start.19 = (f32[128,256]{1,0:T(8,128)}, f32[128,256]{1,0:T(8,128)S(1)}, u32[]{:S(2)}, u32[]{:S(2)}) collective-permute-start(f32[128,256]{1,0:T(8,128)} %get-tuple-element.39.refs_1_), channel_id=1, source_target_pairs={{0,3},{1,2},{2,1},{3,0},{4,7},{5,6},{6,5},{7,4},{8,11},{9,10},{10,... | collective-permute-start | bytes 393224 | tf_op jit(solution)/shard_map/ppermute | solution.py:333
  57.4 9.1 %collective-permute-start.18 = (f32[128,256]{1,0:T(8,128)}, f32[128,256]{1,0:T(8,128)S(1)}, u32[]{:S(2)}, u32[]{:S(2)}) collective-permute-start(f32[128,256]{1,0:T(8,128)} %get-tuple-element.39.refs_1_), channel_id=1, source_target_pairs={{0,2},{1,3},{2,0},{3,1},{4,6},{5,7},{6,4},{7,5},{8,10},{9,11},{10,... | collective-permute-start | bytes 393224 | tf_op jit(solution)/shard_map/ppermute | solution.py:333
  58.0 8.6 %collective-permute-start.17 = (f32[128,256]{1,0:T(8,128)}, f32[128,256]{1,0:T(8,128)S(1)}, u32[]{:S(2)}, u32[]{:S(2)}) collective-permute-start(f32[128,256]{1,0:T(8,128)} %get-tuple-element.39.refs_1_), channel_id=1, source_target_pairs={{0,1},{1,0},{2,3},{3,2},{4,5},{5,4},{6,7},{7,6},{8,9},{9,8},{10,11... | collective-permute-start | bytes 393224 | tf_op jit(solution)/shard_map/ppermute | solution.py:333
  58.2 6.9 %collective-permute-start.21 = (f32[136,128]{1,0:T(8,128)}, f32[136,128]{1,0:T(8,128)S(1)}, u32[]{:S(2)}, u32[]{:S(2)}) collective-permute-start(f32[136,128]{1,0:T(8,128)} %get-tuple-element.40.refs_5_), channel_id=1, source_target_pairs={{0,16},{4,20},{8,24},{12,28},{16,0},{20,4},{24,8},{28,12},{1,17},{... | collective-permute-start | bytes 208904 | tf_op jit(solution)/shard_map/ppermute | solution.py:333
  72.5 5.1 %collective-permute-start.31 = (f32[136,128]{1,0:T(8,128)}, f32[136,128]{1,0:T(8,128)S(1)}, u32[]{:S(2)}, u32[]{:S(2)}) collective-permute-start(f32[136,128]{1,0:T(8,128)} %get-tuple-element.49.refs_4_), channel_id=1, source_target_pairs={{0,3},{1,2},{2,1},{3,0},{4,7},{5,6},{6,5},{7,4},{8,11},{9,10},{10,... | collective-permute-start | bytes 208904 | tf_op jit(solution)/shard_map/ppermute | solution.py:333
  72.6 10.0 %collective-permute-start.26 = (f32[128,256]{1,0:T(8,128)}, f32[128,256]{1,0:T(8,128)S(1)}, u32[]{:S(2)}, u32[]{:S(2)}) collective-permute-start(f32[128,256]{1,0:T(8,128)} %get-tuple-element.46), channel_id=1, source_target_pairs={{0,4},{4,0},{8,12},{12,8},{16,20},{20,16},{24,28},{28,24},{1,5},{5... | collective-permute-start | bytes 393224 | tf_op jit(solution)/shard_map/ppermute | solution.py:333
  73.8 10.8 %collective-permute-start.27 = (f32[128,256]{1,0:T(8,128)}, f32[128,256]{1,0:T(8,128)S(1)}, u32[]{:S(2)}, u32[]{:S(2)}) collective-permute-start(f32[128,256]{1,0:T(8,128)} %get-tuple-element.47), channel_id=1, source_target_pairs={{0,8},{4,12},{8,0},{12,4},{16,24},{20,28},{24,16},{28,20},{1,9},{5... | collective-permute-start | bytes 393224 | tf_op jit(solution)/shard_map/ppermute | solution.py:333
  74.2 10.4 %collective-permute-start.28 = (f32[128,256]{1,0:T(8,128)}, f32[128,256]{1,0:T(8,128)S(1)}, u32[]{:S(2)}, u32[]{:S(2)}) collective-permute-start(f32[128,256]{1,0:T(8,128)} %get-tuple-element.48), channel_id=1, source_target_pairs={{0,12},{4,8},{8,4},{12,0},{16,28},{20,24},{24,20},{28,16},{1,13},{... | collective-permute-start | bytes 393224 | tf_op jit(solution)/shard_map/ppermute | solution.py:333
  81.1 8.9 %collective-permute-start.23 = (f32[128,256]{1,0:T(8,128)}, f32[128,256]{1,0:T(8,128)S(1)}, u32[]{:S(2)}, u32[]{:S(2)}) collective-permute-start(f32[128,256]{1,0:T(8,128)} %get-tuple-element.42), channel_id=1, source_target_pairs={{0,4},{4,0},{8,12},{12,8},{16,20},{20,16},{24,28},{28,24},{1,5},{5... | collective-permute-start | bytes 393224 | tf_op jit(solution)/shard_map/ppermute | solution.py:333
  82.3 7.7 %collective-permute-start.24 = (f32[128,256]{1,0:T(8,128)}, f32[128,256]{1,0:T(8,128)S(1)}, u32[]{:S(2)}, u32[]{:S(2)}) collective-permute-start(f32[128,256]{1,0:T(8,128)} %get-tuple-element.43), channel_id=1, source_target_pairs={{0,8},{4,12},{8,0},{12,4},{16,24},{20,28},{24,16},{28,20},{1,9},{5... | collective-permute-start | bytes 393224 | tf_op jit(solution)/shard_map/ppermute | solution.py:333
  82.6 8.5 %collective-permute-start.25 = (f32[128,256]{1,0:T(8,128)}, f32[128,256]{1,0:T(8,128)S(1)}, u32[]{:S(2)}, u32[]{:S(2)}) collective-permute-start(f32[128,256]{1,0:T(8,128)} %get-tuple-element.44), channel_id=1, source_target_pairs={{0,12},{4,8},{8,4},{12,0},{16,28},{20,24},{24,20},{28,16},{1,13},{... | collective-permute-start | bytes 393224 | tf_op jit(solution)/shard_map/ppermute | solution.py:333
  87.3 8.2 %collective-permute-start.32 = (f32[128,256]{1,0:T(8,128)}, f32[128,256]{1,0:T(8,128)S(1)}, u32[]{:S(2)}, u32[]{:S(2)}) collective-permute-start(f32[128,256]{1,0:T(8,128)} %get-tuple-element.50), channel_id=1, source_target_pairs={{0,16},{4,20},{8,24},{12,28},{16,0},{20,4},{24,8},{28,12},{1,17},{... | collective-permute-start | bytes 393224 | tf_op jit(solution)/shard_map/ppermute | solution.py:333
  (45 other events, 193.1 us)

commit v2 on v0

v2 whole, which is shorter than its diff:
```python
import functools

import jax
import jax.numpy as jnp
from jax import lax
from jax.experimental import pallas as pl
from jax.experimental.pallas import tpu as pltpu
from jax.sharding import PartitionSpec as P

TILE = 128
PAD = 8
F32 = jnp.float32
BF16 = jnp.bfloat16
HIGHEST = lax.Precision.HIGHEST
MIB = 1024 * 1024


def nt_dot(lhs, rhs, **kw):
    return lax.dot_general(lhs, rhs, (((1,), (1,)), ((), ())), preferred_element_type=F32, **kw)


def tn_dot(lhs, rhs, **kw):
    return lax.dot_general(lhs, rhs, (((0,), (0,)), ((), ())), preferred_element_type=F32, **kw)


def split(value):
    high = value.astype(BF16)
    low = (value - high.astype(F32)).astype(BF16)
    return high, low


def total_of(refs):
    total = refs[0][...]
    for ref in refs[1:]:
        total = total + ref[...]
    return total


def vmem(*shape, dtype=F32):
    return pltpu.VMEM(shape, dtype)


def hbm(*shape, dtype=F32):
    return jax.ShapeDtypeStruct(shape, dtype)


def call(kernel, name, args, outs, flops=0, room=4, scratch=(), before=(), before_specs=()):
    spec = pl.BlockSpec(memory_space=pltpu.VMEM)
    return pl.pallas_call(
        kernel,
        out_shape=tuple(outs),
        in_specs=list(before_specs) + [spec] * len(args),
        out_specs=(spec,) * len(outs),
        scratch_shapes=list(scratch),
        compiler_params=pltpu.CompilerParams(vmem_limit_bytes=room * MIB),
        cost_estimate=pl.CostEstimate(
            flops=int(flops), bytes_accessed=sum(4 * arg.size for arg in args), transcendentals=0
        ),
        name=name,
    )(*before, *[pltpu.with_memory_space_constraint(arg, pltpu.VMEM) for arg in args])


def densify_kernel(
    tile_rows, tile_cols, pieces, slots_ref, counts_ref, tiles_hbm,
    dense_ref, col_ref, row_ref, tiles, col_acc, row_acc, sems,
):
    slot_total = tiles.shape[0]
    piece = slot_total // pieces
    copies = [
        pltpu.make_async_copy(
            tiles_hbm.at[pl.ds(p * piece, piece)], tiles.at[pl.ds(p * piece, piece)], sems.at[p]
        )
        for p in range(pieces)
    ]
    for copy in copies:
        copy.start()
    if slot_total < tile_rows * tile_cols:
        dense_ref[...] = jnp.zeros_like(dense_ref)
    col_acc[...] = jnp.zeros_like(col_acc)
    row_acc[...] = jnp.zeros_like(row_acc)
    live = counts_ref[0]

    def place(k, carry):
        slot = slots_ref[k]
        r = slot // tile_cols
        c = slot % tile_cols
        keep = jnp.where(k < live, 1, 0)
        tile = tiles[k] * keep
        dense_ref[
            pl.ds(pl.multiple_of(r * TILE, TILE), TILE), pl.ds(pl.multiple_of(c * TILE, TILE), TILE)
        ] = tile.astype(F32).astype(BF16)
        col_acc[c] += jnp.sum(tile.reshape(TILE // 8, 8, TILE), axis=0)
        row_acc[r] += tile
        return carry

    for p in range(pieces):
        copies[p].wait()
        lax.fori_loop(p * piece, (p + 1) * piece, place, 0, unroll=4)
    col_ref[...] = jnp.sum(col_acc[...], axis=1).astype(F32)
    ones = jnp.ones((8, TILE), BF16)
    for r in range(tile_rows):
        sums = nt_dot(ones, row_acc[r].astype(F32).astype(BF16))
        row_ref[pl.ds(r, 1), :] = sums[0:1, :]


def densify(slots, counts, tiles, tile_rows, tile_cols):
    pieces = 8
    return call(
        functools.partial(densify_kernel, tile_rows, tile_cols, pieces),
        "densify",
        (),
        (
            vmem(tile_rows * TILE, tile_cols * TILE, dtype=BF16),
            vmem(tile_cols, TILE),
            vmem(tile_rows, TILE),
        ),
        flops=tiles.size * 400,
        room=16,
        scratch=(
            vmem(*tiles.shape, dtype=jnp.int32),
            vmem(tile_cols, 8, TILE, dtype=jnp.int32),
            vmem(tile_rows, TILE, TILE, dtype=jnp.int32),
            pltpu.SemaphoreType.DMA((pieces,)),
        ),
        before=(slots, counts, pltpu.with_memory_space_constraint(tiles, pltpu.HBM)),
        before_specs=(
            pl.BlockSpec(memory_space=pltpu.SMEM),
            pl.BlockSpec(memory_space=pltpu.SMEM),
            pl.BlockSpec(memory_space=pl.ANY),
        ),
    )


def scales_kernel(*refs):
    parts, (wide_ref, scale_ref) = refs[:-2], refs[-2:]
    scale = lax.rsqrt(1.0 + total_of(parts))
    for c in range(scale.shape[0]):
        wide_ref[pl.ds(c * TILE, TILE), :] = jnp.broadcast_to(scale[c : c + 1, :], (TILE, TILE)).T
    scale_ref[...] = scale


def source_scales(parts):
    tile_cols = parts[0].shape[0]
    return call(
        scales_kernel,
        "source_scales",
        parts,
        (vmem(tile_cols * TILE, TILE), vmem(tile_cols, TILE)),
    )


def forward_chunks(peers, dense_ref, row_ref, rhs, out_ref):
    col = lax.axis_index("col")
    node_rows, width = out_ref.shape[1] - PAD, out_ref.shape[2]
    own_tiles = node_rows // TILE
    for h, m in enumerate(peers):
        peer = col ^ m
        start = pl.multiple_of(peer * node_rows, node_rows)
        both = jnp.dot(dense_ref[pl.ds(start, node_rows), :], rhs[...], preferred_element_type=F32)
        out_ref[h, pl.ds(0, node_rows), :] = both[:, :width] + both[:, width:]
        out_ref[h, pl.ds(node_rows, PAD), :] = jnp.zeros((PAD, width), F32)
        for t in range(own_tiles):
            out_ref[h, pl.ds(node_rows + t, 1), :] = row_ref[pl.ds(peer * own_tiles + t, 1), :]


def forward_first_kernel(peers, row_count, *refs):
    dense_ref, row_ref, wide_ref = refs[:3]
    blocks = refs[3 : 3 + row_count]
    out_ref, rhs = refs[3 + row_count :]
    row = lax.axis_index("row")
    node_rows, width = blocks[0].shape
    for m in range(row_count):
        start = pl.multiple_of((row ^ m) * node_rows, node_rows)
        high, low = split(blocks[m][...] * wide_ref[pl.ds(start, node_rows), :])
        rhs[pl.ds(start, node_rows), :width] = high
        rhs[pl.ds(start, node_rows), width:] = low
    forward_chunks(peers, dense_ref, row_ref, rhs, out_ref)


def forward_second_kernel(peers, dense_ref, row_ref, rhs, out_ref):
    forward_chunks(peers, dense_ref, row_ref, rhs, out_ref)


def forward_first(peers, dense, row_sums, wide, blocks):
    node_rows, width = blocks[0].shape
    cols = dense.shape[1]
    return call(
        functools.partial(forward_first_kernel, peers, len(blocks)),
        "forward_first",
        (dense, row_sums, wide, *blocks),
        (vmem(len(peers), node_rows + PAD, width), vmem(cols, 2 * width, dtype=BF16)),
        flops=4 * len(peers) * node_rows * cols * width,
    )


def forward_second(peers, dense, row_sums, rhs, node_rows):
    cols = dense.shape[1]
    width = rhs.shape[1] // 2
    return call(
        functools.partial(forward_second_kernel, peers),
        "forward_second",
        (dense, row_sums, rhs),
        (vmem(len(peers), node_rows + PAD, width),),
        flops=4 * len(peers) * node_rows * cols * width,
    )[0]


def pair_kernel(kept_ref, got_ref, *outs):
    for h, out_ref in enumerate(outs):
        out_ref[...] = kept_ref[h + 1] + got_ref[h + 1]


def pair_sums(kept, got):
    return call(
        pair_kernel, "pair_sums", (kept, got), [vmem(*kept.shape[1:])] * (kept.shape[0] - 1)
    )


def node_kernel(*refs):
    kept_ref, got_ref = refs[:2]
    others = refs[2:-7]
    cot_ref, weight_ref, bias_ref, act_ref, back_ref, agg_ref, pre_ref = refs[-7:]
    node_rows, width = cot_ref.shape
    total = kept_ref[0] + got_ref[0]
    for ref in others:
        total = total + ref[...]
    own_tiles = node_rows // TILE
    scale = lax.rsqrt(1.0 + total[node_rows:, :])
    wide = jnp.concatenate(
        [jnp.broadcast_to(scale[t : t + 1, :], (TILE, TILE)).T for t in range(own_tiles)], axis=0
    )
    flat = jnp.concatenate([scale[t : t + 1, :] for t in range(own_tiles)], axis=1)
    weight = weight_ref[...]
    aggregated = total[:node_rows, :] * wide
    preact = (
        jnp.dot(aggregated, weight, precision=HIGHEST, preferred_element_type=F32) + bias_ref[...]
    )
    logistic = jax.nn.sigmoid(preact)
    act_ref[...] = preact * logistic
    pre_grad = cot_ref[...] * logistic * (1.0 + preact * (1.0 - logistic))
    back_ref[...] = nt_dot(weight, pre_grad, precision=HIGHEST) * flat
    agg_ref[...] = aggregated
    pre_ref[...] = pre_grad


def node_step(kept, got, others, cotangent, weight, bias):
    node_rows, width = cotangent.shape
    return call(
        node_kernel,
        "node_step",
        (kept, got, *others, cotangent, weight, bias),
        (
            vmem(node_rows, width),
            vmem(width, node_rows),
            vmem(node_rows, width),
            vmem(node_rows, width),
        ),
        flops=24 * node_rows * width * width,
    )


def grads_kernel(agg_ref, pre_ref, out_ref):
    width = agg_ref.shape[1]
    pre_grad = pre_ref[...]
    out_ref[pl.ds(0, width), :] = tn_dot(agg_ref[...], pre_grad, precision=HIGHEST)
    out_ref[pl.ds(width, PAD), :] = jnp.broadcast_to(
        jnp.sum(pre_grad, axis=0, keepdims=True), (PAD, width)
    )


def weight_parts(aggregated, pre_grad):
    node_rows, width = aggregated.shape
    return call(
        grads_kernel,
        "weight_parts",
        (aggregated, pre_grad),
        (vmem(width + PAD, width),),
        flops=12 * node_rows * width * width,
    )[0]


def backward_chunks(peers, dense_ref, lhs, outs):
    row = lax.axis_index("row")
    width, node_rows = outs[0].shape
    for m, out_ref in zip(peers, outs):
        start = pl.multiple_of((row ^ m) * node_rows, node_rows)
        both = jnp.dot(lhs[...], dense_ref[:, pl.ds(start, node_rows)], preferred_element_type=F32)
        out_ref[...] = both[:width, :] + both[width:, :]


def backward_first_kernel(peers, col_count, *refs):
    dense_ref = refs[0]
    blocks = refs[1 : 1 + col_count]
    outs, lhs = refs[1 + col_count : -1], refs[-1]
    col = lax.axis_index("col")
    width, node_rows = blocks[0].shape
    for m in range(col_count):
        start = pl.multiple_of((col ^ m) * node_rows, node_rows)
        high, low = split(blocks[m][...])
        lhs[:width, pl.ds(start, node_rows)] = high
        lhs[width:, pl.ds(start, node_rows)] = low
    backward_chunks(peers, dense_ref, lhs, outs)


def backward_second_kernel(peers, dense_ref, lhs, *outs):
    backward_chunks(peers, dense_ref, lhs, outs)


def backward_first(peers, dense, blocks):
    width, node_rows = blocks[0].shape
    rows = dense.shape[0]
    out = call(
        functools.partial(backward_first_kernel, peers, len(blocks)),
        "backward_first",
        (dense, *blocks),
        [vmem(width, node_rows)] * len(peers) + [vmem(2 * width, rows, dtype=BF16)],
        flops=4 * len(peers) * node_rows * rows * width,
    )
    return dict(zip(peers, out)), out[-1]


def backward_second(peers, dense, lhs, node_rows):
    rows = dense.shape[0]
    width = lhs.shape[0] // 2
    out = call(
        functools.partial(backward_second_kernel, peers),
        "backward_second",
        (dense, lhs),
        [vmem(width, node_rows)] * len(peers),
        flops=4 * len(peers) * node_rows * rows * width,
    )
    return dict(zip(peers, out))


def sum_kernel(*refs):
    refs[-1][...] = total_of(refs[:-1])


def sum_all(parts, name):
    return call(sum_kernel, name, parts, (vmem(*parts[0].shape),))[0]


def finish_kernel(parts, *refs):
    total = total_of(refs[:parts])
    grads = total_of(refs[parts:-4])
    scale_ref, out_ref, weight_ref, bias_ref = refs[-4:]
    row = lax.axis_index("row")
    width, node_rows = total.shape
    own_tiles = node_rows // TILE
    for t in range(own_tiles):
        part = total[:, t * TILE : (t + 1) * TILE] * scale_ref[pl.ds(row * own_tiles + t, 1), :]
        out_ref[pl.ds(t * TILE, TILE), :] = part.T
    weight_ref[...] = grads[:width, :]
    bias_ref[...] = grads[width : width + 1, :]


def finish(parts, grads, scale):
    width, node_rows = parts[0].shape
    return call(
        functools.partial(finish_kernel, len(parts)),
        "finish",
        (*parts, *grads, scale),
        (hbm(node_rows, width), hbm(width, width), hbm(1, width)),
    )


def swap(value, axis, mask):
    count = lax.axis_size(axis)
    return lax.ppermute(value, axis, [(i, i ^ mask) for i in range(count)])


def local(features, weight, bias_vector, out_grad, adj_tiles, tile_slots, tile_counts):
    row_count = lax.axis_size("row")
    col_count = lax.axis_size("col")
    node_rows, width = features.shape
    tile_rows = node_rows * col_count // TILE
    tile_cols = node_rows * row_count // TILE
    top = row_count // 2
    near, far = list(range(top)), list(range(top, row_count))
    even, odd = list(range(0, col_count, 2)), list(range(1, col_count, 2))

    blocks = [None] * row_count
    blocks[0] = features
    blocks[top] = swap(features, "row", top)
    for m in near[1:]:
        blocks[m] = swap(features, "row", m)
    for m in near[1:]:
        blocks[top | m] = swap(blocks[top], "row", m)

    dense, col_sums, row_sums = densify(
        tile_slots[0, 0], tile_counts[0], adj_tiles[0, 0], tile_rows, tile_cols
    )
    col_sums = sum_all([col_sums] + [swap(col_sums, "row", m) for m in near[1:]], "near_sums")
    wide, scale = source_scales([col_sums, swap(col_sums, "row", top)])

    given, rhs = forward_first(odd, dense, row_sums, wide, blocks)
    got = swap(given, "col", 1)
    kept = forward_second(even, dense, row_sums, rhs, node_rows)
    paired = pair_sums(kept, got)
    others = [swap(part, "col", m) for m, part in zip(even[1:], paired)]
    activated, back, aggregated, pre_grad = node_step(
        kept, got, others, out_grad, weight, bias_vector[None, :]
    )

    backs = [None] * col_count
    backs[0] = back
    for m in even[1:]:
        backs[m] = swap(back, "col", m)
    for m in even:
        backs[m | 1] = swap(backs[m], "col", 1)
    grads = weight_parts(aggregated, pre_grad)
    late = 2
    early = [m for m in range(1, row_count) if not m & late]
    grads = sum_all([grads] + [swap(grads, "row", m) for m in early], "early_grads")

    chunks, lhs = backward_first(far, dense, backs)
    ahead = [chunks[top]] + [swap(chunks[top | m], "row", m) for m in near[1:]]
    chunks = backward_second(near, dense, lhs, node_rows)
    mine = [chunks[0]] + [swap(chunks[m], "row", m) for m in near[1:]]
    grads = sum_all([grads] + [swap(grads, "col", m) for m in range(1, col_count)], "col_grads")
    mine.append(swap(sum_all(ahead, "ahead_sums"), "row", top))
    feature_grad, weight_grad, bias_grad = finish(
        mine, [grads, swap(grads, "row", late)], scale
    )
    return activated, feature_grad, weight_grad, bias_grad[0]


def solution(mesh):
    return jax.shard_map(
        local,
        mesh=mesh,
        in_specs=(
            P(("col", "row"), None),
            P(),
            P(),
            P(("row", "col"), None),
            P("row", "col", None, None, None),
            P("row", "col", None),
            P("row", "col"),
        ),
        out_specs=(P(("row", "col"), None), P(("col", "row"), None), P(), P()),
        check_vma=False,
    )
```

time: 340 us -> 72.7 us (0.21)
  waiting for transfers between devices: 166 us -> 22.5 us
  matrix products: 58.5 us -> 0 us
  blocking collectives: 58.3 us -> 0 us
  starting transfers between devices: 0.16 us -> 37.2 us
  local copies, waits for them, and re-layouts: 32.7 us -> 1.32 us
  between operations: 15.3 us -> 1.45 us
  Pallas kernels: 0 us -> 10.1 us
  other arithmetic: 8.96 us -> 0 us
    psum x2 -> x0, waiting for transfers between devices: 96.4 us -> none  [the longest x1 70.1 us: local(): weight_grad, bias_grad = lax.psum((weight_part, bias_part), 'row')]
    dot_general x9 -> x0, matrix products: 58.5 us -> none  [the longest x1 21.5 us: local(): jnp.einsum('kab,kbh->kah', adjacency, taken, precision=lax.Precision.HIGH...]
    reduce_scatter x1 -> x0, waiting for transfers between devices: 39.5 us -> none  [local(): lax.psum_scatter(partial_back, 'row', scatter_dimension=0, tiled=True)]
    ppermute x0 -> x30, starting transfers between devices: none -> 37.2 us  [swap(): return lax.ppermute(value, axis, [(i, i ^ mask) for i in range(count)])]
    all_gather x1 -> x0, waiting for transfers between devices: 30 us -> none  [local(): gathered = lax.all_gather(scaled, 'row', axis=0, tiled=True)]
    psum x2 -> x0, blocking collectives: 27.5 us -> none  [the longest x1 21.9 us: local(): weight_grad, bias_grad = lax.psum((weight_part, bias_part), 'row')]
    unnamed x1 -> x0, blocking collectives: 23.4 us -> none
    ppermute x0 -> x30, waiting for transfers between devices: none -> 22.5 us  [swap(): return lax.ppermute(value, axis, [(i, i ^ mask) for i in range(count)])]
  transfers between devices with their start and end apart: 4 -> 30, of which waited for: 4 -> 14; matrix products, arithmetic and copies ran while one was open for 1% -> 1% of each run, Pallas kernels for 0% -> 10%
where the time goes in v2:
time: 72.7 us; the launch traced here: 72.6 us
  starting transfers between devices  37.2 us (51%)
  waiting for transfers between devices  22.5 us (31%)
  Pallas kernels  10.1 us (14%)
  between operations  1.45 us (2%)
  local copies, waits for them, and re-layouts  1.32 us (2%)
    ppermute x30, starting transfers between devices, swap(): return lax.ppermute(value, axis, [(i, i ^ mask) for i in range(count)])  37.2 us
    ppermute x30, waiting for transfers between devices, swap(): return lax.ppermute(value, axis, [(i, i ^ mask) for i in range(count)])  22.5 us
    pallas_call x14, Pallas kernels, call(): pl.pallas_call(kernel, out_shape=tuple(outs), in_specs=list(before_specs)...  10.1 us
  transfers between devices with their start and end apart: 30, of which 14 were waited for; matrix products, arithmetic and copies ran while one was open for 1% of the time, Pallas kernels for 10%

profile of v2, /device:TPU:0, one launch (start us, length us, event | category | flops | bytes accessed | tf_op | source)
XLA Modules:
  0.0 72.6 jit_solution(2123959399146593480)
XLA Ops:
  0.6 4.1 %collective-permute-start.7 = (f32[256,128]{1,0:T(8,128)}, f32[256,128]{1,0:T(8,128)S(1)}, u32[]{:S(2)}, u32[]{:S(2)}) collective-permute-start(f32[256,128]{1,0:T(8,128)} %refs_3_.2), channel_id=1, source_target_pairs={{0,16},{4,20},{8,24},{12,28},{16,0},{20,4},{24,8},{28,12},{1,17},{... | collective-permute-start | bytes 393224 | tf_op jit(solution)/shard_map/ppermute | solution.py:369
  4.7 2.5 %collective-permute-start.6 = (f32[256,128]{1,0:T(8,128)}, f32[256,128]{1,0:T(8,128)S(1)}, u32[]{:S(2)}, u32[]{:S(2)}) collective-permute-start(f32[256,128]{1,0:T(8,128)} %refs_3_.2), channel_id=1, source_target_pairs={{0,12},{4,8},{8,4},{12,0},{16,28},{20,24},{24,20},{28,16},{1,13},{... | collective-permute-start | bytes 393224 | tf_op jit(solution)/shard_map/ppermute | solution.py:369
  8.6 4.6 %densify.1 = (bf16[1024,2048]{1,0:T(8,128)(2,1)S(1)}, f32[16,128]{1,0:T(8,128)S(1)}, f32[8,128]{1,0:T(8,128)S(1)}) custom-call(s32[128]{0:T(128)S(1)} %bitcast.6, s32[1]{0:T(128)} %bitcast.5.counts_ref, s32[128,128,128]{2,1,0:T(8,128)} %bitcast.8), custom_call_target="tpu_custom_call" | custom-call | flops 838860800 | tf_op jit(solution)/shard_map/densify/pallas_call | solution.py:49
  13.6 1.6 %collective-permute-start.1 = (f32[16,128]{1,0:T(8,128)S(1)}, f32[16,128]{1,0:T(8,128)S(1)}, u32[]{:S(2)}, u32[]{:S(2)}) collective-permute-start(f32[16,128]{1,0:T(8,128)S(1)} %get-tuple-element.29.refs_0_), channel_id=1, source_target_pairs={{0,8},{4,12},{8,0},{12,4},{16,24},{20,28},{24,16},{28,20},{1,9},{5... | collective-permute-start | bytes 24584 | tf_op jit(solution)/shard_map/ppermute | solution.py:369
  15.2 1.5 %collective-permute-start = (f32[16,128]{1,0:T(8,128)S(1)}, f32[16,128]{1,0:T(8,128)S(1)}, u32[]{:S(2)}, u32[]{:S(2)}) collective-permute-start(f32[16,128]{1,0:T(8,128)S(1)} %get-tuple-element.29.refs_0_), channel_id=1, source_target_pairs={{0,4},{4,0},{8,12},{12,8},{16,20},{20,16},{24,28},{28,24},{1,5},{5... | collective-permute-start | bytes 24584 | tf_op jit(solution)/shard_map/ppermute | solution.py:369
  19.4 1.8 %collective-permute-start.4 = (f32[256,128]{1,0:T(8,128)S(1)}, f32[256,128]{1,0:T(8,128)S(1)}, u32[]{:S(2)}, u32[]{:S(2)}) collective-permute-start(f32[256,128]{1,0:T(8,128)S(1)} %copy-done), channel_id=1, source_target_pairs={{0,4},{4,0},{8,12},{12,8},{16,20},{20,16},{24,28},{28,24},{1,5},{5... | collective-permute-start | bytes 393224 | tf_op jit(solution)/shard_map/ppermute | solution.py:369
  21.2 1.5 %collective-permute-start.10 = (f32[256,128]{1,0:T(8,128)S(1)}, f32[256,128]{1,0:T(8,128)S(1)}, u32[]{:S(2)}, u32[]{:S(2)}) collective-permute-start(f32[256,128]{1,0:T(8,128)S(1)} %collective-permute-done.7.refs_7_), channel_id=1, source_target_pairs={{0,12},{4,8},{8,4},{12,0},{16,28},{20,24},{24,20},{28,16},{1,13},{... | collective-permute-start | bytes 393224 | tf_op jit(solution)/shard_map/ppermute | solution.py:369
  23.9 1.6 %collective-permute-start.8 = (f32[256,128]{1,0:T(8,128)S(1)}, f32[256,128]{1,0:T(8,128)S(1)}, u32[]{:S(2)}, u32[]{:S(2)}) collective-permute-start(f32[256,128]{1,0:T(8,128)S(1)} %collective-permute-done.7.refs_7_), channel_id=1, source_target_pairs={{0,4},{4,0},{8,12},{12,8},{16,20},{20,16},{24,28},{28,24},{1,5},{5... | collective-permute-start | bytes 393224 | tf_op jit(solution)/shard_map/ppermute | solution.py:369
  26.2 1.9 %collective-permute-done.10.refs_10_ = f32[256,128]{1,0:T(8,128)S(1)} collective-permute-done((f32[256,128]{1,0:T(8,128)S(1)}, f32[256,128]{1,0:T(8,128)S(1)}, u32[]{:S(2)}, u32[]{:S(2)}) %collective-permute-start.10) | collective-permute-done | bytes 131104 | tf_op jit(solution)/shard_map/ppermute | solution.py:369
  32.0 1.6 %collective-permute-start.12 = (f32[264,128]{1,0:T(8,128)S(1)}, f32[264,128]{1,0:T(8,128)S(1)}, u32[]{:S(2)}, u32[]{:S(2)}) collective-permute-start(f32[264,128]{1,0:T(8,128)S(1)} %pair_sums.1), channel_id=1, source_target_pairs={{0,2},{1,3},{2,0},{3,1},{4,6},{5,7},{6,4},{7,5},{8,10},{9,11},{10,... | collective-permute-start | bytes 405512 | tf_op jit(solution)/shard_map/ppermute | solution.py:369
  33.6 4.1 %collective-permute-done.12.refs_2_ = f32[264,128]{1,0:T(8,128)S(1)} collective-permute-done((f32[264,128]{1,0:T(8,128)S(1)}, f32[264,128]{1,0:T(8,128)S(1)}, u32[]{:S(2)}, u32[]{:S(2)}) %collective-permute-start.12) | collective-permute-done | bytes 135200 | tf_op jit(solution)/shard_map/ppermute | solution.py:369
  38.5 1.6 %collective-permute-start.14 = (f32[128,256]{1,0:T(8,128)S(1)}, f32[128,256]{1,0:T(8,128)S(1)}, u32[]{:S(2)}, u32[]{:S(2)}) collective-permute-start(f32[128,256]{1,0:T(8,128)S(1)} %get-tuple-element.34.refs_1_), channel_id=1, source_target_pairs={{0,2},{1,3},{2,0},{3,1},{4,6},{5,7},{6,4},{7,5},{8,10},{9,11},{10,... | collective-permute-start | bytes 393224 | tf_op jit(solution)/shard_map/ppermute | solution.py:369
  40.1 3.5 %collective-permute-done.14.refs_3_ = f32[128,256]{1,0:T(8,128)S(1)} collective-permute-done((f32[128,256]{1,0:T(8,128)S(1)}, f32[128,256]{1,0:T(8,128)S(1)}, u32[]{:S(2)}, u32[]{:S(2)}) %collective-permute-start.14) | collective-permute-done | bytes 131104 | tf_op jit(solution)/shard_map/ppermute | solution.py:369
  43.9 2.3 %collective-permute-start.25 = (f32[136,128]{1,0:T(8,128)S(1)}, f32[136,128]{1,0:T(8,128)S(1)}, u32[]{:S(2)}, u32[]{:S(2)}) collective-permute-start(f32[136,128]{1,0:T(8,128)S(1)} %weight_parts.1.refs_0_), channel_id=1, source_target_pairs={{0,20},{4,16},{8,28},{12,24},{16,4},{20,0},{24,12},{28,8},{1,21},{... | collective-permute-start | bytes 208904 | tf_op jit(solution)/shard_map/ppermute | solution.py:369
  47.0 1.3 %collective-permute-start.19 = (f32[128,256]{1,0:T(8,128)S(1)}, f32[128,256]{1,0:T(8,128)S(1)}, u32[]{:S(2)}, u32[]{:S(2)}) collective-permute-start(f32[128,256]{1,0:T(8,128)S(1)} %get-tuple-element.41), channel_id=1, source_target_pairs={{0,4},{4,0},{8,12},{12,8},{16,20},{20,16},{24,28},{28,24},{1,5},{5... | collective-permute-start | bytes 393224 | tf_op jit(solution)/shard_map/ppermute | solution.py:369
  50.3 1.6 %collective-permute-start.20 = (f32[128,256]{1,0:T(8,128)S(1)}, f32[128,256]{1,0:T(8,128)S(1)}, u32[]{:S(2)}, u32[]{:S(2)}) collective-permute-start(f32[128,256]{1,0:T(8,128)S(1)} %get-tuple-element.42), channel_id=1, source_target_pairs={{0,8},{4,12},{8,0},{12,4},{16,24},{20,28},{24,16},{28,20},{1,9},{5... | collective-permute-start | bytes 393224 | tf_op jit(solution)/shard_map/ppermute | solution.py:369
  51.9 1.3 %collective-permute-start.21 = (f32[128,256]{1,0:T(8,128)S(1)}, f32[128,256]{1,0:T(8,128)S(1)}, u32[]{:S(2)}, u32[]{:S(2)}) collective-permute-start(f32[128,256]{1,0:T(8,128)S(1)} %get-tuple-element.43), channel_id=1, source_target_pairs={{0,12},{4,8},{8,4},{12,0},{16,28},{20,24},{24,20},{28,16},{1,13},{... | collective-permute-start | bytes 393224 | tf_op jit(solution)/shard_map/ppermute | solution.py:369
  53.2 1.4 %collective-permute-done.24.refs_2_ = f32[136,128]{1,0:T(8,128)S(1)} collective-permute-done((f32[136,128]{1,0:T(8,128)S(1)}, f32[136,128]{1,0:T(8,128)S(1)}, u32[]{:S(2)}, u32[]{:S(2)}) %collective-permute-start.24) | collective-permute-done | bytes 69664 | tf_op jit(solution)/shard_map/ppermute | solution.py:369
  55.6 1.1 %collective-permute-start.27 = (f32[136,128]{1,0:T(8,128)S(1)}, f32[136,128]{1,0:T(8,128)S(1)}, u32[]{:S(2)}, u32[]{:S(2)}) collective-permute-start(f32[136,128]{1,0:T(8,128)S(1)} %early_grads.1.refs_0_), channel_id=1, source_target_pairs={{0,2},{1,3},{2,0},{3,1},{4,6},{5,7},{6,4},{7,5},{8,10},{9,11},{10,... | collective-permute-start | bytes 208904 | tf_op jit(solution)/shard_map/ppermute | solution.py:369
  59.1 2.0 %collective-permute-start.17 = (f32[128,256]{1,0:T(8,128)S(1)}, f32[128,256]{1,0:T(8,128)S(1)}, u32[]{:S(2)}, u32[]{:S(2)}) collective-permute-start(f32[128,256]{1,0:T(8,128)S(1)} %get-tuple-element.38), channel_id=1, source_target_pairs={{0,8},{4,12},{8,0},{12,4},{16,24},{20,28},{24,16},{28,20},{1,9},{5... | collective-permute-start | bytes 393224 | tf_op jit(solution)/shard_map/ppermute | solution.py:369
  61.1 1.1 %collective-permute-start.18 = (f32[128,256]{1,0:T(8,128)S(1)}, f32[128,256]{1,0:T(8,128)S(1)}, u32[]{:S(2)}, u32[]{:S(2)}) collective-permute-start(f32[128,256]{1,0:T(8,128)S(1)} %get-tuple-element.39), channel_id=1, source_target_pairs={{0,12},{4,8},{8,4},{12,0},{16,28},{20,24},{24,20},{28,16},{1,13},{... | collective-permute-start | bytes 393224 | tf_op jit(solution)/shard_map/ppermute | solution.py:369
  62.3 1.6 %collective-permute-start.22 = (f32[128,256]{1,0:T(8,128)S(1)}, f32[128,256]{1,0:T(8,128)S(1)}, u32[]{:S(2)}, u32[]{:S(2)}) collective-permute-start(f32[128,256]{1,0:T(8,128)S(1)} %ahead_sums.1), channel_id=1, source_target_pairs={{0,16},{4,20},{8,24},{12,28},{16,0},{20,4},{24,8},{28,12},{1,17},{... | collective-permute-start | bytes 393224 | tf_op jit(solution)/shard_map/ppermute | solution.py:369
  63.9 2.1 %collective-permute-start.29 = (f32[136,128]{1,0:T(8,128)S(1)}, f32[136,128]{1,0:T(8,128)S(1)}, u32[]{:S(2)}, u32[]{:S(2)}) collective-permute-start(f32[136,128]{1,0:T(8,128)S(1)} %col_grads.1.refs_5_), channel_id=1, source_target_pairs={{0,8},{4,12},{8,0},{12,4},{16,24},{20,28},{24,16},{28,20},{1,9},{5... | collective-permute-start | bytes 208904 | tf_op jit(solution)/shard_map/ppermute | solution.py:369
  66.7 5.1 %collective-permute-done.29.refs_6_ = f32[136,128]{1,0:T(8,128)S(1)} collective-permute-done((f32[136,128]{1,0:T(8,128)S(1)}, f32[136,128]{1,0:T(8,128)S(1)}, u32[]{:S(2)}, u32[]{:S(2)}) %collective-permute-start.29) | collective-permute-done | bytes 69664 | tf_op jit(solution)/shard_map/ppermute | solution.py:369
  (61 shorter events, 18.4 us)
Async XLA Ops:
  0.6 20.5 %collective-permute-start.7 = (f32[256,128]{1,0:T(8,128)}, f32[256,128]{1,0:T(8,128)S(1)}, u32[]{:S(2)}, u32[]{:S(2)}) collective-permute-start(f32[256,128]{1,0:T(8,128)} %refs_3_.2), channel_id=1, source_target_pairs={{0,16},{4,20},{8,24},{12,28},{16,0},{20,4},{24,8},{28,12},{1,17},{... | collective-permute-start | bytes 393224 | tf_op jit(solution)/shard_map/ppermute | solution.py:369
  4.7 19.1 %collective-permute-start.6 = (f32[256,128]{1,0:T(8,128)}, f32[256,128]{1,0:T(8,128)S(1)}, u32[]{:S(2)}, u32[]{:S(2)}) collective-permute-start(f32[256,128]{1,0:T(8,128)} %refs_3_.2), channel_id=1, source_target_pairs={{0,12},{4,8},{8,4},{12,0},{16,28},{20,24},{24,20},{28,16},{1,13},{... | collective-permute-start | bytes 393224 | tf_op jit(solution)/shard_map/ppermute | solution.py:369
  19.2 6.7 %collective-permute-start.5 = (f32[256,128]{1,0:T(8,128)S(1)}, f32[256,128]{1,0:T(8,128)S(1)}, u32[]{:S(2)}, u32[]{:S(2)}) collective-permute-start(f32[256,128]{1,0:T(8,128)S(1)} %copy-done), channel_id=1, source_target_pairs={{0,8},{4,12},{8,0},{12,4},{16,24},{20,28},{24,16},{28,20},{1,9},{5... | collective-permute-start | bytes 393224 | tf_op jit(solution)/shard_map/ppermute | solution.py:369
  19.4 6.8 %collective-permute-start.4 = (f32[256,128]{1,0:T(8,128)S(1)}, f32[256,128]{1,0:T(8,128)S(1)}, u32[]{:S(2)}, u32[]{:S(2)}) collective-permute-start(f32[256,128]{1,0:T(8,128)S(1)} %copy-done), channel_id=1, source_target_pairs={{0,4},{4,0},{8,12},{12,8},{16,20},{20,16},{24,28},{28,24},{1,5},{5... | collective-permute-start | bytes 393224 | tf_op jit(solution)/shard_map/ppermute | solution.py:369
  21.2 6.9 %collective-permute-start.10 = (f32[256,128]{1,0:T(8,128)S(1)}, f32[256,128]{1,0:T(8,128)S(1)}, u32[]{:S(2)}, u32[]{:S(2)}) collective-permute-start(f32[256,128]{1,0:T(8,128)S(1)} %collective-permute-done.7.refs_7_), channel_id=1, source_target_pairs={{0,12},{4,8},{8,4},{12,0},{16,28},{20,24},{24,20},{28,16},{1,13},{... | collective-permute-start | bytes 393224 | tf_op jit(solution)/shard_map/ppermute | solution.py:369
  23.5 5.0 %collective-permute-start.9 = (f32[256,128]{1,0:T(8,128)S(1)}, f32[256,128]{1,0:T(8,128)S(1)}, u32[]{:S(2)}, u32[]{:S(2)}) collective-permute-start(f32[256,128]{1,0:T(8,128)S(1)} %collective-permute-done.7.refs_7_), channel_id=1, source_target_pairs={{0,8},{4,12},{8,0},{12,4},{16,24},{20,28},{24,16},{28,20},{1,9},{5... | collective-permute-start | bytes 393224 | tf_op jit(solution)/shard_map/ppermute | solution.py:369
  23.9 5.5 %collective-permute-start.8 = (f32[256,128]{1,0:T(8,128)S(1)}, f32[256,128]{1,0:T(8,128)S(1)}, u32[]{:S(2)}, u32[]{:S(2)}) collective-permute-start(f32[256,128]{1,0:T(8,128)S(1)} %collective-permute-done.7.refs_7_), channel_id=1, source_target_pairs={{0,4},{4,0},{8,12},{12,8},{16,20},{20,16},{24,28},{28,24},{1,5},{5... | collective-permute-start | bytes 393224 | tf_op jit(solution)/shard_map/ppermute | solution.py:369
  32.0 5.7 %collective-permute-start.12 = (f32[264,128]{1,0:T(8,128)S(1)}, f32[264,128]{1,0:T(8,128)S(1)}, u32[]{:S(2)}, u32[]{:S(2)}) collective-permute-start(f32[264,128]{1,0:T(8,128)S(1)} %pair_sums.1), channel_id=1, source_target_pairs={{0,2},{1,3},{2,0},{3,1},{4,6},{5,7},{6,4},{7,5},{8,10},{9,11},{10,... | collective-permute-start | bytes 405512 | tf_op jit(solution)/shard_map/ppermute | solution.py:369
  38.5 5.0 %collective-permute-start.14 = (f32[128,256]{1,0:T(8,128)S(1)}, f32[128,256]{1,0:T(8,128)S(1)}, u32[]{:S(2)}, u32[]{:S(2)}) collective-permute-start(f32[128,256]{1,0:T(8,128)S(1)} %get-tuple-element.34.refs_1_), channel_id=1, source_target_pairs={{0,2},{1,3},{2,0},{3,1},{4,6},{5,7},{6,4},{7,5},{8,10},{9,11},{10,... | collective-permute-start | bytes 393224 | tf_op jit(solution)/shard_map/ppermute | solution.py:369
  40.1 6.1 %collective-permute-start.13 = (f32[128,256]{1,0:T(8,128)S(1)}, f32[128,256]{1,0:T(8,128)S(1)}, u32[]{:S(2)}, u32[]{:S(2)}) collective-permute-start(f32[128,256]{1,0:T(8,128)S(1)} %get-tuple-element.34.refs_1_), channel_id=1, source_target_pairs={{0,1},{1,0},{2,3},{3,2},{4,5},{5,4},{6,7},{7,6},{8,9},{9,8},{10,11... | collective-permute-start | bytes 393224 | tf_op jit(solution)/shard_map/ppermute | solution.py:369
  43.9 8.1 %collective-permute-start.25 = (f32[136,128]{1,0:T(8,128)S(1)}, f32[136,128]{1,0:T(8,128)S(1)}, u32[]{:S(2)}, u32[]{:S(2)}) collective-permute-start(f32[136,128]{1,0:T(8,128)S(1)} %weight_parts.1.refs_0_), channel_id=1, source_target_pairs={{0,20},{4,16},{8,28},{12,24},{16,4},{20,0},{24,12},{28,8},{1,21},{... | collective-permute-start | bytes 208904 | tf_op jit(solution)/shard_map/ppermute | solution.py:369
  47.0 9.7 %collective-permute-start.19 = (f32[128,256]{1,0:T(8,128)S(1)}, f32[128,256]{1,0:T(8,128)S(1)}, u32[]{:S(2)}, u32[]{:S(2)}) collective-permute-start(f32[128,256]{1,0:T(8,128)S(1)} %get-tuple-element.41), channel_id=1, source_target_pairs={{0,4},{4,0},{8,12},{12,8},{16,20},{20,16},{24,28},{28,24},{1,5},{5... | collective-permute-start | bytes 393224 | tf_op jit(solution)/shard_map/ppermute | solution.py:369
  48.3 6.3 %collective-permute-start.24 = (f32[136,128]{1,0:T(8,128)S(1)}, f32[136,128]{1,0:T(8,128)S(1)}, u32[]{:S(2)}, u32[]{:S(2)}) collective-permute-start(f32[136,128]{1,0:T(8,128)S(1)} %weight_parts.1.refs_0_), channel_id=1, source_target_pairs={{0,16},{4,20},{8,24},{12,28},{16,0},{20,4},{24,8},{28,12},{1,17},{... | collective-permute-start | bytes 208904 | tf_op jit(solution)/shard_map/ppermute | solution.py:369
  49.2 5.9 %collective-permute-start.23 = (f32[136,128]{1,0:T(8,128)S(1)}, f32[136,128]{1,0:T(8,128)S(1)}, u32[]{:S(2)}, u32[]{:S(2)}) collective-permute-start(f32[136,128]{1,0:T(8,128)S(1)} %weight_parts.1.refs_0_), channel_id=1, source_target_pairs={{0,4},{4,0},{8,12},{12,8},{16,20},{20,16},{24,28},{28,24},{1,5},{5... | collective-permute-start | bytes 208904 | tf_op jit(solution)/shard_map/ppermute | solution.py:369
  50.3 7.5 %collective-permute-start.20 = (f32[128,256]{1,0:T(8,128)S(1)}, f32[128,256]{1,0:T(8,128)S(1)}, u32[]{:S(2)}, u32[]{:S(2)}) collective-permute-start(f32[128,256]{1,0:T(8,128)S(1)} %get-tuple-element.42), channel_id=1, source_target_pairs={{0,8},{4,12},{8,0},{12,4},{16,24},{20,28},{24,16},{28,20},{1,9},{5... | collective-permute-start | bytes 393224 | tf_op jit(solution)/shard_map/ppermute | solution.py:369
  51.9 7.2 %collective-permute-start.21 = (f32[128,256]{1,0:T(8,128)S(1)}, f32[128,256]{1,0:T(8,128)S(1)}, u32[]{:S(2)}, u32[]{:S(2)}) collective-permute-start(f32[128,256]{1,0:T(8,128)S(1)} %get-tuple-element.43), channel_id=1, source_target_pairs={{0,12},{4,8},{8,4},{12,0},{16,28},{20,24},{24,20},{28,16},{1,13},{... | collective-permute-start | bytes 393224 | tf_op jit(solution)/shard_map/ppermute | solution.py:369
  55.1 6.0 %collective-permute-start.28 = (f32[136,128]{1,0:T(8,128)S(1)}, f32[136,128]{1,0:T(8,128)S(1)}, u32[]{:S(2)}, u32[]{:S(2)}) collective-permute-start(f32[136,128]{1,0:T(8,128)S(1)} %early_grads.1.refs_0_), channel_id=1, source_target_pairs={{0,3},{1,2},{2,1},{3,0},{4,7},{5,6},{6,5},{7,4},{8,11},{9,10},{10,... | collective-permute-start | bytes 208904 | tf_op jit(solution)/shard_map/ppermute | solution.py:369
  55.6 6.6 %collective-permute-start.27 = (f32[136,128]{1,0:T(8,128)S(1)}, f32[136,128]{1,0:T(8,128)S(1)}, u32[]{:S(2)}, u32[]{:S(2)}) collective-permute-start(f32[136,128]{1,0:T(8,128)S(1)} %early_grads.1.refs_0_), channel_id=1, source_target_pairs={{0,2},{1,3},{2,0},{3,1},{4,6},{5,7},{6,4},{7,5},{8,10},{9,11},{10,... | collective-permute-start | bytes 208904 | tf_op jit(solution)/shard_map/ppermute | solution.py:369
  56.7 7.2 %collective-permute-start.26 = (f32[136,128]{1,0:T(8,128)S(1)}, f32[136,128]{1,0:T(8,128)S(1)}, u32[]{:S(2)}, u32[]{:S(2)}) collective-permute-start(f32[136,128]{1,0:T(8,128)S(1)} %early_grads.1.refs_0_), channel_id=1, source_target_pairs={{0,1},{1,0},{2,3},{3,2},{4,5},{5,4},{6,7},{7,6},{8,9},{9,8},{10,11... | collective-permute-start | bytes 208904 | tf_op jit(solution)/shard_map/ppermute | solution.py:369
  57.8 14.0 %collective-permute-start.16 = (f32[128,256]{1,0:T(8,128)S(1)}, f32[128,256]{1,0:T(8,128)S(1)}, u32[]{:S(2)}, u32[]{:S(2)}) collective-permute-start(f32[128,256]{1,0:T(8,128)S(1)} %get-tuple-element.37), channel_id=1, source_target_pairs={{0,4},{4,0},{8,12},{12,8},{16,20},{20,16},{24,28},{28,24},{1,5},{5... | collective-permute-start | bytes 393224 | tf_op jit(solution)/shard_map/ppermute | solution.py:369
  59.1 12.7 %collective-permute-start.17 = (f32[128,256]{1,0:T(8,128)S(1)}, f32[128,256]{1,0:T(8,128)S(1)}, u32[]{:S(2)}, u32[]{:S(2)}) collective-permute-start(f32[128,256]{1,0:T(8,128)S(1)} %get-tuple-element.38), channel_id=1, source_target_pairs={{0,8},{4,12},{8,0},{12,4},{16,24},{20,28},{24,16},{28,20},{1,9},{5... | collective-permute-start | bytes 393224 | tf_op jit(solution)/shard_map/ppermute | solution.py:369
  61.1 10.7 %collective-permute-start.18 = (f32[128,256]{1,0:T(8,128)S(1)}, f32[128,256]{1,0:T(8,128)S(1)}, u32[]{:S(2)}, u32[]{:S(2)}) collective-permute-start(f32[128,256]{1,0:T(8,128)S(1)} %get-tuple-element.39), channel_id=1, source_target_pairs={{0,12},{4,8},{8,4},{12,0},{16,28},{20,24},{24,20},{28,16},{1,13},{... | collective-permute-start | bytes 393224 | tf_op jit(solution)/shard_map/ppermute | solution.py:369
  62.3 9.5 %collective-permute-start.22 = (f32[128,256]{1,0:T(8,128)S(1)}, f32[128,256]{1,0:T(8,128)S(1)}, u32[]{:S(2)}, u32[]{:S(2)}) collective-permute-start(f32[128,256]{1,0:T(8,128)S(1)} %ahead_sums.1), channel_id=1, source_target_pairs={{0,16},{4,20},{8,24},{12,28},{16,0},{20,4},{24,8},{28,12},{1,17},{... | collective-permute-start | bytes 393224 | tf_op jit(solution)/shard_map/ppermute | solution.py:369
  63.9 7.8 %collective-permute-start.29 = (f32[136,128]{1,0:T(8,128)S(1)}, f32[136,128]{1,0:T(8,128)S(1)}, u32[]{:S(2)}, u32[]{:S(2)}) collective-permute-start(f32[136,128]{1,0:T(8,128)S(1)} %col_grads.1.refs_5_), channel_id=1, source_target_pairs={{0,8},{4,12},{8,0},{12,4},{16,24},{20,28},{24,16},{28,20},{1,9},{5... | collective-permute-start | bytes 208904 | tf_op jit(solution)/shard_map/ppermute | solution.py:369
  (11 other events, 127.9 us)

commit v3 on v2

--- a/solution.py
+++ b/solution.py
@@ -13,6 +13,7 @@
 BF16 = jnp.bfloat16
 HIGHEST = lax.Precision.HIGHEST
 MIB = 1024 * 1024
+HINT = 2 * 10**9
 
 
 def nt_dot(lhs, rhs, **kw):
@@ -61,11 +62,15 @@
 
 
 def densify_kernel(
-    tile_rows, tile_cols, pieces, slots_ref, counts_ref, tiles_hbm,
-    dense_ref, col_ref, row_ref, tiles, col_acc, row_acc, sems,
+    tile_cols, pieces, slots_hbm, counts_hbm, tiles_hbm, dense_ref, col_ref,
+    tiles, col_acc, slots, counts, sems, slot_sem, count_sem,
 ):
     slot_total = tiles.shape[0]
     piece = slot_total // pieces
+    slot_copy = pltpu.make_async_copy(slots_hbm.at[0], slots, slot_sem)
+    count_copy = pltpu.make_async_copy(counts_hbm, counts, count_sem)
+    slot_copy.start()
+    count_copy.start()
     copies = [
         pltpu.make_async_copy(
             tiles_hbm.at[pl.ds(p * piece, piece)], tiles.at[pl.ds(p * piece, piece)], sems.at[p]
@@ -74,75 +79,97 @@
     ]
     for copy in copies:
         copy.start()
-    if slot_total < tile_rows * tile_cols:
+    if slot_total * TILE * TILE < dense_ref.shape[0] * dense_ref.shape[1]:
         dense_ref[...] = jnp.zeros_like(dense_ref)
     col_acc[...] = jnp.zeros_like(col_acc)
-    row_acc[...] = jnp.zeros_like(row_acc)
-    live = counts_ref[0]
+    slot_copy.wait()
+    count_copy.wait()
+    live = counts[0, 0]
 
     def place(k, carry):
-        slot = slots_ref[k]
+        slot = slots[k]
         r = slot // tile_cols
         c = slot % tile_cols
-        keep = jnp.where(k < live, 1, 0)
-        tile = tiles[k] * keep
+        keep = jnp.where(k < live, 1.0, 0.0)
+        tile = (tiles[k].astype(F32) * keep).astype(BF16)
         dense_ref[
             pl.ds(pl.multiple_of(r * TILE, TILE), TILE), pl.ds(pl.multiple_of(c * TILE, TILE), TILE)
-        ] = tile.astype(F32).astype(BF16)
-        col_acc[c] += jnp.sum(tile.reshape(TILE // 8, 8, TILE), axis=0)
-        row_acc[r] += tile
+        ] = tile
+        col_acc[c] += jnp.sum(tile.reshape(TILE // 16, 16, TILE), axis=0, dtype=BF16).astype(F32)
         return carry
 
     for p in range(pieces):
         copies[p].wait()
         lax.fori_loop(p * piece, (p + 1) * piece, place, 0, unroll=4)
-    col_ref[...] = jnp.sum(col_acc[...], axis=1).astype(F32)
-    ones = jnp.ones((8, TILE), BF16)
-    for r in range(tile_rows):
-        sums = nt_dot(ones, row_acc[r].astype(F32).astype(BF16))
-        row_ref[pl.ds(r, 1), :] = sums[0:1, :]
+    col_ref[...] = jnp.sum(col_acc[...], axis=1)
 
 
 def densify(slots, counts, tiles, tile_rows, tile_cols):
     pieces = 8
     return call(
-        functools.partial(densify_kernel, tile_rows, tile_cols, pieces),
+        functools.partial(densify_kernel, tile_cols, pieces),
         "densify",
         (),
-        (
-            vmem(tile_rows * TILE, tile_cols * TILE, dtype=BF16),
-            vmem(tile_cols, TILE),
-            vmem(tile_rows, TILE),
-        ),
+        (vmem(tile_rows * TILE, tile_cols * TILE, dtype=BF16), vmem(tile_cols, TILE)),
         flops=tiles.size * 400,
         room=16,
         scratch=(
             vmem(*tiles.shape, dtype=jnp.int32),
-            vmem(tile_cols, 8, TILE, dtype=jnp.int32),
-            vmem(tile_rows, TILE, TILE, dtype=jnp.int32),
+            vmem(tile_cols, 16, TILE),
+            pltpu.SMEM(slots.shape[1:], jnp.int32),
+            pltpu.SMEM(counts.shape, jnp.int32),
             pltpu.SemaphoreType.DMA((pieces,)),
+            pltpu.SemaphoreType.DMA,
+            pltpu.SemaphoreType.DMA,
         ),
         before=(slots, counts, pltpu.with_memory_space_constraint(tiles, pltpu.HBM)),
-        before_specs=(
-            pl.BlockSpec(memory_space=pltpu.SMEM),
-            pl.BlockSpec(memory_space=pltpu.SMEM),
-            pl.BlockSpec(memory_space=pl.ANY),
-        ),
-    )
-
-
-def scales_kernel(*refs):
+        before_specs=[pl.BlockSpec(memory_space=pl.ANY)] * 3,
+    )
+
+
+def row_kernel(dense_ref, row_ref):
+    ones = jnp.ones((8, TILE), BF16)
+    tile_rows = row_ref.shape[0]
+    for r in range(tile_rows):
+        total = dense_ref[pl.ds(r * TILE, TILE), pl.ds(0, TILE)].astype(F32)
+        for c in range(1, dense_ref.shape[1] // TILE):
+            total += dense_ref[pl.ds(r * TILE, TILE), pl.ds(c * TILE, TILE)].astype(F32)
+        row_ref[pl.ds(r, 1), :] = nt_dot(ones, total.astype(BF16))[0:1, :]
+
+
+def row_totals(dense):
+    return call(row_kernel, "row_totals", (dense,), (vmem(dense.shape[0] // TILE, TILE),))[0]
+
+
+def message_kernel(block_ref, own_ref, got_ref, *refs):
+    out_ref = refs[-1]
+    node_rows = block_ref.shape[0]
+    out_ref[pl.ds(0, node_rows), :] = block_ref[...]
+    out_ref[pl.ds(node_rows, own_ref.shape[0]), :] = own_ref[...] + got_ref[...]
+
+
+def message(block, own, got, after):
+    rows = block.shape[0] + own.shape[0]
+    return call(
+        message_kernel, "message", (block, own, got, *after), (vmem(rows, block.shape[1]),)
+    )[0]
+
+
+def scales_kernel(skip, *refs):
     parts, (wide_ref, scale_ref) = refs[:-2], refs[-2:]
-    scale = lax.rsqrt(1.0 + total_of(parts))
+    total = parts[0][skip:, :]
+    for ref in parts[1:]:
+        total = total + ref[skip:, :]
+    scale = lax.rsqrt(1.0 + total)
     for c in range(scale.shape[0]):
         wide_ref[pl.ds(c * TILE, TILE), :] = jnp.broadcast_to(scale[c : c + 1, :], (TILE, TILE)).T
     scale_ref[...] = scale
 
 
-def source_scales(parts):
-    tile_cols = parts[0].shape[0]
-    return call(
-        scales_kernel,
+def source_scales(parts, skip):
+    tile_cols = parts[0].shape[0] - skip
+    return call(
+        functools.partial(scales_kernel, skip),
         "source_scales",
         parts,
         (vmem(tile_cols * TILE, TILE), vmem(tile_cols, TILE)),
@@ -171,7 +198,8 @@
     node_rows, width = blocks[0].shape
     for m in range(row_count):
         start = pl.multiple_of((row ^ m) * node_rows, node_rows)
-        high, low = split(blocks[m][...] * wide_ref[pl.ds(start, node_rows), :])
+        block = blocks[m][pl.ds(0, node_rows), :]
+        high, low = split(block * wide_ref[pl.ds(start, node_rows), :])
         rhs[pl.ds(start, node_rows), :width] = high
         rhs[pl.ds(start, node_rows), width:] = low
     forward_chunks(peers, dense_ref, row_ref, rhs, out_ref)
@@ -332,12 +360,13 @@
     return dict(zip(peers, out))
 
 
-def sum_kernel(*refs):
-    refs[-1][...] = total_of(refs[:-1])
-
-
-def sum_all(parts, name):
-    return call(sum_kernel, name, parts, (vmem(*parts[0].shape),))[0]
+def sum_kernel(count, *refs):
+    refs[-1][...] = total_of(refs[:count])
+
+
+def sum_all(parts, name, after=(), flops=0):
+    kernel = functools.partial(sum_kernel, len(parts))
+    return call(kernel, name, (*parts, *after), (vmem(*parts[0].shape),), flops=flops)[0]
 
 
 def finish_kernel(parts, *refs):
@@ -384,14 +413,11 @@
     blocks[top] = swap(features, "row", top)
     for m in near[1:]:
         blocks[m] = swap(features, "row", m)
-    for m in near[1:]:
-        blocks[top | m] = swap(blocks[top], "row", m)
-
-    dense, col_sums, row_sums = densify(
-        tile_slots[0, 0], tile_counts[0], adj_tiles[0, 0], tile_rows, tile_cols
-    )
-    col_sums = sum_all([col_sums] + [swap(col_sums, "row", m) for m in near[1:]], "near_sums")
-    wide, scale = source_scales([col_sums, swap(col_sums, "row", top)])
+    dense, col_sums = densify(tile_slots[0], tile_counts, adj_tiles[0, 0], tile_rows, tile_cols)
+    sent = message(blocks[top], col_sums, swap(col_sums, "row", top), blocks[1:top])
+    row_sums = row_totals(dense)
+    blocks[top:] = [sent] + [swap(sent, "row", m) for m in near[1:]]
+    wide, scale = source_scales(blocks[top:], node_rows)
 
     given, rhs = forward_first(odd, dense, row_sums, wide, blocks)
     got = swap(given, "col", 1)
@@ -409,18 +435,24 @@
     for m in even:
         backs[m | 1] = swap(backs[m], "col", 1)
     grads = weight_parts(aggregated, pre_grad)
-    late = 2
-    early = [m for m in range(1, row_count) if not m & late]
-    grads = sum_all([grads] + [swap(grads, "row", m) for m in early], "early_grads")
 
     chunks, lhs = backward_first(far, dense, backs)
     ahead = [chunks[top]] + [swap(chunks[top | m], "row", m) for m in near[1:]]
     chunks = backward_second(near, dense, lhs, node_rows)
     mine = [chunks[0]] + [swap(chunks[m], "row", m) for m in near[1:]]
-    grads = sum_all([grads] + [swap(grads, "col", m) for m in range(1, col_count)], "col_grads")
-    mine.append(swap(sum_all(ahead, "ahead_sums"), "row", top))
+    ahead = sum_all(ahead, "ahead_sums")
+    passed = swap(ahead, "row", top)
+
+    rounds = [("row", top), ("row", 1)] if top > 1 else [("row", 1)]
+    rounds += [("col", 1 << b) for b in range(col_count.bit_length() - 1)]
+    rounds += [("row", 1 << b) for b in range(1, top.bit_length() - 1)]
+    behind = [(chunks[0],), ()] + [(ahead,)] * (len(rounds) - 2)
+    for (axis, mask), after in zip(rounds[:-1], behind):
+        grads = sum_all([grads, swap(grads, axis, mask)], f"{axis}{mask}_grads", after)
+    mine = sum_all(mine, "mine_sums", (grads,), HINT)
+    axis, mask = rounds[-1]
     feature_grad, weight_grad, bias_grad = finish(
-        mine, [grads, swap(grads, "row", late)], scale
+        [mine, passed], [grads, swap(grads, axis, mask)], scale
     )
     return activated, feature_grad, weight_grad, bias_grad[0]
 

time: 72.7 us -> 69 us (0.949)
  starting transfers between devices: 37.2 us -> 28.9 us
  waiting for transfers between devices: 22.5 us -> 27.1 us
    ppermute x30 -> x25, starting transfers between devices: 37.2 us -> 28.9 us  [swap(): return lax.ppermute(value, axis, [(i, i ^ mask) for i in range(count)])]
    ppermute x30 -> x25, waiting for transfers between devices: 22.5 us -> 27.1 us  [swap(): return lax.ppermute(value, axis, [(i, i ^ mask) for i in range(count)])]
    pallas_call x14 -> x18, Pallas kernels: 10.1 us -> 10 us  [call(): pl.pallas_call(kernel, out_shape=tuple(outs), in_specs=list(before_specs)...]
  transfers between devices with their start and end apart: 30 -> 25, of which waited for: 14 -> 13; matrix products, arithmetic and copies ran while one was open for 1% -> 1% of each run, Pallas kernels for 10% -> 10%
where the time goes in v3:
time: 69 us; the launch traced here: 68.8 us
  starting transfers between devices  28.9 us (42%)
  waiting for transfers between devices  27.1 us (39%)
  Pallas kernels  10 us (14%)
  between operations  1.47 us (2%)
  local copies, waits for them, and re-layouts  1.32 us (2%)
    ppermute x25, starting transfers between devices, swap(): return lax.ppermute(value, axis, [(i, i ^ mask) for i in range(count)])  28.9 us
    ppermute x25, waiting for transfers between devices, swap(): return lax.ppermute(value, axis, [(i, i ^ mask) for i in range(count)])  27.1 us
    pallas_call x18, Pallas kernels, call(): pl.pallas_call(kernel, out_shape=tuple(outs), in_specs=list(before_specs)...  10 us
  transfers between devices with their start and end apart: 25, of which 13 were waited for; matrix products, arithmetic and copies ran while one was open for 1% of the time, Pallas kernels for 10%

profile of v3, /device:TPU:0, one launch (start us, length us, event | category | flops | bytes accessed | tf_op | source)
XLA Modules:
  0.0 68.8 jit_solution(4286081265887052795)
XLA Ops:
  0.6 3.1 %collective-permute-start.3 = (f32[256,128]{1,0:T(8,128)}, f32[256,128]{1,0:T(8,128)S(1)}, u32[]{:S(2)}, u32[]{:S(2)}) collective-permute-start(f32[256,128]{1,0:T(8,128)} %refs_3_.2), channel_id=1, source_target_pairs={{0,8},{4,12},{8,0},{12,4},{16,24},{20,28},{24,16},{28,20},{1,9},{5... | collective-permute-start | bytes 393224 | tf_op jit(solution)/shard_map/ppermute | solution.py:398
  3.7 1.5 %collective-permute-start.2 = (f32[256,128]{1,0:T(8,128)}, f32[256,128]{1,0:T(8,128)S(1)}, u32[]{:S(2)}, u32[]{:S(2)}) collective-permute-start(f32[256,128]{1,0:T(8,128)} %refs_3_.2), channel_id=1, source_target_pairs={{0,4},{4,0},{8,12},{12,8},{16,20},{20,16},{24,28},{28,24},{1,5},{5... | collective-permute-start | bytes 393224 | tf_op jit(solution)/shard_map/ppermute | solution.py:398
  5.3 2.6 %collective-permute-start = (f32[256,128]{1,0:T(8,128)}, f32[256,128]{1,0:T(8,128)S(1)}, u32[]{:S(2)}, u32[]{:S(2)}) collective-permute-start(f32[256,128]{1,0:T(8,128)} %refs_3_.2), channel_id=1, source_target_pairs={{0,16},{4,20},{8,24},{12,28},{16,0},{20,4},{24,8},{28,12},{1,17},{... | collective-permute-start | bytes 393224 | tf_op jit(solution)/shard_map/ppermute | solution.py:398
  9.5 3.8 %densify.1 = (bf16[1024,2048]{1,0:T(8,128)(2,1)S(1)}, f32[16,128]{1,0:T(8,128)S(1)}) custom-call(s32[1,128]{1,0:T(1,128)S(1)} %bitcast.4, s32[1,1]{1,0:T(1,128)S(6)} %copy.12.counts_hbm, s32[128,128,128]{2,1,0:T(8,128)} %bitcast.6), custom_call_target="tpu_custom_call" | custom-call | flops 838860800 | tf_op jit(solution)/shard_map/densify/pallas_call | solution.py:50
  13.4 4.5 %collective-permute-done.1.got_ref = f32[16,128]{1,0:T(8,128)S(1)} collective-permute-done((f32[16,128]{1,0:T(8,128)S(1)}, f32[16,128]{1,0:T(8,128)S(1)}, u32[]{:S(2)}, u32[]{:S(2)}) %collective-permute-start.1) | collective-permute-done | bytes 8224 | tf_op jit(solution)/shard_map/ppermute | solution.py:398
  18.0 2.6 %collective-permute-start.7 = (f32[272,128]{1,0:T(8,128)S(1)}, f32[272,128]{1,0:T(8,128)S(1)}, u32[]{:S(2)}, u32[]{:S(2)}) collective-permute-start(f32[272,128]{1,0:T(8,128)S(1)} %message.1.refs_0_.refs_7_), channel_id=1, source_target_pairs={{0,12},{4,8},{8,4},{12,0},{16,28},{20,24},{24,20},{28,16},{1,13},{... | collective-permute-start | bytes 417800 | tf_op jit(solution)/shard_map/ppermute | solution.py:398
  22.2 1.8 %collective-permute-done.7.refs_3_.refs_10_ = f32[272,128]{1,0:T(8,128)S(1)} collective-permute-done((f32[272,128]{1,0:T(8,128)S(1)}, f32[272,128]{1,0:T(8,128)S(1)}, u32[]{:S(2)}, u32[]{:S(2)}) %collective-permute-start.7) | collective-permute-done | bytes 139296 | tf_op jit(solution)/shard_map/ppermute | solution.py:398
  24.0 1.6 %collective-permute-done.6.refs_2_.refs_9_ = f32[272,128]{1,0:T(8,128)S(1)} collective-permute-done((f32[272,128]{1,0:T(8,128)S(1)}, f32[272,128]{1,0:T(8,128)S(1)}, u32[]{:S(2)}, u32[]{:S(2)}) %collective-permute-start.6) | collective-permute-done | bytes 139296 | tf_op jit(solution)/shard_map/ppermute | solution.py:398
  29.0 1.6 %collective-permute-start.9 = (f32[264,128]{1,0:T(8,128)S(1)}, f32[264,128]{1,0:T(8,128)S(1)}, u32[]{:S(2)}, u32[]{:S(2)}) collective-permute-start(f32[264,128]{1,0:T(8,128)S(1)} %pair_sums.1), channel_id=1, source_target_pairs={{0,2},{1,3},{2,0},{3,1},{4,6},{5,7},{6,4},{7,5},{8,10},{9,11},{10,... | collective-permute-start | bytes 405512 | tf_op jit(solution)/shard_map/ppermute | solution.py:398
  30.6 4.1 %collective-permute-done.9.refs_2_ = f32[264,128]{1,0:T(8,128)S(1)} collective-permute-done((f32[264,128]{1,0:T(8,128)S(1)}, f32[264,128]{1,0:T(8,128)S(1)}, u32[]{:S(2)}, u32[]{:S(2)}) %collective-permute-start.9) | collective-permute-done | bytes 135200 | tf_op jit(solution)/shard_map/ppermute | solution.py:398
  35.5 1.6 %collective-permute-start.11 = (f32[128,256]{1,0:T(8,128)S(1)}, f32[128,256]{1,0:T(8,128)S(1)}, u32[]{:S(2)}, u32[]{:S(2)}) collective-permute-start(f32[128,256]{1,0:T(8,128)S(1)} %get-tuple-element.32.refs_1_), channel_id=1, source_target_pairs={{0,2},{1,3},{2,0},{3,1},{4,6},{5,7},{6,4},{7,5},{8,10},{9,11},{10,... | collective-permute-start | bytes 393224 | tf_op jit(solution)/shard_map/ppermute | solution.py:398
  37.1 3.5 %collective-permute-done.11.refs_3_ = f32[128,256]{1,0:T(8,128)S(1)} collective-permute-done((f32[128,256]{1,0:T(8,128)S(1)}, f32[128,256]{1,0:T(8,128)S(1)}, u32[]{:S(2)}, u32[]{:S(2)}) %collective-permute-start.11) | collective-permute-done | bytes 131104 | tf_op jit(solution)/shard_map/ppermute | solution.py:398
  42.8 1.0 %collective-permute-start.19 = (f32[128,256]{1,0:T(8,128)S(1)}, f32[128,256]{1,0:T(8,128)S(1)}, u32[]{:S(2)}, u32[]{:S(2)}) collective-permute-start(f32[128,256]{1,0:T(8,128)S(1)} %get-tuple-element.41), channel_id=1, source_target_pairs={{0,4},{4,0},{8,12},{12,8},{16,20},{20,16},{24,28},{28,24},{1,5},{5... | collective-permute-start | bytes 393224 | tf_op jit(solution)/shard_map/ppermute | solution.py:398
  43.7 1.6 %collective-permute-start.20 = (f32[128,256]{1,0:T(8,128)S(1)}, f32[128,256]{1,0:T(8,128)S(1)}, u32[]{:S(2)}, u32[]{:S(2)}) collective-permute-start(f32[128,256]{1,0:T(8,128)S(1)} %get-tuple-element.42), channel_id=1, source_target_pairs={{0,8},{4,12},{8,0},{12,4},{16,24},{20,28},{24,16},{28,20},{1,9},{5... | collective-permute-start | bytes 393224 | tf_op jit(solution)/shard_map/ppermute | solution.py:398
  46.1 2.0 %collective-permute-done.16.refs_1_ = f32[136,128]{1,0:T(8,128)S(1)} collective-permute-done((f32[136,128]{1,0:T(8,128)S(1)}, f32[136,128]{1,0:T(8,128)S(1)}, u32[]{:S(2)}, u32[]{:S(2)}) %collective-permute-start.16) | collective-permute-done | bytes 69664 | tf_op jit(solution)/shard_map/ppermute | solution.py:398
  48.0 1.0 %collective-permute-start.17 = (f32[136,128]{1,0:T(8,128)S(1)}, f32[136,128]{1,0:T(8,128)S(1)}, u32[]{:S(2)}, u32[]{:S(2)}) collective-permute-start(f32[136,128]{1,0:T(8,128)S(1)} %row4_grads.1.refs_0_), channel_id=1, source_target_pairs={{0,4},{4,0},{8,12},{12,8},{16,20},{20,16},{24,28},{28,24},{1,5},{5... | collective-permute-start | bytes 208904 | tf_op jit(solution)/shard_map/ppermute | solution.py:398
  49.7 2.9 %collective-permute-done.17.refs_1_ = f32[136,128]{1,0:T(8,128)S(1)} collective-permute-done((f32[136,128]{1,0:T(8,128)S(1)}, f32[136,128]{1,0:T(8,128)S(1)}, u32[]{:S(2)}, u32[]{:S(2)}) %collective-permute-start.17) | collective-permute-done | bytes 69664 | tf_op jit(solution)/shard_map/ppermute | solution.py:398
  52.6 1.2 %collective-permute-start.13 = (f32[128,256]{1,0:T(8,128)S(1)}, f32[128,256]{1,0:T(8,128)S(1)}, u32[]{:S(2)}, u32[]{:S(2)}) collective-permute-start(f32[128,256]{1,0:T(8,128)S(1)} %get-tuple-element.35), channel_id=1, source_target_pairs={{0,4},{4,0},{8,12},{12,8},{16,20},{20,16},{24,28},{28,24},{1,5},{5... | collective-permute-start | bytes 393224 | tf_op jit(solution)/shard_map/ppermute | solution.py:398
  53.8 2.6 %collective-permute-start.14 = (f32[128,256]{1,0:T(8,128)S(1)}, f32[128,256]{1,0:T(8,128)S(1)}, u32[]{:S(2)}, u32[]{:S(2)}) collective-permute-start(f32[128,256]{1,0:T(8,128)S(1)} %get-tuple-element.36), channel_id=1, source_target_pairs={{0,8},{4,12},{8,0},{12,4},{16,24},{20,28},{24,16},{28,20},{1,9},{5... | collective-permute-start | bytes 393224 | tf_op jit(solution)/shard_map/ppermute | solution.py:398
  57.1 1.6 %collective-permute-start.22 = (f32[136,128]{1,0:T(8,128)S(1)}, f32[136,128]{1,0:T(8,128)S(1)}, u32[]{:S(2)}, u32[]{:S(2)}) collective-permute-start(f32[136,128]{1,0:T(8,128)S(1)} %col1_grads.1.refs_0_), channel_id=1, source_target_pairs={{0,2},{1,3},{2,0},{3,1},{4,6},{5,7},{6,4},{7,5},{8,10},{9,11},{10,... | collective-permute-start | bytes 208904 | tf_op jit(solution)/shard_map/ppermute | solution.py:398
  59.3 1.9 %collective-permute-start.23 = (f32[128,256]{1,0:T(8,128)S(1)}, f32[128,256]{1,0:T(8,128)S(1)}, u32[]{:S(2)}, u32[]{:S(2)}) collective-permute-start(f32[128,256]{1,0:T(8,128)S(1)} %ahead_sums.1.refs_2_), channel_id=1, source_target_pairs={{0,16},{4,20},{8,24},{12,28},{16,0},{20,4},{24,8},{28,12},{1,17},{... | collective-permute-start | bytes 393224 | tf_op jit(solution)/shard_map/ppermute | solution.py:398
  61.5 2.0 %collective-permute-start.24 = (f32[136,128]{1,0:T(8,128)S(1)}, f32[136,128]{1,0:T(8,128)S(1)}, u32[]{:S(2)}, u32[]{:S(2)}) collective-permute-start(f32[136,128]{1,0:T(8,128)S(1)} %col2_grads.1.refs_4_.refs_2_), channel_id=1, source_target_pairs={{0,8},{4,12},{8,0},{12,4},{16,24},{20,28},{24,16},{28,20},{1,9},{5... | collective-permute-start | bytes 208904 | tf_op jit(solution)/shard_map/ppermute | solution.py:398
  63.5 2.5 %collective-permute-done.15.refs_3_ = f32[128,256]{1,0:T(8,128)S(1)} collective-permute-done((f32[128,256]{1,0:T(8,128)S(1)}, f32[128,256]{1,0:T(8,128)S(1)}, u32[]{:S(2)}, u32[]{:S(2)}) %collective-permute-start.15) | collective-permute-done | bytes 131104 | tf_op jit(solution)/shard_map/ppermute | solution.py:398
  66.0 2.0 %collective-permute-done.23.refs_1_ = f32[128,256]{1,0:T(8,128)S(1)} collective-permute-done((f32[128,256]{1,0:T(8,128)S(1)}, f32[128,256]{1,0:T(8,128)S(1)}, u32[]{:S(2)}, u32[]{:S(2)}) %collective-permute-start.23) | collective-permute-done | bytes 131104 | tf_op jit(solution)/shard_map/ppermute | solution.py:398
  (55 shorter events, 12.9 us)
Async XLA Ops:
  0.6 17.3 %collective-permute-start.3 = (f32[256,128]{1,0:T(8,128)}, f32[256,128]{1,0:T(8,128)S(1)}, u32[]{:S(2)}, u32[]{:S(2)}) collective-permute-start(f32[256,128]{1,0:T(8,128)} %refs_3_.2), channel_id=1, source_target_pairs={{0,8},{4,12},{8,0},{12,4},{16,24},{20,28},{24,16},{28,20},{1,9},{5... | collective-permute-start | bytes 393224 | tf_op jit(solution)/shard_map/ppermute | solution.py:398
  3.7 14.2 %collective-permute-start.2 = (f32[256,128]{1,0:T(8,128)}, f32[256,128]{1,0:T(8,128)S(1)}, u32[]{:S(2)}, u32[]{:S(2)}) collective-permute-start(f32[256,128]{1,0:T(8,128)} %refs_3_.2), channel_id=1, source_target_pairs={{0,4},{4,0},{8,12},{12,8},{16,20},{20,16},{24,28},{28,24},{1,5},{5... | collective-permute-start | bytes 393224 | tf_op jit(solution)/shard_map/ppermute | solution.py:398
  5.3 12.7 %collective-permute-start = (f32[256,128]{1,0:T(8,128)}, f32[256,128]{1,0:T(8,128)S(1)}, u32[]{:S(2)}, u32[]{:S(2)}) collective-permute-start(f32[256,128]{1,0:T(8,128)} %refs_3_.2), channel_id=1, source_target_pairs={{0,16},{4,20},{8,24},{12,28},{16,0},{20,4},{24,8},{28,12},{1,17},{... | collective-permute-start | bytes 393224 | tf_op jit(solution)/shard_map/ppermute | solution.py:398
  7.8 10.1 %collective-permute-start.4 = (f32[256,128]{1,0:T(8,128)}, f32[256,128]{1,0:T(8,128)S(1)}, u32[]{:S(2)}, u32[]{:S(2)}) collective-permute-start(f32[256,128]{1,0:T(8,128)} %refs_3_.2), channel_id=1, source_target_pairs={{0,12},{4,8},{8,4},{12,0},{16,28},{20,24},{24,20},{28,16},{1,13},{... | collective-permute-start | bytes 393224 | tf_op jit(solution)/shard_map/ppermute | solution.py:398
  13.3 4.6 %collective-permute-start.1 = (f32[16,128]{1,0:T(8,128)S(1)}, f32[16,128]{1,0:T(8,128)S(1)}, u32[]{:S(2)}, u32[]{:S(2)}) collective-permute-start(f32[16,128]{1,0:T(8,128)S(1)} %get-tuple-element.27.own_ref), channel_id=1, source_target_pairs={{0,16},{4,20},{8,24},{12,28},{16,0},{20,4},{24,8},{28,12},{1,17},{... | collective-permute-start | bytes 24584 | tf_op jit(solution)/shard_map/ppermute | solution.py:398
  18.0 6.0 %collective-permute-start.7 = (f32[272,128]{1,0:T(8,128)S(1)}, f32[272,128]{1,0:T(8,128)S(1)}, u32[]{:S(2)}, u32[]{:S(2)}) collective-permute-start(f32[272,128]{1,0:T(8,128)S(1)} %message.1.refs_0_.refs_7_), channel_id=1, source_target_pairs={{0,12},{4,8},{8,4},{12,0},{16,28},{20,24},{24,20},{28,16},{1,13},{... | collective-permute-start | bytes 417800 | tf_op jit(solution)/shard_map/ppermute | solution.py:398
  20.6 5.1 %collective-permute-start.6 = (f32[272,128]{1,0:T(8,128)S(1)}, f32[272,128]{1,0:T(8,128)S(1)}, u32[]{:S(2)}, u32[]{:S(2)}) collective-permute-start(f32[272,128]{1,0:T(8,128)S(1)} %message.1.refs_0_.refs_7_), channel_id=1, source_target_pairs={{0,8},{4,12},{8,0},{12,4},{16,24},{20,28},{24,16},{28,20},{1,9},{5... | collective-permute-start | bytes 417800 | tf_op jit(solution)/shard_map/ppermute | solution.py:398
  21.0 5.1 %collective-permute-start.5 = (f32[272,128]{1,0:T(8,128)S(1)}, f32[272,128]{1,0:T(8,128)S(1)}, u32[]{:S(2)}, u32[]{:S(2)}) collective-permute-start(f32[272,128]{1,0:T(8,128)S(1)} %message.1.refs_0_.refs_7_), channel_id=1, source_target_pairs={{0,4},{4,0},{8,12},{12,8},{16,20},{20,16},{24,28},{28,24},{1,5},{5... | collective-permute-start | bytes 417800 | tf_op jit(solution)/shard_map/ppermute | solution.py:398
  27.4 1.6 %collective-permute-start.8 = (f32[2,264,128]{2,1,0:T(8,128)S(1)}, f32[2,264,128]{2,1,0:T(8,128)S(1)}, u32[]{:S(2)}, u32[]{:S(2)}) collective-permute-start(f32[2,264,128]{2,1,0:T(8,128)S(1)} %get-tuple-element.30), channel_id=1, source_target_pairs={{0,1},{1,0},{2,3},{3,2},{4,5},{5,4},{6,7},{7,6},{8,9},{9,8},{10,11... | collective-permute-start | bytes 811016 | tf_op jit(solution)/shard_map/ppermute | solution.py:398
  29.0 5.7 %collective-permute-start.9 = (f32[264,128]{1,0:T(8,128)S(1)}, f32[264,128]{1,0:T(8,128)S(1)}, u32[]{:S(2)}, u32[]{:S(2)}) collective-permute-start(f32[264,128]{1,0:T(8,128)S(1)} %pair_sums.1), channel_id=1, source_target_pairs={{0,2},{1,3},{2,0},{3,1},{4,6},{5,7},{6,4},{7,5},{8,10},{9,11},{10,... | collective-permute-start | bytes 405512 | tf_op jit(solution)/shard_map/ppermute | solution.py:398
  35.5 5.0 %collective-permute-start.11 = (f32[128,256]{1,0:T(8,128)S(1)}, f32[128,256]{1,0:T(8,128)S(1)}, u32[]{:S(2)}, u32[]{:S(2)}) collective-permute-start(f32[128,256]{1,0:T(8,128)S(1)} %get-tuple-element.32.refs_1_), channel_id=1, source_target_pairs={{0,2},{1,3},{2,0},{3,1},{4,6},{5,7},{6,4},{7,5},{8,10},{9,11},{10,... | collective-permute-start | bytes 393224 | tf_op jit(solution)/shard_map/ppermute | solution.py:398
  37.1 4.2 %collective-permute-start.10 = (f32[128,256]{1,0:T(8,128)S(1)}, f32[128,256]{1,0:T(8,128)S(1)}, u32[]{:S(2)}, u32[]{:S(2)}) collective-permute-start(f32[128,256]{1,0:T(8,128)S(1)} %get-tuple-element.32.refs_1_), channel_id=1, source_target_pairs={{0,1},{1,0},{2,3},{3,2},{4,5},{5,4},{6,7},{7,6},{8,9},{9,8},{10,11... | collective-permute-start | bytes 393224 | tf_op jit(solution)/shard_map/ppermute | solution.py:398
  40.9 7.2 %collective-permute-start.16 = (f32[136,128]{1,0:T(8,128)S(1)}, f32[136,128]{1,0:T(8,128)S(1)}, u32[]{:S(2)}, u32[]{:S(2)}) collective-permute-start(f32[136,128]{1,0:T(8,128)S(1)} %weight_parts.1.refs_0_), channel_id=1, source_target_pairs={{0,16},{4,20},{8,24},{12,28},{16,0},{20,4},{24,8},{28,12},{1,17},{... | collective-permute-start | bytes 208904 | tf_op jit(solution)/shard_map/ppermute | solution.py:398
  42.8 11.0 %collective-permute-start.19 = (f32[128,256]{1,0:T(8,128)S(1)}, f32[128,256]{1,0:T(8,128)S(1)}, u32[]{:S(2)}, u32[]{:S(2)}) collective-permute-start(f32[128,256]{1,0:T(8,128)S(1)} %get-tuple-element.41), channel_id=1, source_target_pairs={{0,4},{4,0},{8,12},{12,8},{16,20},{20,16},{24,28},{28,24},{1,5},{5... | collective-permute-start | bytes 393224 | tf_op jit(solution)/shard_map/ppermute | solution.py:398
  43.7 12.7 %collective-permute-start.20 = (f32[128,256]{1,0:T(8,128)S(1)}, f32[128,256]{1,0:T(8,128)S(1)}, u32[]{:S(2)}, u32[]{:S(2)}) collective-permute-start(f32[128,256]{1,0:T(8,128)S(1)} %get-tuple-element.42), channel_id=1, source_target_pairs={{0,8},{4,12},{8,0},{12,4},{16,24},{20,28},{24,16},{28,20},{1,9},{5... | collective-permute-start | bytes 393224 | tf_op jit(solution)/shard_map/ppermute | solution.py:398
  48.0 4.5 %collective-permute-start.17 = (f32[136,128]{1,0:T(8,128)S(1)}, f32[136,128]{1,0:T(8,128)S(1)}, u32[]{:S(2)}, u32[]{:S(2)}) collective-permute-start(f32[136,128]{1,0:T(8,128)S(1)} %row4_grads.1.refs_0_), channel_id=1, source_target_pairs={{0,4},{4,0},{8,12},{12,8},{16,20},{20,16},{24,28},{28,24},{1,5},{5... | collective-permute-start | bytes 208904 | tf_op jit(solution)/shard_map/ppermute | solution.py:398
  49.0 8.0 %collective-permute-start.21 = (f32[128,256]{1,0:T(8,128)S(1)}, f32[128,256]{1,0:T(8,128)S(1)}, u32[]{:S(2)}, u32[]{:S(2)}) collective-permute-start(f32[128,256]{1,0:T(8,128)S(1)} %get-tuple-element.43), channel_id=1, source_target_pairs={{0,12},{4,8},{8,4},{12,0},{16,28},{20,24},{24,20},{28,16},{1,13},{... | collective-permute-start | bytes 393224 | tf_op jit(solution)/shard_map/ppermute | solution.py:398
  52.6 4.5 %collective-permute-start.18 = (f32[136,128]{1,0:T(8,128)S(1)}, f32[136,128]{1,0:T(8,128)S(1)}, u32[]{:S(2)}, u32[]{:S(2)}) collective-permute-start(f32[136,128]{1,0:T(8,128)S(1)} %row1_grads.1.refs_0_), channel_id=1, source_target_pairs={{0,1},{1,0},{2,3},{3,2},{4,5},{5,4},{6,7},{7,6},{8,9},{9,8},{10,11... | collective-permute-start | bytes 208904 | tf_op jit(solution)/shard_map/ppermute | solution.py:398
  52.6 10.9 %collective-permute-start.13 = (f32[128,256]{1,0:T(8,128)S(1)}, f32[128,256]{1,0:T(8,128)S(1)}, u32[]{:S(2)}, u32[]{:S(2)}) collective-permute-start(f32[128,256]{1,0:T(8,128)S(1)} %get-tuple-element.35), channel_id=1, source_target_pairs={{0,4},{4,0},{8,12},{12,8},{16,20},{20,16},{24,28},{28,24},{1,5},{5... | collective-permute-start | bytes 393224 | tf_op jit(solution)/shard_map/ppermute | solution.py:398
  53.8 9.7 %collective-permute-start.14 = (f32[128,256]{1,0:T(8,128)S(1)}, f32[128,256]{1,0:T(8,128)S(1)}, u32[]{:S(2)}, u32[]{:S(2)}) collective-permute-start(f32[128,256]{1,0:T(8,128)S(1)} %get-tuple-element.36), channel_id=1, source_target_pairs={{0,8},{4,12},{8,0},{12,4},{16,24},{20,28},{24,16},{28,20},{1,9},{5... | collective-permute-start | bytes 393224 | tf_op jit(solution)/shard_map/ppermute | solution.py:398
  56.4 9.6 %collective-permute-start.15 = (f32[128,256]{1,0:T(8,128)S(1)}, f32[128,256]{1,0:T(8,128)S(1)}, u32[]{:S(2)}, u32[]{:S(2)}) collective-permute-start(f32[128,256]{1,0:T(8,128)S(1)} %get-tuple-element.37), channel_id=1, source_target_pairs={{0,12},{4,8},{8,4},{12,0},{16,28},{20,24},{24,20},{28,16},{1,13},{... | collective-permute-start | bytes 393224 | tf_op jit(solution)/shard_map/ppermute | solution.py:398
  57.1 4.4 %collective-permute-start.22 = (f32[136,128]{1,0:T(8,128)S(1)}, f32[136,128]{1,0:T(8,128)S(1)}, u32[]{:S(2)}, u32[]{:S(2)}) collective-permute-start(f32[136,128]{1,0:T(8,128)S(1)} %col1_grads.1.refs_0_), channel_id=1, source_target_pairs={{0,2},{1,3},{2,0},{3,1},{4,6},{5,7},{6,4},{7,5},{8,10},{9,11},{10,... | collective-permute-start | bytes 208904 | tf_op jit(solution)/shard_map/ppermute | solution.py:398
  59.3 8.8 %collective-permute-start.23 = (f32[128,256]{1,0:T(8,128)S(1)}, f32[128,256]{1,0:T(8,128)S(1)}, u32[]{:S(2)}, u32[]{:S(2)}) collective-permute-start(f32[128,256]{1,0:T(8,128)S(1)} %ahead_sums.1.refs_2_), channel_id=1, source_target_pairs={{0,16},{4,20},{8,24},{12,28},{16,0},{20,4},{24,8},{28,12},{1,17},{... | collective-permute-start | bytes 393224 | tf_op jit(solution)/shard_map/ppermute | solution.py:398
  61.5 6.6 %collective-permute-start.24 = (f32[136,128]{1,0:T(8,128)S(1)}, f32[136,128]{1,0:T(8,128)S(1)}, u32[]{:S(2)}, u32[]{:S(2)}) collective-permute-start(f32[136,128]{1,0:T(8,128)S(1)} %col2_grads.1.refs_4_.refs_2_), channel_id=1, source_target_pairs={{0,8},{4,12},{8,0},{12,4},{16,24},{20,28},{24,16},{28,20},{1,9},{5... | collective-permute-start | bytes 208904 | tf_op jit(solution)/shard_map/ppermute | solution.py:398
  (6 other events, 67.4 us)

commit v4 on v3

--- a/solution.py
+++ b/solution.py
@@ -122,7 +122,11 @@
             pltpu.SemaphoreType.DMA,
             pltpu.SemaphoreType.DMA,
         ),
-        before=(slots, counts, pltpu.with_memory_space_constraint(tiles, pltpu.HBM)),
+        before=(
+            pltpu.with_memory_space_constraint(slots, pltpu.HBM),
+            counts,
+            pltpu.with_memory_space_constraint(tiles, pltpu.HBM),
+        ),
         before_specs=[pl.BlockSpec(memory_space=pl.ANY)] * 3,
     )
 
@@ -307,6 +311,33 @@
     )[0]
 
 
+def folds(rows, width, node_rows):
+    step = -(-rows * width // node_rows // 8) * 8
+    return [(at, min(step, rows - at)) for at in range(0, rows, step)], step
+
+
+def carried_kernel(block_ref, own_ref, got_ref, out_ref):
+    width, node_rows = block_ref.shape
+    parts, step = folds(own_ref.shape[0], width, node_rows)
+    out_ref[pl.ds(0, width), :] = block_ref[...]
+    for j, (at, size) in enumerate(parts):
+        out_ref[pl.ds(width, size), pl.ds(j * width, width)] = (
+            own_ref[pl.ds(at, size), :] + got_ref[pl.ds(at, size), :]
+        )
+        if size < step:
+            out_ref[pl.ds(width + size, step - size), pl.ds(j * width, width)] = jnp.zeros(
+                (step - size, width), F32
+            )
+
+
+def carried(block, own, got):
+    width, node_rows = block.shape
+    step = folds(own.shape[0], width, node_rows)[1]
+    return call(
+        carried_kernel, "carried", (block, own, got), (vmem(width + step, node_rows),)
+    )[0]
+
+
 def backward_chunks(peers, dense_ref, lhs, outs):
     row = lax.axis_index("row")
     width, node_rows = outs[0].shape
@@ -316,18 +347,21 @@
         out_ref[...] = both[:width, :] + both[width:, :]
 
 
-def backward_first_kernel(peers, col_count, *refs):
-    dense_ref = refs[0]
-    blocks = refs[1 : 1 + col_count]
-    outs, lhs = refs[1 + col_count : -1], refs[-1]
+def backward_first_kernel(peers, carrier, *refs):
+    outs, lhs, grad_ref = refs[-2 - len(peers) : -2], refs[-2], refs[-1]
+    dense_ref, blocks = refs[0], refs[1 : -2 - len(peers)]
     col = lax.axis_index("col")
     width, node_rows = blocks[0].shape
-    for m in range(col_count):
+    for m, block in enumerate(blocks):
         start = pl.multiple_of((col ^ m) * node_rows, node_rows)
-        high, low = split(blocks[m][...])
+        high, low = split(block[pl.ds(0, width), :])
         lhs[:width, pl.ds(start, node_rows)] = high
         lhs[width:, pl.ds(start, node_rows)] = low
     backward_chunks(peers, dense_ref, lhs, outs)
+    parts, step = folds(grad_ref.shape[0], width, node_rows)
+    for j, (at, size) in enumerate(parts):
+        rows, cols = pl.ds(width, size), pl.ds(j * width, width)
+        grad_ref[pl.ds(at, size), :] = blocks[carrier][rows, cols] + blocks[carrier | 1][rows, cols]
 
 
 def backward_second_kernel(peers, dense_ref, lhs, *outs):
@@ -338,13 +372,14 @@
     width, node_rows = blocks[0].shape
     rows = dense.shape[0]
     out = call(
-        functools.partial(backward_first_kernel, peers, len(blocks)),
+        functools.partial(backward_first_kernel, peers, len(blocks) - 2),
         "backward_first",
         (dense, *blocks),
-        [vmem(width, node_rows)] * len(peers) + [vmem(2 * width, rows, dtype=BF16)],
+        [vmem(width, node_rows)] * len(peers)
+        + [vmem(2 * width, rows, dtype=BF16), vmem(width + PAD, width)],
         flops=4 * len(peers) * node_rows * rows * width,
     )
-    return dict(zip(peers, out)), out[-1]
+    return dict(zip(peers, out)), out[-2], out[-1]
 
 
 def backward_second(peers, dense, lhs, node_rows):
@@ -367,6 +402,14 @@
 def sum_all(parts, name, after=(), flops=0):
     kernel = functools.partial(sum_kernel, len(parts))
     return call(kernel, name, (*parts, *after), (vmem(*parts[0].shape),), flops=flops)[0]
+
+
+def hand_over_kernel(value_ref, *refs):
+    refs[-1][...] = value_ref[...]
+
+
+def hand_over(value, after):
+    return call(hand_over_kernel, "hand_over", (value, *after), (hbm(*value.shape),))[0]
 
 
 def finish_kernel(parts, *refs):
@@ -432,27 +475,29 @@
     backs[0] = back
     for m in even[1:]:
         backs[m] = swap(back, "col", m)
+    grads = weight_parts(aggregated, pre_grad)
+    carrier = even[-1]
+    backs[carrier] = carried(backs[carrier], grads, swap(grads, "row", top))
     for m in even:
         backs[m | 1] = swap(backs[m], "col", 1)
-    grads = weight_parts(aggregated, pre_grad)
-
-    chunks, lhs = backward_first(far, dense, backs)
+    rounds = [("row", 1)] if top > 1 else []
+    rounds += [("col", 1 << b) for b in range(1, col_count.bit_length() - 1)]
+    rounds += [("row", 1 << b) for b in range(1, top.bit_length() - 1)]
+
+    chunks, lhs, grads = backward_first(far, dense, backs)
     ahead = [chunks[top]] + [swap(chunks[top | m], "row", m) for m in near[1:]]
     chunks = backward_second(near, dense, lhs, node_rows)
     mine = [chunks[0]] + [swap(chunks[m], "row", m) for m in near[1:]]
     ahead = sum_all(ahead, "ahead_sums")
     passed = swap(ahead, "row", top)
-
-    rounds = [("row", top), ("row", 1)] if top > 1 else [("row", 1)]
-    rounds += [("col", 1 << b) for b in range(col_count.bit_length() - 1)]
-    rounds += [("row", 1 << b) for b in range(1, top.bit_length() - 1)]
-    behind = [(chunks[0],), ()] + [(ahead,)] * (len(rounds) - 2)
-    for (axis, mask), after in zip(rounds[:-1], behind):
-        grads = sum_all([grads, swap(grads, axis, mask)], f"{axis}{mask}_grads", after)
-    mine = sum_all(mine, "mine_sums", (grads,), HINT)
+    for axis, mask in rounds[:-1]:
+        grads = sum_all([grads, swap(grads, axis, mask)], f"{axis}{mask}_grads")
+    activated = hand_over(activated, (grads,))
+    mine = sum_all(mine, "mine_sums", (grads,), 2 * HINT)
+    mine = sum_all([mine, passed], "last_sums", (), HINT // 2)
     axis, mask = rounds[-1]
     feature_grad, weight_grad, bias_grad = finish(
-        [mine, passed], [grads, swap(grads, axis, mask)], scale
+        [mine], [grads, swap(grads, axis, mask)], scale
     )
     return activated, feature_grad, weight_grad, bias_grad[0]
 

time: 69 us -> 66.9 us (0.970)
  starting transfers between devices: 28.9 us -> 26.9 us
  local copies, waits for them, and re-layouts: 1.32 us -> 0.02 us
  Pallas kernels: 10 us -> 10.7 us
    ppermute x25 -> x24, starting transfers between devices: 28.9 us -> 26.9 us  [swap(): return lax.ppermute(value, axis, [(i, i ^ mask) for i in range(count)])]
    unnamed x11 -> x8, local copies, waits for them, and re-layouts: 1.32 us -> 0.02 us
    pallas_call x18 -> x19, Pallas kernels: 10 us -> 10.7 us  [call(): pl.pallas_call(kernel, out_shape=tuple(outs), in_specs=list(before_specs)...]
    ppermute x25 -> x24, waiting for transfers between devices: 27.1 us -> 27.7 us  [swap(): return lax.ppermute(value, axis, [(i, i ^ mask) for i in range(count)])]
  transfers between devices with their start and end apart: 25 -> 24, of which waited for: 13 -> 11; matrix products, arithmetic and copies ran while one was open for 1% -> 0% of each run, Pallas kernels for 10% -> 10%
where the time goes in v4:
time: 66.9 us; the launch traced here: 66.8 us
  waiting for transfers between devices  27.7 us (41%)
  starting transfers between devices  26.9 us (40%)
  Pallas kernels  10.7 us (16%)
  between operations  1.45 us (2%)
    ppermute x24, waiting for transfers between devices, swap(): return lax.ppermute(value, axis, [(i, i ^ mask) for i in range(count)])  27.7 us
    ppermute x24, starting transfers between devices, swap(): return lax.ppermute(value, axis, [(i, i ^ mask) for i in range(count)])  26.9 us
    pallas_call x19, Pallas kernels, call(): pl.pallas_call(kernel, out_shape=tuple(outs), in_specs=list(before_specs)...  10.7 us
  transfers between devices with their start and end apart: 24, of which 11 were waited for; matrix products, arithmetic and copies ran while one was open for 0% of the time, Pallas kernels for 10%

profile of v4, /device:TPU:0, one launch (start us, length us, event | category | flops | bytes accessed | tf_op | source)
XLA Modules:
  0.0 66.8 jit_solution(16662420948207840276)
XLA Ops:
  0.6 3.1 %collective-permute-start.3 = (f32[256,128]{1,0:T(8,128)}, f32[256,128]{1,0:T(8,128)S(1)}, u32[]{:S(2)}, u32[]{:S(2)}) collective-permute-start(f32[256,128]{1,0:T(8,128)} %refs_3_.2), channel_id=1, source_target_pairs={{0,8},{4,12},{8,0},{12,4},{16,24},{20,28},{24,16},{28,20},{1,9},{5... | collective-permute-start | bytes 393224 | tf_op jit(solution)/shard_map/ppermute | solution.py:441
  3.7 1.5 %collective-permute-start.2 = (f32[256,128]{1,0:T(8,128)}, f32[256,128]{1,0:T(8,128)S(1)}, u32[]{:S(2)}, u32[]{:S(2)}) collective-permute-start(f32[256,128]{1,0:T(8,128)} %refs_3_.2), channel_id=1, source_target_pairs={{0,4},{4,0},{8,12},{12,8},{16,20},{20,16},{24,28},{28,24},{1,5},{5... | collective-permute-start | bytes 393224 | tf_op jit(solution)/shard_map/ppermute | solution.py:441
  5.3 2.6 %collective-permute-start = (f32[256,128]{1,0:T(8,128)}, f32[256,128]{1,0:T(8,128)S(1)}, u32[]{:S(2)}, u32[]{:S(2)}) collective-permute-start(f32[256,128]{1,0:T(8,128)} %refs_3_.2), channel_id=1, source_target_pairs={{0,16},{4,20},{8,24},{12,28},{16,0},{20,4},{24,8},{28,12},{1,17},{... | collective-permute-start | bytes 393224 | tf_op jit(solution)/shard_map/ppermute | solution.py:441
  8.9 3.7 %densify.1 = (bf16[1024,2048]{1,0:T(8,128)(2,1)S(1)}, f32[16,128]{1,0:T(8,128)S(1)}) custom-call(s32[1,128]{1,0:T(1,128)} %bitcast.6, s32[1,1]{1,0:T(1,128)S(6)} %copy.11.counts_hbm, s32[128,128,128]{2,1,0:T(8,128)} %bitcast.5), custom_call_target="tpu_custom_call" | custom-call | flops 838860800 | tf_op jit(solution)/shard_map/densify/pallas_call | solution.py:50
  12.7 4.5 %collective-permute-done.1.got_ref = f32[16,128]{1,0:T(8,128)S(1)} collective-permute-done((f32[16,128]{1,0:T(8,128)S(1)}, f32[16,128]{1,0:T(8,128)S(1)}, u32[]{:S(2)}, u32[]{:S(2)}) %collective-permute-start.1) | collective-permute-done | bytes 8224 | tf_op jit(solution)/shard_map/ppermute | solution.py:441
  17.3 2.6 %collective-permute-start.7 = (f32[272,128]{1,0:T(8,128)S(1)}, f32[272,128]{1,0:T(8,128)S(1)}, u32[]{:S(2)}, u32[]{:S(2)}) collective-permute-start(f32[272,128]{1,0:T(8,128)S(1)} %message.1.refs_0_.refs_7_), channel_id=1, source_target_pairs={{0,12},{4,8},{8,4},{12,0},{16,28},{20,24},{24,20},{28,16},{1,13},{... | collective-permute-start | bytes 417800 | tf_op jit(solution)/shard_map/ppermute | solution.py:441
  21.5 1.8 %collective-permute-done.7.refs_3_.refs_10_ = f32[272,128]{1,0:T(8,128)S(1)} collective-permute-done((f32[272,128]{1,0:T(8,128)S(1)}, f32[272,128]{1,0:T(8,128)S(1)}, u32[]{:S(2)}, u32[]{:S(2)}) %collective-permute-start.7) | collective-permute-done | bytes 139296 | tf_op jit(solution)/shard_map/ppermute | solution.py:441
  23.3 1.6 %collective-permute-done.6.refs_2_.refs_9_ = f32[272,128]{1,0:T(8,128)S(1)} collective-permute-done((f32[272,128]{1,0:T(8,128)S(1)}, f32[272,128]{1,0:T(8,128)S(1)}, u32[]{:S(2)}, u32[]{:S(2)}) %collective-permute-start.6) | collective-permute-done | bytes 139296 | tf_op jit(solution)/shard_map/ppermute | solution.py:441
  25.8 1.0 %forward_first.1 = (f32[2,264,128]{2,1,0:T(8,128)S(1)}, bf16[2048,256]{1,0:T(8,128)(2,1)S(1)}) custom-call(bf16[1024,2048]{1,0:T(8,128)(2,1)S(1)} %get-tuple-element.27.dense_ref.refs_0_, f32[8,128]{1,0:T(8,128)S(1)} %row_totals.1.refs_1_.row_ref, f32[2048,128]{1,0:T(8,128)S(1)} %get-tuple-element.29.refs_2_, f32[256,128]{1,0:T(8,128)S(1)} %copy-done, ...), custom_call_target="tpu_custom_call" | custom-call | flops 536870912 | bytes 10522624 | tf_op jit(solution)/shard_map/forward_first/pallas_call | solution.py:50
  28.4 1.6 %collective-permute-start.9 = (f32[264,128]{1,0:T(8,128)S(1)}, f32[264,128]{1,0:T(8,128)S(1)}, u32[]{:S(2)}, u32[]{:S(2)}) collective-permute-start(f32[264,128]{1,0:T(8,128)S(1)} %pair_sums.1), channel_id=1, source_target_pairs={{0,2},{1,3},{2,0},{3,1},{4,6},{5,7},{6,4},{7,5},{8,10},{9,11},{10,... | collective-permute-start | bytes 405512 | tf_op jit(solution)/shard_map/ppermute | solution.py:441
  29.9 4.1 %collective-permute-done.9.refs_2_ = f32[264,128]{1,0:T(8,128)S(1)} collective-permute-done((f32[264,128]{1,0:T(8,128)S(1)}, f32[264,128]{1,0:T(8,128)S(1)}, u32[]{:S(2)}, u32[]{:S(2)}) %collective-permute-start.9) | collective-permute-done | bytes 135200 | tf_op jit(solution)/shard_map/ppermute | solution.py:441
  34.9 1.6 %collective-permute-start.11 = (f32[128,256]{1,0:T(8,128)S(1)}, f32[128,256]{1,0:T(8,128)S(1)}, u32[]{:S(2)}, u32[]{:S(2)}) collective-permute-start(f32[128,256]{1,0:T(8,128)S(1)} %get-tuple-element.33.refs_1_), channel_id=1, source_target_pairs={{0,2},{1,3},{2,0},{3,1},{4,6},{5,7},{6,4},{7,5},{8,10},{9,11},{10,... | collective-permute-start | bytes 393224 | tf_op jit(solution)/shard_map/ppermute | solution.py:441
  37.1 4.9 %collective-permute-done.12.got_ref = f32[136,128]{1,0:T(8,128)S(1)} collective-permute-done((f32[136,128]{1,0:T(8,128)S(1)}, f32[136,128]{1,0:T(8,128)S(1)}, u32[]{:S(2)}, u32[]{:S(2)}) %collective-permute-start.12) | collective-permute-done | bytes 69664 | tf_op jit(solution)/shard_map/ppermute | solution.py:441
  42.6 1.1 %collective-permute-done.10.refs_2_ = f32[128,256]{1,0:T(8,128)S(1)} collective-permute-done((f32[128,256]{1,0:T(8,128)S(1)}, f32[128,256]{1,0:T(8,128)S(1)}, u32[]{:S(2)}, u32[]{:S(2)}) %collective-permute-start.10) | collective-permute-done | bytes 131104 | tf_op jit(solution)/shard_map/ppermute | solution.py:441
  44.6 1.0 %collective-permute-start.19 = (f32[128,256]{1,0:T(8,128)S(1)}, f32[128,256]{1,0:T(8,128)S(1)}, u32[]{:S(2)}, u32[]{:S(2)}) collective-permute-start(f32[128,256]{1,0:T(8,128)S(1)} %get-tuple-element.43), channel_id=1, source_target_pairs={{0,4},{4,0},{8,12},{12,8},{16,20},{20,16},{24,28},{28,24},{1,5},{5... | collective-permute-start | bytes 393224 | tf_op jit(solution)/shard_map/ppermute | solution.py:441
  45.6 1.6 %collective-permute-start.20 = (f32[128,256]{1,0:T(8,128)S(1)}, f32[128,256]{1,0:T(8,128)S(1)}, u32[]{:S(2)}, u32[]{:S(2)}) collective-permute-start(f32[128,256]{1,0:T(8,128)S(1)} %get-tuple-element.44), channel_id=1, source_target_pairs={{0,8},{4,12},{8,0},{12,4},{16,24},{20,28},{24,16},{28,20},{1,9},{5... | collective-permute-start | bytes 393224 | tf_op jit(solution)/shard_map/ppermute | solution.py:441
  47.1 1.1 %collective-permute-start.14 = (f32[136,128]{1,0:T(8,128)S(1)}, f32[136,128]{1,0:T(8,128)S(1)}, u32[]{:S(2)}, u32[]{:S(2)}) collective-permute-start(f32[136,128]{1,0:T(8,128)S(1)} %get-tuple-element.36.refs_0_), channel_id=1, source_target_pairs={{0,4},{4,0},{8,12},{12,8},{16,20},{20,16},{24,28},{28,24},{1,5},{5... | collective-permute-start | bytes 208904 | tf_op jit(solution)/shard_map/ppermute | solution.py:441
  49.8 1.2 %collective-permute-start.16 = (f32[128,256]{1,0:T(8,128)S(1)}, f32[128,256]{1,0:T(8,128)S(1)}, u32[]{:S(2)}, u32[]{:S(2)}) collective-permute-start(f32[128,256]{1,0:T(8,128)S(1)} %get-tuple-element.39), channel_id=1, source_target_pairs={{0,4},{4,0},{8,12},{12,8},{16,20},{20,16},{24,28},{28,24},{1,5},{5... | collective-permute-start | bytes 393224 | tf_op jit(solution)/shard_map/ppermute | solution.py:441
  51.0 3.9 %collective-permute-done.14.refs_1_ = f32[136,128]{1,0:T(8,128)S(1)} collective-permute-done((f32[136,128]{1,0:T(8,128)S(1)}, f32[136,128]{1,0:T(8,128)S(1)}, u32[]{:S(2)}, u32[]{:S(2)}) %collective-permute-start.14) | collective-permute-done | bytes 69664 | tf_op jit(solution)/shard_map/ppermute | solution.py:441
  54.9 1.9 %collective-permute-start.17 = (f32[128,256]{1,0:T(8,128)S(1)}, f32[128,256]{1,0:T(8,128)S(1)}, u32[]{:S(2)}, u32[]{:S(2)}) collective-permute-start(f32[128,256]{1,0:T(8,128)S(1)} %get-tuple-element.40), channel_id=1, source_target_pairs={{0,8},{4,12},{8,0},{12,4},{16,24},{20,28},{24,16},{28,20},{1,9},{5... | collective-permute-start | bytes 393224 | tf_op jit(solution)/shard_map/ppermute | solution.py:441
  57.9 1.0 %collective-permute-start.22 = (f32[128,256]{1,0:T(8,128)S(1)}, f32[128,256]{1,0:T(8,128)S(1)}, u32[]{:S(2)}, u32[]{:S(2)}) collective-permute-start(f32[128,256]{1,0:T(8,128)S(1)} %ahead_sums.1), channel_id=1, source_target_pairs={{0,16},{4,20},{8,24},{12,28},{16,0},{20,4},{24,8},{28,12},{1,17},{... | collective-permute-start | bytes 393224 | tf_op jit(solution)/shard_map/ppermute | solution.py:441
  58.9 2.8 %collective-permute-done.15.refs_1_ = f32[136,128]{1,0:T(8,128)S(1)} collective-permute-done((f32[136,128]{1,0:T(8,128)S(1)}, f32[136,128]{1,0:T(8,128)S(1)}, u32[]{:S(2)}, u32[]{:S(2)}) %collective-permute-start.15) | collective-permute-done | bytes 69664 | tf_op jit(solution)/shard_map/ppermute | solution.py:441
  61.6 2.0 %collective-permute-start.23 = (f32[136,128]{1,0:T(8,128)S(1)}, f32[136,128]{1,0:T(8,128)S(1)}, u32[]{:S(2)}, u32[]{:S(2)}) collective-permute-start(f32[136,128]{1,0:T(8,128)S(1)} %col2_grads.1.refs_0_.refs_4_.refs_1_), channel_id=1, source_target_pairs={{0,8},{4,12},{8,0},{12,4},{16,24},{20,28},{24,16},{28,20},{1,9},{5... | collective-permute-start | bytes 208904 | tf_op jit(solution)/shard_map/ppermute | solution.py:441
  64.4 1.7 %collective-permute-done.23.refs_2_ = f32[136,128]{1,0:T(8,128)S(1)} collective-permute-done((f32[136,128]{1,0:T(8,128)S(1)}, f32[136,128]{1,0:T(8,128)S(1)}, u32[]{:S(2)}, u32[]{:S(2)}) %collective-permute-start.23) | collective-permute-done | bytes 69664 | tf_op jit(solution)/shard_map/ppermute | solution.py:441
  (51 shorter events, 11.5 us)
Async XLA Ops:
  0.6 16.6 %collective-permute-start.3 = (f32[256,128]{1,0:T(8,128)}, f32[256,128]{1,0:T(8,128)S(1)}, u32[]{:S(2)}, u32[]{:S(2)}) collective-permute-start(f32[256,128]{1,0:T(8,128)} %refs_3_.2), channel_id=1, source_target_pairs={{0,8},{4,12},{8,0},{12,4},{16,24},{20,28},{24,16},{28,20},{1,9},{5... | collective-permute-start | bytes 393224 | tf_op jit(solution)/shard_map/ppermute | solution.py:441
  3.7 13.5 %collective-permute-start.2 = (f32[256,128]{1,0:T(8,128)}, f32[256,128]{1,0:T(8,128)S(1)}, u32[]{:S(2)}, u32[]{:S(2)}) collective-permute-start(f32[256,128]{1,0:T(8,128)} %refs_3_.2), channel_id=1, source_target_pairs={{0,4},{4,0},{8,12},{12,8},{16,20},{20,16},{24,28},{28,24},{1,5},{5... | collective-permute-start | bytes 393224 | tf_op jit(solution)/shard_map/ppermute | solution.py:441
  5.3 12.0 %collective-permute-start = (f32[256,128]{1,0:T(8,128)}, f32[256,128]{1,0:T(8,128)S(1)}, u32[]{:S(2)}, u32[]{:S(2)}) collective-permute-start(f32[256,128]{1,0:T(8,128)} %refs_3_.2), channel_id=1, source_target_pairs={{0,16},{4,20},{8,24},{12,28},{16,0},{20,4},{24,8},{28,12},{1,17},{... | collective-permute-start | bytes 393224 | tf_op jit(solution)/shard_map/ppermute | solution.py:441
  7.8 9.4 %collective-permute-start.4 = (f32[256,128]{1,0:T(8,128)}, f32[256,128]{1,0:T(8,128)S(1)}, u32[]{:S(2)}, u32[]{:S(2)}) collective-permute-start(f32[256,128]{1,0:T(8,128)} %refs_3_.2), channel_id=1, source_target_pairs={{0,12},{4,8},{8,4},{12,0},{16,28},{20,24},{24,20},{28,16},{1,13},{... | collective-permute-start | bytes 393224 | tf_op jit(solution)/shard_map/ppermute | solution.py:441
  12.6 4.6 %collective-permute-start.1 = (f32[16,128]{1,0:T(8,128)S(1)}, f32[16,128]{1,0:T(8,128)S(1)}, u32[]{:S(2)}, u32[]{:S(2)}) collective-permute-start(f32[16,128]{1,0:T(8,128)S(1)} %get-tuple-element.28.own_ref), channel_id=1, source_target_pairs={{0,16},{4,20},{8,24},{12,28},{16,0},{20,4},{24,8},{28,12},{1,17},{... | collective-permute-start | bytes 24584 | tf_op jit(solution)/shard_map/ppermute | solution.py:441
  17.3 6.0 %collective-permute-start.7 = (f32[272,128]{1,0:T(8,128)S(1)}, f32[272,128]{1,0:T(8,128)S(1)}, u32[]{:S(2)}, u32[]{:S(2)}) collective-permute-start(f32[272,128]{1,0:T(8,128)S(1)} %message.1.refs_0_.refs_7_), channel_id=1, source_target_pairs={{0,12},{4,8},{8,4},{12,0},{16,28},{20,24},{24,20},{28,16},{1,13},{... | collective-permute-start | bytes 417800 | tf_op jit(solution)/shard_map/ppermute | solution.py:441
  19.9 5.1 %collective-permute-start.6 = (f32[272,128]{1,0:T(8,128)S(1)}, f32[272,128]{1,0:T(8,128)S(1)}, u32[]{:S(2)}, u32[]{:S(2)}) collective-permute-start(f32[272,128]{1,0:T(8,128)S(1)} %message.1.refs_0_.refs_7_), channel_id=1, source_target_pairs={{0,8},{4,12},{8,0},{12,4},{16,24},{20,28},{24,16},{28,20},{1,9},{5... | collective-permute-start | bytes 417800 | tf_op jit(solution)/shard_map/ppermute | solution.py:441
  20.4 5.1 %collective-permute-start.5 = (f32[272,128]{1,0:T(8,128)S(1)}, f32[272,128]{1,0:T(8,128)S(1)}, u32[]{:S(2)}, u32[]{:S(2)}) collective-permute-start(f32[272,128]{1,0:T(8,128)S(1)} %message.1.refs_0_.refs_7_), channel_id=1, source_target_pairs={{0,4},{4,0},{8,12},{12,8},{16,20},{20,16},{24,28},{28,24},{1,5},{5... | collective-permute-start | bytes 417800 | tf_op jit(solution)/shard_map/ppermute | solution.py:441
  26.8 1.6 %collective-permute-start.8 = (f32[2,264,128]{2,1,0:T(8,128)S(1)}, f32[2,264,128]{2,1,0:T(8,128)S(1)}, u32[]{:S(2)}, u32[]{:S(2)}) collective-permute-start(f32[2,264,128]{2,1,0:T(8,128)S(1)} %get-tuple-element.31), channel_id=1, source_target_pairs={{0,1},{1,0},{2,3},{3,2},{4,5},{5,4},{6,7},{7,6},{8,9},{9,8},{10,11... | collective-permute-start | bytes 811016 | tf_op jit(solution)/shard_map/ppermute | solution.py:441
  28.4 5.7 %collective-permute-start.9 = (f32[264,128]{1,0:T(8,128)S(1)}, f32[264,128]{1,0:T(8,128)S(1)}, u32[]{:S(2)}, u32[]{:S(2)}) collective-permute-start(f32[264,128]{1,0:T(8,128)S(1)} %pair_sums.1), channel_id=1, source_target_pairs={{0,2},{1,3},{2,0},{3,1},{4,6},{5,7},{6,4},{7,5},{8,10},{9,11},{10,... | collective-permute-start | bytes 405512 | tf_op jit(solution)/shard_map/ppermute | solution.py:441
  34.9 7.1 %collective-permute-start.11 = (f32[128,256]{1,0:T(8,128)S(1)}, f32[128,256]{1,0:T(8,128)S(1)}, u32[]{:S(2)}, u32[]{:S(2)}) collective-permute-start(f32[128,256]{1,0:T(8,128)S(1)} %get-tuple-element.33.refs_1_), channel_id=1, source_target_pairs={{0,2},{1,3},{2,0},{3,1},{4,6},{5,7},{6,4},{7,5},{8,10},{9,11},{10,... | collective-permute-start | bytes 393224 | tf_op jit(solution)/shard_map/ppermute | solution.py:441
  36.7 5.3 %collective-permute-start.12 = (f32[136,128]{1,0:T(8,128)S(1)}, f32[136,128]{1,0:T(8,128)S(1)}, u32[]{:S(2)}, u32[]{:S(2)}) collective-permute-start(f32[136,128]{1,0:T(8,128)S(1)} %weight_parts.1.own_ref), channel_id=1, source_target_pairs={{0,16},{4,20},{8,24},{12,28},{16,0},{20,4},{24,8},{28,12},{1,17},{... | collective-permute-start | bytes 208904 | tf_op jit(solution)/shard_map/ppermute | solution.py:441
  42.0 1.7 %collective-permute-start.13 = (f32[200,256]{1,0:T(8,128)S(1)}, f32[200,256]{1,0:T(8,128)S(1)}, u32[]{:S(2)}, u32[]{:S(2)}) collective-permute-start(f32[200,256]{1,0:T(8,128)S(1)} %carried.1.refs_3_), channel_id=1, source_target_pairs={{0,1},{1,0},{2,3},{3,2},{4,5},{5,4},{6,7},{7,6},{8,9},{9,8},{10,11... | collective-permute-start | bytes 614408 | tf_op jit(solution)/shard_map/ppermute | solution.py:441
  42.1 1.6 %collective-permute-start.10 = (f32[128,256]{1,0:T(8,128)S(1)}, f32[128,256]{1,0:T(8,128)S(1)}, u32[]{:S(2)}, u32[]{:S(2)}) collective-permute-start(f32[128,256]{1,0:T(8,128)S(1)} %get-tuple-element.33.refs_1_), channel_id=1, source_target_pairs={{0,1},{1,0},{2,3},{3,2},{4,5},{5,4},{6,7},{7,6},{8,9},{9,8},{10,11... | collective-permute-start | bytes 393224 | tf_op jit(solution)/shard_map/ppermute | solution.py:441
  44.6 12.3 %collective-permute-start.19 = (f32[128,256]{1,0:T(8,128)S(1)}, f32[128,256]{1,0:T(8,128)S(1)}, u32[]{:S(2)}, u32[]{:S(2)}) collective-permute-start(f32[128,256]{1,0:T(8,128)S(1)} %get-tuple-element.43), channel_id=1, source_target_pairs={{0,4},{4,0},{8,12},{12,8},{16,20},{20,16},{24,28},{28,24},{1,5},{5... | collective-permute-start | bytes 393224 | tf_op jit(solution)/shard_map/ppermute | solution.py:441
  45.6 11.7 %collective-permute-start.20 = (f32[128,256]{1,0:T(8,128)S(1)}, f32[128,256]{1,0:T(8,128)S(1)}, u32[]{:S(2)}, u32[]{:S(2)}) collective-permute-start(f32[128,256]{1,0:T(8,128)S(1)} %get-tuple-element.44), channel_id=1, source_target_pairs={{0,8},{4,12},{8,0},{12,4},{16,24},{20,28},{24,16},{28,20},{1,9},{5... | collective-permute-start | bytes 393224 | tf_op jit(solution)/shard_map/ppermute | solution.py:441
  47.1 7.8 %collective-permute-start.14 = (f32[136,128]{1,0:T(8,128)S(1)}, f32[136,128]{1,0:T(8,128)S(1)}, u32[]{:S(2)}, u32[]{:S(2)}) collective-permute-start(f32[136,128]{1,0:T(8,128)S(1)} %get-tuple-element.36.refs_0_), channel_id=1, source_target_pairs={{0,4},{4,0},{8,12},{12,8},{16,20},{20,16},{24,28},{28,24},{1,5},{5... | collective-permute-start | bytes 208904 | tf_op jit(solution)/shard_map/ppermute | solution.py:441
  48.2 9.6 %collective-permute-start.21 = (f32[128,256]{1,0:T(8,128)S(1)}, f32[128,256]{1,0:T(8,128)S(1)}, u32[]{:S(2)}, u32[]{:S(2)}) collective-permute-start(f32[128,256]{1,0:T(8,128)S(1)} %get-tuple-element.45), channel_id=1, source_target_pairs={{0,12},{4,8},{8,4},{12,0},{16,28},{20,24},{24,20},{28,16},{1,13},{... | collective-permute-start | bytes 393224 | tf_op jit(solution)/shard_map/ppermute | solution.py:441
  49.8 13.8 %collective-permute-start.16 = (f32[128,256]{1,0:T(8,128)S(1)}, f32[128,256]{1,0:T(8,128)S(1)}, u32[]{:S(2)}, u32[]{:S(2)}) collective-permute-start(f32[128,256]{1,0:T(8,128)S(1)} %get-tuple-element.39), channel_id=1, source_target_pairs={{0,4},{4,0},{8,12},{12,8},{16,20},{20,16},{24,28},{28,24},{1,5},{5... | collective-permute-start | bytes 393224 | tf_op jit(solution)/shard_map/ppermute | solution.py:441
  54.9 8.7 %collective-permute-start.17 = (f32[128,256]{1,0:T(8,128)S(1)}, f32[128,256]{1,0:T(8,128)S(1)}, u32[]{:S(2)}, u32[]{:S(2)}) collective-permute-start(f32[128,256]{1,0:T(8,128)S(1)} %get-tuple-element.40), channel_id=1, source_target_pairs={{0,8},{4,12},{8,0},{12,4},{16,24},{20,28},{24,16},{28,20},{1,9},{5... | collective-permute-start | bytes 393224 | tf_op jit(solution)/shard_map/ppermute | solution.py:441
  56.9 6.8 %collective-permute-start.18 = (f32[128,256]{1,0:T(8,128)S(1)}, f32[128,256]{1,0:T(8,128)S(1)}, u32[]{:S(2)}, u32[]{:S(2)}) collective-permute-start(f32[128,256]{1,0:T(8,128)S(1)} %get-tuple-element.41), channel_id=1, source_target_pairs={{0,12},{4,8},{8,4},{12,0},{16,28},{20,24},{24,20},{28,16},{1,13},{... | collective-permute-start | bytes 393224 | tf_op jit(solution)/shard_map/ppermute | solution.py:441
  57.3 4.4 %collective-permute-start.15 = (f32[136,128]{1,0:T(8,128)S(1)}, f32[136,128]{1,0:T(8,128)S(1)}, u32[]{:S(2)}, u32[]{:S(2)}) collective-permute-start(f32[136,128]{1,0:T(8,128)S(1)} %row1_grads.1.refs_0_), channel_id=1, source_target_pairs={{0,2},{1,3},{2,0},{3,1},{4,6},{5,7},{6,4},{7,5},{8,10},{9,11},{10,... | collective-permute-start | bytes 208904 | tf_op jit(solution)/shard_map/ppermute | solution.py:441
  57.9 6.5 %collective-permute-start.22 = (f32[128,256]{1,0:T(8,128)S(1)}, f32[128,256]{1,0:T(8,128)S(1)}, u32[]{:S(2)}, u32[]{:S(2)}) collective-permute-start(f32[128,256]{1,0:T(8,128)S(1)} %ahead_sums.1), channel_id=1, source_target_pairs={{0,16},{4,20},{8,24},{12,28},{16,0},{20,4},{24,8},{28,12},{1,17},{... | collective-permute-start | bytes 393224 | tf_op jit(solution)/shard_map/ppermute | solution.py:441
  61.6 4.4 %collective-permute-start.23 = (f32[136,128]{1,0:T(8,128)S(1)}, f32[136,128]{1,0:T(8,128)S(1)}, u32[]{:S(2)}, u32[]{:S(2)}) collective-permute-start(f32[136,128]{1,0:T(8,128)S(1)} %col2_grads.1.refs_0_.refs_4_.refs_1_), channel_id=1, source_target_pairs={{0,8},{4,12},{8,0},{12,4},{16,24},{20,28},{24,16},{28,20},{1,9},{5... | collective-permute-start | bytes 208904 | tf_op jit(solution)/shard_map/ppermute | solution.py:441
  (4 other events, 64.8 us)

commit v5 on v3

--- a/solution.py
+++ b/solution.py
@@ -122,7 +122,11 @@
             pltpu.SemaphoreType.DMA,
             pltpu.SemaphoreType.DMA,
         ),
-        before=(slots, counts, pltpu.with_memory_space_constraint(tiles, pltpu.HBM)),
+        before=(
+            pltpu.with_memory_space_constraint(slots, pltpu.HBM),
+            counts,
+            pltpu.with_memory_space_constraint(tiles, pltpu.HBM),
+        ),
         before_specs=[pl.BlockSpec(memory_space=pl.ANY)] * 3,
     )
 
@@ -317,14 +321,13 @@
 
 
 def backward_first_kernel(peers, col_count, *refs):
-    dense_ref = refs[0]
-    blocks = refs[1 : 1 + col_count]
-    outs, lhs = refs[1 + col_count : -1], refs[-1]
+    outs, lhs = refs[-1 - len(peers) : -1], refs[-1]
+    dense_ref, blocks = refs[0], refs[1 : 1 + col_count]
     col = lax.axis_index("col")
     width, node_rows = blocks[0].shape
-    for m in range(col_count):
+    for m, block in enumerate(blocks):
         start = pl.multiple_of((col ^ m) * node_rows, node_rows)
-        high, low = split(blocks[m][...])
+        high, low = split(block[...])
         lhs[:width, pl.ds(start, node_rows)] = high
         lhs[width:, pl.ds(start, node_rows)] = low
     backward_chunks(peers, dense_ref, lhs, outs)
@@ -334,13 +337,13 @@
     backward_chunks(peers, dense_ref, lhs, outs)
 
 
-def backward_first(peers, dense, blocks):
+def backward_first(peers, dense, blocks, after):
     width, node_rows = blocks[0].shape
     rows = dense.shape[0]
     out = call(
         functools.partial(backward_first_kernel, peers, len(blocks)),
         "backward_first",
-        (dense, *blocks),
+        (dense, *blocks, *after),
         [vmem(width, node_rows)] * len(peers) + [vmem(2 * width, rows, dtype=BF16)],
         flops=4 * len(peers) * node_rows * rows * width,
     )
@@ -367,6 +370,14 @@
 def sum_all(parts, name, after=(), flops=0):
     kernel = functools.partial(sum_kernel, len(parts))
     return call(kernel, name, (*parts, *after), (vmem(*parts[0].shape),), flops=flops)[0]
+
+
+def hand_over_kernel(value_ref, *refs):
+    refs[-1][...] = value_ref[...]
+
+
+def hand_over(value, after):
+    return call(hand_over_kernel, "hand_over", (value, *after), (hbm(*value.shape),))[0]
 
 
 def finish_kernel(parts, *refs):
@@ -435,24 +446,26 @@
     for m in even:
         backs[m | 1] = swap(backs[m], "col", 1)
     grads = weight_parts(aggregated, pre_grad)
-
-    chunks, lhs = backward_first(far, dense, backs)
+    grads = sum_all([grads, swap(grads, "row", top)], "top_grads", (), HINT)
+    chunks, lhs = backward_first(far, dense, backs, (grads,))
     ahead = [chunks[top]] + [swap(chunks[top | m], "row", m) for m in near[1:]]
     chunks = backward_second(near, dense, lhs, node_rows)
     mine = [chunks[0]] + [swap(chunks[m], "row", m) for m in near[1:]]
-    ahead = sum_all(ahead, "ahead_sums")
+    ahead = sum_all(ahead, "ahead_sums", (), HINT)
     passed = swap(ahead, "row", top)
 
-    rounds = [("row", top), ("row", 1)] if top > 1 else [("row", 1)]
-    rounds += [("col", 1 << b) for b in range(col_count.bit_length() - 1)]
-    rounds += [("row", 1 << b) for b in range(1, top.bit_length() - 1)]
-    behind = [(chunks[0],), ()] + [(ahead,)] * (len(rounds) - 2)
-    for (axis, mask), after in zip(rounds[:-1], behind):
+    rounds = [("col", 1 << b) for b in range(col_count.bit_length() - 1)]
+    rounds += [("row", 1 << b) for b in range(top.bit_length() - 1)]
+    grads = sum_all([grads], "held_grads", (chunks[0],))
+    for step, (axis, mask) in enumerate(rounds[:-1]):
+        after = (ahead,) if axis == "col" and mask * 2 == col_count else ()
         grads = sum_all([grads, swap(grads, axis, mask)], f"{axis}{mask}_grads", after)
-    mine = sum_all(mine, "mine_sums", (grads,), HINT)
+    activated = hand_over(activated, (grads,))
+    mine = sum_all(mine, "mine_sums", (grads,), 3 * HINT)
+    mine = sum_all([mine, passed], "last_sums", (), HINT // 2)
     axis, mask = rounds[-1]
     feature_grad, weight_grad, bias_grad = finish(
-        [mine, passed], [grads, swap(grads, axis, mask)], scale
+        [mine], [grads, swap(grads, axis, mask)], scale
     )
     return activated, feature_grad, weight_grad, bias_grad[0]
 

time: 69 us -> 65.7 us (0.952)
  starting transfers between devices: 28.9 us -> 26.6 us
  local copies, waits for them, and re-layouts: 1.32 us -> 0.02 us
  Pallas kernels: 10 us -> 10.7 us
    ppermute x25, starting transfers between devices: 28.9 us -> 26.6 us  [swap(): return lax.ppermute(value, axis, [(i, i ^ mask) for i in range(count)])]
    unnamed x11 -> x8, local copies, waits for them, and re-layouts: 1.32 us -> 0.02 us
    pallas_call x18 -> x21, Pallas kernels: 10 us -> 10.7 us  [call(): pl.pallas_call(kernel, out_shape=tuple(outs), in_specs=list(before_specs)...]
  transfers between devices with their start and end apart: 25 -> 25, of which waited for: 13 -> 14; matrix products, arithmetic and copies ran while one was open for 1% -> 0% of each run, Pallas kernels for 10% -> 11%
where the time goes in v5:
time: 65.7 us; the launch traced here: 65.5 us
  waiting for transfers between devices  26.7 us (41%)
  starting transfers between devices  26.6 us (40%)
  Pallas kernels  10.7 us (16%)
  between operations  1.48 us (2%)
    ppermute x25, waiting for transfers between devices, swap(): return lax.ppermute(value, axis, [(i, i ^ mask) for i in range(count)])  26.7 us
    ppermute x25, starting transfers between devices, swap(): return lax.ppermute(value, axis, [(i, i ^ mask) for i in range(count)])  26.6 us
    pallas_call x21, Pallas kernels, call(): pl.pallas_call(kernel, out_shape=tuple(outs), in_specs=list(before_specs)...  10.7 us
  transfers between devices with their start and end apart: 25, of which 14 were waited for; matrix products, arithmetic and copies ran while one was open for 0% of the time, Pallas kernels for 11%

profile of v5, /device:TPU:0, one launch (start us, length us, event | category | flops | bytes accessed | tf_op | source)
XLA Modules:
  0.0 65.5 jit_solution(2166790940844454826)
XLA Ops:
  0.6 3.1 %collective-permute-start.3 = (f32[256,128]{1,0:T(8,128)}, f32[256,128]{1,0:T(8,128)S(1)}, u32[]{:S(2)}, u32[]{:S(2)}) collective-permute-start(f32[256,128]{1,0:T(8,128)} %refs_3_.2), channel_id=1, source_target_pairs={{0,8},{4,12},{8,0},{12,4},{16,24},{20,28},{24,16},{28,20},{1,9},{5... | collective-permute-start | bytes 393224 | tf_op jit(solution)/shard_map/ppermute | solution.py:409
  3.7 1.5 %collective-permute-start.2 = (f32[256,128]{1,0:T(8,128)}, f32[256,128]{1,0:T(8,128)S(1)}, u32[]{:S(2)}, u32[]{:S(2)}) collective-permute-start(f32[256,128]{1,0:T(8,128)} %refs_3_.2), channel_id=1, source_target_pairs={{0,4},{4,0},{8,12},{12,8},{16,20},{20,16},{24,28},{28,24},{1,5},{5... | collective-permute-start | bytes 393224 | tf_op jit(solution)/shard_map/ppermute | solution.py:409
  5.3 2.6 %collective-permute-start = (f32[256,128]{1,0:T(8,128)}, f32[256,128]{1,0:T(8,128)S(1)}, u32[]{:S(2)}, u32[]{:S(2)}) collective-permute-start(f32[256,128]{1,0:T(8,128)} %refs_3_.2), channel_id=1, source_target_pairs={{0,16},{4,20},{8,24},{12,28},{16,0},{20,4},{24,8},{28,12},{1,17},{... | collective-permute-start | bytes 393224 | tf_op jit(solution)/shard_map/ppermute | solution.py:409
  8.9 3.7 %densify.1 = (bf16[1024,2048]{1,0:T(8,128)(2,1)S(1)}, f32[16,128]{1,0:T(8,128)S(1)}) custom-call(s32[1,128]{1,0:T(1,128)} %bitcast.6, s32[1,1]{1,0:T(1,128)S(6)} %copy.11.counts_hbm, s32[128,128,128]{2,1,0:T(8,128)} %bitcast.5), custom_call_target="tpu_custom_call" | custom-call | flops 838860800 | tf_op jit(solution)/shard_map/densify/pallas_call | solution.py:50
  12.7 4.5 %collective-permute-done.1.got_ref = f32[16,128]{1,0:T(8,128)S(1)} collective-permute-done((f32[16,128]{1,0:T(8,128)S(1)}, f32[16,128]{1,0:T(8,128)S(1)}, u32[]{:S(2)}, u32[]{:S(2)}) %collective-permute-start.1) | collective-permute-done | bytes 8224 | tf_op jit(solution)/shard_map/ppermute | solution.py:409
  17.3 2.6 %collective-permute-start.7 = (f32[272,128]{1,0:T(8,128)S(1)}, f32[272,128]{1,0:T(8,128)S(1)}, u32[]{:S(2)}, u32[]{:S(2)}) collective-permute-start(f32[272,128]{1,0:T(8,128)S(1)} %message.1.refs_0_.refs_7_), channel_id=1, source_target_pairs={{0,12},{4,8},{8,4},{12,0},{16,28},{20,24},{24,20},{28,16},{1,13},{... | collective-permute-start | bytes 417800 | tf_op jit(solution)/shard_map/ppermute | solution.py:409
  21.5 1.8 %collective-permute-done.7.refs_3_.refs_10_ = f32[272,128]{1,0:T(8,128)S(1)} collective-permute-done((f32[272,128]{1,0:T(8,128)S(1)}, f32[272,128]{1,0:T(8,128)S(1)}, u32[]{:S(2)}, u32[]{:S(2)}) %collective-permute-start.7) | collective-permute-done | bytes 139296 | tf_op jit(solution)/shard_map/ppermute | solution.py:409
  23.3 1.6 %collective-permute-done.6.refs_2_.refs_9_ = f32[272,128]{1,0:T(8,128)S(1)} collective-permute-done((f32[272,128]{1,0:T(8,128)S(1)}, f32[272,128]{1,0:T(8,128)S(1)}, u32[]{:S(2)}, u32[]{:S(2)}) %collective-permute-start.6) | collective-permute-done | bytes 139296 | tf_op jit(solution)/shard_map/ppermute | solution.py:409
  28.4 1.6 %collective-permute-start.9 = (f32[264,128]{1,0:T(8,128)S(1)}, f32[264,128]{1,0:T(8,128)S(1)}, u32[]{:S(2)}, u32[]{:S(2)}) collective-permute-start(f32[264,128]{1,0:T(8,128)S(1)} %pair_sums.1), channel_id=1, source_target_pairs={{0,2},{1,3},{2,0},{3,1},{4,6},{5,7},{6,4},{7,5},{8,10},{9,11},{10,... | collective-permute-start | bytes 405512 | tf_op jit(solution)/shard_map/ppermute | solution.py:409
  29.9 4.1 %collective-permute-done.9.refs_2_ = f32[264,128]{1,0:T(8,128)S(1)} collective-permute-done((f32[264,128]{1,0:T(8,128)S(1)}, f32[264,128]{1,0:T(8,128)S(1)}, u32[]{:S(2)}, u32[]{:S(2)}) %collective-permute-start.9) | collective-permute-done | bytes 135200 | tf_op jit(solution)/shard_map/ppermute | solution.py:409
  34.9 1.6 %collective-permute-start.12 = (f32[128,256]{1,0:T(8,128)S(1)}, f32[128,256]{1,0:T(8,128)S(1)}, u32[]{:S(2)}, u32[]{:S(2)}) collective-permute-start(f32[128,256]{1,0:T(8,128)S(1)} %get-tuple-element.34.refs_1_), channel_id=1, source_target_pairs={{0,2},{1,3},{2,0},{3,1},{4,6},{5,7},{6,4},{7,5},{8,10},{9,11},{10,... | collective-permute-start | bytes 393224 | tf_op jit(solution)/shard_map/ppermute | solution.py:409
  37.1 2.8 %collective-permute-done.12.refs_3_ = f32[128,256]{1,0:T(8,128)S(1)} collective-permute-done((f32[128,256]{1,0:T(8,128)S(1)}, f32[128,256]{1,0:T(8,128)S(1)}, u32[]{:S(2)}, u32[]{:S(2)}) %collective-permute-start.12) | collective-permute-done | bytes 131104 | tf_op jit(solution)/shard_map/ppermute | solution.py:409
  39.9 2.1 %collective-permute-done.10.refs_1_ = f32[136,128]{1,0:T(8,128)S(1)} collective-permute-done((f32[136,128]{1,0:T(8,128)S(1)}, f32[136,128]{1,0:T(8,128)S(1)}, u32[]{:S(2)}, u32[]{:S(2)}) %collective-permute-start.10) | collective-permute-done | bytes 69664 | tf_op jit(solution)/shard_map/ppermute | solution.py:409
  42.9 1.0 %collective-permute-start.16 = (f32[128,256]{1,0:T(8,128)S(1)}, f32[128,256]{1,0:T(8,128)S(1)}, u32[]{:S(2)}, u32[]{:S(2)}) collective-permute-start(f32[128,256]{1,0:T(8,128)S(1)} %get-tuple-element.38), channel_id=1, source_target_pairs={{0,4},{4,0},{8,12},{12,8},{16,20},{20,16},{24,28},{28,24},{1,5},{5... | collective-permute-start | bytes 393224 | tf_op jit(solution)/shard_map/ppermute | solution.py:409
  43.9 1.6 %collective-permute-start.17 = (f32[128,256]{1,0:T(8,128)S(1)}, f32[128,256]{1,0:T(8,128)S(1)}, u32[]{:S(2)}, u32[]{:S(2)}) collective-permute-start(f32[128,256]{1,0:T(8,128)S(1)} %get-tuple-element.39), channel_id=1, source_target_pairs={{0,8},{4,12},{8,0},{12,4},{16,24},{20,28},{24,16},{28,20},{1,9},{5... | collective-permute-start | bytes 393224 | tf_op jit(solution)/shard_map/ppermute | solution.py:409
  45.5 1.0 %collective-permute-start.18 = (f32[128,256]{1,0:T(8,128)S(1)}, f32[128,256]{1,0:T(8,128)S(1)}, u32[]{:S(2)}, u32[]{:S(2)}) collective-permute-start(f32[128,256]{1,0:T(8,128)S(1)} %get-tuple-element.40), channel_id=1, source_target_pairs={{0,12},{4,8},{8,4},{12,0},{16,28},{20,24},{24,20},{28,16},{1,13},{... | collective-permute-start | bytes 393224 | tf_op jit(solution)/shard_map/ppermute | solution.py:409
  47.3 1.0 %collective-permute-start.20 = (f32[128,256]{1,0:T(8,128)S(1)}, f32[128,256]{1,0:T(8,128)S(1)}, u32[]{:S(2)}, u32[]{:S(2)}) collective-permute-start(f32[128,256]{1,0:T(8,128)S(1)} %get-tuple-element.41), channel_id=1, source_target_pairs={{0,4},{4,0},{8,12},{12,8},{16,20},{20,16},{24,28},{28,24},{1,5},{5... | collective-permute-start | bytes 393224 | tf_op jit(solution)/shard_map/ppermute | solution.py:409
  48.5 1.6 %collective-permute-start.21 = (f32[128,256]{1,0:T(8,128)S(1)}, f32[128,256]{1,0:T(8,128)S(1)}, u32[]{:S(2)}, u32[]{:S(2)}) collective-permute-start(f32[128,256]{1,0:T(8,128)S(1)} %get-tuple-element.42), channel_id=1, source_target_pairs={{0,8},{4,12},{8,0},{12,4},{16,24},{20,28},{24,16},{28,20},{1,9},{5... | collective-permute-start | bytes 393224 | tf_op jit(solution)/shard_map/ppermute | solution.py:409
  52.2 3.1 %collective-permute-done.15.refs_1_ = f32[136,128]{1,0:T(8,128)S(1)} collective-permute-done((f32[136,128]{1,0:T(8,128)S(1)}, f32[136,128]{1,0:T(8,128)S(1)}, u32[]{:S(2)}, u32[]{:S(2)}) %collective-permute-start.15) | collective-permute-done | bytes 69664 | tf_op jit(solution)/shard_map/ppermute | solution.py:409
  55.3 1.2 %collective-permute-start.19 = (f32[136,128]{1,0:T(8,128)S(1)}, f32[136,128]{1,0:T(8,128)S(1)}, u32[]{:S(2)}, u32[]{:S(2)}) collective-permute-start(f32[136,128]{1,0:T(8,128)S(1)} %col2_grads.1.refs_0_), channel_id=1, source_target_pairs={{0,4},{4,0},{8,12},{12,8},{16,20},{20,16},{24,28},{28,24},{1,5},{5... | collective-permute-start | bytes 208904 | tf_op jit(solution)/shard_map/ppermute | solution.py:409
  56.5 1.2 %collective-permute-start.23 = (f32[128,256]{1,0:T(8,128)S(1)}, f32[128,256]{1,0:T(8,128)S(1)}, u32[]{:S(2)}, u32[]{:S(2)}) collective-permute-start(f32[128,256]{1,0:T(8,128)S(1)} %ahead_sums.1.refs_2_), channel_id=1, source_target_pairs={{0,16},{4,20},{8,24},{12,28},{16,0},{20,4},{24,8},{28,12},{1,17},{... | collective-permute-start | bytes 393224 | tf_op jit(solution)/shard_map/ppermute | solution.py:409
  57.7 2.0 %collective-permute-done.19.refs_1_ = f32[136,128]{1,0:T(8,128)S(1)} collective-permute-done((f32[136,128]{1,0:T(8,128)S(1)}, f32[136,128]{1,0:T(8,128)S(1)}, u32[]{:S(2)}, u32[]{:S(2)}) %collective-permute-start.19) | collective-permute-done | bytes 69664 | tf_op jit(solution)/shard_map/ppermute | solution.py:409
  59.7 1.6 %collective-permute-start.24 = (f32[136,128]{1,0:T(8,128)S(1)}, f32[136,128]{1,0:T(8,128)S(1)}, u32[]{:S(2)}, u32[]{:S(2)}) collective-permute-start(f32[136,128]{1,0:T(8,128)S(1)} %row1_grads.1.refs_0_.refs_4_.refs_1_), channel_id=1, source_target_pairs={{0,8},{4,12},{8,0},{12,4},{16,24},{20,28},{24,16},{28,20},{1,9},{5... | collective-permute-start | bytes 208904 | tf_op jit(solution)/shard_map/ppermute | solution.py:409
  62.1 2.1 %collective-permute-done.23.refs_1_ = f32[128,256]{1,0:T(8,128)S(1)} collective-permute-done((f32[128,256]{1,0:T(8,128)S(1)}, f32[128,256]{1,0:T(8,128)S(1)}, u32[]{:S(2)}, u32[]{:S(2)}) %collective-permute-start.23) | collective-permute-done | bytes 131104 | tf_op jit(solution)/shard_map/ppermute | solution.py:409
  (55 shorter events, 13.0 us)
Async XLA Ops:
  0.6 16.6 %collective-permute-start.3 = (f32[256,128]{1,0:T(8,128)}, f32[256,128]{1,0:T(8,128)S(1)}, u32[]{:S(2)}, u32[]{:S(2)}) collective-permute-start(f32[256,128]{1,0:T(8,128)} %refs_3_.2), channel_id=1, source_target_pairs={{0,8},{4,12},{8,0},{12,4},{16,24},{20,28},{24,16},{28,20},{1,9},{5... | collective-permute-start | bytes 393224 | tf_op jit(solution)/shard_map/ppermute | solution.py:409
  3.7 13.5 %collective-permute-start.2 = (f32[256,128]{1,0:T(8,128)}, f32[256,128]{1,0:T(8,128)S(1)}, u32[]{:S(2)}, u32[]{:S(2)}) collective-permute-start(f32[256,128]{1,0:T(8,128)} %refs_3_.2), channel_id=1, source_target_pairs={{0,4},{4,0},{8,12},{12,8},{16,20},{20,16},{24,28},{28,24},{1,5},{5... | collective-permute-start | bytes 393224 | tf_op jit(solution)/shard_map/ppermute | solution.py:409
  5.3 12.0 %collective-permute-start = (f32[256,128]{1,0:T(8,128)}, f32[256,128]{1,0:T(8,128)S(1)}, u32[]{:S(2)}, u32[]{:S(2)}) collective-permute-start(f32[256,128]{1,0:T(8,128)} %refs_3_.2), channel_id=1, source_target_pairs={{0,16},{4,20},{8,24},{12,28},{16,0},{20,4},{24,8},{28,12},{1,17},{... | collective-permute-start | bytes 393224 | tf_op jit(solution)/shard_map/ppermute | solution.py:409
  7.8 9.4 %collective-permute-start.4 = (f32[256,128]{1,0:T(8,128)}, f32[256,128]{1,0:T(8,128)S(1)}, u32[]{:S(2)}, u32[]{:S(2)}) collective-permute-start(f32[256,128]{1,0:T(8,128)} %refs_3_.2), channel_id=1, source_target_pairs={{0,12},{4,8},{8,4},{12,0},{16,28},{20,24},{24,20},{28,16},{1,13},{... | collective-permute-start | bytes 393224 | tf_op jit(solution)/shard_map/ppermute | solution.py:409
  12.6 4.6 %collective-permute-start.1 = (f32[16,128]{1,0:T(8,128)S(1)}, f32[16,128]{1,0:T(8,128)S(1)}, u32[]{:S(2)}, u32[]{:S(2)}) collective-permute-start(f32[16,128]{1,0:T(8,128)S(1)} %get-tuple-element.27.own_ref), channel_id=1, source_target_pairs={{0,16},{4,20},{8,24},{12,28},{16,0},{20,4},{24,8},{28,12},{1,17},{... | collective-permute-start | bytes 24584 | tf_op jit(solution)/shard_map/ppermute | solution.py:409
  17.3 6.0 %collective-permute-start.7 = (f32[272,128]{1,0:T(8,128)S(1)}, f32[272,128]{1,0:T(8,128)S(1)}, u32[]{:S(2)}, u32[]{:S(2)}) collective-permute-start(f32[272,128]{1,0:T(8,128)S(1)} %message.1.refs_0_.refs_7_), channel_id=1, source_target_pairs={{0,12},{4,8},{8,4},{12,0},{16,28},{20,24},{24,20},{28,16},{1,13},{... | collective-permute-start | bytes 417800 | tf_op jit(solution)/shard_map/ppermute | solution.py:409
  19.9 5.1 %collective-permute-start.6 = (f32[272,128]{1,0:T(8,128)S(1)}, f32[272,128]{1,0:T(8,128)S(1)}, u32[]{:S(2)}, u32[]{:S(2)}) collective-permute-start(f32[272,128]{1,0:T(8,128)S(1)} %message.1.refs_0_.refs_7_), channel_id=1, source_target_pairs={{0,8},{4,12},{8,0},{12,4},{16,24},{20,28},{24,16},{28,20},{1,9},{5... | collective-permute-start | bytes 417800 | tf_op jit(solution)/shard_map/ppermute | solution.py:409
  20.3 5.1 %collective-permute-start.5 = (f32[272,128]{1,0:T(8,128)S(1)}, f32[272,128]{1,0:T(8,128)S(1)}, u32[]{:S(2)}, u32[]{:S(2)}) collective-permute-start(f32[272,128]{1,0:T(8,128)S(1)} %message.1.refs_0_.refs_7_), channel_id=1, source_target_pairs={{0,4},{4,0},{8,12},{12,8},{16,20},{20,16},{24,28},{28,24},{1,5},{5... | collective-permute-start | bytes 417800 | tf_op jit(solution)/shard_map/ppermute | solution.py:409
  26.8 1.6 %collective-permute-start.8 = (f32[2,264,128]{2,1,0:T(8,128)S(1)}, f32[2,264,128]{2,1,0:T(8,128)S(1)}, u32[]{:S(2)}, u32[]{:S(2)}) collective-permute-start(f32[2,264,128]{2,1,0:T(8,128)S(1)} %get-tuple-element.30), channel_id=1, source_target_pairs={{0,1},{1,0},{2,3},{3,2},{4,5},{5,4},{6,7},{7,6},{8,9},{9,8},{10,11... | collective-permute-start | bytes 811016 | tf_op jit(solution)/shard_map/ppermute | solution.py:409
  28.4 5.7 %collective-permute-start.9 = (f32[264,128]{1,0:T(8,128)S(1)}, f32[264,128]{1,0:T(8,128)S(1)}, u32[]{:S(2)}, u32[]{:S(2)}) collective-permute-start(f32[264,128]{1,0:T(8,128)S(1)} %pair_sums.1), channel_id=1, source_target_pairs={{0,2},{1,3},{2,0},{3,1},{4,6},{5,7},{6,4},{7,5},{8,10},{9,11},{10,... | collective-permute-start | bytes 405512 | tf_op jit(solution)/shard_map/ppermute | solution.py:409
  34.9 5.0 %collective-permute-start.12 = (f32[128,256]{1,0:T(8,128)S(1)}, f32[128,256]{1,0:T(8,128)S(1)}, u32[]{:S(2)}, u32[]{:S(2)}) collective-permute-start(f32[128,256]{1,0:T(8,128)S(1)} %get-tuple-element.34.refs_1_), channel_id=1, source_target_pairs={{0,2},{1,3},{2,0},{3,1},{4,6},{5,7},{6,4},{7,5},{8,10},{9,11},{10,... | collective-permute-start | bytes 393224 | tf_op jit(solution)/shard_map/ppermute | solution.py:409
  36.7 5.3 %collective-permute-start.10 = (f32[136,128]{1,0:T(8,128)S(1)}, f32[136,128]{1,0:T(8,128)S(1)}, u32[]{:S(2)}, u32[]{:S(2)}) collective-permute-start(f32[136,128]{1,0:T(8,128)S(1)} %weight_parts.1.refs_0_), channel_id=1, source_target_pairs={{0,16},{4,20},{8,24},{12,28},{16,0},{20,4},{24,8},{28,12},{1,17},{... | collective-permute-start | bytes 208904 | tf_op jit(solution)/shard_map/ppermute | solution.py:409
  37.1 4.9 %collective-permute-start.11 = (f32[128,256]{1,0:T(8,128)S(1)}, f32[128,256]{1,0:T(8,128)S(1)}, u32[]{:S(2)}, u32[]{:S(2)}) collective-permute-start(f32[128,256]{1,0:T(8,128)S(1)} %get-tuple-element.34.refs_1_), channel_id=1, source_target_pairs={{0,1},{1,0},{2,3},{3,2},{4,5},{5,4},{6,7},{7,6},{8,9},{9,8},{10,11... | collective-permute-start | bytes 393224 | tf_op jit(solution)/shard_map/ppermute | solution.py:409
  39.9 2.1 %collective-permute-start.13 = (f32[128,256]{1,0:T(8,128)S(1)}, f32[128,256]{1,0:T(8,128)S(1)}, u32[]{:S(2)}, u32[]{:S(2)}) collective-permute-start(f32[128,256]{1,0:T(8,128)S(1)} %collective-permute-done.12.refs_3_), channel_id=1, source_target_pairs={{0,1},{1,0},{2,3},{3,2},{4,5},{5,4},{6,7},{7,6},{8,9},{9,8},{10,11... | collective-permute-start | bytes 393224 | tf_op jit(solution)/shard_map/ppermute | solution.py:409
  42.9 7.2 %collective-permute-start.16 = (f32[128,256]{1,0:T(8,128)S(1)}, f32[128,256]{1,0:T(8,128)S(1)}, u32[]{:S(2)}, u32[]{:S(2)}) collective-permute-start(f32[128,256]{1,0:T(8,128)S(1)} %get-tuple-element.38), channel_id=1, source_target_pairs={{0,4},{4,0},{8,12},{12,8},{16,20},{20,16},{24,28},{28,24},{1,5},{5... | collective-permute-start | bytes 393224 | tf_op jit(solution)/shard_map/ppermute | solution.py:409
  43.9 7.1 %collective-permute-start.17 = (f32[128,256]{1,0:T(8,128)S(1)}, f32[128,256]{1,0:T(8,128)S(1)}, u32[]{:S(2)}, u32[]{:S(2)}) collective-permute-start(f32[128,256]{1,0:T(8,128)S(1)} %get-tuple-element.39), channel_id=1, source_target_pairs={{0,8},{4,12},{8,0},{12,4},{16,24},{20,28},{24,16},{28,20},{1,9},{5... | collective-permute-start | bytes 393224 | tf_op jit(solution)/shard_map/ppermute | solution.py:409
  45.5 6.7 %collective-permute-start.18 = (f32[128,256]{1,0:T(8,128)S(1)}, f32[128,256]{1,0:T(8,128)S(1)}, u32[]{:S(2)}, u32[]{:S(2)}) collective-permute-start(f32[128,256]{1,0:T(8,128)S(1)} %get-tuple-element.40), channel_id=1, source_target_pairs={{0,12},{4,8},{8,4},{12,0},{16,28},{20,24},{24,20},{28,16},{1,13},{... | collective-permute-start | bytes 393224 | tf_op jit(solution)/shard_map/ppermute | solution.py:409
  47.3 14.1 %collective-permute-start.20 = (f32[128,256]{1,0:T(8,128)S(1)}, f32[128,256]{1,0:T(8,128)S(1)}, u32[]{:S(2)}, u32[]{:S(2)}) collective-permute-start(f32[128,256]{1,0:T(8,128)S(1)} %get-tuple-element.41), channel_id=1, source_target_pairs={{0,4},{4,0},{8,12},{12,8},{16,20},{20,16},{24,28},{28,24},{1,5},{5... | collective-permute-start | bytes 393224 | tf_op jit(solution)/shard_map/ppermute | solution.py:409
  48.5 12.8 %collective-permute-start.21 = (f32[128,256]{1,0:T(8,128)S(1)}, f32[128,256]{1,0:T(8,128)S(1)}, u32[]{:S(2)}, u32[]{:S(2)}) collective-permute-start(f32[128,256]{1,0:T(8,128)S(1)} %get-tuple-element.42), channel_id=1, source_target_pairs={{0,8},{4,12},{8,0},{12,4},{16,24},{20,28},{24,16},{28,20},{1,9},{5... | collective-permute-start | bytes 393224 | tf_op jit(solution)/shard_map/ppermute | solution.py:409
  50.1 11.2 %collective-permute-start.22 = (f32[128,256]{1,0:T(8,128)S(1)}, f32[128,256]{1,0:T(8,128)S(1)}, u32[]{:S(2)}, u32[]{:S(2)}) collective-permute-start(f32[128,256]{1,0:T(8,128)S(1)} %get-tuple-element.43), channel_id=1, source_target_pairs={{0,12},{4,8},{8,4},{12,0},{16,28},{20,24},{24,20},{28,16},{1,13},{... | collective-permute-start | bytes 393224 | tf_op jit(solution)/shard_map/ppermute | solution.py:409
  51.0 4.3 %collective-permute-start.15 = (f32[136,128]{1,0:T(8,128)S(1)}, f32[136,128]{1,0:T(8,128)S(1)}, u32[]{:S(2)}, u32[]{:S(2)}) collective-permute-start(f32[136,128]{1,0:T(8,128)S(1)} %col1_grads.1.refs_0_), channel_id=1, source_target_pairs={{0,2},{1,3},{2,0},{3,1},{4,6},{5,7},{6,4},{7,5},{8,10},{9,11},{10,... | collective-permute-start | bytes 208904 | tf_op jit(solution)/shard_map/ppermute | solution.py:409
  55.3 4.4 %collective-permute-start.19 = (f32[136,128]{1,0:T(8,128)S(1)}, f32[136,128]{1,0:T(8,128)S(1)}, u32[]{:S(2)}, u32[]{:S(2)}) collective-permute-start(f32[136,128]{1,0:T(8,128)S(1)} %col2_grads.1.refs_0_), channel_id=1, source_target_pairs={{0,4},{4,0},{8,12},{12,8},{16,20},{20,16},{24,28},{28,24},{1,5},{5... | collective-permute-start | bytes 208904 | tf_op jit(solution)/shard_map/ppermute | solution.py:409
  56.5 7.7 %collective-permute-start.23 = (f32[128,256]{1,0:T(8,128)S(1)}, f32[128,256]{1,0:T(8,128)S(1)}, u32[]{:S(2)}, u32[]{:S(2)}) collective-permute-start(f32[128,256]{1,0:T(8,128)S(1)} %ahead_sums.1.refs_2_), channel_id=1, source_target_pairs={{0,16},{4,20},{8,24},{12,28},{16,0},{20,4},{24,8},{28,12},{1,17},{... | collective-permute-start | bytes 393224 | tf_op jit(solution)/shard_map/ppermute | solution.py:409
  59.7 5.0 %collective-permute-start.24 = (f32[136,128]{1,0:T(8,128)S(1)}, f32[136,128]{1,0:T(8,128)S(1)}, u32[]{:S(2)}, u32[]{:S(2)}) collective-permute-start(f32[136,128]{1,0:T(8,128)S(1)} %row1_grads.1.refs_0_.refs_4_.refs_1_), channel_id=1, source_target_pairs={{0,8},{4,12},{8,0},{12,4},{16,24},{20,28},{24,16},{28,20},{1,9},{5... | collective-permute-start | bytes 208904 | tf_op jit(solution)/shard_map/ppermute | solution.py:409
  (5 other events, 66.1 us)

commit v6 on v5

--- a/solution.py
+++ b/solution.py
@@ -461,8 +461,8 @@
         after = (ahead,) if axis == "col" and mask * 2 == col_count else ()
         grads = sum_all([grads, swap(grads, axis, mask)], f"{axis}{mask}_grads", after)
     activated = hand_over(activated, (grads,))
-    mine = sum_all(mine, "mine_sums", (grads,), 3 * HINT)
-    mine = sum_all([mine, passed], "last_sums", (), HINT // 2)
+    mine = sum_all(mine, "mine_sums", (grads,), HINT // 4)
+    mine = sum_all([mine, passed], "last_sums", (), HINT)
     axis, mask = rounds[-1]
     feature_grad, weight_grad, bias_grad = finish(
         [mine], [grads, swap(grads, axis, mask)], scale

time: 65.7 us -> 65.8 us (level)
  waiting for transfers between devices: 26.7 us -> 28.5 us
  starting transfers between devices: 26.6 us -> 24.9 us
    ppermute x25, waiting for transfers between devices: 26.7 us -> 28.5 us  [swap(): return lax.ppermute(value, axis, [(i, i ^ mask) for i in range(count)])]
    ppermute x25, starting transfers between devices: 26.6 us -> 24.9 us  [swap(): return lax.ppermute(value, axis, [(i, i ^ mask) for i in range(count)])]
  transfers between devices with their start and end apart: 25 -> 25, of which waited for: 14 -> 13; matrix products, arithmetic and copies ran while one was open for 0% -> 0% of each run, Pallas kernels for 11% -> 11%
where the time goes in v6:
time: 65.8 us; the launch traced here: 65.6 us
  waiting for transfers between devices  28.5 us (43%)
  starting transfers between devices  24.9 us (38%)
  Pallas kernels  10.7 us (16%)
  between operations  1.49 us (2%)
    ppermute x25, waiting for transfers between devices, swap(): return lax.ppermute(value, axis, [(i, i ^ mask) for i in range(count)])  28.5 us
    ppermute x25, starting transfers between devices, swap(): return lax.ppermute(value, axis, [(i, i ^ mask) for i in range(count)])  24.9 us
    pallas_call x21, Pallas kernels, call(): pl.pallas_call(kernel, out_shape=tuple(outs), in_specs=list(before_specs)...  10.7 us
  transfers between devices with their start and end apart: 25, of which 13 were waited for; matrix products, arithmetic and copies ran while one was open for 0% of the time, Pallas kernels for 11%

profile of v6, /device:TPU:0, one launch (start us, length us, event | category | flops | bytes accessed | tf_op | source)
XLA Modules:
  0.0 65.6 jit_solution(17228843000426547870)
XLA Ops:
  0.6 3.1 %collective-permute-start.3 = (f32[256,128]{1,0:T(8,128)}, f32[256,128]{1,0:T(8,128)S(1)}, u32[]{:S(2)}, u32[]{:S(2)}) collective-permute-start(f32[256,128]{1,0:T(8,128)} %refs_3_.2), channel_id=1, source_target_pairs={{0,8},{4,12},{8,0},{12,4},{16,24},{20,28},{24,16},{28,20},{1,9},{5... | collective-permute-start | bytes 393224 | tf_op jit(solution)/shard_map/ppermute | solution.py:409
  3.7 1.5 %collective-permute-start.2 = (f32[256,128]{1,0:T(8,128)}, f32[256,128]{1,0:T(8,128)S(1)}, u32[]{:S(2)}, u32[]{:S(2)}) collective-permute-start(f32[256,128]{1,0:T(8,128)} %refs_3_.2), channel_id=1, source_target_pairs={{0,4},{4,0},{8,12},{12,8},{16,20},{20,16},{24,28},{28,24},{1,5},{5... | collective-permute-start | bytes 393224 | tf_op jit(solution)/shard_map/ppermute | solution.py:409
  5.3 2.6 %collective-permute-start = (f32[256,128]{1,0:T(8,128)}, f32[256,128]{1,0:T(8,128)S(1)}, u32[]{:S(2)}, u32[]{:S(2)}) collective-permute-start(f32[256,128]{1,0:T(8,128)} %refs_3_.2), channel_id=1, source_target_pairs={{0,16},{4,20},{8,24},{12,28},{16,0},{20,4},{24,8},{28,12},{1,17},{... | collective-permute-start | bytes 393224 | tf_op jit(solution)/shard_map/ppermute | solution.py:409
  8.9 3.8 %densify.1 = (bf16[1024,2048]{1,0:T(8,128)(2,1)S(1)}, f32[16,128]{1,0:T(8,128)S(1)}) custom-call(s32[1,128]{1,0:T(1,128)} %bitcast.6, s32[1,1]{1,0:T(1,128)S(6)} %copy.11.counts_hbm, s32[128,128,128]{2,1,0:T(8,128)} %bitcast.5), custom_call_target="tpu_custom_call" | custom-call | flops 838860800 | tf_op jit(solution)/shard_map/densify/pallas_call | solution.py:50
  12.7 4.5 %collective-permute-done.1.got_ref = f32[16,128]{1,0:T(8,128)S(1)} collective-permute-done((f32[16,128]{1,0:T(8,128)S(1)}, f32[16,128]{1,0:T(8,128)S(1)}, u32[]{:S(2)}, u32[]{:S(2)}) %collective-permute-start.1) | collective-permute-done | bytes 8224 | tf_op jit(solution)/shard_map/ppermute | solution.py:409
  17.3 2.6 %collective-permute-start.7 = (f32[272,128]{1,0:T(8,128)S(1)}, f32[272,128]{1,0:T(8,128)S(1)}, u32[]{:S(2)}, u32[]{:S(2)}) collective-permute-start(f32[272,128]{1,0:T(8,128)S(1)} %message.1.refs_0_.refs_7_), channel_id=1, source_target_pairs={{0,12},{4,8},{8,4},{12,0},{16,28},{20,24},{24,20},{28,16},{1,13},{... | collective-permute-start | bytes 417800 | tf_op jit(solution)/shard_map/ppermute | solution.py:409
  21.5 1.8 %collective-permute-done.7.refs_3_.refs_10_ = f32[272,128]{1,0:T(8,128)S(1)} collective-permute-done((f32[272,128]{1,0:T(8,128)S(1)}, f32[272,128]{1,0:T(8,128)S(1)}, u32[]{:S(2)}, u32[]{:S(2)}) %collective-permute-start.7) | collective-permute-done | bytes 139296 | tf_op jit(solution)/shard_map/ppermute | solution.py:409
  23.3 1.6 %collective-permute-done.6.refs_2_.refs_9_ = f32[272,128]{1,0:T(8,128)S(1)} collective-permute-done((f32[272,128]{1,0:T(8,128)S(1)}, f32[272,128]{1,0:T(8,128)S(1)}, u32[]{:S(2)}, u32[]{:S(2)}) %collective-permute-start.6) | collective-permute-done | bytes 139296 | tf_op jit(solution)/shard_map/ppermute | solution.py:409
  25.8 1.0 %forward_first.1 = (f32[2,264,128]{2,1,0:T(8,128)S(1)}, bf16[2048,256]{1,0:T(8,128)(2,1)S(1)}) custom-call(bf16[1024,2048]{1,0:T(8,128)(2,1)S(1)} %get-tuple-element.26.dense_ref.refs_0_, f32[8,128]{1,0:T(8,128)S(1)} %row_totals.1.refs_1_.row_ref, f32[2048,128]{1,0:T(8,128)S(1)} %get-tuple-element.28.refs_2_, f32[256,128]{1,0:T(8,128)S(1)} %copy-done, ...), custom_call_target="tpu_custom_call" | custom-call | flops 536870912 | bytes 10522624 | tf_op jit(solution)/shard_map/forward_first/pallas_call | solution.py:50
  28.4 1.6 %collective-permute-start.9 = (f32[264,128]{1,0:T(8,128)S(1)}, f32[264,128]{1,0:T(8,128)S(1)}, u32[]{:S(2)}, u32[]{:S(2)}) collective-permute-start(f32[264,128]{1,0:T(8,128)S(1)} %pair_sums.1), channel_id=1, source_target_pairs={{0,2},{1,3},{2,0},{3,1},{4,6},{5,7},{6,4},{7,5},{8,10},{9,11},{10,... | collective-permute-start | bytes 405512 | tf_op jit(solution)/shard_map/ppermute | solution.py:409
  29.9 4.1 %collective-permute-done.9.refs_2_ = f32[264,128]{1,0:T(8,128)S(1)} collective-permute-done((f32[264,128]{1,0:T(8,128)S(1)}, f32[264,128]{1,0:T(8,128)S(1)}, u32[]{:S(2)}, u32[]{:S(2)}) %collective-permute-start.9) | collective-permute-done | bytes 135200 | tf_op jit(solution)/shard_map/ppermute | solution.py:409
  34.9 1.5 %collective-permute-start.12 = (f32[128,256]{1,0:T(8,128)S(1)}, f32[128,256]{1,0:T(8,128)S(1)}, u32[]{:S(2)}, u32[]{:S(2)}) collective-permute-start(f32[128,256]{1,0:T(8,128)S(1)} %get-tuple-element.34.refs_1_), channel_id=1, source_target_pairs={{0,2},{1,3},{2,0},{3,1},{4,6},{5,7},{6,4},{7,5},{8,10},{9,11},{10,... | collective-permute-start | bytes 393224 | tf_op jit(solution)/shard_map/ppermute | solution.py:409
  37.1 2.8 %collective-permute-done.12.refs_3_ = f32[128,256]{1,0:T(8,128)S(1)} collective-permute-done((f32[128,256]{1,0:T(8,128)S(1)}, f32[128,256]{1,0:T(8,128)S(1)}, u32[]{:S(2)}, u32[]{:S(2)}) %collective-permute-start.12) | collective-permute-done | bytes 131104 | tf_op jit(solution)/shard_map/ppermute | solution.py:409
  39.9 2.1 %collective-permute-done.10.refs_1_ = f32[136,128]{1,0:T(8,128)S(1)} collective-permute-done((f32[136,128]{1,0:T(8,128)S(1)}, f32[136,128]{1,0:T(8,128)S(1)}, u32[]{:S(2)}, u32[]{:S(2)}) %collective-permute-start.10) | collective-permute-done | bytes 69664 | tf_op jit(solution)/shard_map/ppermute | solution.py:409
  42.9 1.0 %collective-permute-start.16 = (f32[128,256]{1,0:T(8,128)S(1)}, f32[128,256]{1,0:T(8,128)S(1)}, u32[]{:S(2)}, u32[]{:S(2)}) collective-permute-start(f32[128,256]{1,0:T(8,128)S(1)} %get-tuple-element.38), channel_id=1, source_target_pairs={{0,4},{4,0},{8,12},{12,8},{16,20},{20,16},{24,28},{28,24},{1,5},{5... | collective-permute-start | bytes 393224 | tf_op jit(solution)/shard_map/ppermute | solution.py:409
  43.9 1.6 %collective-permute-start.17 = (f32[128,256]{1,0:T(8,128)S(1)}, f32[128,256]{1,0:T(8,128)S(1)}, u32[]{:S(2)}, u32[]{:S(2)}) collective-permute-start(f32[128,256]{1,0:T(8,128)S(1)} %get-tuple-element.39), channel_id=1, source_target_pairs={{0,8},{4,12},{8,0},{12,4},{16,24},{20,28},{24,16},{28,20},{1,9},{5... | collective-permute-start | bytes 393224 | tf_op jit(solution)/shard_map/ppermute | solution.py:409
  45.4 1.0 %collective-permute-start.18 = (f32[128,256]{1,0:T(8,128)S(1)}, f32[128,256]{1,0:T(8,128)S(1)}, u32[]{:S(2)}, u32[]{:S(2)}) collective-permute-start(f32[128,256]{1,0:T(8,128)S(1)} %get-tuple-element.40), channel_id=1, source_target_pairs={{0,12},{4,8},{8,4},{12,0},{16,28},{20,24},{24,20},{28,16},{1,13},{... | collective-permute-start | bytes 393224 | tf_op jit(solution)/shard_map/ppermute | solution.py:409
  47.3 1.0 %collective-permute-start.20 = (f32[128,256]{1,0:T(8,128)S(1)}, f32[128,256]{1,0:T(8,128)S(1)}, u32[]{:S(2)}, u32[]{:S(2)}) collective-permute-start(f32[128,256]{1,0:T(8,128)S(1)} %get-tuple-element.41), channel_id=1, source_target_pairs={{0,4},{4,0},{8,12},{12,8},{16,20},{20,16},{24,28},{28,24},{1,5},{5... | collective-permute-start | bytes 393224 | tf_op jit(solution)/shard_map/ppermute | solution.py:409
  48.5 1.6 %collective-permute-start.21 = (f32[128,256]{1,0:T(8,128)S(1)}, f32[128,256]{1,0:T(8,128)S(1)}, u32[]{:S(2)}, u32[]{:S(2)}) collective-permute-start(f32[128,256]{1,0:T(8,128)S(1)} %get-tuple-element.42), channel_id=1, source_target_pairs={{0,8},{4,12},{8,0},{12,4},{16,24},{20,28},{24,16},{28,20},{1,9},{5... | collective-permute-start | bytes 393224 | tf_op jit(solution)/shard_map/ppermute | solution.py:409
  50.1 0.9 %collective-permute-start.22 = (f32[128,256]{1,0:T(8,128)S(1)}, f32[128,256]{1,0:T(8,128)S(1)}, u32[]{:S(2)}, u32[]{:S(2)}) collective-permute-start(f32[128,256]{1,0:T(8,128)S(1)} %get-tuple-element.43), channel_id=1, source_target_pairs={{0,12},{4,8},{8,4},{12,0},{16,28},{20,24},{24,20},{28,16},{1,13},{... | collective-permute-start | bytes 393224 | tf_op jit(solution)/shard_map/ppermute | solution.py:409
  52.5 2.9 %collective-permute-done.15.refs_1_ = f32[136,128]{1,0:T(8,128)S(1)} collective-permute-done((f32[136,128]{1,0:T(8,128)S(1)}, f32[136,128]{1,0:T(8,128)S(1)}, u32[]{:S(2)}, u32[]{:S(2)}) %collective-permute-start.15) | collective-permute-done | bytes 69664 | tf_op jit(solution)/shard_map/ppermute | solution.py:409
  55.4 1.2 %collective-permute-start.19 = (f32[136,128]{1,0:T(8,128)S(1)}, f32[136,128]{1,0:T(8,128)S(1)}, u32[]{:S(2)}, u32[]{:S(2)}) collective-permute-start(f32[136,128]{1,0:T(8,128)S(1)} %col2_grads.1.refs_0_), channel_id=1, source_target_pairs={{0,4},{4,0},{8,12},{12,8},{16,20},{20,16},{24,28},{28,24},{1,5},{5... | collective-permute-start | bytes 208904 | tf_op jit(solution)/shard_map/ppermute | solution.py:409
  56.5 4.0 %collective-permute-done.19.refs_1_ = f32[136,128]{1,0:T(8,128)S(1)} collective-permute-done((f32[136,128]{1,0:T(8,128)S(1)}, f32[136,128]{1,0:T(8,128)S(1)}, u32[]{:S(2)}, u32[]{:S(2)}) %collective-permute-start.19) | collective-permute-done | bytes 69664 | tf_op jit(solution)/shard_map/ppermute | solution.py:409
  62.1 2.7 %collective-permute-done.24.refs_2_ = f32[136,128]{1,0:T(8,128)S(1)} collective-permute-done((f32[136,128]{1,0:T(8,128)S(1)}, f32[136,128]{1,0:T(8,128)S(1)}, u32[]{:S(2)}, u32[]{:S(2)}) %collective-permute-start.24) | collective-permute-done | bytes 69664 | tf_op jit(solution)/shard_map/ppermute | solution.py:409
  (55 shorter events, 11.8 us)
Async XLA Ops:
  0.6 16.6 %collective-permute-start.3 = (f32[256,128]{1,0:T(8,128)}, f32[256,128]{1,0:T(8,128)S(1)}, u32[]{:S(2)}, u32[]{:S(2)}) collective-permute-start(f32[256,128]{1,0:T(8,128)} %refs_3_.2), channel_id=1, source_target_pairs={{0,8},{4,12},{8,0},{12,4},{16,24},{20,28},{24,16},{28,20},{1,9},{5... | collective-permute-start | bytes 393224 | tf_op jit(solution)/shard_map/ppermute | solution.py:409
  3.7 13.5 %collective-permute-start.2 = (f32[256,128]{1,0:T(8,128)}, f32[256,128]{1,0:T(8,128)S(1)}, u32[]{:S(2)}, u32[]{:S(2)}) collective-permute-start(f32[256,128]{1,0:T(8,128)} %refs_3_.2), channel_id=1, source_target_pairs={{0,4},{4,0},{8,12},{12,8},{16,20},{20,16},{24,28},{28,24},{1,5},{5... | collective-permute-start | bytes 393224 | tf_op jit(solution)/shard_map/ppermute | solution.py:409
  5.3 12.0 %collective-permute-start = (f32[256,128]{1,0:T(8,128)}, f32[256,128]{1,0:T(8,128)S(1)}, u32[]{:S(2)}, u32[]{:S(2)}) collective-permute-start(f32[256,128]{1,0:T(8,128)} %refs_3_.2), channel_id=1, source_target_pairs={{0,16},{4,20},{8,24},{12,28},{16,0},{20,4},{24,8},{28,12},{1,17},{... | collective-permute-start | bytes 393224 | tf_op jit(solution)/shard_map/ppermute | solution.py:409
  7.8 9.4 %collective-permute-start.4 = (f32[256,128]{1,0:T(8,128)}, f32[256,128]{1,0:T(8,128)S(1)}, u32[]{:S(2)}, u32[]{:S(2)}) collective-permute-start(f32[256,128]{1,0:T(8,128)} %refs_3_.2), channel_id=1, source_target_pairs={{0,12},{4,8},{8,4},{12,0},{16,28},{20,24},{24,20},{28,16},{1,13},{... | collective-permute-start | bytes 393224 | tf_op jit(solution)/shard_map/ppermute | solution.py:409
  12.6 4.6 %collective-permute-start.1 = (f32[16,128]{1,0:T(8,128)S(1)}, f32[16,128]{1,0:T(8,128)S(1)}, u32[]{:S(2)}, u32[]{:S(2)}) collective-permute-start(f32[16,128]{1,0:T(8,128)S(1)} %get-tuple-element.27.own_ref), channel_id=1, source_target_pairs={{0,16},{4,20},{8,24},{12,28},{16,0},{20,4},{24,8},{28,12},{1,17},{... | collective-permute-start | bytes 24584 | tf_op jit(solution)/shard_map/ppermute | solution.py:409
  17.3 6.0 %collective-permute-start.7 = (f32[272,128]{1,0:T(8,128)S(1)}, f32[272,128]{1,0:T(8,128)S(1)}, u32[]{:S(2)}, u32[]{:S(2)}) collective-permute-start(f32[272,128]{1,0:T(8,128)S(1)} %message.1.refs_0_.refs_7_), channel_id=1, source_target_pairs={{0,12},{4,8},{8,4},{12,0},{16,28},{20,24},{24,20},{28,16},{1,13},{... | collective-permute-start | bytes 417800 | tf_op jit(solution)/shard_map/ppermute | solution.py:409
  19.9 5.1 %collective-permute-start.6 = (f32[272,128]{1,0:T(8,128)S(1)}, f32[272,128]{1,0:T(8,128)S(1)}, u32[]{:S(2)}, u32[]{:S(2)}) collective-permute-start(f32[272,128]{1,0:T(8,128)S(1)} %message.1.refs_0_.refs_7_), channel_id=1, source_target_pairs={{0,8},{4,12},{8,0},{12,4},{16,24},{20,28},{24,16},{28,20},{1,9},{5... | collective-permute-start | bytes 417800 | tf_op jit(solution)/shard_map/ppermute | solution.py:409
  20.4 5.1 %collective-permute-start.5 = (f32[272,128]{1,0:T(8,128)S(1)}, f32[272,128]{1,0:T(8,128)S(1)}, u32[]{:S(2)}, u32[]{:S(2)}) collective-permute-start(f32[272,128]{1,0:T(8,128)S(1)} %message.1.refs_0_.refs_7_), channel_id=1, source_target_pairs={{0,4},{4,0},{8,12},{12,8},{16,20},{20,16},{24,28},{28,24},{1,5},{5... | collective-permute-start | bytes 417800 | tf_op jit(solution)/shard_map/ppermute | solution.py:409
  26.8 1.6 %collective-permute-start.8 = (f32[2,264,128]{2,1,0:T(8,128)S(1)}, f32[2,264,128]{2,1,0:T(8,128)S(1)}, u32[]{:S(2)}, u32[]{:S(2)}) collective-permute-start(f32[2,264,128]{2,1,0:T(8,128)S(1)} %get-tuple-element.30), channel_id=1, source_target_pairs={{0,1},{1,0},{2,3},{3,2},{4,5},{5,4},{6,7},{7,6},{8,9},{9,8},{10,11... | collective-permute-start | bytes 811016 | tf_op jit(solution)/shard_map/ppermute | solution.py:409
  28.4 5.7 %collective-permute-start.9 = (f32[264,128]{1,0:T(8,128)S(1)}, f32[264,128]{1,0:T(8,128)S(1)}, u32[]{:S(2)}, u32[]{:S(2)}) collective-permute-start(f32[264,128]{1,0:T(8,128)S(1)} %pair_sums.1), channel_id=1, source_target_pairs={{0,2},{1,3},{2,0},{3,1},{4,6},{5,7},{6,4},{7,5},{8,10},{9,11},{10,... | collective-permute-start | bytes 405512 | tf_op jit(solution)/shard_map/ppermute | solution.py:409
  34.9 5.0 %collective-permute-start.12 = (f32[128,256]{1,0:T(8,128)S(1)}, f32[128,256]{1,0:T(8,128)S(1)}, u32[]{:S(2)}, u32[]{:S(2)}) collective-permute-start(f32[128,256]{1,0:T(8,128)S(1)} %get-tuple-element.34.refs_1_), channel_id=1, source_target_pairs={{0,2},{1,3},{2,0},{3,1},{4,6},{5,7},{6,4},{7,5},{8,10},{9,11},{10,... | collective-permute-start | bytes 393224 | tf_op jit(solution)/shard_map/ppermute | solution.py:409
  36.7 5.3 %collective-permute-start.10 = (f32[136,128]{1,0:T(8,128)S(1)}, f32[136,128]{1,0:T(8,128)S(1)}, u32[]{:S(2)}, u32[]{:S(2)}) collective-permute-start(f32[136,128]{1,0:T(8,128)S(1)} %weight_parts.1.refs_0_), channel_id=1, source_target_pairs={{0,16},{4,20},{8,24},{12,28},{16,0},{20,4},{24,8},{28,12},{1,17},{... | collective-permute-start | bytes 208904 | tf_op jit(solution)/shard_map/ppermute | solution.py:409
  37.1 4.9 %collective-permute-start.11 = (f32[128,256]{1,0:T(8,128)S(1)}, f32[128,256]{1,0:T(8,128)S(1)}, u32[]{:S(2)}, u32[]{:S(2)}) collective-permute-start(f32[128,256]{1,0:T(8,128)S(1)} %get-tuple-element.34.refs_1_), channel_id=1, source_target_pairs={{0,1},{1,0},{2,3},{3,2},{4,5},{5,4},{6,7},{7,6},{8,9},{9,8},{10,11... | collective-permute-start | bytes 393224 | tf_op jit(solution)/shard_map/ppermute | solution.py:409
  39.9 2.1 %collective-permute-start.13 = (f32[128,256]{1,0:T(8,128)S(1)}, f32[128,256]{1,0:T(8,128)S(1)}, u32[]{:S(2)}, u32[]{:S(2)}) collective-permute-start(f32[128,256]{1,0:T(8,128)S(1)} %collective-permute-done.12.refs_3_), channel_id=1, source_target_pairs={{0,1},{1,0},{2,3},{3,2},{4,5},{5,4},{6,7},{7,6},{8,9},{9,8},{10,11... | collective-permute-start | bytes 393224 | tf_op jit(solution)/shard_map/ppermute | solution.py:409
  42.9 7.2 %collective-permute-start.16 = (f32[128,256]{1,0:T(8,128)S(1)}, f32[128,256]{1,0:T(8,128)S(1)}, u32[]{:S(2)}, u32[]{:S(2)}) collective-permute-start(f32[128,256]{1,0:T(8,128)S(1)} %get-tuple-element.38), channel_id=1, source_target_pairs={{0,4},{4,0},{8,12},{12,8},{16,20},{20,16},{24,28},{28,24},{1,5},{5... | collective-permute-start | bytes 393224 | tf_op jit(solution)/shard_map/ppermute | solution.py:409
  43.9 7.1 %collective-permute-start.17 = (f32[128,256]{1,0:T(8,128)S(1)}, f32[128,256]{1,0:T(8,128)S(1)}, u32[]{:S(2)}, u32[]{:S(2)}) collective-permute-start(f32[128,256]{1,0:T(8,128)S(1)} %get-tuple-element.39), channel_id=1, source_target_pairs={{0,8},{4,12},{8,0},{12,4},{16,24},{20,28},{24,16},{28,20},{1,9},{5... | collective-permute-start | bytes 393224 | tf_op jit(solution)/shard_map/ppermute | solution.py:409
  45.4 6.7 %collective-permute-start.18 = (f32[128,256]{1,0:T(8,128)S(1)}, f32[128,256]{1,0:T(8,128)S(1)}, u32[]{:S(2)}, u32[]{:S(2)}) collective-permute-start(f32[128,256]{1,0:T(8,128)S(1)} %get-tuple-element.40), channel_id=1, source_target_pairs={{0,12},{4,8},{8,4},{12,0},{16,28},{20,24},{24,20},{28,16},{1,13},{... | collective-permute-start | bytes 393224 | tf_op jit(solution)/shard_map/ppermute | solution.py:409
  47.3 14.7 %collective-permute-start.20 = (f32[128,256]{1,0:T(8,128)S(1)}, f32[128,256]{1,0:T(8,128)S(1)}, u32[]{:S(2)}, u32[]{:S(2)}) collective-permute-start(f32[128,256]{1,0:T(8,128)S(1)} %get-tuple-element.41), channel_id=1, source_target_pairs={{0,4},{4,0},{8,12},{12,8},{16,20},{20,16},{24,28},{28,24},{1,5},{5... | collective-permute-start | bytes 393224 | tf_op jit(solution)/shard_map/ppermute | solution.py:409
  48.5 13.5 %collective-permute-start.21 = (f32[128,256]{1,0:T(8,128)S(1)}, f32[128,256]{1,0:T(8,128)S(1)}, u32[]{:S(2)}, u32[]{:S(2)}) collective-permute-start(f32[128,256]{1,0:T(8,128)S(1)} %get-tuple-element.42), channel_id=1, source_target_pairs={{0,8},{4,12},{8,0},{12,4},{16,24},{20,28},{24,16},{28,20},{1,9},{5... | collective-permute-start | bytes 393224 | tf_op jit(solution)/shard_map/ppermute | solution.py:409
  50.1 11.9 %collective-permute-start.22 = (f32[128,256]{1,0:T(8,128)S(1)}, f32[128,256]{1,0:T(8,128)S(1)}, u32[]{:S(2)}, u32[]{:S(2)}) collective-permute-start(f32[128,256]{1,0:T(8,128)S(1)} %get-tuple-element.43), channel_id=1, source_target_pairs={{0,12},{4,8},{8,4},{12,0},{16,28},{20,24},{24,20},{28,16},{1,13},{... | collective-permute-start | bytes 393224 | tf_op jit(solution)/shard_map/ppermute | solution.py:409
  51.0 4.3 %collective-permute-start.15 = (f32[136,128]{1,0:T(8,128)S(1)}, f32[136,128]{1,0:T(8,128)S(1)}, u32[]{:S(2)}, u32[]{:S(2)}) collective-permute-start(f32[136,128]{1,0:T(8,128)S(1)} %col1_grads.1.refs_0_), channel_id=1, source_target_pairs={{0,2},{1,3},{2,0},{3,1},{4,6},{5,7},{6,4},{7,5},{8,10},{9,11},{10,... | collective-permute-start | bytes 208904 | tf_op jit(solution)/shard_map/ppermute | solution.py:409
  52.2 9.9 %collective-permute-start.23 = (f32[128,256]{1,0:T(8,128)S(1)}, f32[128,256]{1,0:T(8,128)S(1)}, u32[]{:S(2)}, u32[]{:S(2)}) collective-permute-start(f32[128,256]{1,0:T(8,128)S(1)} %ahead_sums.1.refs_2_), channel_id=1, source_target_pairs={{0,16},{4,20},{8,24},{12,28},{16,0},{20,4},{24,8},{28,12},{1,17},{... | collective-permute-start | bytes 393224 | tf_op jit(solution)/shard_map/ppermute | solution.py:409
  55.4 5.1 %collective-permute-start.19 = (f32[136,128]{1,0:T(8,128)S(1)}, f32[136,128]{1,0:T(8,128)S(1)}, u32[]{:S(2)}, u32[]{:S(2)}) collective-permute-start(f32[136,128]{1,0:T(8,128)S(1)} %col2_grads.1.refs_0_), channel_id=1, source_target_pairs={{0,4},{4,0},{8,12},{12,8},{16,20},{20,16},{24,28},{28,24},{1,5},{5... | collective-permute-start | bytes 208904 | tf_op jit(solution)/shard_map/ppermute | solution.py:409
  60.5 4.4 %collective-permute-start.24 = (f32[136,128]{1,0:T(8,128)S(1)}, f32[136,128]{1,0:T(8,128)S(1)}, u32[]{:S(2)}, u32[]{:S(2)}) collective-permute-start(f32[136,128]{1,0:T(8,128)S(1)} %row1_grads.1.refs_0_.refs_4_.refs_1_), channel_id=1, source_target_pairs={{0,8},{4,12},{8,0},{12,4},{16,24},{20,28},{24,16},{28,20},{1,9},{5... | collective-permute-start | bytes 208904 | tf_op jit(solution)/shard_map/ppermute | solution.py:409
  (5 other events, 66.1 us)

commit v7 on v6

--- a/solution.py
+++ b/solution.py
@@ -291,23 +291,35 @@
     )
 
 
-def grads_kernel(agg_ref, pre_ref, out_ref):
-    width = agg_ref.shape[1]
+def folds(rows, width, node_rows):
+    step = -(-rows * width // node_rows // 8) * 8
+    return [(at, min(step, rows - at)) for at in range(0, rows, step)], step
+
+
+def grads_kernel(back_ref, agg_ref, pre_ref, out_ref, sums):
+    width, node_rows = back_ref.shape
     pre_grad = pre_ref[...]
-    out_ref[pl.ds(0, width), :] = tn_dot(agg_ref[...], pre_grad, precision=HIGHEST)
-    out_ref[pl.ds(width, PAD), :] = jnp.broadcast_to(
+    out_ref[pl.ds(0, width), :] = back_ref[...]
+    sums[pl.ds(0, width), :] = tn_dot(agg_ref[...], pre_grad, precision=HIGHEST)
+    sums[pl.ds(width, PAD), :] = jnp.broadcast_to(
         jnp.sum(pre_grad, axis=0, keepdims=True), (PAD, width)
     )
-
-
-def weight_parts(aggregated, pre_grad):
+    parts, step = folds(width + PAD, width, node_rows)
+    out_ref[pl.ds(width, step), :] = jnp.zeros((step, node_rows), F32)
+    for j, (at, size) in enumerate(parts):
+        out_ref[pl.ds(width, size), pl.ds(j * width, width)] = sums[pl.ds(at, size), :]
+
+
+def weight_parts(back, aggregated, pre_grad):
     node_rows, width = aggregated.shape
+    step = folds(width + PAD, width, node_rows)[1]
     return call(
         grads_kernel,
         "weight_parts",
-        (aggregated, pre_grad),
-        (vmem(width + PAD, width),),
+        (back, aggregated, pre_grad),
+        (vmem(width + step, node_rows),),
         flops=12 * node_rows * width * width,
+        scratch=(vmem(width + PAD, width),),
     )[0]
 
 
@@ -320,34 +332,38 @@
         out_ref[...] = both[:width, :] + both[width:, :]
 
 
-def backward_first_kernel(peers, col_count, *refs):
-    outs, lhs = refs[-1 - len(peers) : -1], refs[-1]
-    dense_ref, blocks = refs[0], refs[1 : 1 + col_count]
+def backward_first_kernel(peers, *refs):
+    outs, lhs, grad_ref = refs[-2 - len(peers) : -2], refs[-2], refs[-1]
+    dense_ref, blocks = refs[0], refs[1 : -2 - len(peers)]
     col = lax.axis_index("col")
-    width, node_rows = blocks[0].shape
+    width, node_rows = outs[0].shape
     for m, block in enumerate(blocks):
         start = pl.multiple_of((col ^ m) * node_rows, node_rows)
-        high, low = split(block[...])
+        high, low = split(block[pl.ds(0, width), :])
         lhs[:width, pl.ds(start, node_rows)] = high
         lhs[width:, pl.ds(start, node_rows)] = low
     backward_chunks(peers, dense_ref, lhs, outs)
+    for j, (at, size) in enumerate(folds(grad_ref.shape[0], width, node_rows)[0]):
+        rows, cols = pl.ds(width, size), pl.ds(j * width, width)
+        grad_ref[pl.ds(at, size), :] = blocks[0][rows, cols] + blocks[1][rows, cols]
 
 
 def backward_second_kernel(peers, dense_ref, lhs, *outs):
     backward_chunks(peers, dense_ref, lhs, outs)
 
 
-def backward_first(peers, dense, blocks, after):
-    width, node_rows = blocks[0].shape
+def backward_first(peers, dense, blocks, width):
     rows = dense.shape[0]
+    node_rows = blocks[0].shape[1]
     out = call(
-        functools.partial(backward_first_kernel, peers, len(blocks)),
+        functools.partial(backward_first_kernel, peers),
         "backward_first",
-        (dense, *blocks, *after),
-        [vmem(width, node_rows)] * len(peers) + [vmem(2 * width, rows, dtype=BF16)],
+        (dense, *blocks),
+        [vmem(width, node_rows)] * len(peers)
+        + [vmem(2 * width, rows, dtype=BF16), vmem(width + PAD, width)],
         flops=4 * len(peers) * node_rows * rows * width,
     )
-    return dict(zip(peers, out)), out[-1]
+    return dict(zip(peers, out)), out[-2], out[-1]
 
 
 def backward_second(peers, dense, lhs, node_rows):
@@ -440,27 +456,26 @@
     )
 
     backs = [None] * col_count
-    backs[0] = back
     for m in even[1:]:
         backs[m] = swap(back, "col", m)
+    backs[0] = weight_parts(back, aggregated, pre_grad)
     for m in even:
         backs[m | 1] = swap(backs[m], "col", 1)
-    grads = weight_parts(aggregated, pre_grad)
-    grads = sum_all([grads, swap(grads, "row", top)], "top_grads", (), HINT)
-    chunks, lhs = backward_first(far, dense, backs, (grads,))
+    chunks, lhs, grads = backward_first(far, dense, backs, width)
     ahead = [chunks[top]] + [swap(chunks[top | m], "row", m) for m in near[1:]]
     chunks = backward_second(near, dense, lhs, node_rows)
     mine = [chunks[0]] + [swap(chunks[m], "row", m) for m in near[1:]]
     ahead = sum_all(ahead, "ahead_sums", (), HINT)
     passed = swap(ahead, "row", top)
 
-    rounds = [("col", 1 << b) for b in range(col_count.bit_length() - 1)]
-    rounds += [("row", 1 << b) for b in range(top.bit_length() - 1)]
-    grads = sum_all([grads], "held_grads", (chunks[0],))
+    rounds = [("col", 1 << b) for b in range(1, col_count.bit_length() - 1)]
+    rounds += [("row", top)] + [("row", 1 << b) for b in range(top.bit_length() - 1)]
+    grads = sum_all([grads], "held_grads", (lhs,))
     for step, (axis, mask) in enumerate(rounds[:-1]):
-        after = (ahead,) if axis == "col" and mask * 2 == col_count else ()
+        after = (ahead,) if (axis, mask) == ("row", top) else ()
         grads = sum_all([grads, swap(grads, axis, mask)], f"{axis}{mask}_grads", after)
-    activated = hand_over(activated, (grads,))
+        if step == len(rounds) - 3:
+            activated = hand_over(activated, (grads,))
     mine = sum_all(mine, "mine_sums", (grads,), HINT // 4)
     mine = sum_all([mine, passed], "last_sums", (), HINT)
     axis, mask = rounds[-1]

time: 65.8 us -> 68.6 us (1.043)
  starting transfers between devices: 24.9 us -> 28.6 us
  waiting for transfers between devices: 28.5 us -> 27.7 us
    ppermute x25 -> x24, starting transfers between devices: 24.9 us -> 28.6 us  [swap(): return lax.ppermute(value, axis, [(i, i ^ mask) for i in range(count)])]
    ppermute x25 -> x24, waiting for transfers between devices: 28.5 us -> 27.7 us  [swap(): return lax.ppermute(value, axis, [(i, i ^ mask) for i in range(count)])]
    pallas_call x21 -> x20, Pallas kernels: 10.7 us -> 10.7 us  [call(): pl.pallas_call(kernel, out_shape=tuple(outs), in_specs=list(before_specs)...]
  transfers between devices with their start and end apart: 25 -> 24, of which waited for: 13 -> 12; matrix products, arithmetic and copies ran while one was open for 0% -> 0% of each run, Pallas kernels for 11% -> 10%
where the time goes in v7:
time: 68.6 us; the launch traced here: 68.4 us
  starting transfers between devices  28.6 us (42%)
  waiting for transfers between devices  27.7 us (40%)
  Pallas kernels  10.7 us (16%)
  between operations  1.48 us (2%)
    ppermute x24, starting transfers between devices, swap(): return lax.ppermute(value, axis, [(i, i ^ mask) for i in range(count)])  28.6 us
    ppermute x24, waiting for transfers between devices, swap(): return lax.ppermute(value, axis, [(i, i ^ mask) for i in range(count)])  27.7 us
    pallas_call x20, Pallas kernels, call(): pl.pallas_call(kernel, out_shape=tuple(outs), in_specs=list(before_specs)...  10.7 us
  transfers between devices with their start and end apart: 24, of which 12 were waited for; matrix products, arithmetic and copies ran while one was open for 0% of the time, Pallas kernels for 10%

profile of v7, /device:TPU:0, one launch (start us, length us, event | category | flops | bytes accessed | tf_op | source)
XLA Modules:
  0.0 68.4 jit_solution(10931268988450470863)
XLA Ops:
  0.6 3.1 %collective-permute-start.3 = (f32[256,128]{1,0:T(8,128)}, f32[256,128]{1,0:T(8,128)S(1)}, u32[]{:S(2)}, u32[]{:S(2)}) collective-permute-start(f32[256,128]{1,0:T(8,128)} %refs_3_.2), channel_id=1, source_target_pairs={{0,8},{4,12},{8,0},{12,4},{16,24},{20,28},{24,16},{28,20},{1,9},{5... | collective-permute-start | bytes 393224 | tf_op jit(solution)/shard_map/ppermute | solution.py:425
  3.7 1.5 %collective-permute-start.2 = (f32[256,128]{1,0:T(8,128)}, f32[256,128]{1,0:T(8,128)S(1)}, u32[]{:S(2)}, u32[]{:S(2)}) collective-permute-start(f32[256,128]{1,0:T(8,128)} %refs_3_.2), channel_id=1, source_target_pairs={{0,4},{4,0},{8,12},{12,8},{16,20},{20,16},{24,28},{28,24},{1,5},{5... | collective-permute-start | bytes 393224 | tf_op jit(solution)/shard_map/ppermute | solution.py:425
  5.3 2.6 %collective-permute-start = (f32[256,128]{1,0:T(8,128)}, f32[256,128]{1,0:T(8,128)S(1)}, u32[]{:S(2)}, u32[]{:S(2)}) collective-permute-start(f32[256,128]{1,0:T(8,128)} %refs_3_.2), channel_id=1, source_target_pairs={{0,16},{4,20},{8,24},{12,28},{16,0},{20,4},{24,8},{28,12},{1,17},{... | collective-permute-start | bytes 393224 | tf_op jit(solution)/shard_map/ppermute | solution.py:425
  8.9 3.7 %densify.1 = (bf16[1024,2048]{1,0:T(8,128)(2,1)S(1)}, f32[16,128]{1,0:T(8,128)S(1)}) custom-call(s32[1,128]{1,0:T(1,128)} %bitcast.6, s32[1,1]{1,0:T(1,128)S(6)} %copy.11.counts_hbm, s32[128,128,128]{2,1,0:T(8,128)} %bitcast.5), custom_call_target="tpu_custom_call" | custom-call | flops 838860800 | tf_op jit(solution)/shard_map/densify/pallas_call | solution.py:50
  12.7 4.5 %collective-permute-done.1.got_ref = f32[16,128]{1,0:T(8,128)S(1)} collective-permute-done((f32[16,128]{1,0:T(8,128)S(1)}, f32[16,128]{1,0:T(8,128)S(1)}, u32[]{:S(2)}, u32[]{:S(2)}) %collective-permute-start.1) | collective-permute-done | bytes 8224 | tf_op jit(solution)/shard_map/ppermute | solution.py:425
  17.3 2.6 %collective-permute-start.7 = (f32[272,128]{1,0:T(8,128)S(1)}, f32[272,128]{1,0:T(8,128)S(1)}, u32[]{:S(2)}, u32[]{:S(2)}) collective-permute-start(f32[272,128]{1,0:T(8,128)S(1)} %message.1.refs_0_.refs_7_), channel_id=1, source_target_pairs={{0,12},{4,8},{8,4},{12,0},{16,28},{20,24},{24,20},{28,16},{1,13},{... | collective-permute-start | bytes 417800 | tf_op jit(solution)/shard_map/ppermute | solution.py:425
  21.5 1.8 %collective-permute-done.7.refs_3_.refs_10_ = f32[272,128]{1,0:T(8,128)S(1)} collective-permute-done((f32[272,128]{1,0:T(8,128)S(1)}, f32[272,128]{1,0:T(8,128)S(1)}, u32[]{:S(2)}, u32[]{:S(2)}) %collective-permute-start.7) | collective-permute-done | bytes 139296 | tf_op jit(solution)/shard_map/ppermute | solution.py:425
  23.3 1.6 %collective-permute-done.6.refs_2_.refs_9_ = f32[272,128]{1,0:T(8,128)S(1)} collective-permute-done((f32[272,128]{1,0:T(8,128)S(1)}, f32[272,128]{1,0:T(8,128)S(1)}, u32[]{:S(2)}, u32[]{:S(2)}) %collective-permute-start.6) | collective-permute-done | bytes 139296 | tf_op jit(solution)/shard_map/ppermute | solution.py:425
  28.4 1.6 %collective-permute-start.9 = (f32[264,128]{1,0:T(8,128)S(1)}, f32[264,128]{1,0:T(8,128)S(1)}, u32[]{:S(2)}, u32[]{:S(2)}) collective-permute-start(f32[264,128]{1,0:T(8,128)S(1)} %pair_sums.1), channel_id=1, source_target_pairs={{0,2},{1,3},{2,0},{3,1},{4,6},{5,7},{6,4},{7,5},{8,10},{9,11},{10,... | collective-permute-start | bytes 405512 | tf_op jit(solution)/shard_map/ppermute | solution.py:425
  29.9 4.1 %collective-permute-done.9.refs_2_ = f32[264,128]{1,0:T(8,128)S(1)} collective-permute-done((f32[264,128]{1,0:T(8,128)S(1)}, f32[264,128]{1,0:T(8,128)S(1)}, u32[]{:S(2)}, u32[]{:S(2)}) %collective-permute-start.9) | collective-permute-done | bytes 135200 | tf_op jit(solution)/shard_map/ppermute | solution.py:425
  34.9 1.5 %collective-permute-start.11 = (f32[128,256]{1,0:T(8,128)S(1)}, f32[128,256]{1,0:T(8,128)S(1)}, u32[]{:S(2)}, u32[]{:S(2)}) collective-permute-start(f32[128,256]{1,0:T(8,128)S(1)} %get-tuple-element.33.back_ref), channel_id=1, source_target_pairs={{0,2},{1,3},{2,0},{3,1},{4,6},{5,7},{6,4},{7,5},{8,10},{9,11},{10,... | collective-permute-start | bytes 393224 | tf_op jit(solution)/shard_map/ppermute | solution.py:425
  36.8 3.1 %collective-permute-done.11.refs_3_ = f32[128,256]{1,0:T(8,128)S(1)} collective-permute-done((f32[128,256]{1,0:T(8,128)S(1)}, f32[128,256]{1,0:T(8,128)S(1)}, u32[]{:S(2)}, u32[]{:S(2)}) %collective-permute-start.11) | collective-permute-done | bytes 131104 | tf_op jit(solution)/shard_map/ppermute | solution.py:425
  39.9 1.3 %collective-permute-done.12.refs_4_ = f32[128,256]{1,0:T(8,128)S(1)} collective-permute-done((f32[128,256]{1,0:T(8,128)S(1)}, f32[128,256]{1,0:T(8,128)S(1)}, u32[]{:S(2)}, u32[]{:S(2)}) %collective-permute-start.12) | collective-permute-done | bytes 131104 | tf_op jit(solution)/shard_map/ppermute | solution.py:425
  43.1 1.6 %collective-permute-start.16 = (f32[128,256]{1,0:T(8,128)S(1)}, f32[128,256]{1,0:T(8,128)S(1)}, u32[]{:S(2)}, u32[]{:S(2)}) collective-permute-start(f32[128,256]{1,0:T(8,128)S(1)} %get-tuple-element.40), channel_id=1, source_target_pairs={{0,8},{4,12},{8,0},{12,4},{16,24},{20,28},{24,16},{28,20},{1,9},{5... | collective-permute-start | bytes 393224 | tf_op jit(solution)/shard_map/ppermute | solution.py:425
  44.7 1.0 %collective-permute-start.17 = (f32[128,256]{1,0:T(8,128)S(1)}, f32[128,256]{1,0:T(8,128)S(1)}, u32[]{:S(2)}, u32[]{:S(2)}) collective-permute-start(f32[128,256]{1,0:T(8,128)S(1)} %get-tuple-element.41), channel_id=1, source_target_pairs={{0,12},{4,8},{8,4},{12,0},{16,28},{20,24},{24,20},{28,16},{1,13},{... | collective-permute-start | bytes 393224 | tf_op jit(solution)/shard_map/ppermute | solution.py:425
  45.7 1.5 %collective-permute-start.13 = (f32[136,128]{1,0:T(8,128)S(1)}, f32[136,128]{1,0:T(8,128)S(1)}, u32[]{:S(2)}, u32[]{:S(2)}) collective-permute-start(f32[136,128]{1,0:T(8,128)S(1)} %held_grads.1.refs_0_), channel_id=1, source_target_pairs={{0,2},{1,3},{2,0},{3,1},{4,6},{5,7},{6,4},{7,5},{8,10},{9,11},{10,... | collective-permute-start | bytes 208904 | tf_op jit(solution)/shard_map/ppermute | solution.py:425
  48.9 1.1 %collective-permute-done.13.refs_1_ = f32[136,128]{1,0:T(8,128)S(1)} collective-permute-done((f32[136,128]{1,0:T(8,128)S(1)}, f32[136,128]{1,0:T(8,128)S(1)}, u32[]{:S(2)}, u32[]{:S(2)}) %collective-permute-start.13) | collective-permute-done | bytes 69664 | tf_op jit(solution)/shard_map/ppermute | solution.py:425
  50.0 1.6 %collective-permute-start.19 = (f32[128,256]{1,0:T(8,128)S(1)}, f32[128,256]{1,0:T(8,128)S(1)}, u32[]{:S(2)}, u32[]{:S(2)}) collective-permute-start(f32[128,256]{1,0:T(8,128)S(1)} %get-tuple-element.44), channel_id=1, source_target_pairs={{0,8},{4,12},{8,0},{12,4},{16,24},{20,28},{24,16},{28,20},{1,9},{5... | collective-permute-start | bytes 393224 | tf_op jit(solution)/shard_map/ppermute | solution.py:425
  52.9 2.6 %collective-permute-start.22 = (f32[128,256]{1,0:T(8,128)S(1)}, f32[128,256]{1,0:T(8,128)S(1)}, u32[]{:S(2)}, u32[]{:S(2)}) collective-permute-start(f32[128,256]{1,0:T(8,128)S(1)} %ahead_sums.1.refs_2_), channel_id=1, source_target_pairs={{0,16},{4,20},{8,24},{12,28},{16,0},{20,4},{24,8},{28,12},{1,17},{... | collective-permute-start | bytes 393224 | tf_op jit(solution)/shard_map/ppermute | solution.py:425
  55.5 3.4 %collective-permute-done.14.refs_1_ = f32[136,128]{1,0:T(8,128)S(1)} collective-permute-done((f32[136,128]{1,0:T(8,128)S(1)}, f32[136,128]{1,0:T(8,128)S(1)}, u32[]{:S(2)}, u32[]{:S(2)}) %collective-permute-start.14) | collective-permute-done | bytes 69664 | tf_op jit(solution)/shard_map/ppermute | solution.py:425
  58.9 1.1 %collective-permute-start.21 = (f32[136,128]{1,0:T(8,128)S(1)}, f32[136,128]{1,0:T(8,128)S(1)}, u32[]{:S(2)}, u32[]{:S(2)}) collective-permute-start(f32[136,128]{1,0:T(8,128)S(1)} %row4_grads.1.refs_0_), channel_id=1, source_target_pairs={{0,4},{4,0},{8,12},{12,8},{16,20},{20,16},{24,28},{28,24},{1,5},{5... | collective-permute-start | bytes 208904 | tf_op jit(solution)/shard_map/ppermute | solution.py:425
  60.7 2.6 %collective-permute-done.21.refs_1_ = f32[136,128]{1,0:T(8,128)S(1)} collective-permute-done((f32[136,128]{1,0:T(8,128)S(1)}, f32[136,128]{1,0:T(8,128)S(1)}, u32[]{:S(2)}, u32[]{:S(2)}) %collective-permute-start.21) | collective-permute-done | bytes 69664 | tf_op jit(solution)/shard_map/ppermute | solution.py:425
  63.3 1.5 %collective-permute-start.23 = (f32[136,128]{1,0:T(8,128)S(1)}, f32[136,128]{1,0:T(8,128)S(1)}, u32[]{:S(2)}, u32[]{:S(2)}) collective-permute-start(f32[136,128]{1,0:T(8,128)S(1)} %row1_grads.1.refs_4_.refs_1_), channel_id=1, source_target_pairs={{0,8},{4,12},{8,0},{12,4},{16,24},{20,28},{24,16},{28,20},{1,9},{5... | collective-permute-start | bytes 208904 | tf_op jit(solution)/shard_map/ppermute | solution.py:425
  64.8 2.8 %collective-permute-done.23.refs_2_ = f32[136,128]{1,0:T(8,128)S(1)} collective-permute-done((f32[136,128]{1,0:T(8,128)S(1)}, f32[136,128]{1,0:T(8,128)S(1)}, u32[]{:S(2)}, u32[]{:S(2)}) %collective-permute-start.23) | collective-permute-done | bytes 69664 | tf_op jit(solution)/shard_map/ppermute | solution.py:425
  (52 shorter events, 13.0 us)
Async XLA Ops:
  0.6 16.6 %collective-permute-start.3 = (f32[256,128]{1,0:T(8,128)}, f32[256,128]{1,0:T(8,128)S(1)}, u32[]{:S(2)}, u32[]{:S(2)}) collective-permute-start(f32[256,128]{1,0:T(8,128)} %refs_3_.2), channel_id=1, source_target_pairs={{0,8},{4,12},{8,0},{12,4},{16,24},{20,28},{24,16},{28,20},{1,9},{5... | collective-permute-start | bytes 393224 | tf_op jit(solution)/shard_map/ppermute | solution.py:425
  3.7 13.5 %collective-permute-start.2 = (f32[256,128]{1,0:T(8,128)}, f32[256,128]{1,0:T(8,128)S(1)}, u32[]{:S(2)}, u32[]{:S(2)}) collective-permute-start(f32[256,128]{1,0:T(8,128)} %refs_3_.2), channel_id=1, source_target_pairs={{0,4},{4,0},{8,12},{12,8},{16,20},{20,16},{24,28},{28,24},{1,5},{5... | collective-permute-start | bytes 393224 | tf_op jit(solution)/shard_map/ppermute | solution.py:425
  5.3 12.0 %collective-permute-start = (f32[256,128]{1,0:T(8,128)}, f32[256,128]{1,0:T(8,128)S(1)}, u32[]{:S(2)}, u32[]{:S(2)}) collective-permute-start(f32[256,128]{1,0:T(8,128)} %refs_3_.2), channel_id=1, source_target_pairs={{0,16},{4,20},{8,24},{12,28},{16,0},{20,4},{24,8},{28,12},{1,17},{... | collective-permute-start | bytes 393224 | tf_op jit(solution)/shard_map/ppermute | solution.py:425
  7.8 9.4 %collective-permute-start.4 = (f32[256,128]{1,0:T(8,128)}, f32[256,128]{1,0:T(8,128)S(1)}, u32[]{:S(2)}, u32[]{:S(2)}) collective-permute-start(f32[256,128]{1,0:T(8,128)} %refs_3_.2), channel_id=1, source_target_pairs={{0,12},{4,8},{8,4},{12,0},{16,28},{20,24},{24,20},{28,16},{1,13},{... | collective-permute-start | bytes 393224 | tf_op jit(solution)/shard_map/ppermute | solution.py:425
  12.6 4.6 %collective-permute-start.1 = (f32[16,128]{1,0:T(8,128)S(1)}, f32[16,128]{1,0:T(8,128)S(1)}, u32[]{:S(2)}, u32[]{:S(2)}) collective-permute-start(f32[16,128]{1,0:T(8,128)S(1)} %get-tuple-element.28.own_ref), channel_id=1, source_target_pairs={{0,16},{4,20},{8,24},{12,28},{16,0},{20,4},{24,8},{28,12},{1,17},{... | collective-permute-start | bytes 24584 | tf_op jit(solution)/shard_map/ppermute | solution.py:425
  17.3 6.0 %collective-permute-start.7 = (f32[272,128]{1,0:T(8,128)S(1)}, f32[272,128]{1,0:T(8,128)S(1)}, u32[]{:S(2)}, u32[]{:S(2)}) collective-permute-start(f32[272,128]{1,0:T(8,128)S(1)} %message.1.refs_0_.refs_7_), channel_id=1, source_target_pairs={{0,12},{4,8},{8,4},{12,0},{16,28},{20,24},{24,20},{28,16},{1,13},{... | collective-permute-start | bytes 417800 | tf_op jit(solution)/shard_map/ppermute | solution.py:425
  19.9 5.1 %collective-permute-start.6 = (f32[272,128]{1,0:T(8,128)S(1)}, f32[272,128]{1,0:T(8,128)S(1)}, u32[]{:S(2)}, u32[]{:S(2)}) collective-permute-start(f32[272,128]{1,0:T(8,128)S(1)} %message.1.refs_0_.refs_7_), channel_id=1, source_target_pairs={{0,8},{4,12},{8,0},{12,4},{16,24},{20,28},{24,16},{28,20},{1,9},{5... | collective-permute-start | bytes 417800 | tf_op jit(solution)/shard_map/ppermute | solution.py:425
  20.4 5.1 %collective-permute-start.5 = (f32[272,128]{1,0:T(8,128)S(1)}, f32[272,128]{1,0:T(8,128)S(1)}, u32[]{:S(2)}, u32[]{:S(2)}) collective-permute-start(f32[272,128]{1,0:T(8,128)S(1)} %message.1.refs_0_.refs_7_), channel_id=1, source_target_pairs={{0,4},{4,0},{8,12},{12,8},{16,20},{20,16},{24,28},{28,24},{1,5},{5... | collective-permute-start | bytes 417800 | tf_op jit(solution)/shard_map/ppermute | solution.py:425
  26.8 1.6 %collective-permute-start.8 = (f32[2,264,128]{2,1,0:T(8,128)S(1)}, f32[2,264,128]{2,1,0:T(8,128)S(1)}, u32[]{:S(2)}, u32[]{:S(2)}) collective-permute-start(f32[2,264,128]{2,1,0:T(8,128)S(1)} %get-tuple-element.31), channel_id=1, source_target_pairs={{0,1},{1,0},{2,3},{3,2},{4,5},{5,4},{6,7},{7,6},{8,9},{9,8},{10,11... | collective-permute-start | bytes 811016 | tf_op jit(solution)/shard_map/ppermute | solution.py:425
  28.4 5.7 %collective-permute-start.9 = (f32[264,128]{1,0:T(8,128)S(1)}, f32[264,128]{1,0:T(8,128)S(1)}, u32[]{:S(2)}, u32[]{:S(2)}) collective-permute-start(f32[264,128]{1,0:T(8,128)S(1)} %pair_sums.1), channel_id=1, source_target_pairs={{0,2},{1,3},{2,0},{3,1},{4,6},{5,7},{6,4},{7,5},{8,10},{9,11},{10,... | collective-permute-start | bytes 405512 | tf_op jit(solution)/shard_map/ppermute | solution.py:425
  34.9 5.0 %collective-permute-start.11 = (f32[128,256]{1,0:T(8,128)S(1)}, f32[128,256]{1,0:T(8,128)S(1)}, u32[]{:S(2)}, u32[]{:S(2)}) collective-permute-start(f32[128,256]{1,0:T(8,128)S(1)} %get-tuple-element.33.back_ref), channel_id=1, source_target_pairs={{0,2},{1,3},{2,0},{3,1},{4,6},{5,7},{6,4},{7,5},{8,10},{9,11},{10,... | collective-permute-start | bytes 393224 | tf_op jit(solution)/shard_map/ppermute | solution.py:425
  36.7 3.2 %collective-permute-start.10 = (f32[200,256]{1,0:T(8,128)S(1)}, f32[200,256]{1,0:T(8,128)S(1)}, u32[]{:S(2)}, u32[]{:S(2)}) collective-permute-start(f32[200,256]{1,0:T(8,128)S(1)} %weight_parts.1.refs_1_), channel_id=1, source_target_pairs={{0,1},{1,0},{2,3},{3,2},{4,5},{5,4},{6,7},{7,6},{8,9},{9,8},{10,11... | collective-permute-start | bytes 614408 | tf_op jit(solution)/shard_map/ppermute | solution.py:425
  39.9 1.3 %collective-permute-start.12 = (f32[128,256]{1,0:T(8,128)S(1)}, f32[128,256]{1,0:T(8,128)S(1)}, u32[]{:S(2)}, u32[]{:S(2)}) collective-permute-start(f32[128,256]{1,0:T(8,128)S(1)} %collective-permute-done.11.refs_3_), channel_id=1, source_target_pairs={{0,1},{1,0},{2,3},{3,2},{4,5},{5,4},{6,7},{7,6},{8,9},{9,8},{10,11... | collective-permute-start | bytes 393224 | tf_op jit(solution)/shard_map/ppermute | solution.py:425
  42.1 9.4 %collective-permute-start.15 = (f32[128,256]{1,0:T(8,128)S(1)}, f32[128,256]{1,0:T(8,128)S(1)}, u32[]{:S(2)}, u32[]{:S(2)}) collective-permute-start(f32[128,256]{1,0:T(8,128)S(1)} %get-tuple-element.39), channel_id=1, source_target_pairs={{0,4},{4,0},{8,12},{12,8},{16,20},{20,16},{24,28},{28,24},{1,5},{5... | collective-permute-start | bytes 393224 | tf_op jit(solution)/shard_map/ppermute | solution.py:425
  43.1 9.4 %collective-permute-start.16 = (f32[128,256]{1,0:T(8,128)S(1)}, f32[128,256]{1,0:T(8,128)S(1)}, u32[]{:S(2)}, u32[]{:S(2)}) collective-permute-start(f32[128,256]{1,0:T(8,128)S(1)} %get-tuple-element.40), channel_id=1, source_target_pairs={{0,8},{4,12},{8,0},{12,4},{16,24},{20,28},{24,16},{28,20},{1,9},{5... | collective-permute-start | bytes 393224 | tf_op jit(solution)/shard_map/ppermute | solution.py:425
  44.7 8.2 %collective-permute-start.17 = (f32[128,256]{1,0:T(8,128)S(1)}, f32[128,256]{1,0:T(8,128)S(1)}, u32[]{:S(2)}, u32[]{:S(2)}) collective-permute-start(f32[128,256]{1,0:T(8,128)S(1)} %get-tuple-element.41), channel_id=1, source_target_pairs={{0,12},{4,8},{8,4},{12,0},{16,28},{20,24},{24,20},{28,16},{1,13},{... | collective-permute-start | bytes 393224 | tf_op jit(solution)/shard_map/ppermute | solution.py:425
  45.7 4.3 %collective-permute-start.13 = (f32[136,128]{1,0:T(8,128)S(1)}, f32[136,128]{1,0:T(8,128)S(1)}, u32[]{:S(2)}, u32[]{:S(2)}) collective-permute-start(f32[136,128]{1,0:T(8,128)S(1)} %held_grads.1.refs_0_), channel_id=1, source_target_pairs={{0,2},{1,3},{2,0},{3,1},{4,6},{5,7},{6,4},{7,5},{8,10},{9,11},{10,... | collective-permute-start | bytes 208904 | tf_op jit(solution)/shard_map/ppermute | solution.py:425
  47.9 16.9 %collective-permute-start.18 = (f32[128,256]{1,0:T(8,128)S(1)}, f32[128,256]{1,0:T(8,128)S(1)}, u32[]{:S(2)}, u32[]{:S(2)}) collective-permute-start(f32[128,256]{1,0:T(8,128)S(1)} %get-tuple-element.43), channel_id=1, source_target_pairs={{0,4},{4,0},{8,12},{12,8},{16,20},{20,16},{24,28},{28,24},{1,5},{5... | collective-permute-start | bytes 393224 | tf_op jit(solution)/shard_map/ppermute | solution.py:425
  50.0 14.8 %collective-permute-start.19 = (f32[128,256]{1,0:T(8,128)S(1)}, f32[128,256]{1,0:T(8,128)S(1)}, u32[]{:S(2)}, u32[]{:S(2)}) collective-permute-start(f32[128,256]{1,0:T(8,128)S(1)} %get-tuple-element.44), channel_id=1, source_target_pairs={{0,8},{4,12},{8,0},{12,4},{16,24},{20,28},{24,16},{28,20},{1,9},{5... | collective-permute-start | bytes 393224 | tf_op jit(solution)/shard_map/ppermute | solution.py:425
  51.6 13.2 %collective-permute-start.20 = (f32[128,256]{1,0:T(8,128)S(1)}, f32[128,256]{1,0:T(8,128)S(1)}, u32[]{:S(2)}, u32[]{:S(2)}) collective-permute-start(f32[128,256]{1,0:T(8,128)S(1)} %get-tuple-element.45), channel_id=1, source_target_pairs={{0,12},{4,8},{8,4},{12,0},{16,28},{20,24},{24,20},{28,16},{1,13},{... | collective-permute-start | bytes 393224 | tf_op jit(solution)/shard_map/ppermute | solution.py:425
  52.5 6.4 %collective-permute-start.14 = (f32[136,128]{1,0:T(8,128)S(1)}, f32[136,128]{1,0:T(8,128)S(1)}, u32[]{:S(2)}, u32[]{:S(2)}) collective-permute-start(f32[136,128]{1,0:T(8,128)S(1)} %col2_grads.1.refs_0_), channel_id=1, source_target_pairs={{0,16},{4,20},{8,24},{12,28},{16,0},{20,4},{24,8},{28,12},{1,17},{... | collective-permute-start | bytes 208904 | tf_op jit(solution)/shard_map/ppermute | solution.py:425
  52.9 12.0 %collective-permute-start.22 = (f32[128,256]{1,0:T(8,128)S(1)}, f32[128,256]{1,0:T(8,128)S(1)}, u32[]{:S(2)}, u32[]{:S(2)}) collective-permute-start(f32[128,256]{1,0:T(8,128)S(1)} %ahead_sums.1.refs_2_), channel_id=1, source_target_pairs={{0,16},{4,20},{8,24},{12,28},{16,0},{20,4},{24,8},{28,12},{1,17},{... | collective-permute-start | bytes 393224 | tf_op jit(solution)/shard_map/ppermute | solution.py:425
  58.9 4.4 %collective-permute-start.21 = (f32[136,128]{1,0:T(8,128)S(1)}, f32[136,128]{1,0:T(8,128)S(1)}, u32[]{:S(2)}, u32[]{:S(2)}) collective-permute-start(f32[136,128]{1,0:T(8,128)S(1)} %row4_grads.1.refs_0_), channel_id=1, source_target_pairs={{0,4},{4,0},{8,12},{12,8},{16,20},{20,16},{24,28},{28,24},{1,5},{5... | collective-permute-start | bytes 208904 | tf_op jit(solution)/shard_map/ppermute | solution.py:425
  63.3 4.4 %collective-permute-start.23 = (f32[136,128]{1,0:T(8,128)S(1)}, f32[136,128]{1,0:T(8,128)S(1)}, u32[]{:S(2)}, u32[]{:S(2)}) collective-permute-start(f32[136,128]{1,0:T(8,128)S(1)} %row1_grads.1.refs_4_.refs_1_), channel_id=1, source_target_pairs={{0,8},{4,12},{8,0},{12,4},{16,24},{20,28},{24,16},{28,20},{1,9},{5... | collective-permute-start | bytes 208904 | tf_op jit(solution)/shard_map/ppermute | solution.py:425
  (4 other events, 64.8 us)

commit v8 on v7

--- a/solution.py
+++ b/solution.py
@@ -332,9 +332,9 @@
         out_ref[...] = both[:width, :] + both[width:, :]
 
 
-def backward_first_kernel(peers, *refs):
-    outs, lhs, grad_ref = refs[-2 - len(peers) : -2], refs[-2], refs[-1]
-    dense_ref, blocks = refs[0], refs[1 : -2 - len(peers)]
+def backward_first_kernel(peers, col_count, *refs):
+    outs, lhs = refs[-1 - len(peers) : -1], refs[-1]
+    dense_ref, blocks = refs[0], refs[1 : 1 + col_count]
     col = lax.axis_index("col")
     width, node_rows = outs[0].shape
     for m, block in enumerate(blocks):
@@ -343,27 +343,34 @@
         lhs[:width, pl.ds(start, node_rows)] = high
         lhs[width:, pl.ds(start, node_rows)] = low
     backward_chunks(peers, dense_ref, lhs, outs)
-    for j, (at, size) in enumerate(folds(grad_ref.shape[0], width, node_rows)[0]):
-        rows, cols = pl.ds(width, size), pl.ds(j * width, width)
-        grad_ref[pl.ds(at, size), :] = blocks[0][rows, cols] + blocks[1][rows, cols]
+
+
+def unfold_kernel(own_ref, got_ref, out_ref):
+    rows, width = out_ref.shape
+    for j, (at, size) in enumerate(folds(rows, width, own_ref.shape[1])[0]):
+        part = pl.ds(width, size), pl.ds(j * width, width)
+        out_ref[pl.ds(at, size), :] = own_ref[part] + got_ref[part]
+
+
+def unfold_sums(own, got, width):
+    return call(unfold_kernel, "core_grads", (own, got), (vmem(width + PAD, width),))[0]
 
 
 def backward_second_kernel(peers, dense_ref, lhs, *outs):
     backward_chunks(peers, dense_ref, lhs, outs)
 
 
-def backward_first(peers, dense, blocks, width):
+def backward_first(peers, dense, blocks, width, after):
     rows = dense.shape[0]
     node_rows = blocks[0].shape[1]
     out = call(
-        functools.partial(backward_first_kernel, peers),
+        functools.partial(backward_first_kernel, peers, len(blocks)),
         "backward_first",
-        (dense, *blocks),
-        [vmem(width, node_rows)] * len(peers)
-        + [vmem(2 * width, rows, dtype=BF16), vmem(width + PAD, width)],
+        (dense, *blocks, *after),
+        [vmem(width, node_rows)] * len(peers) + [vmem(2 * width, rows, dtype=BF16)],
         flops=4 * len(peers) * node_rows * rows * width,
     )
-    return dict(zip(peers, out)), out[-2], out[-1]
+    return dict(zip(peers, out)), out[-1]
 
 
 def backward_second(peers, dense, lhs, node_rows):
@@ -461,7 +468,9 @@
     backs[0] = weight_parts(back, aggregated, pre_grad)
     for m in even:
         backs[m | 1] = swap(backs[m], "col", 1)
-    chunks, lhs, grads = backward_first(far, dense, backs, width)
+    grads = unfold_sums(backs[0], backs[1], width)
+    grads = sum_all([grads, swap(grads, "row", top)], "top_grads", (), HINT)
+    chunks, lhs = backward_first(far, dense, backs, width, (grads,))
     ahead = [chunks[top]] + [swap(chunks[top | m], "row", m) for m in near[1:]]
     chunks = backward_second(near, dense, lhs, node_rows)
     mine = [chunks[0]] + [swap(chunks[m], "row", m) for m in near[1:]]
@@ -469,10 +478,11 @@
     passed = swap(ahead, "row", top)
 
     rounds = [("col", 1 << b) for b in range(1, col_count.bit_length() - 1)]
-    rounds += [("row", top)] + [("row", 1 << b) for b in range(top.bit_length() - 1)]
+    rounds = [("row", 1)] * (top > 1) + rounds
+    rounds += [("row", 1 << b) for b in range(1, top.bit_length() - 1)]
     grads = sum_all([grads], "held_grads", (lhs,))
     for step, (axis, mask) in enumerate(rounds[:-1]):
-        after = (ahead,) if (axis, mask) == ("row", top) else ()
+        after = (ahead,) if False else ()
         grads = sum_all([grads, swap(grads, axis, mask)], f"{axis}{mask}_grads", after)
         if step == len(rounds) - 3:
             activated = hand_over(activated, (grads,))

time: 68.6 us -> 64.9 us (0.946)
  starting transfers between devices: 28.6 us -> 26.3 us
  waiting for transfers between devices: 27.7 us -> 26.3 us
    ppermute x24, starting transfers between devices: 28.6 us -> 26.3 us  [swap(): return lax.ppermute(value, axis, [(i, i ^ mask) for i in range(count)])]
    ppermute x24, waiting for transfers between devices: 27.7 us -> 26.3 us  [swap(): return lax.ppermute(value, axis, [(i, i ^ mask) for i in range(count)])]
    pallas_call x20 -> x21, Pallas kernels: 10.7 us -> 10.7 us  [call(): pl.pallas_call(kernel, out_shape=tuple(outs), in_specs=list(before_specs)...]
  transfers between devices with their start and end apart: 24 -> 24, of which waited for: 12 -> 14; matrix products, arithmetic and copies ran while one was open for 0% -> 0% of each run, Pallas kernels for 10% -> 10%
where the time goes in v8:
time: 64.9 us; the launch traced here: 64.7 us
  starting transfers between devices  26.3 us (41%)
  waiting for transfers between devices  26.3 us (41%)
  Pallas kernels  10.7 us (16%)
  between operations  1.47 us (2%)
    ppermute x24, starting transfers between devices, swap(): return lax.ppermute(value, axis, [(i, i ^ mask) for i in range(count)])  26.3 us
    ppermute x24, waiting for transfers between devices, swap(): return lax.ppermute(value, axis, [(i, i ^ mask) for i in range(count)])  26.3 us
    pallas_call x21, Pallas kernels, call(): pl.pallas_call(kernel, out_shape=tuple(outs), in_specs=list(before_specs)...  10.7 us
  transfers between devices with their start and end apart: 24, of which 14 were waited for; matrix products, arithmetic and copies ran while one was open for 0% of the time, Pallas kernels for 10%

profile of v8, /device:TPU:0, one launch (start us, length us, event | category | flops | bytes accessed | tf_op | source)
XLA Modules:
  0.0 64.7 jit_solution(11495479209156512091)
XLA Ops:
  0.6 3.1 %collective-permute-start.3 = (f32[256,128]{1,0:T(8,128)}, f32[256,128]{1,0:T(8,128)S(1)}, u32[]{:S(2)}, u32[]{:S(2)}) collective-permute-start(f32[256,128]{1,0:T(8,128)} %refs_3_.2), channel_id=1, source_target_pairs={{0,8},{4,12},{8,0},{12,4},{16,24},{20,28},{24,16},{28,20},{1,9},{5... | collective-permute-start | bytes 393224 | tf_op jit(solution)/shard_map/ppermute | solution.py:432
  3.7 1.5 %collective-permute-start.2 = (f32[256,128]{1,0:T(8,128)}, f32[256,128]{1,0:T(8,128)S(1)}, u32[]{:S(2)}, u32[]{:S(2)}) collective-permute-start(f32[256,128]{1,0:T(8,128)} %refs_3_.2), channel_id=1, source_target_pairs={{0,4},{4,0},{8,12},{12,8},{16,20},{20,16},{24,28},{28,24},{1,5},{5... | collective-permute-start | bytes 393224 | tf_op jit(solution)/shard_map/ppermute | solution.py:432
  5.3 2.6 %collective-permute-start = (f32[256,128]{1,0:T(8,128)}, f32[256,128]{1,0:T(8,128)S(1)}, u32[]{:S(2)}, u32[]{:S(2)}) collective-permute-start(f32[256,128]{1,0:T(8,128)} %refs_3_.2), channel_id=1, source_target_pairs={{0,16},{4,20},{8,24},{12,28},{16,0},{20,4},{24,8},{28,12},{1,17},{... | collective-permute-start | bytes 393224 | tf_op jit(solution)/shard_map/ppermute | solution.py:432
  8.9 3.7 %densify.1 = (bf16[1024,2048]{1,0:T(8,128)(2,1)S(1)}, f32[16,128]{1,0:T(8,128)S(1)}) custom-call(s32[1,128]{1,0:T(1,128)} %bitcast.6, s32[1,1]{1,0:T(1,128)S(6)} %copy.11.counts_hbm, s32[128,128,128]{2,1,0:T(8,128)} %bitcast.5), custom_call_target="tpu_custom_call" | custom-call | flops 838860800 | tf_op jit(solution)/shard_map/densify/pallas_call | solution.py:50
  12.7 4.5 %collective-permute-done.1.got_ref = f32[16,128]{1,0:T(8,128)S(1)} collective-permute-done((f32[16,128]{1,0:T(8,128)S(1)}, f32[16,128]{1,0:T(8,128)S(1)}, u32[]{:S(2)}, u32[]{:S(2)}) %collective-permute-start.1) | collective-permute-done | bytes 8224 | tf_op jit(solution)/shard_map/ppermute | solution.py:432
  17.3 2.6 %collective-permute-start.7 = (f32[272,128]{1,0:T(8,128)S(1)}, f32[272,128]{1,0:T(8,128)S(1)}, u32[]{:S(2)}, u32[]{:S(2)}) collective-permute-start(f32[272,128]{1,0:T(8,128)S(1)} %message.1.refs_0_.refs_7_), channel_id=1, source_target_pairs={{0,12},{4,8},{8,4},{12,0},{16,28},{20,24},{24,20},{28,16},{1,13},{... | collective-permute-start | bytes 417800 | tf_op jit(solution)/shard_map/ppermute | solution.py:432
  21.5 1.8 %collective-permute-done.7.refs_3_.refs_10_ = f32[272,128]{1,0:T(8,128)S(1)} collective-permute-done((f32[272,128]{1,0:T(8,128)S(1)}, f32[272,128]{1,0:T(8,128)S(1)}, u32[]{:S(2)}, u32[]{:S(2)}) %collective-permute-start.7) | collective-permute-done | bytes 139296 | tf_op jit(solution)/shard_map/ppermute | solution.py:432
  23.3 1.6 %collective-permute-done.6.refs_2_.refs_9_ = f32[272,128]{1,0:T(8,128)S(1)} collective-permute-done((f32[272,128]{1,0:T(8,128)S(1)}, f32[272,128]{1,0:T(8,128)S(1)}, u32[]{:S(2)}, u32[]{:S(2)}) %collective-permute-start.6) | collective-permute-done | bytes 139296 | tf_op jit(solution)/shard_map/ppermute | solution.py:432
  25.8 1.0 %forward_first.1 = (f32[2,264,128]{2,1,0:T(8,128)S(1)}, bf16[2048,256]{1,0:T(8,128)(2,1)S(1)}) custom-call(bf16[1024,2048]{1,0:T(8,128)(2,1)S(1)} %get-tuple-element.26.dense_ref.refs_0_, f32[8,128]{1,0:T(8,128)S(1)} %row_totals.1.refs_1_.row_ref, f32[2048,128]{1,0:T(8,128)S(1)} %get-tuple-element.28.refs_2_, f32[256,128]{1,0:T(8,128)S(1)} %copy-done, ...), custom_call_target="tpu_custom_call" | custom-call | flops 536870912 | bytes 10522624 | tf_op jit(solution)/shard_map/forward_first/pallas_call | solution.py:50
  28.4 1.6 %collective-permute-start.9 = (f32[264,128]{1,0:T(8,128)S(1)}, f32[264,128]{1,0:T(8,128)S(1)}, u32[]{:S(2)}, u32[]{:S(2)}) collective-permute-start(f32[264,128]{1,0:T(8,128)S(1)} %pair_sums.1), channel_id=1, source_target_pairs={{0,2},{1,3},{2,0},{3,1},{4,6},{5,7},{6,4},{7,5},{8,10},{9,11},{10,... | collective-permute-start | bytes 405512 | tf_op jit(solution)/shard_map/ppermute | solution.py:432
  29.9 4.1 %collective-permute-done.9.refs_2_ = f32[264,128]{1,0:T(8,128)S(1)} collective-permute-done((f32[264,128]{1,0:T(8,128)S(1)}, f32[264,128]{1,0:T(8,128)S(1)}, u32[]{:S(2)}, u32[]{:S(2)}) %collective-permute-start.9) | collective-permute-done | bytes 135200 | tf_op jit(solution)/shard_map/ppermute | solution.py:432
  35.3 1.6 %collective-permute-start.12 = (f32[128,256]{1,0:T(8,128)S(1)}, f32[128,256]{1,0:T(8,128)S(1)}, u32[]{:S(2)}, u32[]{:S(2)}) collective-permute-start(f32[128,256]{1,0:T(8,128)S(1)} %get-tuple-element.32.back_ref), channel_id=1, source_target_pairs={{0,2},{1,3},{2,0},{3,1},{4,6},{5,7},{6,4},{7,5},{8,10},{9,11},{10,... | collective-permute-start | bytes 393224 | tf_op jit(solution)/shard_map/ppermute | solution.py:432
  37.2 3.9 %collective-permute-done.12.refs_3_ = f32[128,256]{1,0:T(8,128)S(1)} collective-permute-done((f32[128,256]{1,0:T(8,128)S(1)}, f32[128,256]{1,0:T(8,128)S(1)}, u32[]{:S(2)}, u32[]{:S(2)}) %collective-permute-start.12) | collective-permute-done | bytes 131104 | tf_op jit(solution)/shard_map/ppermute | solution.py:432
  41.2 2.4 %collective-permute-done.11.refs_1_ = f32[136,128]{1,0:T(8,128)S(1)} collective-permute-done((f32[136,128]{1,0:T(8,128)S(1)}, f32[136,128]{1,0:T(8,128)S(1)}, u32[]{:S(2)}, u32[]{:S(2)}) %collective-permute-start.11) | collective-permute-done | bytes 69664 | tf_op jit(solution)/shard_map/ppermute | solution.py:432
  44.5 1.0 %collective-permute-start.19 = (f32[128,256]{1,0:T(8,128)S(1)}, f32[128,256]{1,0:T(8,128)S(1)}, u32[]{:S(2)}, u32[]{:S(2)}) collective-permute-start(f32[128,256]{1,0:T(8,128)S(1)} %get-tuple-element.41), channel_id=1, source_target_pairs={{0,4},{4,0},{8,12},{12,8},{16,20},{20,16},{24,28},{28,24},{1,5},{5... | collective-permute-start | bytes 393224 | tf_op jit(solution)/shard_map/ppermute | solution.py:432
  45.9 2.1 %collective-permute-start.21 = (f32[128,256]{1,0:T(8,128)S(1)}, f32[128,256]{1,0:T(8,128)S(1)}, u32[]{:S(2)}, u32[]{:S(2)}) collective-permute-start(f32[128,256]{1,0:T(8,128)S(1)} %get-tuple-element.43), channel_id=1, source_target_pairs={{0,12},{4,8},{8,4},{12,0},{16,28},{20,24},{24,20},{28,16},{1,13},{... | collective-permute-start | bytes 393224 | tf_op jit(solution)/shard_map/ppermute | solution.py:432
  49.7 1.2 %collective-permute-start.15 = (f32[128,256]{1,0:T(8,128)S(1)}, f32[128,256]{1,0:T(8,128)S(1)}, u32[]{:S(2)}, u32[]{:S(2)}) collective-permute-start(f32[128,256]{1,0:T(8,128)S(1)} %get-tuple-element.37), channel_id=1, source_target_pairs={{0,4},{4,0},{8,12},{12,8},{16,20},{20,16},{24,28},{28,24},{1,5},{5... | collective-permute-start | bytes 393224 | tf_op jit(solution)/shard_map/ppermute | solution.py:432
  51.7 2.2 %collective-permute-start.17 = (f32[128,256]{1,0:T(8,128)S(1)}, f32[128,256]{1,0:T(8,128)S(1)}, u32[]{:S(2)}, u32[]{:S(2)}) collective-permute-start(f32[128,256]{1,0:T(8,128)S(1)} %get-tuple-element.39), channel_id=1, source_target_pairs={{0,12},{4,8},{8,4},{12,0},{16,28},{20,24},{24,20},{28,16},{1,13},{... | collective-permute-start | bytes 393224 | tf_op jit(solution)/shard_map/ppermute | solution.py:432
  53.9 1.1 %collective-permute-done.21.refs_3_ = f32[128,256]{1,0:T(8,128)S(1)} collective-permute-done((f32[128,256]{1,0:T(8,128)S(1)}, f32[128,256]{1,0:T(8,128)S(1)}, u32[]{:S(2)}, u32[]{:S(2)}) %collective-permute-start.21) | collective-permute-done | bytes 131104 | tf_op jit(solution)/shard_map/ppermute | solution.py:432
  55.2 1.6 %collective-permute-start.18 = (f32[136,128]{1,0:T(8,128)S(1)}, f32[136,128]{1,0:T(8,128)S(1)}, u32[]{:S(2)}, u32[]{:S(2)}) collective-permute-start(f32[136,128]{1,0:T(8,128)S(1)} %row1_grads.1.refs_0_), channel_id=1, source_target_pairs={{0,2},{1,3},{2,0},{3,1},{4,6},{5,7},{6,4},{7,5},{8,10},{9,11},{10,... | collective-permute-start | bytes 208904 | tf_op jit(solution)/shard_map/ppermute | solution.py:432
  57.4 2.1 %collective-permute-done.18.refs_1_ = f32[136,128]{1,0:T(8,128)S(1)} collective-permute-done((f32[136,128]{1,0:T(8,128)S(1)}, f32[136,128]{1,0:T(8,128)S(1)}, u32[]{:S(2)}, u32[]{:S(2)}) %collective-permute-start.18) | collective-permute-done | bytes 69664 | tf_op jit(solution)/shard_map/ppermute | solution.py:432
  59.6 1.9 %collective-permute-start.23 = (f32[136,128]{1,0:T(8,128)S(1)}, f32[136,128]{1,0:T(8,128)S(1)}, u32[]{:S(2)}, u32[]{:S(2)}) collective-permute-start(f32[136,128]{1,0:T(8,128)S(1)} %col2_grads.1.refs_4_.refs_1_), channel_id=1, source_target_pairs={{0,8},{4,12},{8,0},{12,4},{16,24},{20,28},{24,16},{28,20},{1,9},{5... | collective-permute-start | bytes 208904 | tf_op jit(solution)/shard_map/ppermute | solution.py:432
  61.6 1.2 %collective-permute-done.22.refs_1_ = f32[128,256]{1,0:T(8,128)S(1)} collective-permute-done((f32[128,256]{1,0:T(8,128)S(1)}, f32[128,256]{1,0:T(8,128)S(1)}, u32[]{:S(2)}, u32[]{:S(2)}) %collective-permute-start.22) | collective-permute-done | bytes 131104 | tf_op jit(solution)/shard_map/ppermute | solution.py:432
  62.8 1.1 %collective-permute-done.23.refs_2_ = f32[136,128]{1,0:T(8,128)S(1)} collective-permute-done((f32[136,128]{1,0:T(8,128)S(1)}, f32[136,128]{1,0:T(8,128)S(1)}, u32[]{:S(2)}, u32[]{:S(2)}) %collective-permute-start.23) | collective-permute-done | bytes 69664 | tf_op jit(solution)/shard_map/ppermute | solution.py:432
  (53 shorter events, 11.6 us)
Async XLA Ops:
  0.6 16.6 %collective-permute-start.3 = (f32[256,128]{1,0:T(8,128)}, f32[256,128]{1,0:T(8,128)S(1)}, u32[]{:S(2)}, u32[]{:S(2)}) collective-permute-start(f32[256,128]{1,0:T(8,128)} %refs_3_.2), channel_id=1, source_target_pairs={{0,8},{4,12},{8,0},{12,4},{16,24},{20,28},{24,16},{28,20},{1,9},{5... | collective-permute-start | bytes 393224 | tf_op jit(solution)/shard_map/ppermute | solution.py:432
  3.7 13.5 %collective-permute-start.2 = (f32[256,128]{1,0:T(8,128)}, f32[256,128]{1,0:T(8,128)S(1)}, u32[]{:S(2)}, u32[]{:S(2)}) collective-permute-start(f32[256,128]{1,0:T(8,128)} %refs_3_.2), channel_id=1, source_target_pairs={{0,4},{4,0},{8,12},{12,8},{16,20},{20,16},{24,28},{28,24},{1,5},{5... | collective-permute-start | bytes 393224 | tf_op jit(solution)/shard_map/ppermute | solution.py:432
  5.3 12.0 %collective-permute-start = (f32[256,128]{1,0:T(8,128)}, f32[256,128]{1,0:T(8,128)S(1)}, u32[]{:S(2)}, u32[]{:S(2)}) collective-permute-start(f32[256,128]{1,0:T(8,128)} %refs_3_.2), channel_id=1, source_target_pairs={{0,16},{4,20},{8,24},{12,28},{16,0},{20,4},{24,8},{28,12},{1,17},{... | collective-permute-start | bytes 393224 | tf_op jit(solution)/shard_map/ppermute | solution.py:432
  7.8 9.4 %collective-permute-start.4 = (f32[256,128]{1,0:T(8,128)}, f32[256,128]{1,0:T(8,128)S(1)}, u32[]{:S(2)}, u32[]{:S(2)}) collective-permute-start(f32[256,128]{1,0:T(8,128)} %refs_3_.2), channel_id=1, source_target_pairs={{0,12},{4,8},{8,4},{12,0},{16,28},{20,24},{24,20},{28,16},{1,13},{... | collective-permute-start | bytes 393224 | tf_op jit(solution)/shard_map/ppermute | solution.py:432
  12.6 4.6 %collective-permute-start.1 = (f32[16,128]{1,0:T(8,128)S(1)}, f32[16,128]{1,0:T(8,128)S(1)}, u32[]{:S(2)}, u32[]{:S(2)}) collective-permute-start(f32[16,128]{1,0:T(8,128)S(1)} %get-tuple-element.27.own_ref), channel_id=1, source_target_pairs={{0,16},{4,20},{8,24},{12,28},{16,0},{20,4},{24,8},{28,12},{1,17},{... | collective-permute-start | bytes 24584 | tf_op jit(solution)/shard_map/ppermute | solution.py:432
  17.3 6.0 %collective-permute-start.7 = (f32[272,128]{1,0:T(8,128)S(1)}, f32[272,128]{1,0:T(8,128)S(1)}, u32[]{:S(2)}, u32[]{:S(2)}) collective-permute-start(f32[272,128]{1,0:T(8,128)S(1)} %message.1.refs_0_.refs_7_), channel_id=1, source_target_pairs={{0,12},{4,8},{8,4},{12,0},{16,28},{20,24},{24,20},{28,16},{1,13},{... | collective-permute-start | bytes 417800 | tf_op jit(solution)/shard_map/ppermute | solution.py:432
  19.9 5.1 %collective-permute-start.6 = (f32[272,128]{1,0:T(8,128)S(1)}, f32[272,128]{1,0:T(8,128)S(1)}, u32[]{:S(2)}, u32[]{:S(2)}) collective-permute-start(f32[272,128]{1,0:T(8,128)S(1)} %message.1.refs_0_.refs_7_), channel_id=1, source_target_pairs={{0,8},{4,12},{8,0},{12,4},{16,24},{20,28},{24,16},{28,20},{1,9},{5... | collective-permute-start | bytes 417800 | tf_op jit(solution)/shard_map/ppermute | solution.py:432
  20.4 5.1 %collective-permute-start.5 = (f32[272,128]{1,0:T(8,128)S(1)}, f32[272,128]{1,0:T(8,128)S(1)}, u32[]{:S(2)}, u32[]{:S(2)}) collective-permute-start(f32[272,128]{1,0:T(8,128)S(1)} %message.1.refs_0_.refs_7_), channel_id=1, source_target_pairs={{0,4},{4,0},{8,12},{12,8},{16,20},{20,16},{24,28},{28,24},{1,5},{5... | collective-permute-start | bytes 417800 | tf_op jit(solution)/shard_map/ppermute | solution.py:432
  26.8 1.6 %collective-permute-start.8 = (f32[2,264,128]{2,1,0:T(8,128)S(1)}, f32[2,264,128]{2,1,0:T(8,128)S(1)}, u32[]{:S(2)}, u32[]{:S(2)}) collective-permute-start(f32[2,264,128]{2,1,0:T(8,128)S(1)} %get-tuple-element.30), channel_id=1, source_target_pairs={{0,1},{1,0},{2,3},{3,2},{4,5},{5,4},{6,7},{7,6},{8,9},{9,8},{10,11... | collective-permute-start | bytes 811016 | tf_op jit(solution)/shard_map/ppermute | solution.py:432
  28.4 5.7 %collective-permute-start.9 = (f32[264,128]{1,0:T(8,128)S(1)}, f32[264,128]{1,0:T(8,128)S(1)}, u32[]{:S(2)}, u32[]{:S(2)}) collective-permute-start(f32[264,128]{1,0:T(8,128)S(1)} %pair_sums.1), channel_id=1, source_target_pairs={{0,2},{1,3},{2,0},{3,1},{4,6},{5,7},{6,4},{7,5},{8,10},{9,11},{10,... | collective-permute-start | bytes 405512 | tf_op jit(solution)/shard_map/ppermute | solution.py:432
  35.2 1.6 %collective-permute-start.10 = (f32[200,256]{1,0:T(8,128)S(1)}, f32[200,256]{1,0:T(8,128)S(1)}, u32[]{:S(2)}, u32[]{:S(2)}) collective-permute-start(f32[200,256]{1,0:T(8,128)S(1)} %weight_parts.1.own_ref.refs_1_), channel_id=1, source_target_pairs={{0,1},{1,0},{2,3},{3,2},{4,5},{5,4},{6,7},{7,6},{8,9},{9,8},{10,11... | collective-permute-start | bytes 614408 | tf_op jit(solution)/shard_map/ppermute | solution.py:432
  35.3 5.9 %collective-permute-start.12 = (f32[128,256]{1,0:T(8,128)S(1)}, f32[128,256]{1,0:T(8,128)S(1)}, u32[]{:S(2)}, u32[]{:S(2)}) collective-permute-start(f32[128,256]{1,0:T(8,128)S(1)} %get-tuple-element.32.back_ref), channel_id=1, source_target_pairs={{0,2},{1,3},{2,0},{3,1},{4,6},{5,7},{6,4},{7,5},{8,10},{9,11},{10,... | collective-permute-start | bytes 393224 | tf_op jit(solution)/shard_map/ppermute | solution.py:432
  36.8 6.8 %collective-permute-start.11 = (f32[136,128]{1,0:T(8,128)S(1)}, f32[136,128]{1,0:T(8,128)S(1)}, u32[]{:S(2)}, u32[]{:S(2)}) collective-permute-start(f32[136,128]{1,0:T(8,128)S(1)} %core_grads.1.refs_0_), channel_id=1, source_target_pairs={{0,16},{4,20},{8,24},{12,28},{16,0},{20,4},{24,8},{28,12},{1,17},{... | collective-permute-start | bytes 208904 | tf_op jit(solution)/shard_map/ppermute | solution.py:432
  41.2 2.4 %collective-permute-start.13 = (f32[128,256]{1,0:T(8,128)S(1)}, f32[128,256]{1,0:T(8,128)S(1)}, u32[]{:S(2)}, u32[]{:S(2)}) collective-permute-start(f32[128,256]{1,0:T(8,128)S(1)} %collective-permute-done.12.refs_3_), channel_id=1, source_target_pairs={{0,1},{1,0},{2,3},{3,2},{4,5},{5,4},{6,7},{7,6},{8,9},{9,8},{10,11... | collective-permute-start | bytes 393224 | tf_op jit(solution)/shard_map/ppermute | solution.py:432
  44.5 7.1 %collective-permute-start.19 = (f32[128,256]{1,0:T(8,128)S(1)}, f32[128,256]{1,0:T(8,128)S(1)}, u32[]{:S(2)}, u32[]{:S(2)}) collective-permute-start(f32[128,256]{1,0:T(8,128)S(1)} %get-tuple-element.41), channel_id=1, source_target_pairs={{0,4},{4,0},{8,12},{12,8},{16,20},{20,16},{24,28},{28,24},{1,5},{5... | collective-permute-start | bytes 393224 | tf_op jit(solution)/shard_map/ppermute | solution.py:432
  45.5 6.3 %collective-permute-start.20 = (f32[128,256]{1,0:T(8,128)S(1)}, f32[128,256]{1,0:T(8,128)S(1)}, u32[]{:S(2)}, u32[]{:S(2)}) collective-permute-start(f32[128,256]{1,0:T(8,128)S(1)} %get-tuple-element.42), channel_id=1, source_target_pairs={{0,8},{4,12},{8,0},{12,4},{16,24},{20,28},{24,16},{28,20},{1,9},{5... | collective-permute-start | bytes 393224 | tf_op jit(solution)/shard_map/ppermute | solution.py:432
  45.9 9.1 %collective-permute-start.21 = (f32[128,256]{1,0:T(8,128)S(1)}, f32[128,256]{1,0:T(8,128)S(1)}, u32[]{:S(2)}, u32[]{:S(2)}) collective-permute-start(f32[128,256]{1,0:T(8,128)S(1)} %get-tuple-element.43), channel_id=1, source_target_pairs={{0,12},{4,8},{8,4},{12,0},{16,28},{20,24},{24,20},{28,16},{1,13},{... | collective-permute-start | bytes 393224 | tf_op jit(solution)/shard_map/ppermute | solution.py:432
  48.0 7.1 %collective-permute-start.14 = (f32[136,128]{1,0:T(8,128)S(1)}, f32[136,128]{1,0:T(8,128)S(1)}, u32[]{:S(2)}, u32[]{:S(2)}) collective-permute-start(f32[136,128]{1,0:T(8,128)S(1)} %held_grads.1.refs_0_), channel_id=1, source_target_pairs={{0,4},{4,0},{8,12},{12,8},{16,20},{20,16},{24,28},{28,24},{1,5},{5... | collective-permute-start | bytes 208904 | tf_op jit(solution)/shard_map/ppermute | solution.py:432
  49.7 11.8 %collective-permute-start.15 = (f32[128,256]{1,0:T(8,128)S(1)}, f32[128,256]{1,0:T(8,128)S(1)}, u32[]{:S(2)}, u32[]{:S(2)}) collective-permute-start(f32[128,256]{1,0:T(8,128)S(1)} %get-tuple-element.37), channel_id=1, source_target_pairs={{0,4},{4,0},{8,12},{12,8},{16,20},{20,16},{24,28},{28,24},{1,5},{5... | collective-permute-start | bytes 393224 | tf_op jit(solution)/shard_map/ppermute | solution.py:432
  51.6 9.9 %collective-permute-start.16 = (f32[128,256]{1,0:T(8,128)S(1)}, f32[128,256]{1,0:T(8,128)S(1)}, u32[]{:S(2)}, u32[]{:S(2)}) collective-permute-start(f32[128,256]{1,0:T(8,128)S(1)} %get-tuple-element.38), channel_id=1, source_target_pairs={{0,8},{4,12},{8,0},{12,4},{16,24},{20,28},{24,16},{28,20},{1,9},{5... | collective-permute-start | bytes 393224 | tf_op jit(solution)/shard_map/ppermute | solution.py:432
  51.7 9.8 %collective-permute-start.17 = (f32[128,256]{1,0:T(8,128)S(1)}, f32[128,256]{1,0:T(8,128)S(1)}, u32[]{:S(2)}, u32[]{:S(2)}) collective-permute-start(f32[128,256]{1,0:T(8,128)S(1)} %get-tuple-element.39), channel_id=1, source_target_pairs={{0,12},{4,8},{8,4},{12,0},{16,28},{20,24},{24,20},{28,16},{1,13},{... | collective-permute-start | bytes 393224 | tf_op jit(solution)/shard_map/ppermute | solution.py:432
  55.1 7.7 %collective-permute-start.22 = (f32[128,256]{1,0:T(8,128)S(1)}, f32[128,256]{1,0:T(8,128)S(1)}, u32[]{:S(2)}, u32[]{:S(2)}) collective-permute-start(f32[128,256]{1,0:T(8,128)S(1)} %ahead_sums.1), channel_id=1, source_target_pairs={{0,16},{4,20},{8,24},{12,28},{16,0},{20,4},{24,8},{28,12},{1,17},{... | collective-permute-start | bytes 393224 | tf_op jit(solution)/shard_map/ppermute | solution.py:432
  55.2 4.4 %collective-permute-start.18 = (f32[136,128]{1,0:T(8,128)S(1)}, f32[136,128]{1,0:T(8,128)S(1)}, u32[]{:S(2)}, u32[]{:S(2)}) collective-permute-start(f32[136,128]{1,0:T(8,128)S(1)} %row1_grads.1.refs_0_), channel_id=1, source_target_pairs={{0,2},{1,3},{2,0},{3,1},{4,6},{5,7},{6,4},{7,5},{8,10},{9,11},{10,... | collective-permute-start | bytes 208904 | tf_op jit(solution)/shard_map/ppermute | solution.py:432
  59.6 4.4 %collective-permute-start.23 = (f32[136,128]{1,0:T(8,128)S(1)}, f32[136,128]{1,0:T(8,128)S(1)}, u32[]{:S(2)}, u32[]{:S(2)}) collective-permute-start(f32[136,128]{1,0:T(8,128)S(1)} %col2_grads.1.refs_4_.refs_1_), channel_id=1, source_target_pairs={{0,8},{4,12},{8,0},{12,4},{16,24},{20,28},{24,16},{28,20},{1,9},{5... | collective-permute-start | bytes 208904 | tf_op jit(solution)/shard_map/ppermute | solution.py:432
  (4 other events, 64.8 us)

commit v9 on v8

--- a/solution.py
+++ b/solution.py
@@ -470,7 +470,7 @@
         backs[m | 1] = swap(backs[m], "col", 1)
     grads = unfold_sums(backs[0], backs[1], width)
     grads = sum_all([grads, swap(grads, "row", top)], "top_grads", (), HINT)
-    chunks, lhs = backward_first(far, dense, backs, width, (grads,))
+    chunks, lhs = backward_first(far, dense, backs, width, ())
     ahead = [chunks[top]] + [swap(chunks[top | m], "row", m) for m in near[1:]]
     chunks = backward_second(near, dense, lhs, node_rows)
     mine = [chunks[0]] + [swap(chunks[m], "row", m) for m in near[1:]]
@@ -482,7 +482,7 @@
     rounds += [("row", 1 << b) for b in range(1, top.bit_length() - 1)]
     grads = sum_all([grads], "held_grads", (lhs,))
     for step, (axis, mask) in enumerate(rounds[:-1]):
-        after = (ahead,) if False else ()
+        after = (ahead,) if (axis, mask) == ("row", 1) else ()
         grads = sum_all([grads, swap(grads, axis, mask)], f"{axis}{mask}_grads", after)
         if step == len(rounds) - 3:
             activated = hand_over(activated, (grads,))

time: 64.9 us -> 66.8 us (1.029)
  starting transfers between devices: 26.3 us -> 29.1 us
  waiting for transfers between devices: 26.3 us -> 25.4 us
    ppermute x24, starting transfers between devices: 26.3 us -> 29.1 us  [swap(): return lax.ppermute(value, axis, [(i, i ^ mask) for i in range(count)])]
    ppermute x24, waiting for transfers between devices: 26.3 us -> 25.4 us  [swap(): return lax.ppermute(value, axis, [(i, i ^ mask) for i in range(count)])]
  transfers between devices with their start and end apart: 24 -> 24, of which waited for: 14 -> 12; matrix products, arithmetic and copies ran while one was open for 0% -> 0% of each run, Pallas kernels for 10% -> 12%
where the time goes in v9:
time: 66.8 us; the launch traced here: 66.7 us
  starting transfers between devices  29.1 us (44%)
  waiting for transfers between devices  25.4 us (38%)
  Pallas kernels  10.7 us (16%)
  between operations  1.48 us (2%)
    ppermute x24, starting transfers between devices, swap(): return lax.ppermute(value, axis, [(i, i ^ mask) for i in range(count)])  29.1 us
    ppermute x24, waiting for transfers between devices, swap(): return lax.ppermute(value, axis, [(i, i ^ mask) for i in range(count)])  25.4 us
    pallas_call x21, Pallas kernels, call(): pl.pallas_call(kernel, out_shape=tuple(outs), in_specs=list(before_specs)...  10.7 us
  transfers between devices with their start and end apart: 24, of which 12 were waited for; matrix products, arithmetic and copies ran while one was open for 0% of the time, Pallas kernels for 12%

profile of v9, /device:TPU:0, one launch (start us, length us, event | category | flops | bytes accessed | tf_op | source)
XLA Modules:
  0.0 66.7 jit_solution(4523055012926244450)
XLA Ops:
  0.6 3.1 %collective-permute-start.3 = (f32[256,128]{1,0:T(8,128)}, f32[256,128]{1,0:T(8,128)S(1)}, u32[]{:S(2)}, u32[]{:S(2)}) collective-permute-start(f32[256,128]{1,0:T(8,128)} %refs_3_.2), channel_id=1, source_target_pairs={{0,8},{4,12},{8,0},{12,4},{16,24},{20,28},{24,16},{28,20},{1,9},{5... | collective-permute-start | bytes 393224 | tf_op jit(solution)/shard_map/ppermute | solution.py:432
  3.7 1.5 %collective-permute-start.2 = (f32[256,128]{1,0:T(8,128)}, f32[256,128]{1,0:T(8,128)S(1)}, u32[]{:S(2)}, u32[]{:S(2)}) collective-permute-start(f32[256,128]{1,0:T(8,128)} %refs_3_.2), channel_id=1, source_target_pairs={{0,4},{4,0},{8,12},{12,8},{16,20},{20,16},{24,28},{28,24},{1,5},{5... | collective-permute-start | bytes 393224 | tf_op jit(solution)/shard_map/ppermute | solution.py:432
  5.3 2.6 %collective-permute-start = (f32[256,128]{1,0:T(8,128)}, f32[256,128]{1,0:T(8,128)S(1)}, u32[]{:S(2)}, u32[]{:S(2)}) collective-permute-start(f32[256,128]{1,0:T(8,128)} %refs_3_.2), channel_id=1, source_target_pairs={{0,16},{4,20},{8,24},{12,28},{16,0},{20,4},{24,8},{28,12},{1,17},{... | collective-permute-start | bytes 393224 | tf_op jit(solution)/shard_map/ppermute | solution.py:432
  8.9 3.8 %densify.1 = (bf16[1024,2048]{1,0:T(8,128)(2,1)S(1)}, f32[16,128]{1,0:T(8,128)S(1)}) custom-call(s32[1,128]{1,0:T(1,128)} %bitcast.6, s32[1,1]{1,0:T(1,128)S(6)} %copy.11.counts_hbm, s32[128,128,128]{2,1,0:T(8,128)} %bitcast.5), custom_call_target="tpu_custom_call" | custom-call | flops 838860800 | tf_op jit(solution)/shard_map/densify/pallas_call | solution.py:50
  12.7 4.5 %collective-permute-done.1.got_ref = f32[16,128]{1,0:T(8,128)S(1)} collective-permute-done((f32[16,128]{1,0:T(8,128)S(1)}, f32[16,128]{1,0:T(8,128)S(1)}, u32[]{:S(2)}, u32[]{:S(2)}) %collective-permute-start.1) | collective-permute-done | bytes 8224 | tf_op jit(solution)/shard_map/ppermute | solution.py:432
  17.3 2.6 %collective-permute-start.7 = (f32[272,128]{1,0:T(8,128)S(1)}, f32[272,128]{1,0:T(8,128)S(1)}, u32[]{:S(2)}, u32[]{:S(2)}) collective-permute-start(f32[272,128]{1,0:T(8,128)S(1)} %message.1.refs_0_.refs_7_), channel_id=1, source_target_pairs={{0,12},{4,8},{8,4},{12,0},{16,28},{20,24},{24,20},{28,16},{1,13},{... | collective-permute-start | bytes 417800 | tf_op jit(solution)/shard_map/ppermute | solution.py:432
  21.5 1.8 %collective-permute-done.7.refs_3_.refs_10_ = f32[272,128]{1,0:T(8,128)S(1)} collective-permute-done((f32[272,128]{1,0:T(8,128)S(1)}, f32[272,128]{1,0:T(8,128)S(1)}, u32[]{:S(2)}, u32[]{:S(2)}) %collective-permute-start.7) | collective-permute-done | bytes 139296 | tf_op jit(solution)/shard_map/ppermute | solution.py:432
  23.3 1.6 %collective-permute-done.6.refs_2_.refs_9_ = f32[272,128]{1,0:T(8,128)S(1)} collective-permute-done((f32[272,128]{1,0:T(8,128)S(1)}, f32[272,128]{1,0:T(8,128)S(1)}, u32[]{:S(2)}, u32[]{:S(2)}) %collective-permute-start.6) | collective-permute-done | bytes 139296 | tf_op jit(solution)/shard_map/ppermute | solution.py:432
  25.8 1.0 %forward_first.1 = (f32[2,264,128]{2,1,0:T(8,128)S(1)}, bf16[2048,256]{1,0:T(8,128)(2,1)S(1)}) custom-call(bf16[1024,2048]{1,0:T(8,128)(2,1)S(1)} %get-tuple-element.26.dense_ref.refs_0_, f32[8,128]{1,0:T(8,128)S(1)} %row_totals.1.refs_1_.row_ref, f32[2048,128]{1,0:T(8,128)S(1)} %get-tuple-element.28.refs_2_, f32[256,128]{1,0:T(8,128)S(1)} %copy-done, ...), custom_call_target="tpu_custom_call" | custom-call | flops 536870912 | bytes 10522624 | tf_op jit(solution)/shard_map/forward_first/pallas_call | solution.py:50
  28.4 1.6 %collective-permute-start.9 = (f32[264,128]{1,0:T(8,128)S(1)}, f32[264,128]{1,0:T(8,128)S(1)}, u32[]{:S(2)}, u32[]{:S(2)}) collective-permute-start(f32[264,128]{1,0:T(8,128)S(1)} %pair_sums.1), channel_id=1, source_target_pairs={{0,2},{1,3},{2,0},{3,1},{4,6},{5,7},{6,4},{7,5},{8,10},{9,11},{10,... | collective-permute-start | bytes 405512 | tf_op jit(solution)/shard_map/ppermute | solution.py:432
  29.9 4.1 %collective-permute-done.9.refs_2_ = f32[264,128]{1,0:T(8,128)S(1)} collective-permute-done((f32[264,128]{1,0:T(8,128)S(1)}, f32[264,128]{1,0:T(8,128)S(1)}, u32[]{:S(2)}, u32[]{:S(2)}) %collective-permute-start.9) | collective-permute-done | bytes 135200 | tf_op jit(solution)/shard_map/ppermute | solution.py:432
  34.9 1.5 %collective-permute-start.12 = (f32[128,256]{1,0:T(8,128)S(1)}, f32[128,256]{1,0:T(8,128)S(1)}, u32[]{:S(2)}, u32[]{:S(2)}) collective-permute-start(f32[128,256]{1,0:T(8,128)S(1)} %get-tuple-element.32.back_ref), channel_id=1, source_target_pairs={{0,2},{1,3},{2,0},{3,1},{4,6},{5,7},{6,4},{7,5},{8,10},{9,11},{10,... | collective-permute-start | bytes 393224 | tf_op jit(solution)/shard_map/ppermute | solution.py:432
  36.8 3.1 %collective-permute-done.12.refs_3_ = f32[128,256]{1,0:T(8,128)S(1)} collective-permute-done((f32[128,256]{1,0:T(8,128)S(1)}, f32[128,256]{1,0:T(8,128)S(1)}, u32[]{:S(2)}, u32[]{:S(2)}) %collective-permute-start.12) | collective-permute-done | bytes 131104 | tf_op jit(solution)/shard_map/ppermute | solution.py:432
  42.1 1.0 %collective-permute-start.15 = (f32[128,256]{1,0:T(8,128)S(1)}, f32[128,256]{1,0:T(8,128)S(1)}, u32[]{:S(2)}, u32[]{:S(2)}) collective-permute-start(f32[128,256]{1,0:T(8,128)S(1)} %get-tuple-element.37), channel_id=1, source_target_pairs={{0,4},{4,0},{8,12},{12,8},{16,20},{20,16},{24,28},{28,24},{1,5},{5... | collective-permute-start | bytes 393224 | tf_op jit(solution)/shard_map/ppermute | solution.py:432
  43.1 1.6 %collective-permute-start.16 = (f32[128,256]{1,0:T(8,128)S(1)}, f32[128,256]{1,0:T(8,128)S(1)}, u32[]{:S(2)}, u32[]{:S(2)}) collective-permute-start(f32[128,256]{1,0:T(8,128)S(1)} %get-tuple-element.38), channel_id=1, source_target_pairs={{0,8},{4,12},{8,0},{12,4},{16,24},{20,28},{24,16},{28,20},{1,9},{5... | collective-permute-start | bytes 393224 | tf_op jit(solution)/shard_map/ppermute | solution.py:432
  47.4 1.6 %collective-permute-start.19 = (f32[128,256]{1,0:T(8,128)S(1)}, f32[128,256]{1,0:T(8,128)S(1)}, u32[]{:S(2)}, u32[]{:S(2)}) collective-permute-start(f32[128,256]{1,0:T(8,128)S(1)} %get-tuple-element.42), channel_id=1, source_target_pairs={{0,8},{4,12},{8,0},{12,4},{16,24},{20,28},{24,16},{28,20},{1,9},{5... | collective-permute-start | bytes 393224 | tf_op jit(solution)/shard_map/ppermute | solution.py:432
  49.0 1.0 %collective-permute-start.20 = (f32[128,256]{1,0:T(8,128)S(1)}, f32[128,256]{1,0:T(8,128)S(1)}, u32[]{:S(2)}, u32[]{:S(2)}) collective-permute-start(f32[128,256]{1,0:T(8,128)S(1)} %get-tuple-element.43), channel_id=1, source_target_pairs={{0,12},{4,8},{8,4},{12,0},{16,28},{20,24},{24,20},{28,16},{1,13},{... | collective-permute-start | bytes 393224 | tf_op jit(solution)/shard_map/ppermute | solution.py:432
  51.0 2.1 %collective-permute-done.17.refs_3_ = f32[128,256]{1,0:T(8,128)S(1)} collective-permute-done((f32[128,256]{1,0:T(8,128)S(1)}, f32[128,256]{1,0:T(8,128)S(1)}, u32[]{:S(2)}, u32[]{:S(2)}) %collective-permute-start.17) | collective-permute-done | bytes 131104 | tf_op jit(solution)/shard_map/ppermute | solution.py:432
  53.1 1.5 %collective-permute-start.22 = (f32[128,256]{1,0:T(8,128)S(1)}, f32[128,256]{1,0:T(8,128)S(1)}, u32[]{:S(2)}, u32[]{:S(2)}) collective-permute-start(f32[128,256]{1,0:T(8,128)S(1)} %ahead_sums.1.refs_2_), channel_id=1, source_target_pairs={{0,16},{4,20},{8,24},{12,28},{16,0},{20,4},{24,8},{28,12},{1,17},{... | collective-permute-start | bytes 393224 | tf_op jit(solution)/shard_map/ppermute | solution.py:432
  54.6 1.5 %collective-permute-done.14.refs_1_ = f32[136,128]{1,0:T(8,128)S(1)} collective-permute-done((f32[136,128]{1,0:T(8,128)S(1)}, f32[136,128]{1,0:T(8,128)S(1)}, u32[]{:S(2)}, u32[]{:S(2)}) %collective-permute-start.14) | collective-permute-done | bytes 69664 | tf_op jit(solution)/shard_map/ppermute | solution.py:432
  56.1 1.6 %collective-permute-start.21 = (f32[136,128]{1,0:T(8,128)S(1)}, f32[136,128]{1,0:T(8,128)S(1)}, u32[]{:S(2)}, u32[]{:S(2)}) collective-permute-start(f32[136,128]{1,0:T(8,128)S(1)} %row1_grads.1.refs_0_), channel_id=1, source_target_pairs={{0,2},{1,3},{2,0},{3,1},{4,6},{5,7},{6,4},{7,5},{8,10},{9,11},{10,... | collective-permute-start | bytes 208904 | tf_op jit(solution)/shard_map/ppermute | solution.py:432
  58.3 2.2 %collective-permute-done.21.refs_1_ = f32[136,128]{1,0:T(8,128)S(1)} collective-permute-done((f32[136,128]{1,0:T(8,128)S(1)}, f32[136,128]{1,0:T(8,128)S(1)}, u32[]{:S(2)}, u32[]{:S(2)}) %collective-permute-start.21) | collective-permute-done | bytes 69664 | tf_op jit(solution)/shard_map/ppermute | solution.py:432
  60.4 3.2 %collective-permute-start.23 = (f32[136,128]{1,0:T(8,128)S(1)}, f32[136,128]{1,0:T(8,128)S(1)}, u32[]{:S(2)}, u32[]{:S(2)}) collective-permute-start(f32[136,128]{1,0:T(8,128)S(1)} %col2_grads.1.refs_4_.refs_1_), channel_id=1, source_target_pairs={{0,8},{4,12},{8,0},{12,4},{16,24},{20,28},{24,16},{28,20},{1,9},{5... | collective-permute-start | bytes 208904 | tf_op jit(solution)/shard_map/ppermute | solution.py:432
  63.7 2.2 %collective-permute-done.23.refs_2_ = f32[136,128]{1,0:T(8,128)S(1)} collective-permute-done((f32[136,128]{1,0:T(8,128)S(1)}, f32[136,128]{1,0:T(8,128)S(1)}, u32[]{:S(2)}, u32[]{:S(2)}) %collective-permute-start.23) | collective-permute-done | bytes 69664 | tf_op jit(solution)/shard_map/ppermute | solution.py:432
  (53 shorter events, 13.0 us)
Async XLA Ops:
  0.6 16.6 %collective-permute-start.3 = (f32[256,128]{1,0:T(8,128)}, f32[256,128]{1,0:T(8,128)S(1)}, u32[]{:S(2)}, u32[]{:S(2)}) collective-permute-start(f32[256,128]{1,0:T(8,128)} %refs_3_.2), channel_id=1, source_target_pairs={{0,8},{4,12},{8,0},{12,4},{16,24},{20,28},{24,16},{28,20},{1,9},{5... | collective-permute-start | bytes 393224 | tf_op jit(solution)/shard_map/ppermute | solution.py:432
  3.7 13.5 %collective-permute-start.2 = (f32[256,128]{1,0:T(8,128)}, f32[256,128]{1,0:T(8,128)S(1)}, u32[]{:S(2)}, u32[]{:S(2)}) collective-permute-start(f32[256,128]{1,0:T(8,128)} %refs_3_.2), channel_id=1, source_target_pairs={{0,4},{4,0},{8,12},{12,8},{16,20},{20,16},{24,28},{28,24},{1,5},{5... | collective-permute-start | bytes 393224 | tf_op jit(solution)/shard_map/ppermute | solution.py:432
  5.3 12.0 %collective-permute-start = (f32[256,128]{1,0:T(8,128)}, f32[256,128]{1,0:T(8,128)S(1)}, u32[]{:S(2)}, u32[]{:S(2)}) collective-permute-start(f32[256,128]{1,0:T(8,128)} %refs_3_.2), channel_id=1, source_target_pairs={{0,16},{4,20},{8,24},{12,28},{16,0},{20,4},{24,8},{28,12},{1,17},{... | collective-permute-start | bytes 393224 | tf_op jit(solution)/shard_map/ppermute | solution.py:432
  7.8 9.4 %collective-permute-start.4 = (f32[256,128]{1,0:T(8,128)}, f32[256,128]{1,0:T(8,128)S(1)}, u32[]{:S(2)}, u32[]{:S(2)}) collective-permute-start(f32[256,128]{1,0:T(8,128)} %refs_3_.2), channel_id=1, source_target_pairs={{0,12},{4,8},{8,4},{12,0},{16,28},{20,24},{24,20},{28,16},{1,13},{... | collective-permute-start | bytes 393224 | tf_op jit(solution)/shard_map/ppermute | solution.py:432
  12.6 4.6 %collective-permute-start.1 = (f32[16,128]{1,0:T(8,128)S(1)}, f32[16,128]{1,0:T(8,128)S(1)}, u32[]{:S(2)}, u32[]{:S(2)}) collective-permute-start(f32[16,128]{1,0:T(8,128)S(1)} %get-tuple-element.27.own_ref), channel_id=1, source_target_pairs={{0,16},{4,20},{8,24},{12,28},{16,0},{20,4},{24,8},{28,12},{1,17},{... | collective-permute-start | bytes 24584 | tf_op jit(solution)/shard_map/ppermute | solution.py:432
  17.3 6.0 %collective-permute-start.7 = (f32[272,128]{1,0:T(8,128)S(1)}, f32[272,128]{1,0:T(8,128)S(1)}, u32[]{:S(2)}, u32[]{:S(2)}) collective-permute-start(f32[272,128]{1,0:T(8,128)S(1)} %message.1.refs_0_.refs_7_), channel_id=1, source_target_pairs={{0,12},{4,8},{8,4},{12,0},{16,28},{20,24},{24,20},{28,16},{1,13},{... | collective-permute-start | bytes 417800 | tf_op jit(solution)/shard_map/ppermute | solution.py:432
  19.9 5.1 %collective-permute-start.6 = (f32[272,128]{1,0:T(8,128)S(1)}, f32[272,128]{1,0:T(8,128)S(1)}, u32[]{:S(2)}, u32[]{:S(2)}) collective-permute-start(f32[272,128]{1,0:T(8,128)S(1)} %message.1.refs_0_.refs_7_), channel_id=1, source_target_pairs={{0,8},{4,12},{8,0},{12,4},{16,24},{20,28},{24,16},{28,20},{1,9},{5... | collective-permute-start | bytes 417800 | tf_op jit(solution)/shard_map/ppermute | solution.py:432
  20.4 5.1 %collective-permute-start.5 = (f32[272,128]{1,0:T(8,128)S(1)}, f32[272,128]{1,0:T(8,128)S(1)}, u32[]{:S(2)}, u32[]{:S(2)}) collective-permute-start(f32[272,128]{1,0:T(8,128)S(1)} %message.1.refs_0_.refs_7_), channel_id=1, source_target_pairs={{0,4},{4,0},{8,12},{12,8},{16,20},{20,16},{24,28},{28,24},{1,5},{5... | collective-permute-start | bytes 417800 | tf_op jit(solution)/shard_map/ppermute | solution.py:432
  26.8 1.6 %collective-permute-start.8 = (f32[2,264,128]{2,1,0:T(8,128)S(1)}, f32[2,264,128]{2,1,0:T(8,128)S(1)}, u32[]{:S(2)}, u32[]{:S(2)}) collective-permute-start(f32[2,264,128]{2,1,0:T(8,128)S(1)} %get-tuple-element.30), channel_id=1, source_target_pairs={{0,1},{1,0},{2,3},{3,2},{4,5},{5,4},{6,7},{7,6},{8,9},{9,8},{10,11... | collective-permute-start | bytes 811016 | tf_op jit(solution)/shard_map/ppermute | solution.py:432
  28.4 5.7 %collective-permute-start.9 = (f32[264,128]{1,0:T(8,128)S(1)}, f32[264,128]{1,0:T(8,128)S(1)}, u32[]{:S(2)}, u32[]{:S(2)}) collective-permute-start(f32[264,128]{1,0:T(8,128)S(1)} %pair_sums.1), channel_id=1, source_target_pairs={{0,2},{1,3},{2,0},{3,1},{4,6},{5,7},{6,4},{7,5},{8,10},{9,11},{10,... | collective-permute-start | bytes 405512 | tf_op jit(solution)/shard_map/ppermute | solution.py:432
  34.9 5.0 %collective-permute-start.12 = (f32[128,256]{1,0:T(8,128)S(1)}, f32[128,256]{1,0:T(8,128)S(1)}, u32[]{:S(2)}, u32[]{:S(2)}) collective-permute-start(f32[128,256]{1,0:T(8,128)S(1)} %get-tuple-element.32.back_ref), channel_id=1, source_target_pairs={{0,2},{1,3},{2,0},{3,1},{4,6},{5,7},{6,4},{7,5},{8,10},{9,11},{10,... | collective-permute-start | bytes 393224 | tf_op jit(solution)/shard_map/ppermute | solution.py:432
  36.7 3.2 %collective-permute-start.10 = (f32[200,256]{1,0:T(8,128)S(1)}, f32[200,256]{1,0:T(8,128)S(1)}, u32[]{:S(2)}, u32[]{:S(2)}) collective-permute-start(f32[200,256]{1,0:T(8,128)S(1)} %weight_parts.1.own_ref.refs_1_), channel_id=1, source_target_pairs={{0,1},{1,0},{2,3},{3,2},{4,5},{5,4},{6,7},{7,6},{8,9},{9,8},{10,11... | collective-permute-start | bytes 614408 | tf_op jit(solution)/shard_map/ppermute | solution.py:432
  39.9 1.3 %collective-permute-start.13 = (f32[128,256]{1,0:T(8,128)S(1)}, f32[128,256]{1,0:T(8,128)S(1)}, u32[]{:S(2)}, u32[]{:S(2)}) collective-permute-start(f32[128,256]{1,0:T(8,128)S(1)} %collective-permute-done.12.refs_3_), channel_id=1, source_target_pairs={{0,1},{1,0},{2,3},{3,2},{4,5},{5,4},{6,7},{7,6},{8,9},{9,8},{10,11... | collective-permute-start | bytes 393224 | tf_op jit(solution)/shard_map/ppermute | solution.py:432
  39.9 7.4 %collective-permute-start.11 = (f32[136,128]{1,0:T(8,128)S(1)}, f32[136,128]{1,0:T(8,128)S(1)}, u32[]{:S(2)}, u32[]{:S(2)}) collective-permute-start(f32[136,128]{1,0:T(8,128)S(1)} %core_grads.1.refs_0_), channel_id=1, source_target_pairs={{0,16},{4,20},{8,24},{12,28},{16,0},{20,4},{24,8},{28,12},{1,17},{... | collective-permute-start | bytes 208904 | tf_op jit(solution)/shard_map/ppermute | solution.py:432
  42.1 6.9 %collective-permute-start.15 = (f32[128,256]{1,0:T(8,128)S(1)}, f32[128,256]{1,0:T(8,128)S(1)}, u32[]{:S(2)}, u32[]{:S(2)}) collective-permute-start(f32[128,256]{1,0:T(8,128)S(1)} %get-tuple-element.37), channel_id=1, source_target_pairs={{0,4},{4,0},{8,12},{12,8},{16,20},{20,16},{24,28},{28,24},{1,5},{5... | collective-permute-start | bytes 393224 | tf_op jit(solution)/shard_map/ppermute | solution.py:432
  43.1 7.0 %collective-permute-start.16 = (f32[128,256]{1,0:T(8,128)S(1)}, f32[128,256]{1,0:T(8,128)S(1)}, u32[]{:S(2)}, u32[]{:S(2)}) collective-permute-start(f32[128,256]{1,0:T(8,128)S(1)} %get-tuple-element.38), channel_id=1, source_target_pairs={{0,8},{4,12},{8,0},{12,4},{16,24},{20,28},{24,16},{28,20},{1,9},{5... | collective-permute-start | bytes 393224 | tf_op jit(solution)/shard_map/ppermute | solution.py:432
  44.7 8.4 %collective-permute-start.17 = (f32[128,256]{1,0:T(8,128)S(1)}, f32[128,256]{1,0:T(8,128)S(1)}, u32[]{:S(2)}, u32[]{:S(2)}) collective-permute-start(f32[128,256]{1,0:T(8,128)S(1)} %get-tuple-element.39), channel_id=1, source_target_pairs={{0,12},{4,8},{8,4},{12,0},{16,28},{20,24},{24,20},{28,16},{1,13},{... | collective-permute-start | bytes 393224 | tf_op jit(solution)/shard_map/ppermute | solution.py:432
  46.4 17.2 %collective-permute-start.18 = (f32[128,256]{1,0:T(8,128)S(1)}, f32[128,256]{1,0:T(8,128)S(1)}, u32[]{:S(2)}, u32[]{:S(2)}) collective-permute-start(f32[128,256]{1,0:T(8,128)S(1)} %get-tuple-element.41), channel_id=1, source_target_pairs={{0,4},{4,0},{8,12},{12,8},{16,20},{20,16},{24,28},{28,24},{1,5},{5... | collective-permute-start | bytes 393224 | tf_op jit(solution)/shard_map/ppermute | solution.py:432
  47.4 16.2 %collective-permute-start.19 = (f32[128,256]{1,0:T(8,128)S(1)}, f32[128,256]{1,0:T(8,128)S(1)}, u32[]{:S(2)}, u32[]{:S(2)}) collective-permute-start(f32[128,256]{1,0:T(8,128)S(1)} %get-tuple-element.42), channel_id=1, source_target_pairs={{0,8},{4,12},{8,0},{12,4},{16,24},{20,28},{24,16},{28,20},{1,9},{5... | collective-permute-start | bytes 393224 | tf_op jit(solution)/shard_map/ppermute | solution.py:432
  49.0 14.6 %collective-permute-start.20 = (f32[128,256]{1,0:T(8,128)S(1)}, f32[128,256]{1,0:T(8,128)S(1)}, u32[]{:S(2)}, u32[]{:S(2)}) collective-permute-start(f32[128,256]{1,0:T(8,128)S(1)} %get-tuple-element.43), channel_id=1, source_target_pairs={{0,12},{4,8},{8,4},{12,0},{16,28},{20,24},{24,20},{28,16},{1,13},{... | collective-permute-start | bytes 393224 | tf_op jit(solution)/shard_map/ppermute | solution.py:432
  50.1 6.0 %collective-permute-start.14 = (f32[136,128]{1,0:T(8,128)S(1)}, f32[136,128]{1,0:T(8,128)S(1)}, u32[]{:S(2)}, u32[]{:S(2)}) collective-permute-start(f32[136,128]{1,0:T(8,128)S(1)} %held_grads.1.refs_0_), channel_id=1, source_target_pairs={{0,4},{4,0},{8,12},{12,8},{16,20},{20,16},{24,28},{28,24},{1,5},{5... | collective-permute-start | bytes 208904 | tf_op jit(solution)/shard_map/ppermute | solution.py:432
  53.1 10.6 %collective-permute-start.22 = (f32[128,256]{1,0:T(8,128)S(1)}, f32[128,256]{1,0:T(8,128)S(1)}, u32[]{:S(2)}, u32[]{:S(2)}) collective-permute-start(f32[128,256]{1,0:T(8,128)S(1)} %ahead_sums.1.refs_2_), channel_id=1, source_target_pairs={{0,16},{4,20},{8,24},{12,28},{16,0},{20,4},{24,8},{28,12},{1,17},{... | collective-permute-start | bytes 393224 | tf_op jit(solution)/shard_map/ppermute | solution.py:432
  56.1 4.4 %collective-permute-start.21 = (f32[136,128]{1,0:T(8,128)S(1)}, f32[136,128]{1,0:T(8,128)S(1)}, u32[]{:S(2)}, u32[]{:S(2)}) collective-permute-start(f32[136,128]{1,0:T(8,128)S(1)} %row1_grads.1.refs_0_), channel_id=1, source_target_pairs={{0,2},{1,3},{2,0},{3,1},{4,6},{5,7},{6,4},{7,5},{8,10},{9,11},{10,... | collective-permute-start | bytes 208904 | tf_op jit(solution)/shard_map/ppermute | solution.py:432
  60.4 5.5 %collective-permute-start.23 = (f32[136,128]{1,0:T(8,128)S(1)}, f32[136,128]{1,0:T(8,128)S(1)}, u32[]{:S(2)}, u32[]{:S(2)}) collective-permute-start(f32[136,128]{1,0:T(8,128)S(1)} %col2_grads.1.refs_4_.refs_1_), channel_id=1, source_target_pairs={{0,8},{4,12},{8,0},{12,4},{16,24},{20,28},{24,16},{28,20},{1,9},{5... | collective-permute-start | bytes 208904 | tf_op jit(solution)/shard_map/ppermute | solution.py:432
  (4 other events, 64.8 us)

commit v10 on v9

--- a/solution.py
+++ b/solution.py
@@ -356,8 +356,8 @@
     return call(unfold_kernel, "core_grads", (own, got), (vmem(width + PAD, width),))[0]
 
 
-def backward_second_kernel(peers, dense_ref, lhs, *outs):
-    backward_chunks(peers, dense_ref, lhs, outs)
+def backward_second_kernel(peers, dense_ref, lhs, *refs):
+    backward_chunks(peers, dense_ref, lhs, refs[-len(peers) :])
 
 
 def backward_first(peers, dense, blocks, width, after):
@@ -373,13 +373,13 @@
     return dict(zip(peers, out)), out[-1]
 
 
-def backward_second(peers, dense, lhs, node_rows):
+def backward_second(peers, dense, lhs, node_rows, after):
     rows = dense.shape[0]
     width = lhs.shape[0] // 2
     out = call(
         functools.partial(backward_second_kernel, peers),
         "backward_second",
-        (dense, lhs),
+        (dense, lhs, *after),
         [vmem(width, node_rows)] * len(peers),
         flops=4 * len(peers) * node_rows * rows * width,
     )
@@ -472,7 +472,7 @@
     grads = sum_all([grads, swap(grads, "row", top)], "top_grads", (), HINT)
     chunks, lhs = backward_first(far, dense, backs, width, ())
     ahead = [chunks[top]] + [swap(chunks[top | m], "row", m) for m in near[1:]]
-    chunks = backward_second(near, dense, lhs, node_rows)
+    chunks = backward_second(near, dense, lhs, node_rows, (grads,))
     mine = [chunks[0]] + [swap(chunks[m], "row", m) for m in near[1:]]
     ahead = sum_all(ahead, "ahead_sums", (), HINT)
     passed = swap(ahead, "row", top)
@@ -482,7 +482,7 @@
     rounds += [("row", 1 << b) for b in range(1, top.bit_length() - 1)]
     grads = sum_all([grads], "held_grads", (lhs,))
     for step, (axis, mask) in enumerate(rounds[:-1]):
-        after = (ahead,) if (axis, mask) == ("row", 1) else ()
+        after = (ahead,) if False else ()
         grads = sum_all([grads, swap(grads, axis, mask)], f"{axis}{mask}_grads", after)
         if step == len(rounds) - 3:
             activated = hand_over(activated, (grads,))

time: 66.8 us -> 64.2 us (0.961)
  starting transfers between devices: 29.1 us -> 27.4 us
  waiting for transfers between devices: 25.4 us -> 24.4 us
    ppermute x24, starting transfers between devices: 29.1 us -> 27.4 us  [swap(): return lax.ppermute(value, axis, [(i, i ^ mask) for i in range(count)])]
    ppermute x24, waiting for transfers between devices: 25.4 us -> 24.4 us  [swap(): return lax.ppermute(value, axis, [(i, i ^ mask) for i in range(count)])]
  transfers between devices with their start and end apart: 24 -> 24, of which waited for: 12 -> 13; matrix products, arithmetic and copies ran while one was open for 0% -> 0% of each run, Pallas kernels for 12% -> 12%
where the time goes in v10:
time: 64.2 us; the launch traced here: 64 us
  starting transfers between devices  27.4 us (43%)
  waiting for transfers between devices  24.4 us (38%)
  Pallas kernels  10.7 us (17%)
  between operations  1.46 us (2%)
    ppermute x24, starting transfers between devices, swap(): return lax.ppermute(value, axis, [(i, i ^ mask) for i in range(count)])  27.4 us
    ppermute x24, waiting for transfers between devices, swap(): return lax.ppermute(value, axis, [(i, i ^ mask) for i in range(count)])  24.4 us
    pallas_call x21, Pallas kernels, call(): pl.pallas_call(kernel, out_shape=tuple(outs), in_specs=list(before_specs)...  10.7 us
  transfers between devices with their start and end apart: 24, of which 13 were waited for; matrix products, arithmetic and copies ran while one was open for 0% of the time, Pallas kernels for 12%

profile of v10, /device:TPU:0, one launch (start us, length us, event | category | flops | bytes accessed | tf_op | source)
XLA Modules:
  0.0 64.0 jit_solution(13556610955352864323)
XLA Ops:
  0.6 3.1 %collective-permute-start.3 = (f32[256,128]{1,0:T(8,128)}, f32[256,128]{1,0:T(8,128)S(1)}, u32[]{:S(2)}, u32[]{:S(2)}) collective-permute-start(f32[256,128]{1,0:T(8,128)} %refs_3_.2), channel_id=1, source_target_pairs={{0,8},{4,12},{8,0},{12,4},{16,24},{20,28},{24,16},{28,20},{1,9},{5... | collective-permute-start | bytes 393224 | tf_op jit(solution)/shard_map/ppermute | solution.py:432
  3.7 1.5 %collective-permute-start.2 = (f32[256,128]{1,0:T(8,128)}, f32[256,128]{1,0:T(8,128)S(1)}, u32[]{:S(2)}, u32[]{:S(2)}) collective-permute-start(f32[256,128]{1,0:T(8,128)} %refs_3_.2), channel_id=1, source_target_pairs={{0,4},{4,0},{8,12},{12,8},{16,20},{20,16},{24,28},{28,24},{1,5},{5... | collective-permute-start | bytes 393224 | tf_op jit(solution)/shard_map/ppermute | solution.py:432
  5.3 2.6 %collective-permute-start = (f32[256,128]{1,0:T(8,128)}, f32[256,128]{1,0:T(8,128)S(1)}, u32[]{:S(2)}, u32[]{:S(2)}) collective-permute-start(f32[256,128]{1,0:T(8,128)} %refs_3_.2), channel_id=1, source_target_pairs={{0,16},{4,20},{8,24},{12,28},{16,0},{20,4},{24,8},{28,12},{1,17},{... | collective-permute-start | bytes 393224 | tf_op jit(solution)/shard_map/ppermute | solution.py:432
  8.9 3.8 %densify.1 = (bf16[1024,2048]{1,0:T(8,128)(2,1)S(1)}, f32[16,128]{1,0:T(8,128)S(1)}) custom-call(s32[1,128]{1,0:T(1,128)} %bitcast.6, s32[1,1]{1,0:T(1,128)S(6)} %copy.11.counts_hbm, s32[128,128,128]{2,1,0:T(8,128)} %bitcast.5), custom_call_target="tpu_custom_call" | custom-call | flops 838860800 | tf_op jit(solution)/shard_map/densify/pallas_call | solution.py:50
  12.7 4.5 %collective-permute-done.1.got_ref = f32[16,128]{1,0:T(8,128)S(1)} collective-permute-done((f32[16,128]{1,0:T(8,128)S(1)}, f32[16,128]{1,0:T(8,128)S(1)}, u32[]{:S(2)}, u32[]{:S(2)}) %collective-permute-start.1) | collective-permute-done | bytes 8224 | tf_op jit(solution)/shard_map/ppermute | solution.py:432
  17.3 2.6 %collective-permute-start.7 = (f32[272,128]{1,0:T(8,128)S(1)}, f32[272,128]{1,0:T(8,128)S(1)}, u32[]{:S(2)}, u32[]{:S(2)}) collective-permute-start(f32[272,128]{1,0:T(8,128)S(1)} %message.1.refs_0_.refs_7_), channel_id=1, source_target_pairs={{0,12},{4,8},{8,4},{12,0},{16,28},{20,24},{24,20},{28,16},{1,13},{... | collective-permute-start | bytes 417800 | tf_op jit(solution)/shard_map/ppermute | solution.py:432
  21.5 1.8 %collective-permute-done.7.refs_3_.refs_10_ = f32[272,128]{1,0:T(8,128)S(1)} collective-permute-done((f32[272,128]{1,0:T(8,128)S(1)}, f32[272,128]{1,0:T(8,128)S(1)}, u32[]{:S(2)}, u32[]{:S(2)}) %collective-permute-start.7) | collective-permute-done | bytes 139296 | tf_op jit(solution)/shard_map/ppermute | solution.py:432
  23.3 1.6 %collective-permute-done.6.refs_2_.refs_9_ = f32[272,128]{1,0:T(8,128)S(1)} collective-permute-done((f32[272,128]{1,0:T(8,128)S(1)}, f32[272,128]{1,0:T(8,128)S(1)}, u32[]{:S(2)}, u32[]{:S(2)}) %collective-permute-start.6) | collective-permute-done | bytes 139296 | tf_op jit(solution)/shard_map/ppermute | solution.py:432
  28.4 1.6 %collective-permute-start.9 = (f32[264,128]{1,0:T(8,128)S(1)}, f32[264,128]{1,0:T(8,128)S(1)}, u32[]{:S(2)}, u32[]{:S(2)}) collective-permute-start(f32[264,128]{1,0:T(8,128)S(1)} %pair_sums.1), channel_id=1, source_target_pairs={{0,2},{1,3},{2,0},{3,1},{4,6},{5,7},{6,4},{7,5},{8,10},{9,11},{10,... | collective-permute-start | bytes 405512 | tf_op jit(solution)/shard_map/ppermute | solution.py:432
  29.9 4.1 %collective-permute-done.9.refs_2_ = f32[264,128]{1,0:T(8,128)S(1)} collective-permute-done((f32[264,128]{1,0:T(8,128)S(1)}, f32[264,128]{1,0:T(8,128)S(1)}, u32[]{:S(2)}, u32[]{:S(2)}) %collective-permute-start.9) | collective-permute-done | bytes 135200 | tf_op jit(solution)/shard_map/ppermute | solution.py:432
  34.9 1.6 %collective-permute-start.12 = (f32[128,256]{1,0:T(8,128)S(1)}, f32[128,256]{1,0:T(8,128)S(1)}, u32[]{:S(2)}, u32[]{:S(2)}) collective-permute-start(f32[128,256]{1,0:T(8,128)S(1)} %get-tuple-element.32.back_ref), channel_id=1, source_target_pairs={{0,2},{1,3},{2,0},{3,1},{4,6},{5,7},{6,4},{7,5},{8,10},{9,11},{10,... | collective-permute-start | bytes 393224 | tf_op jit(solution)/shard_map/ppermute | solution.py:432
  36.8 3.1 %collective-permute-done.12.refs_3_ = f32[128,256]{1,0:T(8,128)S(1)} collective-permute-done((f32[128,256]{1,0:T(8,128)S(1)}, f32[128,256]{1,0:T(8,128)S(1)}, u32[]{:S(2)}, u32[]{:S(2)}) %collective-permute-start.12) | collective-permute-done | bytes 131104 | tf_op jit(solution)/shard_map/ppermute | solution.py:432
  42.1 1.0 %collective-permute-start.19 = (f32[128,256]{1,0:T(8,128)S(1)}, f32[128,256]{1,0:T(8,128)S(1)}, u32[]{:S(2)}, u32[]{:S(2)}) collective-permute-start(f32[128,256]{1,0:T(8,128)S(1)} %get-tuple-element.41), channel_id=1, source_target_pairs={{0,4},{4,0},{8,12},{12,8},{16,20},{20,16},{24,28},{28,24},{1,5},{5... | collective-permute-start | bytes 393224 | tf_op jit(solution)/shard_map/ppermute | solution.py:432
  43.1 1.6 %collective-permute-start.20 = (f32[128,256]{1,0:T(8,128)S(1)}, f32[128,256]{1,0:T(8,128)S(1)}, u32[]{:S(2)}, u32[]{:S(2)}) collective-permute-start(f32[128,256]{1,0:T(8,128)S(1)} %get-tuple-element.42), channel_id=1, source_target_pairs={{0,8},{4,12},{8,0},{12,4},{16,24},{20,28},{24,16},{28,20},{1,9},{5... | collective-permute-start | bytes 393224 | tf_op jit(solution)/shard_map/ppermute | solution.py:432
  45.6 1.4 %collective-permute-done.11.refs_1_ = f32[136,128]{1,0:T(8,128)S(1)} collective-permute-done((f32[136,128]{1,0:T(8,128)S(1)}, f32[136,128]{1,0:T(8,128)S(1)}, u32[]{:S(2)}, u32[]{:S(2)}) %collective-permute-start.11) | collective-permute-done | bytes 69664 | tf_op jit(solution)/shard_map/ppermute | solution.py:432
  47.1 1.0 %collective-permute-start.14 = (f32[136,128]{1,0:T(8,128)S(1)}, f32[136,128]{1,0:T(8,128)S(1)}, u32[]{:S(2)}, u32[]{:S(2)}) collective-permute-start(f32[136,128]{1,0:T(8,128)S(1)} %held_grads.1.refs_0_), channel_id=1, source_target_pairs={{0,4},{4,0},{8,12},{12,8},{16,20},{20,16},{24,28},{28,24},{1,5},{5... | collective-permute-start | bytes 208904 | tf_op jit(solution)/shard_map/ppermute | solution.py:432
  48.9 1.2 %collective-permute-start.15 = (f32[128,256]{1,0:T(8,128)S(1)}, f32[128,256]{1,0:T(8,128)S(1)}, u32[]{:S(2)}, u32[]{:S(2)}) collective-permute-start(f32[128,256]{1,0:T(8,128)S(1)} %get-tuple-element.37), channel_id=1, source_target_pairs={{0,4},{4,0},{8,12},{12,8},{16,20},{20,16},{24,28},{28,24},{1,5},{5... | collective-permute-start | bytes 393224 | tf_op jit(solution)/shard_map/ppermute | solution.py:432
  50.2 2.2 %collective-permute-start.17 = (f32[128,256]{1,0:T(8,128)S(1)}, f32[128,256]{1,0:T(8,128)S(1)}, u32[]{:S(2)}, u32[]{:S(2)}) collective-permute-start(f32[128,256]{1,0:T(8,128)S(1)} %get-tuple-element.39), channel_id=1, source_target_pairs={{0,12},{4,8},{8,4},{12,0},{16,28},{20,24},{24,20},{28,16},{1,13},{... | collective-permute-start | bytes 393224 | tf_op jit(solution)/shard_map/ppermute | solution.py:432
  53.1 1.4 %collective-permute-start.22 = (f32[128,256]{1,0:T(8,128)S(1)}, f32[128,256]{1,0:T(8,128)S(1)}, u32[]{:S(2)}, u32[]{:S(2)}) collective-permute-start(f32[128,256]{1,0:T(8,128)S(1)} %ahead_sums.1), channel_id=1, source_target_pairs={{0,16},{4,20},{8,24},{12,28},{16,0},{20,4},{24,8},{28,12},{1,17},{... | collective-permute-start | bytes 393224 | tf_op jit(solution)/shard_map/ppermute | solution.py:432
  54.5 1.6 %collective-permute-start.18 = (f32[136,128]{1,0:T(8,128)S(1)}, f32[136,128]{1,0:T(8,128)S(1)}, u32[]{:S(2)}, u32[]{:S(2)}) collective-permute-start(f32[136,128]{1,0:T(8,128)S(1)} %row1_grads.1.refs_0_), channel_id=1, source_target_pairs={{0,2},{1,3},{2,0},{3,1},{4,6},{5,7},{6,4},{7,5},{8,10},{9,11},{10,... | collective-permute-start | bytes 208904 | tf_op jit(solution)/shard_map/ppermute | solution.py:432
  56.7 2.2 %collective-permute-done.18.refs_1_ = f32[136,128]{1,0:T(8,128)S(1)} collective-permute-done((f32[136,128]{1,0:T(8,128)S(1)}, f32[136,128]{1,0:T(8,128)S(1)}, u32[]{:S(2)}, u32[]{:S(2)}) %collective-permute-start.18) | collective-permute-done | bytes 69664 | tf_op jit(solution)/shard_map/ppermute | solution.py:432
  58.9 1.5 %collective-permute-start.23 = (f32[136,128]{1,0:T(8,128)S(1)}, f32[136,128]{1,0:T(8,128)S(1)}, u32[]{:S(2)}, u32[]{:S(2)}) collective-permute-start(f32[136,128]{1,0:T(8,128)S(1)} %col2_grads.1.refs_4_.refs_1_), channel_id=1, source_target_pairs={{0,8},{4,12},{8,0},{12,4},{16,24},{20,28},{24,16},{28,20},{1,9},{5... | collective-permute-start | bytes 208904 | tf_op jit(solution)/shard_map/ppermute | solution.py:432
  60.5 1.1 %collective-permute-done.22.refs_1_ = f32[128,256]{1,0:T(8,128)S(1)} collective-permute-done((f32[128,256]{1,0:T(8,128)S(1)}, f32[128,256]{1,0:T(8,128)S(1)}, u32[]{:S(2)}, u32[]{:S(2)}) %collective-permute-start.22) | collective-permute-done | bytes 131104 | tf_op jit(solution)/shard_map/ppermute | solution.py:432
  61.5 1.7 %collective-permute-done.23.refs_2_ = f32[136,128]{1,0:T(8,128)S(1)} collective-permute-done((f32[136,128]{1,0:T(8,128)S(1)}, f32[136,128]{1,0:T(8,128)S(1)}, u32[]{:S(2)}, u32[]{:S(2)}) %collective-permute-start.23) | collective-permute-done | bytes 69664 | tf_op jit(solution)/shard_map/ppermute | solution.py:432
  (53 shorter events, 12.9 us)
Async XLA Ops:
  0.6 16.6 %collective-permute-start.3 = (f32[256,128]{1,0:T(8,128)}, f32[256,128]{1,0:T(8,128)S(1)}, u32[]{:S(2)}, u32[]{:S(2)}) collective-permute-start(f32[256,128]{1,0:T(8,128)} %refs_3_.2), channel_id=1, source_target_pairs={{0,8},{4,12},{8,0},{12,4},{16,24},{20,28},{24,16},{28,20},{1,9},{5... | collective-permute-start | bytes 393224 | tf_op jit(solution)/shard_map/ppermute | solution.py:432
  3.7 13.5 %collective-permute-start.2 = (f32[256,128]{1,0:T(8,128)}, f32[256,128]{1,0:T(8,128)S(1)}, u32[]{:S(2)}, u32[]{:S(2)}) collective-permute-start(f32[256,128]{1,0:T(8,128)} %refs_3_.2), channel_id=1, source_target_pairs={{0,4},{4,0},{8,12},{12,8},{16,20},{20,16},{24,28},{28,24},{1,5},{5... | collective-permute-start | bytes 393224 | tf_op jit(solution)/shard_map/ppermute | solution.py:432
  5.3 12.0 %collective-permute-start = (f32[256,128]{1,0:T(8,128)}, f32[256,128]{1,0:T(8,128)S(1)}, u32[]{:S(2)}, u32[]{:S(2)}) collective-permute-start(f32[256,128]{1,0:T(8,128)} %refs_3_.2), channel_id=1, source_target_pairs={{0,16},{4,20},{8,24},{12,28},{16,0},{20,4},{24,8},{28,12},{1,17},{... | collective-permute-start | bytes 393224 | tf_op jit(solution)/shard_map/ppermute | solution.py:432
  7.8 9.4 %collective-permute-start.4 = (f32[256,128]{1,0:T(8,128)}, f32[256,128]{1,0:T(8,128)S(1)}, u32[]{:S(2)}, u32[]{:S(2)}) collective-permute-start(f32[256,128]{1,0:T(8,128)} %refs_3_.2), channel_id=1, source_target_pairs={{0,12},{4,8},{8,4},{12,0},{16,28},{20,24},{24,20},{28,16},{1,13},{... | collective-permute-start | bytes 393224 | tf_op jit(solution)/shard_map/ppermute | solution.py:432
  12.6 4.6 %collective-permute-start.1 = (f32[16,128]{1,0:T(8,128)S(1)}, f32[16,128]{1,0:T(8,128)S(1)}, u32[]{:S(2)}, u32[]{:S(2)}) collective-permute-start(f32[16,128]{1,0:T(8,128)S(1)} %get-tuple-element.27.own_ref), channel_id=1, source_target_pairs={{0,16},{4,20},{8,24},{12,28},{16,0},{20,4},{24,8},{28,12},{1,17},{... | collective-permute-start | bytes 24584 | tf_op jit(solution)/shard_map/ppermute | solution.py:432
  17.3 6.0 %collective-permute-start.7 = (f32[272,128]{1,0:T(8,128)S(1)}, f32[272,128]{1,0:T(8,128)S(1)}, u32[]{:S(2)}, u32[]{:S(2)}) collective-permute-start(f32[272,128]{1,0:T(8,128)S(1)} %message.1.refs_0_.refs_7_), channel_id=1, source_target_pairs={{0,12},{4,8},{8,4},{12,0},{16,28},{20,24},{24,20},{28,16},{1,13},{... | collective-permute-start | bytes 417800 | tf_op jit(solution)/shard_map/ppermute | solution.py:432
  19.9 5.1 %collective-permute-start.6 = (f32[272,128]{1,0:T(8,128)S(1)}, f32[272,128]{1,0:T(8,128)S(1)}, u32[]{:S(2)}, u32[]{:S(2)}) collective-permute-start(f32[272,128]{1,0:T(8,128)S(1)} %message.1.refs_0_.refs_7_), channel_id=1, source_target_pairs={{0,8},{4,12},{8,0},{12,4},{16,24},{20,28},{24,16},{28,20},{1,9},{5... | collective-permute-start | bytes 417800 | tf_op jit(solution)/shard_map/ppermute | solution.py:432
  20.4 5.1 %collective-permute-start.5 = (f32[272,128]{1,0:T(8,128)S(1)}, f32[272,128]{1,0:T(8,128)S(1)}, u32[]{:S(2)}, u32[]{:S(2)}) collective-permute-start(f32[272,128]{1,0:T(8,128)S(1)} %message.1.refs_0_.refs_7_), channel_id=1, source_target_pairs={{0,4},{4,0},{8,12},{12,8},{16,20},{20,16},{24,28},{28,24},{1,5},{5... | collective-permute-start | bytes 417800 | tf_op jit(solution)/shard_map/ppermute | solution.py:432
  26.8 1.6 %collective-permute-start.8 = (f32[2,264,128]{2,1,0:T(8,128)S(1)}, f32[2,264,128]{2,1,0:T(8,128)S(1)}, u32[]{:S(2)}, u32[]{:S(2)}) collective-permute-start(f32[2,264,128]{2,1,0:T(8,128)S(1)} %get-tuple-element.30), channel_id=1, source_target_pairs={{0,1},{1,0},{2,3},{3,2},{4,5},{5,4},{6,7},{7,6},{8,9},{9,8},{10,11... | collective-permute-start | bytes 811016 | tf_op jit(solution)/shard_map/ppermute | solution.py:432
  28.4 5.7 %collective-permute-start.9 = (f32[264,128]{1,0:T(8,128)S(1)}, f32[264,128]{1,0:T(8,128)S(1)}, u32[]{:S(2)}, u32[]{:S(2)}) collective-permute-start(f32[264,128]{1,0:T(8,128)S(1)} %pair_sums.1), channel_id=1, source_target_pairs={{0,2},{1,3},{2,0},{3,1},{4,6},{5,7},{6,4},{7,5},{8,10},{9,11},{10,... | collective-permute-start | bytes 405512 | tf_op jit(solution)/shard_map/ppermute | solution.py:432
  34.9 5.0 %collective-permute-start.12 = (f32[128,256]{1,0:T(8,128)S(1)}, f32[128,256]{1,0:T(8,128)S(1)}, u32[]{:S(2)}, u32[]{:S(2)}) collective-permute-start(f32[128,256]{1,0:T(8,128)S(1)} %get-tuple-element.32.back_ref), channel_id=1, source_target_pairs={{0,2},{1,3},{2,0},{3,1},{4,6},{5,7},{6,4},{7,5},{8,10},{9,11},{10,... | collective-permute-start | bytes 393224 | tf_op jit(solution)/shard_map/ppermute | solution.py:432
  36.7 3.2 %collective-permute-start.10 = (f32[200,256]{1,0:T(8,128)S(1)}, f32[200,256]{1,0:T(8,128)S(1)}, u32[]{:S(2)}, u32[]{:S(2)}) collective-permute-start(f32[200,256]{1,0:T(8,128)S(1)} %weight_parts.1.own_ref.refs_1_), channel_id=1, source_target_pairs={{0,1},{1,0},{2,3},{3,2},{4,5},{5,4},{6,7},{7,6},{8,9},{9,8},{10,11... | collective-permute-start | bytes 614408 | tf_op jit(solution)/shard_map/ppermute | solution.py:432
  39.9 1.3 %collective-permute-start.13 = (f32[128,256]{1,0:T(8,128)S(1)}, f32[128,256]{1,0:T(8,128)S(1)}, u32[]{:S(2)}, u32[]{:S(2)}) collective-permute-start(f32[128,256]{1,0:T(8,128)S(1)} %collective-permute-done.12.refs_3_), channel_id=1, source_target_pairs={{0,1},{1,0},{2,3},{3,2},{4,5},{5,4},{6,7},{7,6},{8,9},{9,8},{10,11... | collective-permute-start | bytes 393224 | tf_op jit(solution)/shard_map/ppermute | solution.py:432
  39.9 7.2 %collective-permute-start.11 = (f32[136,128]{1,0:T(8,128)S(1)}, f32[136,128]{1,0:T(8,128)S(1)}, u32[]{:S(2)}, u32[]{:S(2)}) collective-permute-start(f32[136,128]{1,0:T(8,128)S(1)} %core_grads.1.refs_0_), channel_id=1, source_target_pairs={{0,16},{4,20},{8,24},{12,28},{16,0},{20,4},{24,8},{28,12},{1,17},{... | collective-permute-start | bytes 208904 | tf_op jit(solution)/shard_map/ppermute | solution.py:432
  42.1 7.9 %collective-permute-start.19 = (f32[128,256]{1,0:T(8,128)S(1)}, f32[128,256]{1,0:T(8,128)S(1)}, u32[]{:S(2)}, u32[]{:S(2)}) collective-permute-start(f32[128,256]{1,0:T(8,128)S(1)} %get-tuple-element.41), channel_id=1, source_target_pairs={{0,4},{4,0},{8,12},{12,8},{16,20},{20,16},{24,28},{28,24},{1,5},{5... | collective-permute-start | bytes 393224 | tf_op jit(solution)/shard_map/ppermute | solution.py:432
  43.1 7.1 %collective-permute-start.20 = (f32[128,256]{1,0:T(8,128)S(1)}, f32[128,256]{1,0:T(8,128)S(1)}, u32[]{:S(2)}, u32[]{:S(2)}) collective-permute-start(f32[128,256]{1,0:T(8,128)S(1)} %get-tuple-element.42), channel_id=1, source_target_pairs={{0,8},{4,12},{8,0},{12,4},{16,24},{20,28},{24,16},{28,20},{1,9},{5... | collective-permute-start | bytes 393224 | tf_op jit(solution)/shard_map/ppermute | solution.py:432
  44.7 8.4 %collective-permute-start.21 = (f32[128,256]{1,0:T(8,128)S(1)}, f32[128,256]{1,0:T(8,128)S(1)}, u32[]{:S(2)}, u32[]{:S(2)}) collective-permute-start(f32[128,256]{1,0:T(8,128)S(1)} %get-tuple-element.43), channel_id=1, source_target_pairs={{0,12},{4,8},{8,4},{12,0},{16,28},{20,24},{24,20},{28,16},{1,13},{... | collective-permute-start | bytes 393224 | tf_op jit(solution)/shard_map/ppermute | solution.py:432
  47.1 7.4 %collective-permute-start.14 = (f32[136,128]{1,0:T(8,128)S(1)}, f32[136,128]{1,0:T(8,128)S(1)}, u32[]{:S(2)}, u32[]{:S(2)}) collective-permute-start(f32[136,128]{1,0:T(8,128)S(1)} %held_grads.1.refs_0_), channel_id=1, source_target_pairs={{0,4},{4,0},{8,12},{12,8},{16,20},{20,16},{24,28},{28,24},{1,5},{5... | collective-permute-start | bytes 208904 | tf_op jit(solution)/shard_map/ppermute | solution.py:432
  48.9 11.6 %collective-permute-start.15 = (f32[128,256]{1,0:T(8,128)S(1)}, f32[128,256]{1,0:T(8,128)S(1)}, u32[]{:S(2)}, u32[]{:S(2)}) collective-permute-start(f32[128,256]{1,0:T(8,128)S(1)} %get-tuple-element.37), channel_id=1, source_target_pairs={{0,4},{4,0},{8,12},{12,8},{16,20},{20,16},{24,28},{28,24},{1,5},{5... | collective-permute-start | bytes 393224 | tf_op jit(solution)/shard_map/ppermute | solution.py:432
  50.0 10.4 %collective-permute-start.16 = (f32[128,256]{1,0:T(8,128)S(1)}, f32[128,256]{1,0:T(8,128)S(1)}, u32[]{:S(2)}, u32[]{:S(2)}) collective-permute-start(f32[128,256]{1,0:T(8,128)S(1)} %get-tuple-element.38), channel_id=1, source_target_pairs={{0,8},{4,12},{8,0},{12,4},{16,24},{20,28},{24,16},{28,20},{1,9},{5... | collective-permute-start | bytes 393224 | tf_op jit(solution)/shard_map/ppermute | solution.py:432
  50.2 10.2 %collective-permute-start.17 = (f32[128,256]{1,0:T(8,128)S(1)}, f32[128,256]{1,0:T(8,128)S(1)}, u32[]{:S(2)}, u32[]{:S(2)}) collective-permute-start(f32[128,256]{1,0:T(8,128)S(1)} %get-tuple-element.39), channel_id=1, source_target_pairs={{0,12},{4,8},{8,4},{12,0},{16,28},{20,24},{24,20},{28,16},{1,13},{... | collective-permute-start | bytes 393224 | tf_op jit(solution)/shard_map/ppermute | solution.py:432
  53.1 8.4 %collective-permute-start.22 = (f32[128,256]{1,0:T(8,128)S(1)}, f32[128,256]{1,0:T(8,128)S(1)}, u32[]{:S(2)}, u32[]{:S(2)}) collective-permute-start(f32[128,256]{1,0:T(8,128)S(1)} %ahead_sums.1), channel_id=1, source_target_pairs={{0,16},{4,20},{8,24},{12,28},{16,0},{20,4},{24,8},{28,12},{1,17},{... | collective-permute-start | bytes 393224 | tf_op jit(solution)/shard_map/ppermute | solution.py:432
  54.5 4.4 %collective-permute-start.18 = (f32[136,128]{1,0:T(8,128)S(1)}, f32[136,128]{1,0:T(8,128)S(1)}, u32[]{:S(2)}, u32[]{:S(2)}) collective-permute-start(f32[136,128]{1,0:T(8,128)S(1)} %row1_grads.1.refs_0_), channel_id=1, source_target_pairs={{0,2},{1,3},{2,0},{3,1},{4,6},{5,7},{6,4},{7,5},{8,10},{9,11},{10,... | collective-permute-start | bytes 208904 | tf_op jit(solution)/shard_map/ppermute | solution.py:432
  58.9 4.4 %collective-permute-start.23 = (f32[136,128]{1,0:T(8,128)S(1)}, f32[136,128]{1,0:T(8,128)S(1)}, u32[]{:S(2)}, u32[]{:S(2)}) collective-permute-start(f32[136,128]{1,0:T(8,128)S(1)} %col2_grads.1.refs_4_.refs_1_), channel_id=1, source_target_pairs={{0,8},{4,12},{8,0},{12,4},{16,24},{20,28},{24,16},{28,20},{1,9},{5... | collective-permute-start | bytes 208904 | tf_op jit(solution)/shard_map/ppermute | solution.py:432
  (4 other events, 64.8 us)

commit v11 on v10

--- a/solution.py
+++ b/solution.py
@@ -478,8 +478,8 @@
     passed = swap(ahead, "row", top)
 
     rounds = [("col", 1 << b) for b in range(1, col_count.bit_length() - 1)]
-    rounds = [("row", 1)] * (top > 1) + rounds
-    rounds += [("row", 1 << b) for b in range(1, top.bit_length() - 1)]
+    row_rounds = [("row", 1 << b) for b in range(top.bit_length() - 1)]
+    rounds = row_rounds[-1:] + rounds + row_rounds[:-1]
     grads = sum_all([grads], "held_grads", (lhs,))
     for step, (axis, mask) in enumerate(rounds[:-1]):
         after = (ahead,) if False else ()

time: 64.2 us -> 64.3 us (level)
  waiting for transfers between devices: 24.4 us -> 25.8 us
  starting transfers between devices: 27.4 us -> 26.2 us
    ppermute x24, waiting for transfers between devices: 24.4 us -> 25.8 us  [swap(): return lax.ppermute(value, axis, [(i, i ^ mask) for i in range(count)])]
    ppermute x24, starting transfers between devices: 27.4 us -> 26.2 us  [swap(): return lax.ppermute(value, axis, [(i, i ^ mask) for i in range(count)])]
where the time goes in v11:
time: 64.3 us; the launch traced here: 64.1 us
  starting transfers between devices  26.2 us (41%)
  waiting for transfers between devices  25.8 us (40%)
  Pallas kernels  10.7 us (17%)
  between operations  1.46 us (2%)
    ppermute x24, starting transfers between devices, swap(): return lax.ppermute(value, axis, [(i, i ^ mask) for i in range(count)])  26.2 us
    ppermute x24, waiting for transfers between devices, swap(): return lax.ppermute(value, axis, [(i, i ^ mask) for i in range(count)])  25.8 us
    pallas_call x21, Pallas kernels, call(): pl.pallas_call(kernel, out_shape=tuple(outs), in_specs=list(before_specs)...  10.7 us
  transfers between devices with their start and end apart: 24, of which 13 were waited for; matrix products, arithmetic and copies ran while one was open for 0% of the time, Pallas kernels for 12%

profile of v11, /device:TPU:0, one launch (start us, length us, event | category | flops | bytes accessed | tf_op | source)
XLA Modules:
  0.0 64.1 jit_solution(7750806054029695219)
XLA Ops:
  0.6 3.1 %collective-permute-start.3 = (f32[256,128]{1,0:T(8,128)}, f32[256,128]{1,0:T(8,128)S(1)}, u32[]{:S(2)}, u32[]{:S(2)}) collective-permute-start(f32[256,128]{1,0:T(8,128)} %refs_3_.2), channel_id=1, source_target_pairs={{0,8},{4,12},{8,0},{12,4},{16,24},{20,28},{24,16},{28,20},{1,9},{5... | collective-permute-start | bytes 393224 | tf_op jit(solution)/shard_map/ppermute | solution.py:432
  3.7 1.5 %collective-permute-start.2 = (f32[256,128]{1,0:T(8,128)}, f32[256,128]{1,0:T(8,128)S(1)}, u32[]{:S(2)}, u32[]{:S(2)}) collective-permute-start(f32[256,128]{1,0:T(8,128)} %refs_3_.2), channel_id=1, source_target_pairs={{0,4},{4,0},{8,12},{12,8},{16,20},{20,16},{24,28},{28,24},{1,5},{5... | collective-permute-start | bytes 393224 | tf_op jit(solution)/shard_map/ppermute | solution.py:432
  5.3 2.6 %collective-permute-start = (f32[256,128]{1,0:T(8,128)}, f32[256,128]{1,0:T(8,128)S(1)}, u32[]{:S(2)}, u32[]{:S(2)}) collective-permute-start(f32[256,128]{1,0:T(8,128)} %refs_3_.2), channel_id=1, source_target_pairs={{0,16},{4,20},{8,24},{12,28},{16,0},{20,4},{24,8},{28,12},{1,17},{... | collective-permute-start | bytes 393224 | tf_op jit(solution)/shard_map/ppermute | solution.py:432
  8.9 3.8 %densify.1 = (bf16[1024,2048]{1,0:T(8,128)(2,1)S(1)}, f32[16,128]{1,0:T(8,128)S(1)}) custom-call(s32[1,128]{1,0:T(1,128)} %bitcast.6, s32[1,1]{1,0:T(1,128)S(6)} %copy.11.counts_hbm, s32[128,128,128]{2,1,0:T(8,128)} %bitcast.5), custom_call_target="tpu_custom_call" | custom-call | flops 838860800 | tf_op jit(solution)/shard_map/densify/pallas_call | solution.py:50
  12.7 4.5 %collective-permute-done.1.got_ref = f32[16,128]{1,0:T(8,128)S(1)} collective-permute-done((f32[16,128]{1,0:T(8,128)S(1)}, f32[16,128]{1,0:T(8,128)S(1)}, u32[]{:S(2)}, u32[]{:S(2)}) %collective-permute-start.1) | collective-permute-done | bytes 8224 | tf_op jit(solution)/shard_map/ppermute | solution.py:432
  17.3 2.6 %collective-permute-start.7 = (f32[272,128]{1,0:T(8,128)S(1)}, f32[272,128]{1,0:T(8,128)S(1)}, u32[]{:S(2)}, u32[]{:S(2)}) collective-permute-start(f32[272,128]{1,0:T(8,128)S(1)} %message.1.refs_0_.refs_7_), channel_id=1, source_target_pairs={{0,12},{4,8},{8,4},{12,0},{16,28},{20,24},{24,20},{28,16},{1,13},{... | collective-permute-start | bytes 417800 | tf_op jit(solution)/shard_map/ppermute | solution.py:432
  21.5 1.8 %collective-permute-done.7.refs_3_.refs_10_ = f32[272,128]{1,0:T(8,128)S(1)} collective-permute-done((f32[272,128]{1,0:T(8,128)S(1)}, f32[272,128]{1,0:T(8,128)S(1)}, u32[]{:S(2)}, u32[]{:S(2)}) %collective-permute-start.7) | collective-permute-done | bytes 139296 | tf_op jit(solution)/shard_map/ppermute | solution.py:432
  23.3 1.6 %collective-permute-done.6.refs_2_.refs_9_ = f32[272,128]{1,0:T(8,128)S(1)} collective-permute-done((f32[272,128]{1,0:T(8,128)S(1)}, f32[272,128]{1,0:T(8,128)S(1)}, u32[]{:S(2)}, u32[]{:S(2)}) %collective-permute-start.6) | collective-permute-done | bytes 139296 | tf_op jit(solution)/shard_map/ppermute | solution.py:432
  25.8 1.0 %forward_first.1 = (f32[2,264,128]{2,1,0:T(8,128)S(1)}, bf16[2048,256]{1,0:T(8,128)(2,1)S(1)}) custom-call(bf16[1024,2048]{1,0:T(8,128)(2,1)S(1)} %get-tuple-element.26.dense_ref.refs_0_, f32[8,128]{1,0:T(8,128)S(1)} %row_totals.1.refs_1_.row_ref, f32[2048,128]{1,0:T(8,128)S(1)} %get-tuple-element.28.refs_2_, f32[256,128]{1,0:T(8,128)S(1)} %copy-done, ...), custom_call_target="tpu_custom_call" | custom-call | flops 536870912 | bytes 10522624 | tf_op jit(solution)/shard_map/forward_first/pallas_call | solution.py:50
  28.4 1.6 %collective-permute-start.9 = (f32[264,128]{1,0:T(8,128)S(1)}, f32[264,128]{1,0:T(8,128)S(1)}, u32[]{:S(2)}, u32[]{:S(2)}) collective-permute-start(f32[264,128]{1,0:T(8,128)S(1)} %pair_sums.1), channel_id=1, source_target_pairs={{0,2},{1,3},{2,0},{3,1},{4,6},{5,7},{6,4},{7,5},{8,10},{9,11},{10,... | collective-permute-start | bytes 405512 | tf_op jit(solution)/shard_map/ppermute | solution.py:432
  29.9 4.1 %collective-permute-done.9.refs_2_ = f32[264,128]{1,0:T(8,128)S(1)} collective-permute-done((f32[264,128]{1,0:T(8,128)S(1)}, f32[264,128]{1,0:T(8,128)S(1)}, u32[]{:S(2)}, u32[]{:S(2)}) %collective-permute-start.9) | collective-permute-done | bytes 135200 | tf_op jit(solution)/shard_map/ppermute | solution.py:432
  34.9 1.6 %collective-permute-start.12 = (f32[128,256]{1,0:T(8,128)S(1)}, f32[128,256]{1,0:T(8,128)S(1)}, u32[]{:S(2)}, u32[]{:S(2)}) collective-permute-start(f32[128,256]{1,0:T(8,128)S(1)} %get-tuple-element.32.back_ref), channel_id=1, source_target_pairs={{0,2},{1,3},{2,0},{3,1},{4,6},{5,7},{6,4},{7,5},{8,10},{9,11},{10,... | collective-permute-start | bytes 393224 | tf_op jit(solution)/shard_map/ppermute | solution.py:432
  36.8 3.1 %collective-permute-done.12.refs_3_ = f32[128,256]{1,0:T(8,128)S(1)} collective-permute-done((f32[128,256]{1,0:T(8,128)S(1)}, f32[128,256]{1,0:T(8,128)S(1)}, u32[]{:S(2)}, u32[]{:S(2)}) %collective-permute-start.12) | collective-permute-done | bytes 131104 | tf_op jit(solution)/shard_map/ppermute | solution.py:432
  42.1 1.0 %collective-permute-start.19 = (f32[128,256]{1,0:T(8,128)S(1)}, f32[128,256]{1,0:T(8,128)S(1)}, u32[]{:S(2)}, u32[]{:S(2)}) collective-permute-start(f32[128,256]{1,0:T(8,128)S(1)} %get-tuple-element.41), channel_id=1, source_target_pairs={{0,4},{4,0},{8,12},{12,8},{16,20},{20,16},{24,28},{28,24},{1,5},{5... | collective-permute-start | bytes 393224 | tf_op jit(solution)/shard_map/ppermute | solution.py:432
  43.1 1.6 %collective-permute-start.20 = (f32[128,256]{1,0:T(8,128)S(1)}, f32[128,256]{1,0:T(8,128)S(1)}, u32[]{:S(2)}, u32[]{:S(2)}) collective-permute-start(f32[128,256]{1,0:T(8,128)S(1)} %get-tuple-element.42), channel_id=1, source_target_pairs={{0,8},{4,12},{8,0},{12,4},{16,24},{20,28},{24,16},{28,20},{1,9},{5... | collective-permute-start | bytes 393224 | tf_op jit(solution)/shard_map/ppermute | solution.py:432
  45.6 1.4 %collective-permute-done.11.refs_1_ = f32[136,128]{1,0:T(8,128)S(1)} collective-permute-done((f32[136,128]{1,0:T(8,128)S(1)}, f32[136,128]{1,0:T(8,128)S(1)}, u32[]{:S(2)}, u32[]{:S(2)}) %collective-permute-start.11) | collective-permute-done | bytes 69664 | tf_op jit(solution)/shard_map/ppermute | solution.py:432
  48.1 1.0 %collective-permute-start.15 = (f32[128,256]{1,0:T(8,128)S(1)}, f32[128,256]{1,0:T(8,128)S(1)}, u32[]{:S(2)}, u32[]{:S(2)}) collective-permute-start(f32[128,256]{1,0:T(8,128)S(1)} %get-tuple-element.37), channel_id=1, source_target_pairs={{0,4},{4,0},{8,12},{12,8},{16,20},{20,16},{24,28},{28,24},{1,5},{5... | collective-permute-start | bytes 393224 | tf_op jit(solution)/shard_map/ppermute | solution.py:432
  49.1 1.9 %collective-permute-start.16 = (f32[128,256]{1,0:T(8,128)S(1)}, f32[128,256]{1,0:T(8,128)S(1)}, u32[]{:S(2)}, u32[]{:S(2)}) collective-permute-start(f32[128,256]{1,0:T(8,128)S(1)} %get-tuple-element.38), channel_id=1, source_target_pairs={{0,8},{4,12},{8,0},{12,4},{16,24},{20,28},{24,16},{28,20},{1,9},{5... | collective-permute-start | bytes 393224 | tf_op jit(solution)/shard_map/ppermute | solution.py:432
  51.6 1.4 %collective-permute-done.21.refs_3_ = f32[128,256]{1,0:T(8,128)S(1)} collective-permute-done((f32[128,256]{1,0:T(8,128)S(1)}, f32[128,256]{1,0:T(8,128)S(1)}, u32[]{:S(2)}, u32[]{:S(2)}) %collective-permute-start.21) | collective-permute-done | bytes 131104 | tf_op jit(solution)/shard_map/ppermute | solution.py:432
  53.1 1.5 %collective-permute-start.22 = (f32[128,256]{1,0:T(8,128)S(1)}, f32[128,256]{1,0:T(8,128)S(1)}, u32[]{:S(2)}, u32[]{:S(2)}) collective-permute-start(f32[128,256]{1,0:T(8,128)S(1)} %ahead_sums.1), channel_id=1, source_target_pairs={{0,16},{4,20},{8,24},{12,28},{16,0},{20,4},{24,8},{28,12},{1,17},{... | collective-permute-start | bytes 393224 | tf_op jit(solution)/shard_map/ppermute | solution.py:432
  54.6 1.6 %collective-permute-start.18 = (f32[136,128]{1,0:T(8,128)S(1)}, f32[136,128]{1,0:T(8,128)S(1)}, u32[]{:S(2)}, u32[]{:S(2)}) collective-permute-start(f32[136,128]{1,0:T(8,128)S(1)} %row2_grads.1.refs_0_), channel_id=1, source_target_pairs={{0,2},{1,3},{2,0},{3,1},{4,6},{5,7},{6,4},{7,5},{8,10},{9,11},{10,... | collective-permute-start | bytes 208904 | tf_op jit(solution)/shard_map/ppermute | solution.py:432
  56.8 2.2 %collective-permute-done.18.refs_1_ = f32[136,128]{1,0:T(8,128)S(1)} collective-permute-done((f32[136,128]{1,0:T(8,128)S(1)}, f32[136,128]{1,0:T(8,128)S(1)}, u32[]{:S(2)}, u32[]{:S(2)}) %collective-permute-start.18) | collective-permute-done | bytes 69664 | tf_op jit(solution)/shard_map/ppermute | solution.py:432
  59.9 2.1 %collective-permute-done.17.refs_3_ = f32[128,256]{1,0:T(8,128)S(1)} collective-permute-done((f32[128,256]{1,0:T(8,128)S(1)}, f32[128,256]{1,0:T(8,128)S(1)}, u32[]{:S(2)}, u32[]{:S(2)}) %collective-permute-start.17) | collective-permute-done | bytes 131104 | tf_op jit(solution)/shard_map/ppermute | solution.py:432
  62.1 1.3 %collective-permute-done.23.refs_2_ = f32[136,128]{1,0:T(8,128)S(1)} collective-permute-done((f32[136,128]{1,0:T(8,128)S(1)}, f32[136,128]{1,0:T(8,128)S(1)}, u32[]{:S(2)}, u32[]{:S(2)}) %collective-permute-start.23) | collective-permute-done | bytes 69664 | tf_op jit(solution)/shard_map/ppermute | solution.py:432
  (53 shorter events, 12.9 us)
Async XLA Ops:
  0.6 16.6 %collective-permute-start.3 = (f32[256,128]{1,0:T(8,128)}, f32[256,128]{1,0:T(8,128)S(1)}, u32[]{:S(2)}, u32[]{:S(2)}) collective-permute-start(f32[256,128]{1,0:T(8,128)} %refs_3_.2), channel_id=1, source_target_pairs={{0,8},{4,12},{8,0},{12,4},{16,24},{20,28},{24,16},{28,20},{1,9},{5... | collective-permute-start | bytes 393224 | tf_op jit(solution)/shard_map/ppermute | solution.py:432
  3.7 13.5 %collective-permute-start.2 = (f32[256,128]{1,0:T(8,128)}, f32[256,128]{1,0:T(8,128)S(1)}, u32[]{:S(2)}, u32[]{:S(2)}) collective-permute-start(f32[256,128]{1,0:T(8,128)} %refs_3_.2), channel_id=1, source_target_pairs={{0,4},{4,0},{8,12},{12,8},{16,20},{20,16},{24,28},{28,24},{1,5},{5... | collective-permute-start | bytes 393224 | tf_op jit(solution)/shard_map/ppermute | solution.py:432
  5.3 12.0 %collective-permute-start = (f32[256,128]{1,0:T(8,128)}, f32[256,128]{1,0:T(8,128)S(1)}, u32[]{:S(2)}, u32[]{:S(2)}) collective-permute-start(f32[256,128]{1,0:T(8,128)} %refs_3_.2), channel_id=1, source_target_pairs={{0,16},{4,20},{8,24},{12,28},{16,0},{20,4},{24,8},{28,12},{1,17},{... | collective-permute-start | bytes 393224 | tf_op jit(solution)/shard_map/ppermute | solution.py:432
  7.8 9.4 %collective-permute-start.4 = (f32[256,128]{1,0:T(8,128)}, f32[256,128]{1,0:T(8,128)S(1)}, u32[]{:S(2)}, u32[]{:S(2)}) collective-permute-start(f32[256,128]{1,0:T(8,128)} %refs_3_.2), channel_id=1, source_target_pairs={{0,12},{4,8},{8,4},{12,0},{16,28},{20,24},{24,20},{28,16},{1,13},{... | collective-permute-start | bytes 393224 | tf_op jit(solution)/shard_map/ppermute | solution.py:432
  12.6 4.6 %collective-permute-start.1 = (f32[16,128]{1,0:T(8,128)S(1)}, f32[16,128]{1,0:T(8,128)S(1)}, u32[]{:S(2)}, u32[]{:S(2)}) collective-permute-start(f32[16,128]{1,0:T(8,128)S(1)} %get-tuple-element.27.own_ref), channel_id=1, source_target_pairs={{0,16},{4,20},{8,24},{12,28},{16,0},{20,4},{24,8},{28,12},{1,17},{... | collective-permute-start | bytes 24584 | tf_op jit(solution)/shard_map/ppermute | solution.py:432
  17.3 6.0 %collective-permute-start.7 = (f32[272,128]{1,0:T(8,128)S(1)}, f32[272,128]{1,0:T(8,128)S(1)}, u32[]{:S(2)}, u32[]{:S(2)}) collective-permute-start(f32[272,128]{1,0:T(8,128)S(1)} %message.1.refs_0_.refs_7_), channel_id=1, source_target_pairs={{0,12},{4,8},{8,4},{12,0},{16,28},{20,24},{24,20},{28,16},{1,13},{... | collective-permute-start | bytes 417800 | tf_op jit(solution)/shard_map/ppermute | solution.py:432
  19.9 5.1 %collective-permute-start.6 = (f32[272,128]{1,0:T(8,128)S(1)}, f32[272,128]{1,0:T(8,128)S(1)}, u32[]{:S(2)}, u32[]{:S(2)}) collective-permute-start(f32[272,128]{1,0:T(8,128)S(1)} %message.1.refs_0_.refs_7_), channel_id=1, source_target_pairs={{0,8},{4,12},{8,0},{12,4},{16,24},{20,28},{24,16},{28,20},{1,9},{5... | collective-permute-start | bytes 417800 | tf_op jit(solution)/shard_map/ppermute | solution.py:432
  20.4 5.1 %collective-permute-start.5 = (f32[272,128]{1,0:T(8,128)S(1)}, f32[272,128]{1,0:T(8,128)S(1)}, u32[]{:S(2)}, u32[]{:S(2)}) collective-permute-start(f32[272,128]{1,0:T(8,128)S(1)} %message.1.refs_0_.refs_7_), channel_id=1, source_target_pairs={{0,4},{4,0},{8,12},{12,8},{16,20},{20,16},{24,28},{28,24},{1,5},{5... | collective-permute-start | bytes 417800 | tf_op jit(solution)/shard_map/ppermute | solution.py:432
  26.8 1.6 %collective-permute-start.8 = (f32[2,264,128]{2,1,0:T(8,128)S(1)}, f32[2,264,128]{2,1,0:T(8,128)S(1)}, u32[]{:S(2)}, u32[]{:S(2)}) collective-permute-start(f32[2,264,128]{2,1,0:T(8,128)S(1)} %get-tuple-element.30), channel_id=1, source_target_pairs={{0,1},{1,0},{2,3},{3,2},{4,5},{5,4},{6,7},{7,6},{8,9},{9,8},{10,11... | collective-permute-start | bytes 811016 | tf_op jit(solution)/shard_map/ppermute | solution.py:432
  28.4 5.7 %collective-permute-start.9 = (f32[264,128]{1,0:T(8,128)S(1)}, f32[264,128]{1,0:T(8,128)S(1)}, u32[]{:S(2)}, u32[]{:S(2)}) collective-permute-start(f32[264,128]{1,0:T(8,128)S(1)} %pair_sums.1), channel_id=1, source_target_pairs={{0,2},{1,3},{2,0},{3,1},{4,6},{5,7},{6,4},{7,5},{8,10},{9,11},{10,... | collective-permute-start | bytes 405512 | tf_op jit(solution)/shard_map/ppermute | solution.py:432
  34.9 5.0 %collective-permute-start.12 = (f32[128,256]{1,0:T(8,128)S(1)}, f32[128,256]{1,0:T(8,128)S(1)}, u32[]{:S(2)}, u32[]{:S(2)}) collective-permute-start(f32[128,256]{1,0:T(8,128)S(1)} %get-tuple-element.32.back_ref), channel_id=1, source_target_pairs={{0,2},{1,3},{2,0},{3,1},{4,6},{5,7},{6,4},{7,5},{8,10},{9,11},{10,... | collective-permute-start | bytes 393224 | tf_op jit(solution)/shard_map/ppermute | solution.py:432
  36.7 3.2 %collective-permute-start.10 = (f32[200,256]{1,0:T(8,128)S(1)}, f32[200,256]{1,0:T(8,128)S(1)}, u32[]{:S(2)}, u32[]{:S(2)}) collective-permute-start(f32[200,256]{1,0:T(8,128)S(1)} %weight_parts.1.own_ref.refs_1_), channel_id=1, source_target_pairs={{0,1},{1,0},{2,3},{3,2},{4,5},{5,4},{6,7},{7,6},{8,9},{9,8},{10,11... | collective-permute-start | bytes 614408 | tf_op jit(solution)/shard_map/ppermute | solution.py:432
  39.9 1.3 %collective-permute-start.13 = (f32[128,256]{1,0:T(8,128)S(1)}, f32[128,256]{1,0:T(8,128)S(1)}, u32[]{:S(2)}, u32[]{:S(2)}) collective-permute-start(f32[128,256]{1,0:T(8,128)S(1)} %collective-permute-done.12.refs_3_), channel_id=1, source_target_pairs={{0,1},{1,0},{2,3},{3,2},{4,5},{5,4},{6,7},{7,6},{8,9},{9,8},{10,11... | collective-permute-start | bytes 393224 | tf_op jit(solution)/shard_map/ppermute | solution.py:432
  39.9 7.2 %collective-permute-start.11 = (f32[136,128]{1,0:T(8,128)S(1)}, f32[136,128]{1,0:T(8,128)S(1)}, u32[]{:S(2)}, u32[]{:S(2)}) collective-permute-start(f32[136,128]{1,0:T(8,128)S(1)} %core_grads.1.refs_0_), channel_id=1, source_target_pairs={{0,16},{4,20},{8,24},{12,28},{16,0},{20,4},{24,8},{28,12},{1,17},{... | collective-permute-start | bytes 208904 | tf_op jit(solution)/shard_map/ppermute | solution.py:432
  42.1 7.0 %collective-permute-start.19 = (f32[128,256]{1,0:T(8,128)S(1)}, f32[128,256]{1,0:T(8,128)S(1)}, u32[]{:S(2)}, u32[]{:S(2)}) collective-permute-start(f32[128,256]{1,0:T(8,128)S(1)} %get-tuple-element.41), channel_id=1, source_target_pairs={{0,4},{4,0},{8,12},{12,8},{16,20},{20,16},{24,28},{28,24},{1,5},{5... | collective-permute-start | bytes 393224 | tf_op jit(solution)/shard_map/ppermute | solution.py:432
  43.1 7.9 %collective-permute-start.20 = (f32[128,256]{1,0:T(8,128)S(1)}, f32[128,256]{1,0:T(8,128)S(1)}, u32[]{:S(2)}, u32[]{:S(2)}) collective-permute-start(f32[128,256]{1,0:T(8,128)S(1)} %get-tuple-element.42), channel_id=1, source_target_pairs={{0,8},{4,12},{8,0},{12,4},{16,24},{20,28},{24,16},{28,20},{1,9},{5... | collective-permute-start | bytes 393224 | tf_op jit(solution)/shard_map/ppermute | solution.py:432
  44.7 8.4 %collective-permute-start.21 = (f32[128,256]{1,0:T(8,128)S(1)}, f32[128,256]{1,0:T(8,128)S(1)}, u32[]{:S(2)}, u32[]{:S(2)}) collective-permute-start(f32[128,256]{1,0:T(8,128)S(1)} %get-tuple-element.43), channel_id=1, source_target_pairs={{0,12},{4,8},{8,4},{12,0},{16,28},{20,24},{24,20},{28,16},{1,13},{... | collective-permute-start | bytes 393224 | tf_op jit(solution)/shard_map/ppermute | solution.py:432
  47.1 7.5 %collective-permute-start.14 = (f32[136,128]{1,0:T(8,128)S(1)}, f32[136,128]{1,0:T(8,128)S(1)}, u32[]{:S(2)}, u32[]{:S(2)}) collective-permute-start(f32[136,128]{1,0:T(8,128)S(1)} %held_grads.1.refs_0_), channel_id=1, source_target_pairs={{0,8},{4,12},{8,0},{12,4},{16,24},{20,28},{24,16},{28,20},{1,9},{5... | collective-permute-start | bytes 208904 | tf_op jit(solution)/shard_map/ppermute | solution.py:432
  48.1 11.8 %collective-permute-start.15 = (f32[128,256]{1,0:T(8,128)S(1)}, f32[128,256]{1,0:T(8,128)S(1)}, u32[]{:S(2)}, u32[]{:S(2)}) collective-permute-start(f32[128,256]{1,0:T(8,128)S(1)} %get-tuple-element.37), channel_id=1, source_target_pairs={{0,4},{4,0},{8,12},{12,8},{16,20},{20,16},{24,28},{28,24},{1,5},{5... | collective-permute-start | bytes 393224 | tf_op jit(solution)/shard_map/ppermute | solution.py:432
  49.1 10.8 %collective-permute-start.16 = (f32[128,256]{1,0:T(8,128)S(1)}, f32[128,256]{1,0:T(8,128)S(1)}, u32[]{:S(2)}, u32[]{:S(2)}) collective-permute-start(f32[128,256]{1,0:T(8,128)S(1)} %get-tuple-element.38), channel_id=1, source_target_pairs={{0,8},{4,12},{8,0},{12,4},{16,24},{20,28},{24,16},{28,20},{1,9},{5... | collective-permute-start | bytes 393224 | tf_op jit(solution)/shard_map/ppermute | solution.py:432
  51.0 11.0 %collective-permute-start.17 = (f32[128,256]{1,0:T(8,128)S(1)}, f32[128,256]{1,0:T(8,128)S(1)}, u32[]{:S(2)}, u32[]{:S(2)}) collective-permute-start(f32[128,256]{1,0:T(8,128)S(1)} %get-tuple-element.39), channel_id=1, source_target_pairs={{0,12},{4,8},{8,4},{12,0},{16,28},{20,24},{24,20},{28,16},{1,13},{... | collective-permute-start | bytes 393224 | tf_op jit(solution)/shard_map/ppermute | solution.py:432
  53.1 8.9 %collective-permute-start.22 = (f32[128,256]{1,0:T(8,128)S(1)}, f32[128,256]{1,0:T(8,128)S(1)}, u32[]{:S(2)}, u32[]{:S(2)}) collective-permute-start(f32[128,256]{1,0:T(8,128)S(1)} %ahead_sums.1), channel_id=1, source_target_pairs={{0,16},{4,20},{8,24},{12,28},{16,0},{20,4},{24,8},{28,12},{1,17},{... | collective-permute-start | bytes 393224 | tf_op jit(solution)/shard_map/ppermute | solution.py:432
  54.6 4.4 %collective-permute-start.18 = (f32[136,128]{1,0:T(8,128)S(1)}, f32[136,128]{1,0:T(8,128)S(1)}, u32[]{:S(2)}, u32[]{:S(2)}) collective-permute-start(f32[136,128]{1,0:T(8,128)S(1)} %row2_grads.1.refs_0_), channel_id=1, source_target_pairs={{0,2},{1,3},{2,0},{3,1},{4,6},{5,7},{6,4},{7,5},{8,10},{9,11},{10,... | collective-permute-start | bytes 208904 | tf_op jit(solution)/shard_map/ppermute | solution.py:432
  59.0 4.4 %collective-permute-start.23 = (f32[136,128]{1,0:T(8,128)S(1)}, f32[136,128]{1,0:T(8,128)S(1)}, u32[]{:S(2)}, u32[]{:S(2)}) collective-permute-start(f32[136,128]{1,0:T(8,128)S(1)} %col2_grads.1.refs_4_.refs_1_), channel_id=1, source_target_pairs={{0,4},{4,0},{8,12},{12,8},{16,20},{20,16},{24,28},{28,24},{1,5},{5... | collective-permute-start | bytes 208904 | tf_op jit(solution)/shard_map/ppermute | solution.py:432
  (4 other events, 64.8 us)

commit v12 on v11

--- a/solution.py
+++ b/solution.py
@@ -100,7 +100,7 @@
 
     for p in range(pieces):
         copies[p].wait()
-        lax.fori_loop(p * piece, (p + 1) * piece, place, 0, unroll=4)
+        lax.fori_loop(p * piece, (p + 1) * piece, place, 0, unroll=8)
     col_ref[...] = jnp.sum(col_acc[...], axis=1)
 
 

time: 64.3 us -> 64.2 us (level)
  no operation moved by 1% of the time
where the time goes in v12:
time: 64.2 us; the launch traced here: 64.1 us
  starting transfers between devices  26.1 us (41%)
  waiting for transfers between devices  25.8 us (40%)
  Pallas kernels  10.7 us (17%)
  between operations  1.46 us (2%)
    ppermute x24, starting transfers between devices, swap(): return lax.ppermute(value, axis, [(i, i ^ mask) for i in range(count)])  26.1 us
    ppermute x24, waiting for transfers between devices, swap(): return lax.ppermute(value, axis, [(i, i ^ mask) for i in range(count)])  25.8 us
    pallas_call x21, Pallas kernels, call(): pl.pallas_call(kernel, out_shape=tuple(outs), in_specs=list(before_specs)...  10.7 us
  transfers between devices with their start and end apart: 24, of which 13 were waited for; matrix products, arithmetic and copies ran while one was open for 0% of the time, Pallas kernels for 12%

profile of v12, /device:TPU:0, one launch (start us, length us, event | category | flops | bytes accessed | tf_op | source)
XLA Modules:
  0.0 64.1 jit_solution(3021629207828388215)
XLA Ops:
  0.6 3.1 %collective-permute-start.3 = (f32[256,128]{1,0:T(8,128)}, f32[256,128]{1,0:T(8,128)S(1)}, u32[]{:S(2)}, u32[]{:S(2)}) collective-permute-start(f32[256,128]{1,0:T(8,128)} %refs_3_.2), channel_id=1, source_target_pairs={{0,8},{4,12},{8,0},{12,4},{16,24},{20,28},{24,16},{28,20},{1,9},{5... | collective-permute-start | bytes 393224 | tf_op jit(solution)/shard_map/ppermute | solution.py:432
  3.7 1.5 %collective-permute-start.2 = (f32[256,128]{1,0:T(8,128)}, f32[256,128]{1,0:T(8,128)S(1)}, u32[]{:S(2)}, u32[]{:S(2)}) collective-permute-start(f32[256,128]{1,0:T(8,128)} %refs_3_.2), channel_id=1, source_target_pairs={{0,4},{4,0},{8,12},{12,8},{16,20},{20,16},{24,28},{28,24},{1,5},{5... | collective-permute-start | bytes 393224 | tf_op jit(solution)/shard_map/ppermute | solution.py:432
  5.3 2.6 %collective-permute-start = (f32[256,128]{1,0:T(8,128)}, f32[256,128]{1,0:T(8,128)S(1)}, u32[]{:S(2)}, u32[]{:S(2)}) collective-permute-start(f32[256,128]{1,0:T(8,128)} %refs_3_.2), channel_id=1, source_target_pairs={{0,16},{4,20},{8,24},{12,28},{16,0},{20,4},{24,8},{28,12},{1,17},{... | collective-permute-start | bytes 393224 | tf_op jit(solution)/shard_map/ppermute | solution.py:432
  8.9 3.7 %densify.1 = (bf16[1024,2048]{1,0:T(8,128)(2,1)S(1)}, f32[16,128]{1,0:T(8,128)S(1)}) custom-call(s32[1,128]{1,0:T(1,128)} %bitcast.6, s32[1,1]{1,0:T(1,128)S(6)} %copy.11.counts_hbm, s32[128,128,128]{2,1,0:T(8,128)} %bitcast.5), custom_call_target="tpu_custom_call" | custom-call | flops 838860800 | tf_op jit(solution)/shard_map/densify/pallas_call | solution.py:50
  12.7 4.5 %collective-permute-done.1.got_ref = f32[16,128]{1,0:T(8,128)S(1)} collective-permute-done((f32[16,128]{1,0:T(8,128)S(1)}, f32[16,128]{1,0:T(8,128)S(1)}, u32[]{:S(2)}, u32[]{:S(2)}) %collective-permute-start.1) | collective-permute-done | bytes 8224 | tf_op jit(solution)/shard_map/ppermute | solution.py:432
  17.3 2.6 %collective-permute-start.7 = (f32[272,128]{1,0:T(8,128)S(1)}, f32[272,128]{1,0:T(8,128)S(1)}, u32[]{:S(2)}, u32[]{:S(2)}) collective-permute-start(f32[272,128]{1,0:T(8,128)S(1)} %message.1.refs_0_.refs_7_), channel_id=1, source_target_pairs={{0,12},{4,8},{8,4},{12,0},{16,28},{20,24},{24,20},{28,16},{1,13},{... | collective-permute-start | bytes 417800 | tf_op jit(solution)/shard_map/ppermute | solution.py:432
  21.5 1.8 %collective-permute-done.7.refs_3_.refs_10_ = f32[272,128]{1,0:T(8,128)S(1)} collective-permute-done((f32[272,128]{1,0:T(8,128)S(1)}, f32[272,128]{1,0:T(8,128)S(1)}, u32[]{:S(2)}, u32[]{:S(2)}) %collective-permute-start.7) | collective-permute-done | bytes 139296 | tf_op jit(solution)/shard_map/ppermute | solution.py:432
  23.3 1.6 %collective-permute-done.6.refs_2_.refs_9_ = f32[272,128]{1,0:T(8,128)S(1)} collective-permute-done((f32[272,128]{1,0:T(8,128)S(1)}, f32[272,128]{1,0:T(8,128)S(1)}, u32[]{:S(2)}, u32[]{:S(2)}) %collective-permute-start.6) | collective-permute-done | bytes 139296 | tf_op jit(solution)/shard_map/ppermute | solution.py:432
  25.7 1.0 %forward_first.1 = (f32[2,264,128]{2,1,0:T(8,128)S(1)}, bf16[2048,256]{1,0:T(8,128)(2,1)S(1)}) custom-call(bf16[1024,2048]{1,0:T(8,128)(2,1)S(1)} %get-tuple-element.26.dense_ref.refs_0_, f32[8,128]{1,0:T(8,128)S(1)} %row_totals.1.refs_1_.row_ref, f32[2048,128]{1,0:T(8,128)S(1)} %get-tuple-element.28.refs_2_, f32[256,128]{1,0:T(8,128)S(1)} %copy-done, ...), custom_call_target="tpu_custom_call" | custom-call | flops 536870912 | bytes 10522624 | tf_op jit(solution)/shard_map/forward_first/pallas_call | solution.py:50
  28.4 1.6 %collective-permute-start.9 = (f32[264,128]{1,0:T(8,128)S(1)}, f32[264,128]{1,0:T(8,128)S(1)}, u32[]{:S(2)}, u32[]{:S(2)}) collective-permute-start(f32[264,128]{1,0:T(8,128)S(1)} %pair_sums.1), channel_id=1, source_target_pairs={{0,2},{1,3},{2,0},{3,1},{4,6},{5,7},{6,4},{7,5},{8,10},{9,11},{10,... | collective-permute-start | bytes 405512 | tf_op jit(solution)/shard_map/ppermute | solution.py:432
  29.9 4.1 %collective-permute-done.9.refs_2_ = f32[264,128]{1,0:T(8,128)S(1)} collective-permute-done((f32[264,128]{1,0:T(8,128)S(1)}, f32[264,128]{1,0:T(8,128)S(1)}, u32[]{:S(2)}, u32[]{:S(2)}) %collective-permute-start.9) | collective-permute-done | bytes 135200 | tf_op jit(solution)/shard_map/ppermute | solution.py:432
  34.8 1.6 %collective-permute-start.12 = (f32[128,256]{1,0:T(8,128)S(1)}, f32[128,256]{1,0:T(8,128)S(1)}, u32[]{:S(2)}, u32[]{:S(2)}) collective-permute-start(f32[128,256]{1,0:T(8,128)S(1)} %get-tuple-element.32.back_ref), channel_id=1, source_target_pairs={{0,2},{1,3},{2,0},{3,1},{4,6},{5,7},{6,4},{7,5},{8,10},{9,11},{10,... | collective-permute-start | bytes 393224 | tf_op jit(solution)/shard_map/ppermute | solution.py:432
  36.8 3.1 %collective-permute-done.12.refs_3_ = f32[128,256]{1,0:T(8,128)S(1)} collective-permute-done((f32[128,256]{1,0:T(8,128)S(1)}, f32[128,256]{1,0:T(8,128)S(1)}, u32[]{:S(2)}, u32[]{:S(2)}) %collective-permute-start.12) | collective-permute-done | bytes 131104 | tf_op jit(solution)/shard_map/ppermute | solution.py:432
  42.1 1.0 %collective-permute-start.19 = (f32[128,256]{1,0:T(8,128)S(1)}, f32[128,256]{1,0:T(8,128)S(1)}, u32[]{:S(2)}, u32[]{:S(2)}) collective-permute-start(f32[128,256]{1,0:T(8,128)S(1)} %get-tuple-element.41), channel_id=1, source_target_pairs={{0,4},{4,0},{8,12},{12,8},{16,20},{20,16},{24,28},{28,24},{1,5},{5... | collective-permute-start | bytes 393224 | tf_op jit(solution)/shard_map/ppermute | solution.py:432
  43.1 1.6 %collective-permute-start.20 = (f32[128,256]{1,0:T(8,128)S(1)}, f32[128,256]{1,0:T(8,128)S(1)}, u32[]{:S(2)}, u32[]{:S(2)}) collective-permute-start(f32[128,256]{1,0:T(8,128)S(1)} %get-tuple-element.42), channel_id=1, source_target_pairs={{0,8},{4,12},{8,0},{12,4},{16,24},{20,28},{24,16},{28,20},{1,9},{5... | collective-permute-start | bytes 393224 | tf_op jit(solution)/shard_map/ppermute | solution.py:432
  45.6 1.4 %collective-permute-done.11.refs_1_ = f32[136,128]{1,0:T(8,128)S(1)} collective-permute-done((f32[136,128]{1,0:T(8,128)S(1)}, f32[136,128]{1,0:T(8,128)S(1)}, u32[]{:S(2)}, u32[]{:S(2)}) %collective-permute-start.11) | collective-permute-done | bytes 69664 | tf_op jit(solution)/shard_map/ppermute | solution.py:432
  48.0 1.0 %collective-permute-start.15 = (f32[128,256]{1,0:T(8,128)S(1)}, f32[128,256]{1,0:T(8,128)S(1)}, u32[]{:S(2)}, u32[]{:S(2)}) collective-permute-start(f32[128,256]{1,0:T(8,128)S(1)} %get-tuple-element.37), channel_id=1, source_target_pairs={{0,4},{4,0},{8,12},{12,8},{16,20},{20,16},{24,28},{28,24},{1,5},{5... | collective-permute-start | bytes 393224 | tf_op jit(solution)/shard_map/ppermute | solution.py:432
  49.0 1.9 %collective-permute-start.16 = (f32[128,256]{1,0:T(8,128)S(1)}, f32[128,256]{1,0:T(8,128)S(1)}, u32[]{:S(2)}, u32[]{:S(2)}) collective-permute-start(f32[128,256]{1,0:T(8,128)S(1)} %get-tuple-element.38), channel_id=1, source_target_pairs={{0,8},{4,12},{8,0},{12,4},{16,24},{20,28},{24,16},{28,20},{1,9},{5... | collective-permute-start | bytes 393224 | tf_op jit(solution)/shard_map/ppermute | solution.py:432
  51.6 1.4 %collective-permute-done.21.refs_3_ = f32[128,256]{1,0:T(8,128)S(1)} collective-permute-done((f32[128,256]{1,0:T(8,128)S(1)}, f32[128,256]{1,0:T(8,128)S(1)}, u32[]{:S(2)}, u32[]{:S(2)}) %collective-permute-start.21) | collective-permute-done | bytes 131104 | tf_op jit(solution)/shard_map/ppermute | solution.py:432
  53.1 1.5 %collective-permute-start.22 = (f32[128,256]{1,0:T(8,128)S(1)}, f32[128,256]{1,0:T(8,128)S(1)}, u32[]{:S(2)}, u32[]{:S(2)}) collective-permute-start(f32[128,256]{1,0:T(8,128)S(1)} %ahead_sums.1), channel_id=1, source_target_pairs={{0,16},{4,20},{8,24},{12,28},{16,0},{20,4},{24,8},{28,12},{1,17},{... | collective-permute-start | bytes 393224 | tf_op jit(solution)/shard_map/ppermute | solution.py:432
  54.6 1.6 %collective-permute-start.18 = (f32[136,128]{1,0:T(8,128)S(1)}, f32[136,128]{1,0:T(8,128)S(1)}, u32[]{:S(2)}, u32[]{:S(2)}) collective-permute-start(f32[136,128]{1,0:T(8,128)S(1)} %row2_grads.1.refs_0_), channel_id=1, source_target_pairs={{0,2},{1,3},{2,0},{3,1},{4,6},{5,7},{6,4},{7,5},{8,10},{9,11},{10,... | collective-permute-start | bytes 208904 | tf_op jit(solution)/shard_map/ppermute | solution.py:432
  56.8 2.2 %collective-permute-done.18.refs_1_ = f32[136,128]{1,0:T(8,128)S(1)} collective-permute-done((f32[136,128]{1,0:T(8,128)S(1)}, f32[136,128]{1,0:T(8,128)S(1)}, u32[]{:S(2)}, u32[]{:S(2)}) %collective-permute-start.18) | collective-permute-done | bytes 69664 | tf_op jit(solution)/shard_map/ppermute | solution.py:432
  59.9 2.1 %collective-permute-done.17.refs_3_ = f32[128,256]{1,0:T(8,128)S(1)} collective-permute-done((f32[128,256]{1,0:T(8,128)S(1)}, f32[128,256]{1,0:T(8,128)S(1)}, u32[]{:S(2)}, u32[]{:S(2)}) %collective-permute-start.17) | collective-permute-done | bytes 131104 | tf_op jit(solution)/shard_map/ppermute | solution.py:432
  62.0 1.3 %collective-permute-done.23.refs_2_ = f32[136,128]{1,0:T(8,128)S(1)} collective-permute-done((f32[136,128]{1,0:T(8,128)S(1)}, f32[136,128]{1,0:T(8,128)S(1)}, u32[]{:S(2)}, u32[]{:S(2)}) %collective-permute-start.23) | collective-permute-done | bytes 69664 | tf_op jit(solution)/shard_map/ppermute | solution.py:432
  (53 shorter events, 12.9 us)
Async XLA Ops:
  0.6 16.6 %collective-permute-start.3 = (f32[256,128]{1,0:T(8,128)}, f32[256,128]{1,0:T(8,128)S(1)}, u32[]{:S(2)}, u32[]{:S(2)}) collective-permute-start(f32[256,128]{1,0:T(8,128)} %refs_3_.2), channel_id=1, source_target_pairs={{0,8},{4,12},{8,0},{12,4},{16,24},{20,28},{24,16},{28,20},{1,9},{5... | collective-permute-start | bytes 393224 | tf_op jit(solution)/shard_map/ppermute | solution.py:432
  3.7 13.5 %collective-permute-start.2 = (f32[256,128]{1,0:T(8,128)}, f32[256,128]{1,0:T(8,128)S(1)}, u32[]{:S(2)}, u32[]{:S(2)}) collective-permute-start(f32[256,128]{1,0:T(8,128)} %refs_3_.2), channel_id=1, source_target_pairs={{0,4},{4,0},{8,12},{12,8},{16,20},{20,16},{24,28},{28,24},{1,5},{5... | collective-permute-start | bytes 393224 | tf_op jit(solution)/shard_map/ppermute | solution.py:432
  5.3 12.0 %collective-permute-start = (f32[256,128]{1,0:T(8,128)}, f32[256,128]{1,0:T(8,128)S(1)}, u32[]{:S(2)}, u32[]{:S(2)}) collective-permute-start(f32[256,128]{1,0:T(8,128)} %refs_3_.2), channel_id=1, source_target_pairs={{0,16},{4,20},{8,24},{12,28},{16,0},{20,4},{24,8},{28,12},{1,17},{... | collective-permute-start | bytes 393224 | tf_op jit(solution)/shard_map/ppermute | solution.py:432
  7.8 9.4 %collective-permute-start.4 = (f32[256,128]{1,0:T(8,128)}, f32[256,128]{1,0:T(8,128)S(1)}, u32[]{:S(2)}, u32[]{:S(2)}) collective-permute-start(f32[256,128]{1,0:T(8,128)} %refs_3_.2), channel_id=1, source_target_pairs={{0,12},{4,8},{8,4},{12,0},{16,28},{20,24},{24,20},{28,16},{1,13},{... | collective-permute-start | bytes 393224 | tf_op jit(solution)/shard_map/ppermute | solution.py:432
  12.6 4.6 %collective-permute-start.1 = (f32[16,128]{1,0:T(8,128)S(1)}, f32[16,128]{1,0:T(8,128)S(1)}, u32[]{:S(2)}, u32[]{:S(2)}) collective-permute-start(f32[16,128]{1,0:T(8,128)S(1)} %get-tuple-element.27.own_ref), channel_id=1, source_target_pairs={{0,16},{4,20},{8,24},{12,28},{16,0},{20,4},{24,8},{28,12},{1,17},{... | collective-permute-start | bytes 24584 | tf_op jit(solution)/shard_map/ppermute | solution.py:432
  17.3 6.0 %collective-permute-start.7 = (f32[272,128]{1,0:T(8,128)S(1)}, f32[272,128]{1,0:T(8,128)S(1)}, u32[]{:S(2)}, u32[]{:S(2)}) collective-permute-start(f32[272,128]{1,0:T(8,128)S(1)} %message.1.refs_0_.refs_7_), channel_id=1, source_target_pairs={{0,12},{4,8},{8,4},{12,0},{16,28},{20,24},{24,20},{28,16},{1,13},{... | collective-permute-start | bytes 417800 | tf_op jit(solution)/shard_map/ppermute | solution.py:432
  19.9 5.1 %collective-permute-start.6 = (f32[272,128]{1,0:T(8,128)S(1)}, f32[272,128]{1,0:T(8,128)S(1)}, u32[]{:S(2)}, u32[]{:S(2)}) collective-permute-start(f32[272,128]{1,0:T(8,128)S(1)} %message.1.refs_0_.refs_7_), channel_id=1, source_target_pairs={{0,8},{4,12},{8,0},{12,4},{16,24},{20,28},{24,16},{28,20},{1,9},{5... | collective-permute-start | bytes 417800 | tf_op jit(solution)/shard_map/ppermute | solution.py:432
  20.3 5.1 %collective-permute-start.5 = (f32[272,128]{1,0:T(8,128)S(1)}, f32[272,128]{1,0:T(8,128)S(1)}, u32[]{:S(2)}, u32[]{:S(2)}) collective-permute-start(f32[272,128]{1,0:T(8,128)S(1)} %message.1.refs_0_.refs_7_), channel_id=1, source_target_pairs={{0,4},{4,0},{8,12},{12,8},{16,20},{20,16},{24,28},{28,24},{1,5},{5... | collective-permute-start | bytes 417800 | tf_op jit(solution)/shard_map/ppermute | solution.py:432
  26.7 1.6 %collective-permute-start.8 = (f32[2,264,128]{2,1,0:T(8,128)S(1)}, f32[2,264,128]{2,1,0:T(8,128)S(1)}, u32[]{:S(2)}, u32[]{:S(2)}) collective-permute-start(f32[2,264,128]{2,1,0:T(8,128)S(1)} %get-tuple-element.30), channel_id=1, source_target_pairs={{0,1},{1,0},{2,3},{3,2},{4,5},{5,4},{6,7},{7,6},{8,9},{9,8},{10,11... | collective-permute-start | bytes 811016 | tf_op jit(solution)/shard_map/ppermute | solution.py:432
  28.4 5.7 %collective-permute-start.9 = (f32[264,128]{1,0:T(8,128)S(1)}, f32[264,128]{1,0:T(8,128)S(1)}, u32[]{:S(2)}, u32[]{:S(2)}) collective-permute-start(f32[264,128]{1,0:T(8,128)S(1)} %pair_sums.1), channel_id=1, source_target_pairs={{0,2},{1,3},{2,0},{3,1},{4,6},{5,7},{6,4},{7,5},{8,10},{9,11},{10,... | collective-permute-start | bytes 405512 | tf_op jit(solution)/shard_map/ppermute | solution.py:432
  34.8 5.0 %collective-permute-start.12 = (f32[128,256]{1,0:T(8,128)S(1)}, f32[128,256]{1,0:T(8,128)S(1)}, u32[]{:S(2)}, u32[]{:S(2)}) collective-permute-start(f32[128,256]{1,0:T(8,128)S(1)} %get-tuple-element.32.back_ref), channel_id=1, source_target_pairs={{0,2},{1,3},{2,0},{3,1},{4,6},{5,7},{6,4},{7,5},{8,10},{9,11},{10,... | collective-permute-start | bytes 393224 | tf_op jit(solution)/shard_map/ppermute | solution.py:432
  36.7 3.2 %collective-permute-start.10 = (f32[200,256]{1,0:T(8,128)S(1)}, f32[200,256]{1,0:T(8,128)S(1)}, u32[]{:S(2)}, u32[]{:S(2)}) collective-permute-start(f32[200,256]{1,0:T(8,128)S(1)} %weight_parts.1.own_ref.refs_1_), channel_id=1, source_target_pairs={{0,1},{1,0},{2,3},{3,2},{4,5},{5,4},{6,7},{7,6},{8,9},{9,8},{10,11... | collective-permute-start | bytes 614408 | tf_op jit(solution)/shard_map/ppermute | solution.py:432
  39.9 1.3 %collective-permute-start.13 = (f32[128,256]{1,0:T(8,128)S(1)}, f32[128,256]{1,0:T(8,128)S(1)}, u32[]{:S(2)}, u32[]{:S(2)}) collective-permute-start(f32[128,256]{1,0:T(8,128)S(1)} %collective-permute-done.12.refs_3_), channel_id=1, source_target_pairs={{0,1},{1,0},{2,3},{3,2},{4,5},{5,4},{6,7},{7,6},{8,9},{9,8},{10,11... | collective-permute-start | bytes 393224 | tf_op jit(solution)/shard_map/ppermute | solution.py:432
  39.9 7.2 %collective-permute-start.11 = (f32[136,128]{1,0:T(8,128)S(1)}, f32[136,128]{1,0:T(8,128)S(1)}, u32[]{:S(2)}, u32[]{:S(2)}) collective-permute-start(f32[136,128]{1,0:T(8,128)S(1)} %core_grads.1.refs_0_), channel_id=1, source_target_pairs={{0,16},{4,20},{8,24},{12,28},{16,0},{20,4},{24,8},{28,12},{1,17},{... | collective-permute-start | bytes 208904 | tf_op jit(solution)/shard_map/ppermute | solution.py:432
  42.1 7.0 %collective-permute-start.19 = (f32[128,256]{1,0:T(8,128)S(1)}, f32[128,256]{1,0:T(8,128)S(1)}, u32[]{:S(2)}, u32[]{:S(2)}) collective-permute-start(f32[128,256]{1,0:T(8,128)S(1)} %get-tuple-element.41), channel_id=1, source_target_pairs={{0,4},{4,0},{8,12},{12,8},{16,20},{20,16},{24,28},{28,24},{1,5},{5... | collective-permute-start | bytes 393224 | tf_op jit(solution)/shard_map/ppermute | solution.py:432
  43.1 7.9 %collective-permute-start.20 = (f32[128,256]{1,0:T(8,128)S(1)}, f32[128,256]{1,0:T(8,128)S(1)}, u32[]{:S(2)}, u32[]{:S(2)}) collective-permute-start(f32[128,256]{1,0:T(8,128)S(1)} %get-tuple-element.42), channel_id=1, source_target_pairs={{0,8},{4,12},{8,0},{12,4},{16,24},{20,28},{24,16},{28,20},{1,9},{5... | collective-permute-start | bytes 393224 | tf_op jit(solution)/shard_map/ppermute | solution.py:432
  44.7 8.4 %collective-permute-start.21 = (f32[128,256]{1,0:T(8,128)S(1)}, f32[128,256]{1,0:T(8,128)S(1)}, u32[]{:S(2)}, u32[]{:S(2)}) collective-permute-start(f32[128,256]{1,0:T(8,128)S(1)} %get-tuple-element.43), channel_id=1, source_target_pairs={{0,12},{4,8},{8,4},{12,0},{16,28},{20,24},{24,20},{28,16},{1,13},{... | collective-permute-start | bytes 393224 | tf_op jit(solution)/shard_map/ppermute | solution.py:432
  47.1 7.4 %collective-permute-start.14 = (f32[136,128]{1,0:T(8,128)S(1)}, f32[136,128]{1,0:T(8,128)S(1)}, u32[]{:S(2)}, u32[]{:S(2)}) collective-permute-start(f32[136,128]{1,0:T(8,128)S(1)} %held_grads.1.refs_0_), channel_id=1, source_target_pairs={{0,8},{4,12},{8,0},{12,4},{16,24},{20,28},{24,16},{28,20},{1,9},{5... | collective-permute-start | bytes 208904 | tf_op jit(solution)/shard_map/ppermute | solution.py:432
  48.0 11.8 %collective-permute-start.15 = (f32[128,256]{1,0:T(8,128)S(1)}, f32[128,256]{1,0:T(8,128)S(1)}, u32[]{:S(2)}, u32[]{:S(2)}) collective-permute-start(f32[128,256]{1,0:T(8,128)S(1)} %get-tuple-element.37), channel_id=1, source_target_pairs={{0,4},{4,0},{8,12},{12,8},{16,20},{20,16},{24,28},{28,24},{1,5},{5... | collective-permute-start | bytes 393224 | tf_op jit(solution)/shard_map/ppermute | solution.py:432
  49.0 10.8 %collective-permute-start.16 = (f32[128,256]{1,0:T(8,128)S(1)}, f32[128,256]{1,0:T(8,128)S(1)}, u32[]{:S(2)}, u32[]{:S(2)}) collective-permute-start(f32[128,256]{1,0:T(8,128)S(1)} %get-tuple-element.38), channel_id=1, source_target_pairs={{0,8},{4,12},{8,0},{12,4},{16,24},{20,28},{24,16},{28,20},{1,9},{5... | collective-permute-start | bytes 393224 | tf_op jit(solution)/shard_map/ppermute | solution.py:432
  50.9 11.0 %collective-permute-start.17 = (f32[128,256]{1,0:T(8,128)S(1)}, f32[128,256]{1,0:T(8,128)S(1)}, u32[]{:S(2)}, u32[]{:S(2)}) collective-permute-start(f32[128,256]{1,0:T(8,128)S(1)} %get-tuple-element.39), channel_id=1, source_target_pairs={{0,12},{4,8},{8,4},{12,0},{16,28},{20,24},{24,20},{28,16},{1,13},{... | collective-permute-start | bytes 393224 | tf_op jit(solution)/shard_map/ppermute | solution.py:432
  53.1 8.9 %collective-permute-start.22 = (f32[128,256]{1,0:T(8,128)S(1)}, f32[128,256]{1,0:T(8,128)S(1)}, u32[]{:S(2)}, u32[]{:S(2)}) collective-permute-start(f32[128,256]{1,0:T(8,128)S(1)} %ahead_sums.1), channel_id=1, source_target_pairs={{0,16},{4,20},{8,24},{12,28},{16,0},{20,4},{24,8},{28,12},{1,17},{... | collective-permute-start | bytes 393224 | tf_op jit(solution)/shard_map/ppermute | solution.py:432
  54.6 4.4 %collective-permute-start.18 = (f32[136,128]{1,0:T(8,128)S(1)}, f32[136,128]{1,0:T(8,128)S(1)}, u32[]{:S(2)}, u32[]{:S(2)}) collective-permute-start(f32[136,128]{1,0:T(8,128)S(1)} %row2_grads.1.refs_0_), channel_id=1, source_target_pairs={{0,2},{1,3},{2,0},{3,1},{4,6},{5,7},{6,4},{7,5},{8,10},{9,11},{10,... | collective-permute-start | bytes 208904 | tf_op jit(solution)/shard_map/ppermute | solution.py:432
  58.9 4.4 %collective-permute-start.23 = (f32[136,128]{1,0:T(8,128)S(1)}, f32[136,128]{1,0:T(8,128)S(1)}, u32[]{:S(2)}, u32[]{:S(2)}) collective-permute-start(f32[136,128]{1,0:T(8,128)S(1)} %col2_grads.1.refs_4_.refs_1_), channel_id=1, source_target_pairs={{0,4},{4,0},{8,12},{12,8},{16,20},{20,16},{24,28},{28,24},{1,5},{5... | collective-permute-start | bytes 208904 | tf_op jit(solution)/shard_map/ppermute | solution.py:432
  (4 other events, 64.8 us)
